TPU v7x, 256 devices: a whole 4x4x8 slice. The times are simulated.
256 devices in a mesh: expert: 16 (over z, x_lo), tensor: 16 (over x_hi, y, core).
Axes of the slice: x: 4 (x_hi: 2, x_lo: 2; x = x_hi * 2 + x_lo), y: 4, z: 8, core: 2. Of those that a mesh axis runs over, the one named last changes fastest.
Arguments:
- context: bfloat16 [2048, 8192], P('expert', 'tensor'), may hold values from -6 to 6
- proj_weight: bfloat16 [8192, 4096], P('tensor', 'expert'), may hold values from -0.0625 to 0.0625
- norm_gain: float32 [4096], replicated, may hold values from 0.1 to 1.9
- expert_ids: int32 [2048, 8], P(('expert', 'tensor')), may hold values from 0 to 63, all different within a row; in each aligned block of 8 rows (0 to 7, 8 to 15, ...) at most 2 rows name the same one
- gate_values: float32 [2048, 8], P(('expert', 'tensor')), may hold values from 0.1 to 1
- w_gate: bfloat16 [256, 4096, 384], P(('expert', 'tensor')), may hold values from -0.09375 to 0.09375
- w_up: bfloat16 [256, 4096, 384], P(('expert', 'tensor')), may hold values from -0.09375 to 0.09375
- w_down: bfloat16 [256, 384, 4096], P(('expert', 'tensor')), may hold values from -0.15625 to 0.15625
Outputs:
- mixed: bfloat16 [2048, 4096], P(('expert', 'tensor'))
Inputs may be any that keep to these rules, and one draw needn't show every extreme that they name: `expert_ids`: each row names 8 different experts. The tokens fall into aligned blocks of 8 rows, block b holding tokens b * 8 to (b + 1) * 8 - 1; in every block no expert is named by more than 2 rows, a bound that some block reaches.
All inputs are finite; a program needn't handle non-finite values.
Results may differ from a plain program's by a relative error of at most 0.024.
Values may be sent and summed in bfloat16 or wider, within the bound.
No kernel may reach another device: no remote copies, remote signals or barrier semaphores. Data moves between devices by JAX's collectives and lax.ppermute only.
A program may use at most 128 MiB of HBM per device.

v0:
```python
import jax
import jax.numpy as jnp
from jax import lax
from jax.sharding import PartitionSpec as P

TOPK = 8


def expert_apply(block_rows, w_gate, w_up, w_down):
    row_shape = block_rows.shape
    flat_rows = block_rows.reshape(-1, row_shape[-1])
    gate_act = jnp.dot(flat_rows, w_gate[0], preferred_element_type=jnp.float32)
    up_act = jnp.dot(flat_rows, w_up[0], preferred_element_type=jnp.float32)
    hidden = (jax.nn.silu(gate_act) * up_act).astype(jnp.bfloat16)
    partial_out = jnp.dot(hidden, w_down[0], preferred_element_type=jnp.float32).astype(
        jnp.bfloat16
    )
    return partial_out.reshape(row_shape[:-1] + (partial_out.shape[-1],))


def on_device(context, proj_weight, norm_gain, expert_ids, gate_values, w_gate, w_up, w_down):
    owner_count = lax.axis_size("expert")
    tensor_count = lax.axis_size("tensor")
    full_proj = lax.all_gather(proj_weight, "expert", axis=1, tiled=True)
    row_share = context.shape[0] // tensor_count
    attended = lax.psum_scatter(
        jnp.dot(context, full_proj, preferred_element_type=jnp.float32),
        "tensor",
        scatter_dimension=0,
        tiled=True,
    ).astype(jnp.bfloat16)
    stream = attended.astype(jnp.float32)
    scale = lax.rsqrt(jnp.mean(stream * stream, axis=-1, keepdims=True) + 1e-06)
    normed = (stream * scale * norm_gain).astype(jnp.bfloat16)
    feature_count = normed.shape[1]
    per_index = tensor_count // 4
    expert_total = owner_count * per_index
    capacity = min(row_share, 2 * row_share * TOPK // expert_total)
    labels = jnp.arange(expert_total, dtype=jnp.int32)
    choose = jnp.sum((expert_ids[:, :, None] == labels[None, None, :]).astype(jnp.int32), axis=1)
    slot_rank = jnp.cumsum(choose, axis=0) - choose
    target = expert_ids * capacity + jnp.take_along_axis(slot_rank, expert_ids, axis=1)
    slot_labels = jnp.arange(expert_total * capacity, dtype=jnp.int32)
    placing = jnp.sum(
        (target[:, :, None] == slot_labels[None, None, :]).astype(jnp.bfloat16), axis=1
    )
    outgoing = jnp.einsum("rs,rd->sd", placing, normed, preferred_element_type=jnp.float32).astype(
        jnp.bfloat16
    )
    grouped = outgoing.reshape(owner_count, per_index, capacity, feature_count)
    copies = jnp.repeat(grouped, 4, axis=1)
    arrived = lax.all_to_all(
        lax.all_to_all(copies, "expert", split_axis=0, concat_axis=0, tiled=True),
        "tensor",
        split_axis=1,
        concat_axis=1,
        tiled=True,
    )
    partial_rows = expert_apply(arrived, w_gate, w_up, w_down)
    returned = lax.all_to_all(
        lax.all_to_all(partial_rows, "expert", split_axis=0, concat_axis=0, tiled=True),
        "tensor",
        split_axis=1,
        concat_axis=1,
        tiled=True,
    )
    quarters = returned.reshape(owner_count, per_index, 4, capacity, feature_count)
    summed = jnp.sum(quarters.astype(jnp.float32), axis=2).astype(jnp.bfloat16)
    results = summed.reshape(expert_total * capacity, feature_count)
    picked = jnp.take(results, target.reshape(-1), axis=0).reshape(row_share, TOPK, feature_count)
    mixture = jnp.einsum("rk,rkd->rd", gate_values, picked.astype(jnp.float32))
    return (stream + mixture).astype(jnp.bfloat16)


def solution(mesh):
    return jax.shard_map(
        on_device,
        mesh=mesh,
        in_specs=(
            P("expert", "tensor"),
            P("tensor", "expert"),
            P(),
            P(("expert", "tensor"), None),
            P(("expert", "tensor"), None),
            P(("expert", "tensor"), None, None),
            P(("expert", "tensor"), None, None),
            P(("expert", "tensor"), None, None),
        ),
        out_specs=P(("expert", "tensor"), None),
        check_vma=False,
    )
```

profile of v0, /device:TPU:6, one launch (start us, length us, event | category | flops | bytes accessed | tf_op | source)
XLA Modules:
  0.0 635.9 jit_solution(581380298775688274)
XLA Ops:
  7.3 120.0 %all-gather.2.cloned.1.call-done = bf16[512,4096]{1,0:T(8,128)(2,1)} async-done(((bf16[512,256]{1,0:T(8,128)(2,1)}), bf16[512,4096]{1,0:T(8,128)(2,1)}) %all-gather.2.cloned.1.call-update) | async-done | bytes 4194320 | tf_op jit(solution)/shard_map/all_gather | solution.py:24
  127.3 4.3 fusion.30
  132.8 82.2 %reduce-scatter.2.cloned.1.call-done = f32[8,4096]{1,0:T(8,128)} async-done(((f32[128,4096]{1,0:T(8,128)}), f32[8,4096]{1,0:T(8,128)}) %reduce-scatter.2.cloned.1.call-update) | async-done | bytes 131088 | tf_op jit(solution)/shard_map/reduce_scatter | solution.py:26
  215.1 1.0 fusion.17
  216.1 2.4 convolution_convert_fusion.1
  218.5 2.5 reshape.82
  221.1 7.5 %broadcast_in_dim.25 = bf16[16,4,4,2,4096]{4,3,2,1,0:T(2,128)(2,1)} broadcast(bf16[16,4,2,4096]{3,2,1,0:T(2,128)(2,1)} %reshape.82), dimensions={0,1,3,4} | broadcast | bytes 5242880 | tf_op jit(solution)/shard_map/broadcast_in_dim | solution.py:51
  228.6 101.3 %all_to_all.20 = bf16[16,16,2,4096]{3,2,1,0:T(2,128)(2,1)} all-to-all(bf16[16,16,2,4096]{3,2,1,0:T(2,128)(2,1)} %bitcast.38), channel_id=1, replica_groups=mesh['expert'=16,'tensor'=16] {'expert'}, dimensions={0} | all-to-all | bytes 8388608 | tf_op jit(solution)/shard_map/all_to_all | solution.py:53
  329.9 10.0 %copy.18 = bf16[16,16,2,4096]{3,2,0,1:T(2,128)(2,1)} copy(bf16[16,16,2,4096]{3,2,1,0:T(2,128)(2,1)} %all_to_all.20) | data formatting | bytes 8388608 | tf_op jit(solution)/shard_map/all_to_all | solution.py:53
  339.9 54.8 %all_to_all.21 = bf16[16,16,2,4096]{3,2,0,1:T(2,128)(2,1)} all-to-all(bf16[16,16,2,4096]{3,2,0,1:T(2,128)(2,1)} %copy.18), channel_id=1, replica_groups=mesh['expert'=16,'tensor'=16] {'tensor'}, dimensions={1} | all-to-all | bytes 8388608 | tf_op jit(solution)/shard_map/all_to_all | solution.py:52
  394.7 10.1 %copy.19 = bf16[16,16,2,4096]{3,2,1,0:T(2,128)(2,1)} copy(bf16[16,16,2,4096]{3,2,0,1:T(2,128)(2,1)} %all_to_all.21) | data formatting | bytes 8388608 | tf_op jit(solution)/shard_map/all_to_all | solution.py:52
  404.8 7.2 %reshape.84 = bf16[512,4096]{1,0:T(8,128)(2,1)} reshape(bf16[16,16,2,4096]{3,2,1,0:T(2,128)(2,1)} %copy.19) | data formatting | bytes 8388608 | tf_op jit(solution)/shard_map/reshape | solution.py:11
  412.0 6.4 %fusion.3 = f32[512,384]{1,0:T(8,128)} fusion(bf16[512,4096]{1,0:T(8,128)(2,1)} %reshape.84, bf16[1,4096,384]{2,1,0:T(8,128)(2,1)} %param.13), kind=kOutput, calls=%fused_computation.8 | convolution fusion | flops 1610612736 | bytes 8126464 | tf_op jit(solution)/shard_map/dot_general | solution.py:12
  418.5 9.8 %convolution_convert_fusion = bf16[512,4096]{1,0:T(8,128)(2,1)} fusion(bf16[1,384,4096]{2,1,0:T(8,128)(2,1)S(1)} %copy-done, bf16[512,4096]{1,0:T(8,128)(2,1)} %reshape.84, bf16[1,4096,384]{2,1,0:T(8,128)(2,1)} %param.14, f32[512,384]{1,0:T(8,128)} %fusion.3), kind=kOutput, calls=%fused_computation.2 | convolution fusion | flops 3224502272 | bytes 15466496 | tf_op jit(solution)/shard_map/dot_general | solution.py:15
  428.2 7.6 %reshape.85 = bf16[16,16,2,4096]{3,2,1,0:T(2,128)(2,1)} reshape(bf16[512,4096]{1,0:T(8,128)(2,1)} %convolution_convert_fusion) | data formatting | bytes 8388608 | tf_op jit(solution)/shard_map/reshape | solution.py:18
  435.8 101.5 %all_to_all.22 = bf16[16,16,2,4096]{3,2,1,0:T(2,128)(2,1)} all-to-all(bf16[16,16,2,4096]{3,2,1,0:T(2,128)(2,1)} %reshape.85), channel_id=1, replica_groups=mesh['expert'=16,'tensor'=16] {'expert'}, dimensions={0} | all-to-all | bytes 8388608 | tf_op jit(solution)/shard_map/all_to_all | solution.py:61
  537.3 10.1 %copy.20 = bf16[16,16,2,4096]{3,2,0,1:T(2,128)(2,1)} copy(bf16[16,16,2,4096]{3,2,1,0:T(2,128)(2,1)} %all_to_all.22) | data formatting | bytes 8388608 | tf_op jit(solution)/shard_map/all_to_all | solution.py:61
  547.4 7.0 %all-to-all-start.3 = ((bf16[16,16,2,4096]{3,2,0,1:T(2,128)(2,1)}), bf16[16,16,2,4096]{3,2,0,1:T(2,128)(2,1)}, u32[]{:S(2)}, u32[]{:S(2)}) async-start(bf16[16,16,2,4096]{3,2,0,1:T(2,128)(2,1)} %copy.20), calls=%async_computation.4 | async-start | bytes 8388608 | tf_op jit(solution)/shard_map/all_to_all | solution.py:60
  554.5 53.8 %all-to-all-done.3 = bf16[16,16,2,4096]{3,2,0,1:T(2,128)(2,1)} async-done(((bf16[16,16,2,4096]{3,2,0,1:T(2,128)(2,1)}), bf16[16,16,2,4096]{3,2,0,1:T(2,128)(2,1)}, u32[]{:S(2)}, u32[]{:S(2)}) %all-to-all-start.3) | async-done | bytes 4194336 | tf_op jit(solution)/shard_map/all_to_all | solution.py:60
  608.4 9.3 %bitcast_reduce_fusion = bf16[16,4,2,4096]{3,2,0,1:T(2,128)(2,1)} fusion(bf16[16,16,2,4096]{3,2,0,1:T(2,128)(2,1)} %all-to-all-done.3), kind=kLoop, calls=%fused_computation.4 | loop fusion | flops 1572864 | bytes 5242880 | tf_op jit(solution)/shard_map/reduce_sum | solution.py:68
  617.6 3.5 copy.21
  621.2 2.3 reshape.87
  623.5 3.5 gather_fusion
  627.0 1.4 fusion.13
  (30 shorter events, 2.7 us)
Async XLA Ops:
  6.5 411.9 %copy-start = (bf16[1,384,4096]{2,1,0:T(8,128)(2,1)S(1)}, bf16[1,384,4096]{2,1,0:T(8,128)(2,1)}, u32[]{:S(2)}) copy-start(bf16[1,384,4096]{2,1,0:T(8,128)(2,1)} %param.15) | copy-start | bytes 9437188
  6.5 120.8 %all-gather.2.cloned.1.call-start = ((), (), s32[]{:S(2)}) async-start(), calls=%async_computation.5 | async-start | bytes 4456448 | tf_op jit(solution)/shard_map/all_gather | solution.py:24
  7.3 124.4 %copy-start.3 = (s32[8,8]{1,0:T(8,128)S(1)}, s32[8,8]{1,0:T(8,128)}, u32[]{:S(2)}) copy-start(s32[8,8]{1,0:T(8,128)} %param.11) | copy-start | bytes 772
  7.3 207.8 %reduce-scatter.2.cloned.1.call-start = ((), (), s32[]{:S(2)}) async-start(), calls=%async_computation.6 | async-start | bytes 2228224 | tf_op jit(solution)/shard_map/reduce_scatter | solution.py:26
  131.6 84.5 %copy-start.4 = (f32[4096]{0:T(1024)S(1)}, f32[4096]{0:T(1024)}, u32[]{:S(2)}) copy-start(f32[4096]{0:T(1024)} %param.10) | copy-start | bytes 49156
  547.4 61.0 %all-to-all-start.3 = ((bf16[16,16,2,4096]{3,2,0,1:T(2,128)(2,1)}), bf16[16,16,2,4096]{3,2,0,1:T(2,128)(2,1)}, u32[]{:S(2)}, u32[]{:S(2)}) async-start(bf16[16,16,2,4096]{3,2,0,1:T(2,128)(2,1)} %copy.20), calls=%async_computation.4 | async-start | bytes 8388608 | tf_op jit(solution)/shard_map/all_to_all | solution.py:60
  617.6 9.4 %copy-start.5 = (f32[8,8]{1,0:T(8,128)S(1)}, f32[8,8]{1,0:T(8,128)}, u32[]{:S(2)}) copy-start(f32[8,8]{1,0:T(8,128)} %param.12) | copy-start | bytes 772
  617.6 11.5 %copy-start.1 = (bf16[1,384,4096]{2,1,0:T(8,128)(2,1)S(1)}, bf16[1,384,4096]{2,1,0:T(8,128)(2,1)}, u32[]{:S(2)}) copy-start(bf16[1,384,4096]{2,1,0:T(8,128)(2,1)} %param.15) | copy-start | bytes 9437188
  621.2 7.2 %copy-start.2 = (f32[8,4096]{1,0:T(8,128)S(1)}, f32[8,4096]{1,0:T(8,128)}, u32[]{:S(2)}) copy-start(f32[8,4096]{1,0:T(8,128)} %reduce-scatter.2.cloned.1.call-done) | copy-start | bytes 393220
Sparse Core Ops, SparseCore 0:
  9.1 118.2 all-gather.1
  131.8 83.2 reduce-scatter.1
where the time goes:
time: 645 us; the launch traced here: 636 us
  blocking collectives  258 us (40%)
  waiting for transfers between devices  257 us (40%)
  local copies, waits for them, and re-layouts  65.4 us (10%)
  matrix products  24.3 us (4%)
  between operations  13.5 us (2%)
  other arithmetic  11.3 us (2%)
  starting transfers between devices  7.07 us (1%)
    all_gather x1, waiting for transfers between devices, on_device(): full_proj = lax.all_gather(proj_weight, 'expert', axis=1, tiled=True)  120 us
    all_to_all x1, blocking collectives, on_device(): lax.all_to_all(partial_rows, 'expert', split_axis=0, concat_axis=0, tiled...  101 us
    all_to_all x1, blocking collectives, on_device(): lax.all_to_all(copies, 'expert', split_axis=0, concat_axis=0, tiled=True)  101 us
    reduce_scatter x1, waiting for transfers between devices, on_device(): lax.psum_scatter(jnp.dot(context, full_proj, preferred_element_type=jnp.f...  82.2 us
    all_to_all x1, blocking collectives, on_device(): lax.all_to_all(lax.all_to_all(copies, 'expert', split_axis=0, concat_axis...  54.8 us
    all_to_all x1, waiting for transfers between devices, on_device(): lax.all_to_all(lax.all_to_all(partial_rows, 'expert', split_axis=0, conca...  53.8 us
  transfers between devices with their start and end apart: 3, of which 3 were waited for; matrix products, arithmetic and copies ran while one was open for 0% of the time, Pallas kernels for 0%

commit v1 on v0

v1 whole, which is shorter than its diff:
```python
import jax
import jax.numpy as jnp
from jax import lax
from jax.sharding import Mesh
from jax.sharding import PartitionSpec as P

TOPK = 8
QUARTERS = 4
CAP = 2

FINE = ("z", "xl", "xh", "y", "c")
SIZES = (8, 2, 2, 4, 2)
EXPERT = ("z", "xl")
TENSOR = ("xh", "y", "c")
PLANE = ("xh", "y")
NZ = 8


def swap(x, axis):
    return lax.ppermute(x, axis, [(0, 1), (1, 0)])


def fetch(x, hop):
    return lax.ppermute(x, "z", [((i + hop) % NZ, i) for i in range(NZ)])


def gather_z(x):
    up1, dn1 = fetch(x, 1), fetch(x, -1)
    up2, dn2 = fetch(x, 2), fetch(x, -2)
    up3, dn3 = fetch(up1, 2), fetch(dn1, -2)
    far = fetch(up3, 1)
    return [x, up1, up2, up3, far, dn3, dn2, dn1]


def expert_rows(rows, w_gate, w_up, w_down):
    gate_act = jnp.dot(rows, w_gate, preferred_element_type=jnp.float32)
    up_act = jnp.dot(rows, w_up, preferred_element_type=jnp.float32)
    hidden = (jax.nn.silu(gate_act) * up_act).astype(jnp.bfloat16)
    return jnp.dot(hidden, w_down, preferred_element_type=jnp.float32)


def on_device(context, proj_weight, norm_gain, expert_ids, gate_values, w_gate, w_up, w_down):
    zi, xli = lax.axis_index("z"), lax.axis_index("xl")
    n_tensor = lax.axis_size(TENSOR)
    n_plane = lax.axis_size(PLANE)
    n_expert = lax.axis_size(EXPERT)
    rows = context.shape[0] // n_tensor
    groups = n_tensor // QUARTERS
    cols = proj_weight.shape[1]
    width = cols * n_expert
    tokens = rows * n_expert

    routing = jnp.concatenate([expert_ids.astype(jnp.float32), gate_values], axis=1)
    routing = lax.all_gather(routing, EXPERT, axis=0, tiled=True)

    other = swap(proj_weight, "xl")
    blocks = [b.reshape(n_tensor, 1, rows, -1) for b in gather_z(context)]
    lhs = jnp.concatenate(blocks, axis=1).reshape(NZ * context.shape[0], -1)
    rhs = jnp.concatenate([proj_weight, other], axis=1)
    partial = jnp.dot(lhs, rhs, preferred_element_type=jnp.float32).astype(jnp.bfloat16)
    partial = partial.reshape(n_tensor, NZ * rows, 2 * cols)
    partial = lax.all_to_all(partial, TENSOR, 0, 0, tiled=True)
    part = jnp.sum(partial.astype(jnp.float32), axis=0).astype(jnp.bfloat16)
    part = jnp.where(xli == 0, part, jnp.concatenate([part[:, cols:], part[:, :cols]], axis=1))

    mate = swap(part, "xl")
    part = part.reshape(NZ, 1, rows, 2 * cols)
    mate = mate.reshape(NZ, 1, rows, 2 * cols)
    pair = jnp.where(
        xli == 0, jnp.concatenate([part, mate], axis=1), jnp.concatenate([mate, part], axis=1)
    )
    start = lax.rem(NZ - zi, NZ)
    pair = lax.dynamic_slice_in_dim(jnp.concatenate([pair, pair], axis=0), start, NZ, axis=0)
    pair = pair.reshape(tokens, 2 * cols)
    attended = jnp.zeros((tokens, width), jnp.bfloat16)
    for hop, block in enumerate(gather_z(pair)):
        at = lax.rem(zi + hop, NZ) * (2 * cols)
        attended = lax.dynamic_update_slice_in_dim(attended, block, at, axis=1)
    stream = attended.astype(jnp.float32)
    scale = lax.rsqrt(jnp.mean(stream * stream, axis=-1, keepdims=True) + 1e-06)
    normed = (stream * scale * norm_gain).astype(jnp.bfloat16)

    ids = routing[:, :TOPK].astype(jnp.int32)
    gates = routing[:, TOPK:]
    ei = zi * 2 + xli
    labels = ei * groups + jnp.arange(groups, dtype=jnp.int32)
    match = ids[:, :, None] == labels[None, None, :]
    chosen = jnp.sum(match.astype(jnp.int32), axis=1)
    weight = jnp.sum(jnp.where(match, gates[:, :, None], 0.0), axis=1)
    blocked = chosen.reshape(n_expert, rows, groups)
    rank = (jnp.cumsum(blocked, axis=1) - blocked).reshape(tokens, groups)
    base = (jnp.arange(tokens, dtype=jnp.int32) // rows) * CAP
    slot = jnp.where(chosen > 0, base[:, None] + rank, -1)
    slots = n_expert * CAP
    placing = slot[:, :, None] == jnp.arange(slots, dtype=jnp.int32)[None, None, :]
    placing = jnp.repeat(placing, n_plane // groups, axis=1).reshape(tokens, n_plane * slots)
    weight = jnp.repeat(weight, n_plane // groups, axis=1)
    weight = jnp.where(placing, jnp.repeat(weight, slots, axis=1), 0.0)

    sent = lax.dot_general(
        placing.astype(jnp.bfloat16),
        normed,
        (((0,), (0,)), ((), ())),
        preferred_element_type=jnp.float32,
    ).astype(jnp.bfloat16)
    sent = sent.reshape(n_plane, slots, width)
    mine = lax.all_to_all(sent, PLANE, 0, 0, tiled=True).reshape(n_plane * slots, width)
    theirs = swap(mine, "c")
    theirs_out = expert_rows(theirs, w_gate[0], w_up[0], w_down[0]).astype(jnp.bfloat16)
    from_mate = swap(theirs_out, "c")
    mine_out = expert_rows(mine, w_gate[0], w_up[0], w_down[0])
    summed = (mine_out + from_mate.astype(jnp.float32)).astype(jnp.bfloat16)
    summed = summed.reshape(n_plane, slots, width)
    back = lax.all_to_all(summed, PLANE, 0, 0, tiled=True).reshape(n_plane * slots, width)

    high = weight.astype(jnp.bfloat16)
    low = (weight - high.astype(jnp.float32)).astype(jnp.bfloat16)
    mixture = jnp.dot(high, back, preferred_element_type=jnp.float32) + jnp.dot(
        low, back, preferred_element_type=jnp.float32
    )
    mixture = mixture.astype(jnp.bfloat16).reshape(NZ, 2, rows, width)
    keep = lax.dynamic_index_in_dim(mixture, xli, 1, keepdims=False)
    give = lax.dynamic_index_in_dim(mixture, 1 - xli, 1, keepdims=False)
    got = swap(give, "xl")
    half = (keep.astype(jnp.float32) + got.astype(jnp.float32)).astype(jnp.bfloat16)
    home = lax.all_to_all(half, "z", 0, 0, tiled=True)
    own = lax.dynamic_slice_in_dim(attended, ei * rows, rows, axis=0)
    out = own.astype(jnp.float32) + jnp.sum(home.astype(jnp.float32), axis=0)
    return out.astype(jnp.bfloat16)


def solution(mesh):
    fine = Mesh(mesh.devices.reshape(SIZES), FINE)
    both = EXPERT + TENSOR
    return jax.shard_map(
        on_device,
        mesh=fine,
        in_specs=(
            P(EXPERT, TENSOR),
            P(TENSOR, EXPERT),
            P(),
            P(both, None),
            P(both, None),
            P(both, None, None),
            P(both, None, None),
            P(both, None, None),
        ),
        out_specs=P(both, None),
        check_vma=False,
    )
```

time: 645 us -> 237 us (0.37); the launches traced: 636 us -> 235 us
  blocking collectives: 258 us -> 63.7 us
  waiting for transfers between devices: 257 us -> 77.6 us
  local copies, waits for them, and re-layouts: 65.4 us -> 7.07 us
  starting transfers between devices: 7.07 us -> 52.3 us
  between operations: 13.5 us -> 0.45 us
    all_to_all x3 -> x1, blocking collectives: 258 us -> 24.7 us  [on_device(): lax.all_to_all(sent, PLANE, 0, 0, tiled=True)]
    all_gather x1 -> x0, waiting for transfers between devices: 120 us -> none  [on_device(): full_proj = lax.all_gather(proj_weight, 'expert', axis=1, tiled=True)]
    reduce_scatter x1 -> x0, waiting for transfers between devices: 82.2 us -> none  [on_device(): lax.psum_scatter(jnp.dot(context, full_proj, preferred_element_type=jnp.f...]
    all_gather x0 -> x1, blocking collectives: none -> 39 us  [on_device(): routing = lax.all_gather(routing, EXPERT, axis=0, tiled=True)]
    ppermute x0 -> x19, waiting for transfers between devices: none -> 34.7 us  [the longest x5 18.6 us: swap(): return lax.ppermute(x, axis, [(0, 1), (1, 0)])]
    ppermute x0 -> x19, starting transfers between devices: none -> 32.2 us  [the longest x14 26 us: fetch(): return lax.ppermute(x, 'z', [((i + hop) % NZ, i) for i in range(NZ)])]
    all_to_all x3 -> x0, local copies, waits for them, and re-layouts: 30.2 us -> none  [the longest x1 10.1 us: on_device(): lax.all_to_all(lax.all_to_all(copies, 'expert', split_axis=0, concat_axis...]
    reshape x5 -> x1, local copies, waits for them, and re-layouts: 19.8 us -> 0.1 us  [on_device(): blocked = chosen.reshape(n_expert, rows, groups)]
  transfers between devices with their start and end apart: 3 -> 22, of which waited for: 3 -> 13; matrix products, arithmetic and copies ran while one was open for 0% -> 3% of each run, Pallas kernels for 0% -> 0%
where the time goes in v1:
time: 237 us; the launch traced here: 235 us
  waiting for transfers between devices  77.6 us (33%)
  blocking collectives  63.7 us (27%)
  starting transfers between devices  52.3 us (22%)
  matrix products  26.6 us (11%)
  other arithmetic  7.58 us (3%)
  local copies, waits for them, and re-layouts  7.07 us (3%)
    all_gather x1, blocking collectives, on_device(): routing = lax.all_gather(routing, EXPERT, axis=0, tiled=True)  39 us
    all_to_all x1, waiting for transfers between devices, on_device(): lax.all_to_all(summed, PLANE, 0, 0, tiled=True)  26.2 us
    ppermute x14, starting transfers between devices, fetch(): return lax.ppermute(x, 'z', [((i + hop) % NZ, i) for i in range(NZ)])  26 us
    all_to_all x1, blocking collectives, on_device(): lax.all_to_all(sent, PLANE, 0, 0, tiled=True)  24.7 us
    ppermute x5, waiting for transfers between devices, swap(): return lax.ppermute(x, axis, [(0, 1), (1, 0)])  18.6 us
    all_to_all x1, waiting for transfers between devices, on_device(): home = lax.all_to_all(half, 'z', 0, 0, tiled=True)  16.7 us
    ppermute x14, waiting for transfers between devices, fetch(): return lax.ppermute(x, 'z', [((i + hop) % NZ, i) for i in range(NZ)])  16.1 us
    dot_general x2, matrix products, expert_rows(): return jnp.dot(hidden, w_down, preferred_element_type=jnp.float32)  13.4 us
  transfers between devices with their start and end apart: 22, of which 13 were waited for; matrix products, arithmetic and copies ran while one was open for 3% of the time, Pallas kernels for 0%

profile of v1, /device:TPU:6, one launch (start us, length us, event | category | flops | bytes accessed | tf_op | source)
XLA Modules:
  0.0 235.4 jit_solution(9156243198464693742)
XLA Ops:
  0.0 5.9 %collective-permute-start = (bf16[128,512]{1,0:T(8,128)(2,1)}, bf16[128,512]{1,0:T(8,128)(2,1)S(1)}, u32[]{:S(2)}, u32[]{:S(2)}) collective-permute-start(bf16[128,512]{1,0:T(8,128)(2,1)} %param.8), channel_id=1, source_target_pairs={{32,0},{64,32},{96,64},{128,96},{160,128},{192,160},{224,192},{0,2... | collective-permute-start | bytes 393224 | tf_op jit(solution)/shard_map/ppermute | solution.py:24
  14.3 2.4 %collective-permute-done.4 = bf16[128,512]{1,0:T(8,128)(2,1)S(1)} collective-permute-done((bf16[128,512]{1,0:T(8,128)(2,1)}, bf16[128,512]{1,0:T(8,128)(2,1)S(1)}, u32[]{:S(2)}, u32[]{:S(2)}) %collective-permute-start.4) | collective-permute-done | bytes 131104 | tf_op jit(solution)/shard_map/ppermute | solution.py:24
  19.5 4.2 %collective-permute-start.3 = (bf16[128,512]{1,0:T(8,128)(2,1)S(1)}, bf16[128,512]{1,0:T(8,128)(2,1)S(1)}, u32[]{:S(2)}, u32[]{:S(2)}) collective-permute-start(bf16[128,512]{1,0:T(8,128)(2,1)S(1)} %collective-permute-done.2), channel_id=1, source_target_pairs={{32,0},{64,32},{96,64},{128,96},{160,128},{192,160},{224,192},{0,2... | collective-permute-start | bytes 393224 | tf_op jit(solution)/shard_map/ppermute | solution.py:24
  23.7 2.5 %collective-permute-done.3 = bf16[128,512]{1,0:T(8,128)(2,1)S(1)} collective-permute-done((bf16[128,512]{1,0:T(8,128)(2,1)S(1)}, bf16[128,512]{1,0:T(8,128)(2,1)S(1)}, u32[]{:S(2)}, u32[]{:S(2)}) %collective-permute-start.3) | collective-permute-done | bytes 131104 | tf_op jit(solution)/shard_map/ppermute | solution.py:24
  28.0 7.5 %all-to-all-start = ((bf16[16,64,512]{2,1,0:T(8,128)(2,1)}), bf16[16,64,512]{2,1,0:T(8,128)(2,1)}, u32[]{:S(2)}, u32[]{:S(2)}) async-start(bf16[16,64,512]{2,1,0:T(8,128)(2,1)} %bitcast.87), calls=%async_computation | async-start | bytes 2097152 | tf_op jit(solution)/shard_map/all_to_all | solution.py:62
  35.6 39.0 %all_gather.3 = f32[128,16]{1,0:T(8,128)S(1)} all-gather(f32[8,16]{1,0:T(8,128)S(1)} %pad_maximum_fusion), channel_id=1, replica_groups=mesh['z'=8,'xl'=2,'xh'=2,'y'=4,'c'=2] {'z','xl'}, dimensions={0}, use_global_device_ids=true | all-gather | bytes 8704 | tf_op jit(solution)/shard_map/all_gather | solution.py:54
  77.1 3.1 %collective-permute-start.8 = (bf16[64,512]{1,0:T(8,128)(2,1)S(1)}, bf16[64,512]{1,0:T(8,128)(2,1)S(1)}, u32[]{:S(2)}, u32[]{:S(2)}) collective-permute-start(bf16[64,512]{1,0:T(8,128)(2,1)S(1)} %maximum_select_fusion.2), channel_id=1, source_target_pairs={{0,16},{16,0},{1,17},{17,1},{2,18},{18,2},{3,19},{19,3},{4,20},{20... | collective-permute-start | bytes 196616 | tf_op jit(solution)/shard_map/ppermute | solution.py:20
  80.2 2.2 collective-permute-done.8
  84.8 2.9 %collective-permute-start.15 = (bf16[128,512]{1,0:T(8,128)(2,1)S(1)}, bf16[128,512]{1,0:T(8,128)(2,1)S(1)}, u32[]{:S(2)}, u32[]{:S(2)}) collective-permute-start(bf16[128,512]{1,0:T(8,128)(2,1)S(1)} %bitcast.91), channel_id=1, source_target_pairs={{192,0},{224,32},{0,64},{32,96},{64,128},{96,160},{128,192},{160,2... | collective-permute-start | bytes 393224 | tf_op jit(solution)/shard_map/ppermute | solution.py:24
  92.6 3.3 %collective-permute-done.11 = bf16[128,512]{1,0:T(8,128)(2,1)S(1)} collective-permute-done((bf16[128,512]{1,0:T(8,128)(2,1)}, bf16[128,512]{1,0:T(8,128)(2,1)S(1)}, u32[]{:S(2)}, u32[]{:S(2)}) %collective-permute-start.11) | collective-permute-done | bytes 131104 | tf_op jit(solution)/shard_map/ppermute | solution.py:24
  95.9 3.1 %collective-permute-start.12 = (bf16[128,512]{1,0:T(8,128)(2,1)S(1)}, bf16[128,512]{1,0:T(8,128)(2,1)S(1)}, u32[]{:S(2)}, u32[]{:S(2)}) collective-permute-start(bf16[128,512]{1,0:T(8,128)(2,1)S(1)} %collective-permute-done.11), channel_id=1, source_target_pairs={{32,0},{64,32},{96,64},{128,96},{160,128},{192,160},{224,192},{0,2... | collective-permute-start | bytes 393224 | tf_op jit(solution)/shard_map/ppermute | solution.py:24
  99.0 2.5 %collective-permute-done.12 = bf16[128,512]{1,0:T(8,128)(2,1)S(1)} collective-permute-done((bf16[128,512]{1,0:T(8,128)(2,1)S(1)}, bf16[128,512]{1,0:T(8,128)(2,1)S(1)}, u32[]{:S(2)}, u32[]{:S(2)}) %collective-permute-start.12) | collective-permute-done | bytes 131104 | tf_op jit(solution)/shard_map/ppermute | solution.py:24
  102.8 24.7 %all_to_all.20 = bf16[8,32,4096]{2,1,0:T(8,128)(2,1)S(1)} all-to-all(bf16[8,32,4096]{2,1,0:T(8,128)(2,1)S(1)} %bitcast.80), channel_id=1, replica_groups=mesh['z'=8,'xl'=2,'xh'=2,'y'=4,'c'=2] {'xh','y'}, dimensions={0} | all-to-all | bytes 4194304 | tf_op jit(solution)/shard_map/all_to_all | solution.py:107
  128.8 4.2 %collective-permute-done.16 = bf16[256,4096]{1,0:T(8,128)(2,1)S(1)} collective-permute-done((bf16[256,4096]{1,0:T(8,128)(2,1)S(1)}, bf16[256,4096]{1,0:T(8,128)(2,1)S(1)}, u32[]{:S(2)}, u32[]{:S(2)}) %collective-permute-start.16) | collective-permute-done | bytes 2097184 | tf_op jit(solution)/shard_map/ppermute | solution.py:20
  136.4 6.4 %convolution_convert_fusion.1 = bf16[256,4096]{1,0:T(8,128)(2,1)} fusion(bf16[1,384,4096]{2,1,0:T(8,128)(2,1)S(1)} %copy-done, f32[256,384]{1,0:T(8,128)} %fusion.6, bf16[256,4096]{1,0:T(8,128)(2,1)} %copy-done.8, bf16[1,4096,384]{2,1,0:T(8,128)(2,1)} %param.13), kind=kOutput, calls=%fused_computation.1 | convolution fusion | flops 1612251136 | bytes 10878976 | tf_op jit(solution)/shard_map/dot_general | solution.py:39
  142.9 4.5 %fusion.12 = f32[256,384]{1,0:T(8,128)} fusion(bf16[256,4096]{1,0:T(8,128)(2,1)} %bitcast.85, bf16[1,4096,384]{2,1,0:T(8,128)(2,1)} %param.13), kind=kOutput, calls=%fused_computation.14 | convolution fusion | flops 805306368 | bytes 5636096 | tf_op jit(solution)/shard_map/dot_general | solution.py:36
  147.5 7.0 %add_convert_fusion = bf16[256,4096]{1,0:T(8,128)(2,1)} fusion(bf16[256,4096]{1,0:T(8,128)(2,1)} %collective-permute-done.17, bf16[1,384,4096]{2,1,0:T(8,128)(2,1)S(1)} %copy-done, bf16[256,4096]{1,0:T(8,128)(2,1)} %bitcast.86, bf16[1,4096,384]{2,1,0:T(8,128)(2,1)} %param.14, f32[256,384]{1,0:T(8,128)} %fusion.12), kind=kOutput, calls=%fused_computation.4 | convolution fusion | flops 1614348288 | bytes 12976128 | tf_op jit(solution)/shard_map/dot_general | solution.py:39
  154.5 7.2 %all-to-all-start.2 = ((bf16[8,32,4096]{2,1,0:T(8,128)(2,1)}), bf16[8,32,4096]{2,1,0:T(8,128)(2,1)}, u32[]{:S(2)}, u32[]{:S(2)}) async-start(bf16[8,32,4096]{2,1,0:T(8,128)(2,1)} %bitcast.83), calls=%async_computation.2 | async-start | bytes 4194304 | tf_op jit(solution)/shard_map/all_to_all | solution.py:114
  161.9 26.2 %all-to-all-done.2 = bf16[8,32,4096]{2,1,0:T(8,128)(2,1)} async-done(((bf16[8,32,4096]{2,1,0:T(8,128)(2,1)}), bf16[8,32,4096]{2,1,0:T(8,128)(2,1)}, u32[]{:S(2)}, u32[]{:S(2)}) %all-to-all-start.2) | async-done | bytes 2097184 | tf_op jit(solution)/shard_map/all_to_all | solution.py:114
  194.1 2.1 collective-permute-start.18
  196.2 12.2 %collective-permute-done.18 = bf16[8,8,4096]{2,1,0:T(8,128)(2,1)} collective-permute-done((bf16[8,8,4096]{2,1,0:T(8,128)(2,1)}, bf16[8,8,4096]{2,1,0:T(8,128)(2,1)}, u32[]{:S(2)}, u32[]{:S(2)}) %collective-permute-start.18) | collective-permute-done | bytes 524320 | tf_op jit(solution)/shard_map/ppermute | solution.py:20
  208.4 2.1 fusion.24
  210.6 5.5 %all-to-all-start.3 = ((bf16[8,8,4096]{2,1,0:T(8,128)(2,1)}), bf16[8,8,4096]{2,1,0:T(8,128)(2,1)}, u32[]{:S(2)}, u32[]{:S(2)}) async-start(bf16[8,8,4096]{2,1,0:T(8,128)(2,1)} %fusion.24), calls=%async_computation.3 | async-start | bytes 1048576 | tf_op jit(solution)/shard_map/all_to_all | solution.py:126
  216.1 16.7 %all-to-all-done.3 = bf16[8,8,4096]{2,1,0:T(8,128)(2,1)} async-done(((bf16[8,8,4096]{2,1,0:T(8,128)(2,1)}), bf16[8,8,4096]{2,1,0:T(8,128)(2,1)}, u32[]{:S(2)}, u32[]{:S(2)}) %all-to-all-start.3) | async-done | bytes 524320 | tf_op jit(solution)/shard_map/all_to_all | solution.py:126
  (97 shorter events, 37.6 us)
Async XLA Ops:
  0.0 136.4 %copy-start = (bf16[1,384,4096]{2,1,0:T(8,128)(2,1)S(1)}, bf16[1,384,4096]{2,1,0:T(8,128)(2,1)}, u32[]{:S(2)}) copy-start(bf16[1,384,4096]{2,1,0:T(8,128)(2,1)} %param.15) | copy-start | bytes 9437188
  0.0 12.4 %collective-permute-start = (bf16[128,512]{1,0:T(8,128)(2,1)}, bf16[128,512]{1,0:T(8,128)(2,1)S(1)}, u32[]{:S(2)}, u32[]{:S(2)}) collective-permute-start(bf16[128,512]{1,0:T(8,128)(2,1)} %param.8), channel_id=1, source_target_pairs={{32,0},{64,32},{96,64},{128,96},{160,128},{192,160},{224,192},{0,2... | collective-permute-start | bytes 393224 | tf_op jit(solution)/shard_map/ppermute | solution.py:24
  5.9 12.4 %collective-permute-start.1 = (bf16[128,512]{1,0:T(8,128)(2,1)}, bf16[128,512]{1,0:T(8,128)(2,1)S(1)}, u32[]{:S(2)}, u32[]{:S(2)}) collective-permute-start(bf16[128,512]{1,0:T(8,128)(2,1)} %param.8), channel_id=1, source_target_pairs={{64,0},{96,32},{128,64},{160,96},{192,128},{224,160},{0,192},{32,2... | collective-permute-start | bytes 393224 | tf_op jit(solution)/shard_map/ppermute | solution.py:24
  7.3 9.4 %collective-permute-start.4 = (bf16[128,512]{1,0:T(8,128)(2,1)}, bf16[128,512]{1,0:T(8,128)(2,1)S(1)}, u32[]{:S(2)}, u32[]{:S(2)}) collective-permute-start(bf16[128,512]{1,0:T(8,128)(2,1)} %param.8), channel_id=1, source_target_pairs={{224,0},{0,32},{32,64},{64,96},{96,128},{128,160},{160,192},{192,2... | collective-permute-start | bytes 393224 | tf_op jit(solution)/shard_map/ppermute | solution.py:24
  8.3 17.9 %collective-permute-start.6 = (bf16[128,512]{1,0:T(8,128)(2,1)}, bf16[128,512]{1,0:T(8,128)(2,1)S(1)}, u32[]{:S(2)}, u32[]{:S(2)}) collective-permute-start(bf16[128,512]{1,0:T(8,128)(2,1)} %param.8), channel_id=1, source_target_pairs={{192,0},{224,32},{0,64},{32,96},{64,128},{96,160},{128,192},{160,2... | collective-permute-start | bytes 393224 | tf_op jit(solution)/shard_map/ppermute | solution.py:24
  8.8 17.5 %collective-permute-start.7 = (bf16[512,256]{1,0:T(8,128)(2,1)}, bf16[512,256]{1,0:T(8,128)(2,1)S(1)}, u32[]{:S(2)}, u32[]{:S(2)}) collective-permute-start(bf16[512,256]{1,0:T(8,128)(2,1)} %param.9), channel_id=1, source_target_pairs={{0,16},{16,0},{1,17},{17,1},{2,18},{18,2},{3,19},{19,3},{4,20},{20... | collective-permute-start | bytes 786440 | tf_op jit(solution)/shard_map/ppermute | solution.py:20
  12.4 7.0 %collective-permute-start.2 = (bf16[128,512]{1,0:T(8,128)(2,1)S(1)}, bf16[128,512]{1,0:T(8,128)(2,1)S(1)}, u32[]{:S(2)}, u32[]{:S(2)}) collective-permute-start(bf16[128,512]{1,0:T(8,128)(2,1)S(1)} %collective-permute-done), channel_id=1, source_target_pairs={{64,0},{96,32},{128,64},{160,96},{192,128},{224,160},{0,192},{32,2... | collective-permute-start | bytes 393224 | tf_op jit(solution)/shard_map/ppermute | solution.py:24
  16.7 9.5 %collective-permute-start.5 = (bf16[128,512]{1,0:T(8,128)(2,1)S(1)}, bf16[128,512]{1,0:T(8,128)(2,1)S(1)}, u32[]{:S(2)}, u32[]{:S(2)}) collective-permute-start(bf16[128,512]{1,0:T(8,128)(2,1)S(1)} %collective-permute-done.4), channel_id=1, source_target_pairs={{192,0},{224,32},{0,64},{32,96},{64,128},{96,160},{128,192},{160,2... | collective-permute-start | bytes 393224 | tf_op jit(solution)/shard_map/ppermute | solution.py:24
  19.5 6.7 %collective-permute-start.3 = (bf16[128,512]{1,0:T(8,128)(2,1)S(1)}, bf16[128,512]{1,0:T(8,128)(2,1)S(1)}, u32[]{:S(2)}, u32[]{:S(2)}) collective-permute-start(bf16[128,512]{1,0:T(8,128)(2,1)S(1)} %collective-permute-done.2), channel_id=1, source_target_pairs={{32,0},{64,32},{96,64},{128,96},{160,128},{192,160},{224,192},{0,2... | collective-permute-start | bytes 393224 | tf_op jit(solution)/shard_map/ppermute | solution.py:24
  28.0 47.7 %all-to-all-start = ((bf16[16,64,512]{2,1,0:T(8,128)(2,1)}), bf16[16,64,512]{2,1,0:T(8,128)(2,1)}, u32[]{:S(2)}, u32[]{:S(2)}) async-start(bf16[16,64,512]{2,1,0:T(8,128)(2,1)} %bitcast.87), calls=%async_computation | async-start | bytes 2097152 | tf_op jit(solution)/shard_map/all_to_all | solution.py:62
  77.1 5.3 %collective-permute-start.8 = (bf16[64,512]{1,0:T(8,128)(2,1)S(1)}, bf16[64,512]{1,0:T(8,128)(2,1)S(1)}, u32[]{:S(2)}, u32[]{:S(2)}) collective-permute-start(bf16[64,512]{1,0:T(8,128)(2,1)S(1)} %maximum_select_fusion.2), channel_id=1, source_target_pairs={{0,16},{16,0},{1,17},{17,1},{2,18},{18,2},{3,19},{19,3},{4,20},{20... | collective-permute-start | bytes 196616 | tf_op jit(solution)/shard_map/ppermute | solution.py:20
  82.6 5.8 %collective-permute-start.9 = (bf16[128,512]{1,0:T(8,128)(2,1)S(1)}, bf16[128,512]{1,0:T(8,128)(2,1)}, u32[]{:S(2)}, u32[]{:S(2)}) collective-permute-start(bf16[128,512]{1,0:T(8,128)(2,1)S(1)} %bitcast.88), channel_id=1, source_target_pairs={{32,0},{64,32},{96,64},{128,96},{160,128},{192,160},{224,192},{0,2... | collective-permute-start | bytes 393224 | tf_op jit(solution)/shard_map/ppermute | solution.py:24
  82.9 8.1 %collective-permute-start.13 = (bf16[128,512]{1,0:T(8,128)(2,1)S(1)}, bf16[128,512]{1,0:T(8,128)(2,1)S(1)}, u32[]{:S(2)}, u32[]{:S(2)}) collective-permute-start(bf16[128,512]{1,0:T(8,128)(2,1)S(1)} %bitcast.89), channel_id=1, source_target_pairs={{224,0},{0,32},{32,64},{64,96},{96,128},{128,160},{160,192},{192,2... | collective-permute-start | bytes 393224 | tf_op jit(solution)/shard_map/ppermute | solution.py:24
  84.7 14.2 %collective-permute-start.10 = (bf16[128,512]{1,0:T(8,128)(2,1)S(1)}, bf16[128,512]{1,0:T(8,128)(2,1)S(1)}, u32[]{:S(2)}, u32[]{:S(2)}) collective-permute-start(bf16[128,512]{1,0:T(8,128)(2,1)S(1)} %bitcast.90), channel_id=1, source_target_pairs={{64,0},{96,32},{128,64},{160,96},{192,128},{224,160},{0,192},{32,2... | collective-permute-start | bytes 393224 | tf_op jit(solution)/shard_map/ppermute | solution.py:24
  84.8 16.7 %collective-permute-start.15 = (bf16[128,512]{1,0:T(8,128)(2,1)S(1)}, bf16[128,512]{1,0:T(8,128)(2,1)S(1)}, u32[]{:S(2)}, u32[]{:S(2)}) collective-permute-start(bf16[128,512]{1,0:T(8,128)(2,1)S(1)} %bitcast.91), channel_id=1, source_target_pairs={{192,0},{224,32},{0,64},{32,96},{64,128},{96,160},{128,192},{160,2... | collective-permute-start | bytes 393224 | tf_op jit(solution)/shard_map/ppermute | solution.py:24
  88.3 7.5 %collective-permute-start.11 = (bf16[128,512]{1,0:T(8,128)(2,1)}, bf16[128,512]{1,0:T(8,128)(2,1)S(1)}, u32[]{:S(2)}, u32[]{:S(2)}) collective-permute-start(bf16[128,512]{1,0:T(8,128)(2,1)} %collective-permute-done.9), channel_id=1, source_target_pairs={{64,0},{96,32},{128,64},{160,96},{192,128},{224,160},{0,192},{32,2... | collective-permute-start | bytes 393224 | tf_op jit(solution)/shard_map/ppermute | solution.py:24
  91.1 10.5 %collective-permute-start.14 = (bf16[128,512]{1,0:T(8,128)(2,1)S(1)}, bf16[128,512]{1,0:T(8,128)(2,1)S(1)}, u32[]{:S(2)}, u32[]{:S(2)}) collective-permute-start(bf16[128,512]{1,0:T(8,128)(2,1)S(1)} %collective-permute-done.13), channel_id=1, source_target_pairs={{192,0},{224,32},{0,64},{32,96},{64,128},{96,160},{128,192},{160,2... | collective-permute-start | bytes 393224 | tf_op jit(solution)/shard_map/ppermute | solution.py:24
  95.9 5.7 %collective-permute-start.12 = (bf16[128,512]{1,0:T(8,128)(2,1)S(1)}, bf16[128,512]{1,0:T(8,128)(2,1)S(1)}, u32[]{:S(2)}, u32[]{:S(2)}) collective-permute-start(bf16[128,512]{1,0:T(8,128)(2,1)S(1)} %collective-permute-done.11), channel_id=1, source_target_pairs={{32,0},{64,32},{96,64},{128,96},{160,128},{192,160},{224,192},{0,2... | collective-permute-start | bytes 393224 | tf_op jit(solution)/shard_map/ppermute | solution.py:24
  102.8 31.6 %copy-start.7 = (bf16[1,4096,384]{2,1,0:T(8,128)(2,1)S(1)}, bf16[1,4096,384]{2,1,0:T(8,128)(2,1)}, u32[]{:S(2)}) copy-start(bf16[1,4096,384]{2,1,0:T(8,128)(2,1)} %param.14) | copy-start | bytes 9437188
  128.8 4.2 %collective-permute-start.16 = (bf16[256,4096]{1,0:T(8,128)(2,1)S(1)}, bf16[256,4096]{1,0:T(8,128)(2,1)S(1)}, u32[]{:S(2)}, u32[]{:S(2)}) collective-permute-start(bf16[256,4096]{1,0:T(8,128)(2,1)S(1)} %bitcast.84), channel_id=1, source_target_pairs={{0,1},{1,0},{2,3},{3,2},{4,5},{5,4},{6,7},{7,6},{8,9},{9,8},{10,11... | collective-permute-start | bytes 6291464 | tf_op jit(solution)/shard_map/ppermute | solution.py:20
  142.8 4.7 %collective-permute-start.17 = (bf16[256,4096]{1,0:T(8,128)(2,1)}, bf16[256,4096]{1,0:T(8,128)(2,1)}, u32[]{:S(2)}, u32[]{:S(2)}) collective-permute-start(bf16[256,4096]{1,0:T(8,128)(2,1)} %convolution_convert_fusion.1), channel_id=1, source_target_pairs={{0,1},{1,0},{2,3},{3,2},{4,5},{5,4},{6,7},{7,6},{8,9},{9,8},{10,11... | collective-permute-start | bytes 6291464 | tf_op jit(solution)/shard_map/ppermute | solution.py:20
  154.5 33.6 %all-to-all-start.2 = ((bf16[8,32,4096]{2,1,0:T(8,128)(2,1)}), bf16[8,32,4096]{2,1,0:T(8,128)(2,1)}, u32[]{:S(2)}, u32[]{:S(2)}) async-start(bf16[8,32,4096]{2,1,0:T(8,128)(2,1)} %bitcast.83), calls=%async_computation.2 | async-start | bytes 4194304 | tf_op jit(solution)/shard_map/all_to_all | solution.py:114
  194.1 14.3 %collective-permute-start.18 = (bf16[8,8,4096]{2,1,0:T(8,128)(2,1)}, bf16[8,8,4096]{2,1,0:T(8,128)(2,1)}, u32[]{:S(2)}, u32[]{:S(2)}) collective-permute-start(bf16[8,8,4096]{2,1,0:T(8,128)(2,1)} %dynamic-slice_bitcast_fusion), channel_id=1, source_target_pairs={{0,16},{16,0},{1,17},{17,1},{2,18},{18,2},{3,19},{19,3},{4,20},{20... | collective-permute-start | bytes 1572872 | tf_op jit(solution)/shard_map/ppermute | solution.py:20
  210.6 22.2 %all-to-all-start.3 = ((bf16[8,8,4096]{2,1,0:T(8,128)(2,1)}), bf16[8,8,4096]{2,1,0:T(8,128)(2,1)}, u32[]{:S(2)}, u32[]{:S(2)}) async-start(bf16[8,8,4096]{2,1,0:T(8,128)(2,1)} %fusion.24), calls=%async_computation.3 | async-start | bytes 1048576 | tf_op jit(solution)/shard_map/all_to_all | solution.py:126
  (8 other events, 66.7 us)

commit v2 on v1

v2 whole, which is shorter than its diff:
```python
import jax
import jax.numpy as jnp
from jax import lax
from jax.sharding import Mesh
from jax.sharding import PartitionSpec as P

TOPK = 8
CAP = 2

FINE = ("z", "xl", "xh", "y", "c")
SIZES = (8, 2, 2, 4, 2)
EXPERT = ("z", "xl")
TENSOR = ("xh", "y", "c")
SPREAD = ("xh", "y")
PLANE = ("xl", "xh", "y")
NZ = 8


def swap(x, axis):
    return lax.ppermute(x, axis, [(0, 1), (1, 0)])


def fetch(x, hop):
    return lax.ppermute(x, "z", [((i + hop) % NZ, i) for i in range(NZ)])


def gather_z(x):
    up1, dn1 = fetch(x, 1), fetch(x, -1)
    up2, dn2 = fetch(x, 2), fetch(x, -2)
    up3, dn3 = fetch(up1, 2), fetch(dn1, -2)
    far = fetch(up3, 1)
    return [x, up1, up2, up3, far, dn3, dn2, dn1]


def settle_z(blocks, zi):
    twice = jnp.stack(blocks + blocks, axis=0)
    return lax.dynamic_slice_in_dim(twice, lax.rem(NZ - zi, NZ), NZ, axis=0)


def hidden_rows(rows, w_gate, w_up):
    gate_act = jnp.dot(rows, w_gate, preferred_element_type=jnp.float32)
    up_act = jnp.dot(rows, w_up, preferred_element_type=jnp.float32)
    return (jax.nn.silu(gate_act) * up_act).astype(jnp.bfloat16)


def on_device(context, proj_weight, norm_gain, expert_ids, gate_values, w_gate, w_up, w_down):
    zi, ci = lax.axis_index("z"), lax.axis_index("c")
    xli = lax.axis_index("xl")
    n_tensor = lax.axis_size(TENSOR)
    n_spread = lax.axis_size(SPREAD)
    n_plane = lax.axis_size(PLANE)
    rows = context.shape[0] // n_tensor
    labels_z = n_plane // 2
    cols = proj_weight.shape[1]
    wide = 2 * cols
    width = NZ * wide
    tokens = NZ * rows

    high = gate_values.astype(jnp.bfloat16)
    low = (gate_values - high.astype(jnp.float32)).astype(jnp.bfloat16)
    note = jnp.concatenate([expert_ids.astype(jnp.bfloat16), high, low], axis=1)
    note = jnp.pad(note, ((0, 0), (0, context.shape[1] - note.shape[1])))
    gathered = gather_z(jnp.concatenate([context, note], axis=0))

    rhs = jnp.concatenate([proj_weight, swap(proj_weight, "xl")], axis=1)
    blocks = [g[: context.shape[0]].reshape(n_spread, 2, 1, rows, -1) for g in gathered]
    lhs = jnp.concatenate(blocks, axis=2)

    def partial_sum(core):
        part = lax.dynamic_index_in_dim(lhs, core, 1, keepdims=False)
        part = part.reshape(n_spread * tokens, -1)
        return jnp.dot(part, rhs, preferred_element_type=jnp.float32)

    got = swap(partial_sum(1 - ci).astype(jnp.bfloat16), "c")
    partial = (partial_sum(ci) + got.astype(jnp.float32)).astype(jnp.bfloat16)
    partial = lax.all_to_all(
        partial.reshape(n_spread, tokens, wide), SPREAD, 0, 0, tiled=True
    )
    part = jnp.sum(partial.astype(jnp.float32), axis=0).astype(jnp.bfloat16)
    part = jnp.where(xli == 0, part, jnp.concatenate([part[:, cols:], part[:, :cols]], axis=1))

    part = settle_z([part[k * rows : (k + 1) * rows] for k in range(NZ)], zi)
    attended = jnp.zeros((tokens, width), jnp.bfloat16)
    for hop, block in enumerate(gather_z(part.reshape(tokens, wide))):
        at = lax.rem(zi + hop, NZ) * wide
        attended = lax.dynamic_update_slice_in_dim(attended, block, at, axis=1)
    stream = attended.astype(jnp.float32)
    scale = lax.rsqrt(jnp.mean(stream * stream, axis=-1, keepdims=True) + 1e-06)
    normed = (stream * scale * norm_gain).astype(jnp.bfloat16)

    notes = settle_z([g[context.shape[0] :, : 3 * TOPK] for g in gathered], zi)
    notes = notes.reshape(tokens, 3 * TOPK).astype(jnp.float32)
    ids = notes[:, :TOPK].astype(jnp.int32)
    gates = notes[:, TOPK : 2 * TOPK] + notes[:, 2 * TOPK :]
    labels = zi * labels_z + jnp.arange(labels_z, dtype=jnp.int32)
    match = ids[:, :, None] == labels[None, None, :]
    chosen = jnp.sum(match.astype(jnp.int32), axis=1)
    weight = jnp.sum(jnp.where(match, gates[:, :, None], 0.0), axis=1)
    blocked = chosen.reshape(NZ, rows, labels_z)
    rank = (jnp.cumsum(blocked, axis=1) - blocked).reshape(tokens, labels_z)
    base = (jnp.arange(tokens, dtype=jnp.int32) // rows) * CAP
    slot = jnp.where(chosen > 0, base[:, None] + rank, -1)
    slots = NZ * CAP
    placing = slot[:, :, None] == jnp.arange(slots, dtype=jnp.int32)[None, None, :]
    placing = jnp.repeat(placing, 2, axis=1).reshape(tokens, n_plane * slots)
    weight = jnp.where(placing, jnp.repeat(weight, 2 * slots, axis=1), 0.0)

    sent = lax.dot_general(
        placing.astype(jnp.bfloat16),
        normed,
        (((0,), (0,)), ((), ())),
        preferred_element_type=jnp.float32,
    ).astype(jnp.bfloat16)
    sent = sent.reshape(n_plane, slots, width)
    mine = lax.all_to_all(sent, PLANE, 0, 0, tiled=True).reshape(n_plane * slots, width)
    theirs = swap(mine, "c")
    mine_hidden = hidden_rows(mine, w_gate[0], w_up[0])
    theirs_hidden = hidden_rows(theirs, w_gate[0], w_up[0])
    theirs_out = jnp.dot(theirs_hidden, w_down[0], preferred_element_type=jnp.float32)
    from_mate = swap(theirs_out.astype(jnp.bfloat16), "c")
    mine_out = jnp.dot(mine_hidden, w_down[0], preferred_element_type=jnp.float32)
    summed = (mine_out + from_mate.astype(jnp.float32)).astype(jnp.bfloat16)
    summed = summed.reshape(n_plane, slots, width)
    back = lax.all_to_all(summed, PLANE, 0, 0, tiled=True).reshape(n_plane * slots, width)

    high = weight.astype(jnp.bfloat16)
    low = (weight - high.astype(jnp.float32)).astype(jnp.bfloat16)
    mixture = jnp.dot(high, back, preferred_element_type=jnp.float32) + jnp.dot(
        low, back, preferred_element_type=jnp.float32
    )
    mixture = mixture.astype(jnp.bfloat16).reshape(NZ, rows, width)
    total = lax.dynamic_slice_in_dim(attended, zi * rows, rows, axis=0).astype(jnp.float32)
    total += lax.dynamic_index_in_dim(mixture, zi, 0, keepdims=False).astype(jnp.float32)
    for hop in (4, 1, 7, 2, 6, 3, 5):
        block = lax.dynamic_index_in_dim(mixture, lax.rem(zi + hop, NZ), 0, keepdims=False)
        total += fetch(block, -hop).astype(jnp.float32)
    return total.astype(jnp.bfloat16)


def solution(mesh):
    fine = Mesh(mesh.devices.reshape(SIZES), FINE)
    both = EXPERT + TENSOR
    return jax.shard_map(
        on_device,
        mesh=fine,
        in_specs=(
            P(EXPERT, TENSOR),
            P(TENSOR, EXPERT),
            P(),
            P(both, None),
            P(both, None),
            P(both, None, None),
            P(both, None, None),
            P(both, None, None),
        ),
        out_specs=P(both, None),
        check_vma=False,
    )
```

time: 237 us -> 205 us (0.86)
  blocking collectives: 63.7 us -> 30.3 us
  waiting for transfers between devices: 77.6 us -> 51.3 us
  local copies, waits for them, and re-layouts: 7.07 us -> 25.7 us
  starting transfers between devices: 52.3 us -> 59.3 us
    all_gather x1 -> x0, blocking collectives: 39 us -> none  [on_device(): routing = lax.all_gather(routing, EXPERT, axis=0, tiled=True)]
    ppermute x14 -> x21, starting transfers between devices: 26 us -> 45.2 us  [fetch(): return lax.ppermute(x, 'z', [((i + hop) % NZ, i) for i in range(NZ)])]
    ppermute x5 -> x4, waiting for transfers between devices: 18.6 us -> 4.16 us  [swap(): return lax.ppermute(x, axis, [(0, 1), (1, 0)])]
    unnamed x28 -> x58, local copies, waits for them, and re-layouts: 4.73 us -> 17.5 us
    all_to_all x2 -> x1, waiting for transfers between devices: 16.7 us -> 7.63 us  [on_device(): lax.all_to_all(partial.reshape(n_spread, tokens, wide), SPREAD, 0, 0, til...]
    ppermute x14 -> x21, waiting for transfers between devices: 16.1 us -> 10.4 us  [fetch(): return lax.ppermute(x, 'z', [((i + hop) % NZ, i) for i in range(NZ)])]
    all_to_all x1, blocking collectives: 24.7 us -> 30.3 us  [on_device(): lax.all_to_all(sent, PLANE, 0, 0, tiled=True)]
    all_to_all x2 -> x1, starting transfers between devices: 13 us -> 7.43 us  [on_device(): lax.all_to_all(partial.reshape(n_spread, tokens, wide), SPREAD, 0, 0, til...]
  transfers between devices with their start and end apart: 22 -> 27, of which waited for: 13 -> 9; matrix products, arithmetic and copies ran while one was open for 3% -> 12% of each run, Pallas kernels for 0% -> 0%
where the time goes in v2:
time: 205 us; the launch traced here: 202 us
  starting transfers between devices  59.3 us (29%)
  waiting for transfers between devices  51.3 us (25%)
  blocking collectives  30.3 us (15%)
  matrix products  26.6 us (13%)
  local copies, waits for them, and re-layouts  25.7 us (13%)
  other arithmetic  8.39 us (4%)
    ppermute x21, starting transfers between devices, fetch(): return lax.ppermute(x, 'z', [((i + hop) % NZ, i) for i in range(NZ)])  45.2 us
    all_to_all x1, blocking collectives, on_device(): lax.all_to_all(sent, PLANE, 0, 0, tiled=True)  30.3 us
    all_to_all x1, waiting for transfers between devices, on_device(): lax.all_to_all(summed, PLANE, 0, 0, tiled=True)  29.1 us
    unnamed x58, local copies, waits for them, and re-layouts  17.5 us
    ppermute x21, waiting for transfers between devices, fetch(): return lax.ppermute(x, 'z', [((i + hop) % NZ, i) for i in range(NZ)])  10.4 us
    all_to_all x1, waiting for transfers between devices, on_device(): lax.all_to_all(partial.reshape(n_spread, tokens, wide), SPREAD, 0, 0, til...  7.63 us
    all_to_all x1, starting transfers between devices, on_device(): lax.all_to_all(partial.reshape(n_spread, tokens, wide), SPREAD, 0, 0, til...  7.43 us
    dot_general x1, matrix products, on_device(): jnp.dot(mine_hidden, w_down[0], preferred_element_type=jnp.float32)  7.04 us
  transfers between devices with their start and end apart: 27, of which 9 were waited for; matrix products, arithmetic and copies ran while one was open for 12% of the time, Pallas kernels for 0%

profile of v2, /device:TPU:6, one launch (start us, length us, event | category | flops | bytes accessed | tf_op | source)
XLA Modules:
  0.0 202.1 jit_solution(16117123798749125279)
XLA Ops:
  3.2 5.9 %collective-permute-start = (bf16[136,512]{1,0:T(8,128)(2,1)S(1)}, bf16[136,512]{1,0:T(8,128)(2,1)}, u32[]{:S(2)}, u32[]{:S(2)}) collective-permute-start(bf16[136,512]{1,0:T(8,128)(2,1)S(1)} %fusion.42), channel_id=1, source_target_pairs={{32,0},{64,32},{96,64},{128,96},{160,128},{192,160},{224,192},{0,2... | collective-permute-start | bytes 417800 | tf_op jit(solution)/shard_map/ppermute | solution.py:24
  18.4 3.7 %collective-permute-start.2 = (bf16[136,512]{1,0:T(8,128)(2,1)}, bf16[136,512]{1,0:T(8,128)(2,1)S(1)}, u32[]{:S(2)}, u32[]{:S(2)}) collective-permute-start(bf16[136,512]{1,0:T(8,128)(2,1)} %collective-permute-done), channel_id=1, source_target_pairs={{64,0},{96,32},{128,64},{160,96},{192,128},{224,160},{0,192},{32,2... | collective-permute-start | bytes 417800 | tf_op jit(solution)/shard_map/ppermute | solution.py:24
  28.8 3.7 %collective-permute-start.3 = (bf16[136,512]{1,0:T(8,128)(2,1)S(1)}, bf16[136,512]{1,0:T(8,128)(2,1)S(1)}, u32[]{:S(2)}, u32[]{:S(2)}) collective-permute-start(bf16[136,512]{1,0:T(8,128)(2,1)S(1)} %collective-permute-done.2), channel_id=1, source_target_pairs={{32,0},{64,32},{96,64},{128,96},{160,128},{192,160},{224,192},{0,2... | collective-permute-start | bytes 417800 | tf_op jit(solution)/shard_map/ppermute | solution.py:24
  45.1 7.4 %all-to-all-start = ((bf16[8,64,512]{2,1,0:T(8,128)(2,1)}), bf16[8,64,512]{2,1,0:T(8,128)(2,1)}, u32[]{:S(2)}, u32[]{:S(2)}) async-start(bf16[8,64,512]{2,1,0:T(8,128)(2,1)} %bitcast.187), calls=%async_computation | async-start | bytes 1048576 | tf_op jit(solution)/shard_map/all_to_all | solution.py:76
  54.3 7.6 %all-to-all-done = bf16[8,64,512]{2,1,0:T(8,128)(2,1)} async-done(((bf16[8,64,512]{2,1,0:T(8,128)(2,1)}), bf16[8,64,512]{2,1,0:T(8,128)(2,1)}, u32[]{:S(2)}, u32[]{:S(2)}) %all-to-all-start) | async-done | bytes 524320 | tf_op jit(solution)/shard_map/all_to_all | solution.py:76
  63.3 3.7 %collective-permute-start.9 = (bf16[64,512]{1,0:T(8,128)(2,1)S(1)}, bf16[64,512]{1,0:T(8,128)(2,1)S(1)}, u32[]{:S(2)}, u32[]{:S(2)}) collective-permute-start(bf16[64,512]{1,0:T(8,128)(2,1)S(1)} %get-tuple-element.6), channel_id=1, source_target_pairs={{32,0},{64,32},{96,64},{128,96},{160,128},{192,160},{224,192},{0,2... | collective-permute-start | bytes 196616 | tf_op jit(solution)/shard_map/ppermute | solution.py:24
  70.1 2.8 %collective-permute-start.11 = (bf16[64,512]{1,0:T(8,128)(2,1)S(1)}, bf16[64,512]{1,0:T(8,128)(2,1)S(1)}, u32[]{:S(2)}, u32[]{:S(2)}) collective-permute-start(bf16[64,512]{1,0:T(8,128)(2,1)S(1)} %collective-permute-done.9), channel_id=1, source_target_pairs={{64,0},{96,32},{128,64},{160,96},{192,128},{224,160},{0,192},{32,2... | collective-permute-start | bytes 196616 | tf_op jit(solution)/shard_map/ppermute | solution.py:24
  73.0 2.6 %collective-permute-done.11 = bf16[64,512]{1,0:T(8,128)(2,1)S(1)} collective-permute-done((bf16[64,512]{1,0:T(8,128)(2,1)S(1)}, bf16[64,512]{1,0:T(8,128)(2,1)S(1)}, u32[]{:S(2)}, u32[]{:S(2)}) %collective-permute-start.11) | collective-permute-done | bytes 65568 | tf_op jit(solution)/shard_map/ppermute | solution.py:24
  75.6 5.3 %collective-permute-start.12 = (bf16[64,512]{1,0:T(8,128)(2,1)S(1)}, bf16[64,512]{1,0:T(8,128)(2,1)S(1)}, u32[]{:S(2)}, u32[]{:S(2)}) collective-permute-start(bf16[64,512]{1,0:T(8,128)(2,1)S(1)} %collective-permute-done.11), channel_id=1, source_target_pairs={{32,0},{64,32},{96,64},{128,96},{160,128},{192,160},{224,192},{0,2... | collective-permute-start | bytes 196616 | tf_op jit(solution)/shard_map/ppermute | solution.py:24
  83.9 30.3 %all_to_all.15 = bf16[16,16,4096]{2,1,0:T(8,128)(2,1)S(1)} all-to-all(bf16[16,16,4096]{2,1,0:T(8,128)(2,1)S(1)} %bitcast.180), channel_id=1, replica_groups=mesh['z'=8,'xl'=2,'xh'=2,'y'=4,'c'=2] {'xl','xh','y'}, dimensions={0} | all-to-all | bytes 4194304 | tf_op jit(solution)/shard_map/all_to_all | solution.py:115
  115.6 4.2 %collective-permute-done.16 = bf16[256,4096]{1,0:T(8,128)(2,1)S(1)} collective-permute-done((bf16[256,4096]{1,0:T(8,128)(2,1)S(1)}, bf16[256,4096]{1,0:T(8,128)(2,1)S(1)}, u32[]{:S(2)}, u32[]{:S(2)}) %collective-permute-start.16) | collective-permute-done | bytes 2097184 | tf_op jit(solution)/shard_map/ppermute | solution.py:20
  121.1 2.0 %fusion.7 = f32[256,384]{1,0:T(8,128)} fusion(bf16[256,4096]{1,0:T(8,128)(2,1)S(1)} %collective-permute-done.16, bf16[1,4096,384]{2,1,0:T(8,128)(2,1)S(1)} %copy-done.8), kind=kOutput, calls=%fused_computation.9 | convolution fusion | flops 805306368 | bytes 5636096 | tf_op jit(solution)/shard_map/dot_general | solution.py:42
  123.2 6.4 %convolution_convert_fusion = bf16[256,4096]{1,0:T(8,128)(2,1)} fusion(bf16[1,384,4096]{2,1,0:T(8,128)(2,1)S(1)} %copy-done, f32[256,384]{1,0:T(8,128)} %fusion.7, bf16[256,4096]{1,0:T(8,128)(2,1)} %copy-done.9, bf16[1,4096,384]{2,1,0:T(8,128)(2,1)} %param.13), kind=kOutput, calls=%fused_computation | convolution fusion | flops 1612251136 | bytes 10878976 | tf_op jit(solution)/shard_map/dot_general | solution.py:119
  129.7 4.5 %fusion.13 = f32[256,384]{1,0:T(8,128)} fusion(bf16[256,4096]{1,0:T(8,128)(2,1)} %bitcast.184, bf16[1,4096,384]{2,1,0:T(8,128)(2,1)} %param.13), kind=kOutput, calls=%fused_computation.15 | convolution fusion | flops 805306368 | bytes 5636096 | tf_op jit(solution)/shard_map/dot_general | solution.py:41
  134.2 7.0 %add_convert_fusion = bf16[256,4096]{1,0:T(8,128)(2,1)} fusion(bf16[256,4096]{1,0:T(8,128)(2,1)} %collective-permute-done.17, bf16[1,384,4096]{2,1,0:T(8,128)(2,1)S(1)} %copy-done, bf16[256,4096]{1,0:T(8,128)(2,1)} %bitcast.185, bf16[1,4096,384]{2,1,0:T(8,128)(2,1)} %param.14, f32[256,384]{1,0:T(8,128)} %fusion.13), kind=kOutput, calls=%fused_computation.5 | convolution fusion | flops 1614348288 | bytes 12976128 | tf_op jit(solution)/shard_map/dot_general | solution.py:121
  141.2 5.7 %all-to-all-start.2 = ((bf16[16,16,4096]{2,1,0:T(8,128)(2,1)}), bf16[16,16,4096]{2,1,0:T(8,128)(2,1)}, u32[]{:S(2)}, u32[]{:S(2)}) async-start(bf16[16,16,4096]{2,1,0:T(8,128)(2,1)} %bitcast.182), calls=%async_computation.2 | async-start | bytes 4194304 | tf_op jit(solution)/shard_map/all_to_all | solution.py:124
  147.1 29.1 %all-to-all-done.2 = bf16[16,16,4096]{2,1,0:T(8,128)(2,1)} async-done(((bf16[16,16,4096]{2,1,0:T(8,128)(2,1)}), bf16[16,16,4096]{2,1,0:T(8,128)(2,1)}, u32[]{:S(2)}, u32[]{:S(2)}) %all-to-all-start.2) | async-done | bytes 2097184 | tf_op jit(solution)/shard_map/all_to_all | solution.py:124
  176.2 2.1 %fusion.59 = f32[64,4096]{1,0:T(8,128)S(1)} fusion(bf16[64,256]{0,1:T(8,128)(2,1)S(1)} %bitcast.197, bf16[256,4096]{1,0:T(8,128)(2,1)} %bitcast.38), kind=kOutput, calls=%fused_computation.149 | convolution fusion | flops 134217728 | bytes 3178496 | tf_op jit(solution)/shard_map/dot_general | solution.py:128
  178.3 2.1 %fusion.1 = bf16[8,8,4096]{2,1,0:T(8,128)(2,1)S(1)} fusion(f32[64,4096]{1,0:T(8,128)S(1)} %fusion.59, bf16[64,256]{0,1:T(8,128)(2,1)S(1)} %bitcast.196, bf16[256,4096]{1,0:T(8,128)(2,1)} %bitcast.38), kind=kOutput, calls=%fused_computation.4 | convolution fusion | flops 134742016 | bytes 3702784 | tf_op jit(solution)/shard_map/dot_general | solution.py:128
  184.7 2.1 %collective-permute-start.20 = (bf16[8,4096]{1,0:T(8,128)(2,1)}, bf16[8,4096]{1,0:T(8,128)(2,1)S(1)}, u32[]{:S(2)}, u32[]{:S(2)}) collective-permute-start(bf16[8,4096]{1,0:T(8,128)(2,1)} %get-tuple-element.18), channel_id=1, source_target_pairs={{32,0},{64,32},{96,64},{128,96},{160,128},{192,160},{224,192},{0,2... | collective-permute-start | bytes 196616 | tf_op jit(solution)/shard_map/ppermute | solution.py:24
  186.7 2.1 %collective-permute-start.21 = (bf16[8,4096]{1,0:T(8,128)(2,1)}, bf16[8,4096]{1,0:T(8,128)(2,1)S(1)}, u32[]{:S(2)}, u32[]{:S(2)}) collective-permute-start(bf16[8,4096]{1,0:T(8,128)(2,1)} %get-tuple-element.17), channel_id=1, source_target_pairs={{192,0},{224,32},{0,64},{32,96},{64,128},{96,160},{128,192},{160,2... | collective-permute-start | bytes 196616 | tf_op jit(solution)/shard_map/ppermute | solution.py:24
  188.8 2.1 %collective-permute-start.22 = (bf16[8,4096]{1,0:T(8,128)(2,1)}, bf16[8,4096]{1,0:T(8,128)(2,1)S(1)}, u32[]{:S(2)}, u32[]{:S(2)}) collective-permute-start(bf16[8,4096]{1,0:T(8,128)(2,1)} %get-tuple-element.16), channel_id=1, source_target_pairs={{64,0},{96,32},{128,64},{160,96},{192,128},{224,160},{0,192},{32,2... | collective-permute-start | bytes 196616 | tf_op jit(solution)/shard_map/ppermute | solution.py:24
  193.2 3.3 %collective-permute-start.24 = (bf16[8,4096]{1,0:T(8,128)(2,1)}, bf16[8,4096]{1,0:T(8,128)(2,1)}, u32[]{:S(2)}, u32[]{:S(2)}) collective-permute-start(bf16[8,4096]{1,0:T(8,128)(2,1)} %get-tuple-element.14), channel_id=1, source_target_pairs={{96,0},{128,32},{160,64},{192,96},{224,128},{0,160},{32,192},{64,2... | collective-permute-start | bytes 196616 | tf_op jit(solution)/shard_map/ppermute | solution.py:24
  196.5 3.1 %collective-permute-done.23 = bf16[8,4096]{1,0:T(8,128)(2,1)S(1)} collective-permute-done((bf16[8,4096]{1,0:T(8,128)(2,1)}, bf16[8,4096]{1,0:T(8,128)(2,1)S(1)}, u32[]{:S(2)}, u32[]{:S(2)}) %collective-permute-start.23) | collective-permute-done | bytes 65568 | tf_op jit(solution)/shard_map/ppermute | solution.py:24
  (148 shorter events, 52.9 us)
Async XLA Ops:
  3.2 13.6 %collective-permute-start = (bf16[136,512]{1,0:T(8,128)(2,1)S(1)}, bf16[136,512]{1,0:T(8,128)(2,1)}, u32[]{:S(2)}, u32[]{:S(2)}) collective-permute-start(bf16[136,512]{1,0:T(8,128)(2,1)S(1)} %fusion.42), channel_id=1, source_target_pairs={{32,0},{64,32},{96,64},{128,96},{160,128},{192,160},{224,192},{0,2... | collective-permute-start | bytes 417800 | tf_op jit(solution)/shard_map/ppermute | solution.py:24
  9.2 12.9 %collective-permute-start.1 = (bf16[136,512]{1,0:T(8,128)(2,1)S(1)}, bf16[136,512]{1,0:T(8,128)(2,1)}, u32[]{:S(2)}, u32[]{:S(2)}) collective-permute-start(bf16[136,512]{1,0:T(8,128)(2,1)S(1)} %fusion.42), channel_id=1, source_target_pairs={{64,0},{96,32},{128,64},{160,96},{192,128},{224,160},{0,192},{32,2... | collective-permute-start | bytes 417800 | tf_op jit(solution)/shard_map/ppermute | solution.py:24
  10.6 13.0 %collective-permute-start.4 = (bf16[136,512]{1,0:T(8,128)(2,1)S(1)}, bf16[136,512]{1,0:T(8,128)(2,1)}, u32[]{:S(2)}, u32[]{:S(2)}) collective-permute-start(bf16[136,512]{1,0:T(8,128)(2,1)S(1)} %fusion.42), channel_id=1, source_target_pairs={{224,0},{0,32},{32,64},{64,96},{96,128},{128,160},{160,192},{192,2... | collective-permute-start | bytes 417800 | tf_op jit(solution)/shard_map/ppermute | solution.py:24
  11.6 15.4 %collective-permute-start.6 = (bf16[136,512]{1,0:T(8,128)(2,1)S(1)}, bf16[136,512]{1,0:T(8,128)(2,1)}, u32[]{:S(2)}, u32[]{:S(2)}) collective-permute-start(bf16[136,512]{1,0:T(8,128)(2,1)S(1)} %fusion.42), channel_id=1, source_target_pairs={{192,0},{224,32},{0,64},{32,96},{64,128},{96,160},{128,192},{160,2... | collective-permute-start | bytes 417800 | tf_op jit(solution)/shard_map/ppermute | solution.py:24
  12.1 15.9 %collective-permute-start.7 = (bf16[512,256]{1,0:T(8,128)(2,1)}, bf16[512,256]{1,0:T(8,128)(2,1)S(1)}, u32[]{:S(2)}, u32[]{:S(2)}) collective-permute-start(bf16[512,256]{1,0:T(8,128)(2,1)} %param.9), channel_id=1, source_target_pairs={{0,16},{16,0},{1,17},{17,1},{2,18},{18,2},{3,19},{19,3},{4,20},{20... | collective-permute-start | bytes 786440 | tf_op jit(solution)/shard_map/ppermute | solution.py:20
  18.4 10.4 %collective-permute-start.2 = (bf16[136,512]{1,0:T(8,128)(2,1)}, bf16[136,512]{1,0:T(8,128)(2,1)S(1)}, u32[]{:S(2)}, u32[]{:S(2)}) collective-permute-start(bf16[136,512]{1,0:T(8,128)(2,1)} %collective-permute-done), channel_id=1, source_target_pairs={{64,0},{96,32},{128,64},{160,96},{192,128},{224,160},{0,192},{32,2... | collective-permute-start | bytes 417800 | tf_op jit(solution)/shard_map/ppermute | solution.py:24
  23.7 9.4 %collective-permute-start.5 = (bf16[136,512]{1,0:T(8,128)(2,1)}, bf16[136,512]{1,0:T(8,128)(2,1)S(1)}, u32[]{:S(2)}, u32[]{:S(2)}) collective-permute-start(bf16[136,512]{1,0:T(8,128)(2,1)} %collective-permute-done.4), channel_id=1, source_target_pairs={{192,0},{224,32},{0,64},{32,96},{64,128},{96,160},{128,192},{160,2... | collective-permute-start | bytes 417800 | tf_op jit(solution)/shard_map/ppermute | solution.py:24
  28.8 6.3 %collective-permute-start.3 = (bf16[136,512]{1,0:T(8,128)(2,1)S(1)}, bf16[136,512]{1,0:T(8,128)(2,1)S(1)}, u32[]{:S(2)}, u32[]{:S(2)}) collective-permute-start(bf16[136,512]{1,0:T(8,128)(2,1)S(1)} %collective-permute-done.2), channel_id=1, source_target_pairs={{32,0},{64,32},{96,64},{128,96},{160,128},{192,160},{224,192},{0,2... | collective-permute-start | bytes 417800 | tf_op jit(solution)/shard_map/ppermute | solution.py:24
  45.1 16.8 %all-to-all-start = ((bf16[8,64,512]{2,1,0:T(8,128)(2,1)}), bf16[8,64,512]{2,1,0:T(8,128)(2,1)}, u32[]{:S(2)}, u32[]{:S(2)}) async-start(bf16[8,64,512]{2,1,0:T(8,128)(2,1)} %bitcast.187), calls=%async_computation | async-start | bytes 1048576 | tf_op jit(solution)/shard_map/all_to_all | solution.py:76
  63.3 6.8 %collective-permute-start.9 = (bf16[64,512]{1,0:T(8,128)(2,1)S(1)}, bf16[64,512]{1,0:T(8,128)(2,1)S(1)}, u32[]{:S(2)}, u32[]{:S(2)}) collective-permute-start(bf16[64,512]{1,0:T(8,128)(2,1)S(1)} %get-tuple-element.6), channel_id=1, source_target_pairs={{32,0},{64,32},{96,64},{128,96},{160,128},{192,160},{224,192},{0,2... | collective-permute-start | bytes 196616 | tf_op jit(solution)/shard_map/ppermute | solution.py:24
  67.0 5.8 %collective-permute-start.13 = (bf16[64,512]{1,0:T(8,128)(2,1)S(1)}, bf16[64,512]{1,0:T(8,128)(2,1)S(1)}, u32[]{:S(2)}, u32[]{:S(2)}) collective-permute-start(bf16[64,512]{1,0:T(8,128)(2,1)S(1)} %get-tuple-element.6), channel_id=1, source_target_pairs={{224,0},{0,32},{32,64},{64,96},{96,128},{128,160},{160,192},{192,2... | collective-permute-start | bytes 196616 | tf_op jit(solution)/shard_map/ppermute | solution.py:24
  67.1 6.0 %collective-permute-start.10 = (bf16[64,512]{1,0:T(8,128)(2,1)S(1)}, bf16[64,512]{1,0:T(8,128)(2,1)S(1)}, u32[]{:S(2)}, u32[]{:S(2)}) collective-permute-start(bf16[64,512]{1,0:T(8,128)(2,1)S(1)} %get-tuple-element.6), channel_id=1, source_target_pairs={{64,0},{96,32},{128,64},{160,96},{192,128},{224,160},{0,192},{32,2... | collective-permute-start | bytes 196616 | tf_op jit(solution)/shard_map/ppermute | solution.py:24
  68.7 14.1 %collective-permute-start.15 = (bf16[64,512]{1,0:T(8,128)(2,1)S(1)}, bf16[64,512]{1,0:T(8,128)(2,1)S(1)}, u32[]{:S(2)}, u32[]{:S(2)}) collective-permute-start(bf16[64,512]{1,0:T(8,128)(2,1)S(1)} %get-tuple-element.6), channel_id=1, source_target_pairs={{192,0},{224,32},{0,64},{32,96},{64,128},{96,160},{128,192},{160,2... | collective-permute-start | bytes 196616 | tf_op jit(solution)/shard_map/ppermute | solution.py:24
  70.1 5.5 %collective-permute-start.11 = (bf16[64,512]{1,0:T(8,128)(2,1)S(1)}, bf16[64,512]{1,0:T(8,128)(2,1)S(1)}, u32[]{:S(2)}, u32[]{:S(2)}) collective-permute-start(bf16[64,512]{1,0:T(8,128)(2,1)S(1)} %collective-permute-done.9), channel_id=1, source_target_pairs={{64,0},{96,32},{128,64},{160,96},{192,128},{224,160},{0,192},{32,2... | collective-permute-start | bytes 196616 | tf_op jit(solution)/shard_map/ppermute | solution.py:24
  72.8 10.0 %collective-permute-start.14 = (bf16[64,512]{1,0:T(8,128)(2,1)S(1)}, bf16[64,512]{1,0:T(8,128)(2,1)S(1)}, u32[]{:S(2)}, u32[]{:S(2)}) collective-permute-start(bf16[64,512]{1,0:T(8,128)(2,1)S(1)} %collective-permute-done.13), channel_id=1, source_target_pairs={{192,0},{224,32},{0,64},{32,96},{64,128},{96,160},{128,192},{160,2... | collective-permute-start | bytes 196616 | tf_op jit(solution)/shard_map/ppermute | solution.py:24
  75.6 7.2 %collective-permute-start.12 = (bf16[64,512]{1,0:T(8,128)(2,1)S(1)}, bf16[64,512]{1,0:T(8,128)(2,1)S(1)}, u32[]{:S(2)}, u32[]{:S(2)}) collective-permute-start(bf16[64,512]{1,0:T(8,128)(2,1)S(1)} %collective-permute-done.11), channel_id=1, source_target_pairs={{32,0},{64,32},{96,64},{128,96},{160,128},{192,160},{224,192},{0,2... | collective-permute-start | bytes 196616 | tf_op jit(solution)/shard_map/ppermute | solution.py:24
  141.2 35.0 %all-to-all-start.2 = ((bf16[16,16,4096]{2,1,0:T(8,128)(2,1)}), bf16[16,16,4096]{2,1,0:T(8,128)(2,1)}, u32[]{:S(2)}, u32[]{:S(2)}) async-start(bf16[16,16,4096]{2,1,0:T(8,128)(2,1)} %bitcast.182), calls=%async_computation.2 | async-start | bytes 4194304 | tf_op jit(solution)/shard_map/all_to_all | solution.py:124
  181.9 9.6 %collective-permute-start.18 = (bf16[8,4096]{1,0:T(8,128)(2,1)S(1)}, bf16[8,4096]{1,0:T(8,128)(2,1)S(1)}, u32[]{:S(2)}, u32[]{:S(2)}) collective-permute-start(bf16[8,4096]{1,0:T(8,128)(2,1)S(1)} %get-tuple-element.13), channel_id=1, source_target_pairs={{128,0},{160,32},{192,64},{224,96},{0,128},{32,160},{64,192},{96,2... | collective-permute-start | bytes 196616 | tf_op jit(solution)/shard_map/ppermute | solution.py:24
  183.5 9.7 %collective-permute-start.19 = (bf16[8,4096]{1,0:T(8,128)(2,1)S(1)}, bf16[8,4096]{1,0:T(8,128)(2,1)S(1)}, u32[]{:S(2)}, u32[]{:S(2)}) collective-permute-start(bf16[8,4096]{1,0:T(8,128)(2,1)S(1)} %get-tuple-element.19), channel_id=1, source_target_pairs={{224,0},{0,32},{32,64},{64,96},{96,128},{128,160},{160,192},{192,2... | collective-permute-start | bytes 196616 | tf_op jit(solution)/shard_map/ppermute | solution.py:24
  184.7 11.8 %collective-permute-start.20 = (bf16[8,4096]{1,0:T(8,128)(2,1)}, bf16[8,4096]{1,0:T(8,128)(2,1)S(1)}, u32[]{:S(2)}, u32[]{:S(2)}) collective-permute-start(bf16[8,4096]{1,0:T(8,128)(2,1)} %get-tuple-element.18), channel_id=1, source_target_pairs={{32,0},{64,32},{96,64},{128,96},{160,128},{192,160},{224,192},{0,2... | collective-permute-start | bytes 196616 | tf_op jit(solution)/shard_map/ppermute | solution.py:24
  186.7 9.8 %collective-permute-start.21 = (bf16[8,4096]{1,0:T(8,128)(2,1)}, bf16[8,4096]{1,0:T(8,128)(2,1)S(1)}, u32[]{:S(2)}, u32[]{:S(2)}) collective-permute-start(bf16[8,4096]{1,0:T(8,128)(2,1)} %get-tuple-element.17), channel_id=1, source_target_pairs={{192,0},{224,32},{0,64},{32,96},{64,128},{96,160},{128,192},{160,2... | collective-permute-start | bytes 196616 | tf_op jit(solution)/shard_map/ppermute | solution.py:24
  188.8 7.7 %collective-permute-start.22 = (bf16[8,4096]{1,0:T(8,128)(2,1)}, bf16[8,4096]{1,0:T(8,128)(2,1)S(1)}, u32[]{:S(2)}, u32[]{:S(2)}) collective-permute-start(bf16[8,4096]{1,0:T(8,128)(2,1)} %get-tuple-element.16), channel_id=1, source_target_pairs={{64,0},{96,32},{128,64},{160,96},{192,128},{224,160},{0,192},{32,2... | collective-permute-start | bytes 196616 | tf_op jit(solution)/shard_map/ppermute | solution.py:24
  191.5 8.2 %collective-permute-start.23 = (bf16[8,4096]{1,0:T(8,128)(2,1)}, bf16[8,4096]{1,0:T(8,128)(2,1)S(1)}, u32[]{:S(2)}, u32[]{:S(2)}) collective-permute-start(bf16[8,4096]{1,0:T(8,128)(2,1)} %get-tuple-element.15), channel_id=1, source_target_pairs={{160,0},{192,32},{224,64},{0,96},{32,128},{64,160},{96,192},{128,2... | collective-permute-start | bytes 196616 | tf_op jit(solution)/shard_map/ppermute | solution.py:24
  193.2 7.3 %collective-permute-start.24 = (bf16[8,4096]{1,0:T(8,128)(2,1)}, bf16[8,4096]{1,0:T(8,128)(2,1)}, u32[]{:S(2)}, u32[]{:S(2)}) collective-permute-start(bf16[8,4096]{1,0:T(8,128)(2,1)} %get-tuple-element.14), channel_id=1, source_target_pairs={{96,0},{128,32},{160,64},{192,96},{224,128},{0,160},{32,192},{64,2... | collective-permute-start | bytes 196616 | tf_op jit(solution)/shard_map/ppermute | solution.py:24
  (13 other events, 258.4 us)

commit v3 on v2

v3 whole, which is shorter than its diff:
```python
import functools

import jax
import jax.numpy as jnp
from jax import lax
from jax.experimental import pallas as pl
from jax.experimental.pallas import tpu as pltpu
from jax.sharding import Mesh
from jax.sharding import PartitionSpec as P

TOPK = 8
CAP = 2
LANES = 128
F32, BF16 = jnp.float32, jnp.bfloat16

FINE = ("z", "xl", "xh", "y", "c")
SIZES = (8, 2, 2, 4, 2)
EXPERT = ("z", "xl")
TENSOR = ("xh", "y", "c")
SPREAD = ("xh", "y")
PLANE = ("xl", "xh", "y")
NZ = 8
MIB = 1 << 20

VMEM = pl.BlockSpec(memory_space=pltpu.VMEM)
SMEM = pl.BlockSpec(memory_space=pltpu.SMEM)


def swap(x, axis):
    return lax.ppermute(x, axis, [(0, 1), (1, 0)])


def fetch(x, hop):
    return lax.ppermute(x, "z", [((i + hop) % NZ, i) for i in range(NZ)])


def gather_z(x):
    up1, dn1 = fetch(x, 1), fetch(x, -1)
    up2, dn2 = fetch(x, 2), fetch(x, -2)
    up3, dn3 = fetch(up1, 2), fetch(dn1, -2)
    far = fetch(up3, 1)
    return [x, up1, up2, up3, far, dn3, dn2, dn1]


def params(mib):
    return pltpu.CompilerParams(vmem_limit_bytes=mib * MIB)


def dot(a, b):
    return jnp.dot(a, b, preferred_element_type=F32)


def project_kernel(place, *refs):
    blocks, (own, other, give, keep, rhs, held) = refs[:NZ], refs[NZ:]
    core, xl = place[0], place[1]
    cols = own.shape[1]
    rhs[:, pl.ds(pl.multiple_of(xl * cols, LANES), cols)] = own[...]
    rhs[:, pl.ds(pl.multiple_of((1 - xl) * cols, LANES), cols)] = other[...]
    lhs = jnp.concatenate([b[...] for b in blocks], axis=0)
    total = dot(lhs, rhs[...])
    spread = give.shape[0]
    rows = lhs.shape[0] // (NZ * spread * 2)
    total = total.reshape(NZ, spread, 2, rows, 2 * cols)
    for k in range(NZ):
        at = slice(k * rows, (k + 1) * rows)
        first, second = total[k, :, 0], total[k, :, 1]
        keep[:, at, :] = jnp.where(core == 0, first, second)
        held[:, at, :] = jnp.where(core == 0, second, first)
    give[...] = held[...].astype(BF16)


def project(place, blocks, own, other, spread):
    rows = blocks[0].shape[0] // (2 * spread)
    shape = (spread, NZ * rows, 2 * own.shape[1])
    return pl.pallas_call(
        project_kernel,
        out_shape=(jax.ShapeDtypeStruct(shape, BF16), jax.ShapeDtypeStruct(shape, F32)),
        in_specs=[SMEM] + [VMEM] * (NZ + 2),
        out_specs=(VMEM, VMEM),
        scratch_shapes=[
            pltpu.VMEM((own.shape[0], 2 * own.shape[1]), BF16),
            pltpu.VMEM(shape, F32),
        ],
        compiler_params=params(32),
    )(place, *blocks, own, other)


def settle_kernel(place, parts, note, out, held):
    z = place[0]
    tokens = parts.shape[1]
    rows = tokens // NZ
    total = parts[0].astype(F32)
    for i in range(1, parts.shape[0]):
        total += parts[i].astype(F32)
    held[tokens:, :] = jnp.zeros((held.shape[0] - tokens, held.shape[1]), F32)
    held[tokens : tokens + rows, :LANES] = note[...]
    for k in range(NZ):
        at = pl.multiple_of(lax.rem(z + k, NZ) * rows, rows)
        held[pl.ds(at, rows), :] = total[k * rows : (k + 1) * rows]
    out[...] = held[...].astype(BF16)


def settle(place, parts, note):
    shape = (parts.shape[1] + 16, parts.shape[2])
    return pl.pallas_call(
        settle_kernel,
        out_shape=jax.ShapeDtypeStruct(shape, BF16),
        in_specs=[SMEM, VMEM, VMEM],
        out_specs=VMEM,
        scratch_shapes=[pltpu.VMEM(shape, F32)],
        compiler_params=params(16),
    )(place, parts, note)


def place_kernel(place, *refs):
    blocks, (gain, sent, own, high, low, stream, notes, mass) = refs[:NZ], refs[NZ:]
    z = place[0]
    tokens, width = stream.shape
    rows, wide = tokens // NZ, width // NZ
    lanes = sent.shape[0]
    for hop in range(NZ):
        there = lax.rem(z + hop, NZ)
        at = pl.multiple_of(there * wide, LANES)
        stream[:, pl.ds(at, wide)] = blocks[hop][:tokens, :].astype(F32)
        note = blocks[hop][tokens:, :LANES].astype(F32)
        notes[pl.ds(pl.multiple_of(there * rows, rows), rows), :] = note[:rows]
    own[...] = stream[pl.ds(pl.multiple_of(z * rows, rows), rows), :]

    slots = NZ * CAP
    lane = lax.broadcasted_iota(jnp.int32, (tokens, lanes), 1)
    token = lax.broadcasted_iota(jnp.int32, (tokens, lanes), 0)
    label = (z * (lanes // (2 * slots)) + lane // (2 * slots)).astype(F32)
    listed = notes[...]
    match = jnp.zeros((tokens, lanes), F32)
    gate = jnp.zeros((tokens, lanes), F32)
    for k in range(TOPK):
        hit = listed[:, k : k + 1] == label
        value = listed[:, TOPK + k : TOPK + k + 1] + listed[:, 2 * TOPK + k : 2 * TOPK + k + 1]
        match += jnp.where(hit, 1.0, 0.0)
        gate += jnp.where(hit, value, 0.0)
    before = lax.broadcasted_iota(jnp.int32, (tokens, tokens), 1)
    after = lax.broadcasted_iota(jnp.int32, (tokens, tokens), 0)
    earlier = (before // rows == after // rows) & (before < after)
    rank = dot(jnp.where(earlier, 1.0, 0.0).astype(BF16), match.astype(BF16))
    slot = (token // rows) * CAP + rank.astype(jnp.int32)
    placed = (match > 0.5) & (slot == lane % slots) & (rank < CAP - 0.5)
    mass[...] = jnp.where(placed, gate, 0.0)
    spots = jnp.transpose(jnp.where(placed, 1.0, 0.0)).astype(BF16)

    weight = jnp.concatenate(
        [
            mass[pl.ds(pl.multiple_of(lax.rem(z + hop, NZ) * rows, rows), rows), :]
            for hop in range(NZ)
        ],
        axis=0,
    )
    top = weight.astype(BF16)
    high[...] = top
    low[...] = (weight - top.astype(F32)).astype(BF16)

    square = jnp.zeros((tokens, 1), F32)
    for hop in range(NZ):
        part = stream[:, hop * wide : (hop + 1) * wide]
        square += jnp.sum(part * part, axis=-1, keepdims=True)
    scale = lax.rsqrt(square / width + 1e-06)
    for hop in range(NZ):
        at = slice(hop * wide, (hop + 1) * wide)
        normed = (stream[:, at] * scale * gain[:, at]).astype(BF16)
        sent[:, at] = dot(spots, normed).astype(BF16)


def place_rows(place, blocks, gain, plane):
    tokens = blocks[0].shape[0] - 16
    width = NZ * blocks[0].shape[1]
    rows = tokens // NZ
    lanes = plane * NZ * CAP
    return pl.pallas_call(
        place_kernel,
        out_shape=(
            jax.ShapeDtypeStruct((lanes, width), BF16),
            jax.ShapeDtypeStruct((rows, width), F32),
            jax.ShapeDtypeStruct((tokens, lanes), BF16),
            jax.ShapeDtypeStruct((tokens, lanes), BF16),
        ),
        in_specs=[SMEM] + [VMEM] * (NZ + 1),
        out_specs=(VMEM,) * 4,
        scratch_shapes=[
            pltpu.VMEM((tokens, width), F32),
            pltpu.VMEM((tokens, LANES), F32),
            pltpu.VMEM((tokens, lanes), F32),
        ],
        compiler_params=params(32),
    )(place, *blocks, gain.reshape(1, width))


def hidden_step(step, steps, rows, w_gate, w_up, gate_acc, up_acc):
    @pl.when(step == 0)
    def _():
        gate_acc[...] = dot(rows[...], w_gate[0])
        up_acc[...] = dot(rows[...], w_up[0])

    @pl.when((step > 0) & (step < steps))
    def _():
        gate_acc[...] += dot(rows[...], w_gate[0])
        up_acc[...] += dot(rows[...], w_up[0])


def hidden_of(gate_acc, up_acc):
    return (jax.nn.silu(gate_acc[...]) * up_acc[...]).astype(BF16)


def hidden_kernel(steps, rows, w_gate, w_up, out, gate_acc, up_acc):
    step = pl.program_id(0)
    hidden_step(step, steps, rows, w_gate, w_up, gate_acc, up_acc)

    @pl.when(step == steps - 1)
    def _():
        out[...] = hidden_of(gate_acc, up_acc)


def hidden_rows(rows, w_gate, w_up, steps=4):
    count, width = rows.shape
    units = w_gate.shape[2]
    deep = width // steps
    return pl.pallas_call(
        functools.partial(hidden_kernel, steps),
        grid=(steps,),
        out_shape=jax.ShapeDtypeStruct((count, units), BF16),
        in_specs=[
            pl.BlockSpec((count, deep), lambda i: (0, i)),
            pl.BlockSpec((1, deep, units), lambda i: (0, i, 0)),
            pl.BlockSpec((1, deep, units), lambda i: (0, i, 0)),
        ],
        out_specs=pl.BlockSpec((count, units), lambda i: (0, 0)),
        scratch_shapes=[pltpu.VMEM((count, units), F32)] * 2,
        compiler_params=params(32),
    )(rows, w_gate, w_up)


def expert_kernel(steps, rows, w_gate, w_up, w_down, out, gate_acc, up_acc, hidden):
    step = pl.program_id(0)
    hidden_step(step, steps, rows, w_gate, w_up, gate_acc, up_acc)

    @pl.when(step == steps)
    def _():
        hidden[...] = hidden_of(gate_acc, up_acc)

    @pl.when(step >= steps)
    def _():
        out[...] = dot(hidden[...], w_down[0]).astype(BF16)


def expert_rows(rows, w_gate, w_up, w_down, steps=4):
    count, width = rows.shape
    units = w_gate.shape[2]
    deep = width // steps
    early = lambda i: jnp.minimum(i, steps - 1)
    late = lambda i: jnp.maximum(i - steps, 0)
    return pl.pallas_call(
        functools.partial(expert_kernel, steps),
        grid=(2 * steps,),
        out_shape=jax.ShapeDtypeStruct((count, width), BF16),
        in_specs=[
            pl.BlockSpec((count, deep), lambda i: (0, early(i))),
            pl.BlockSpec((1, deep, units), lambda i: (0, early(i), 0)),
            pl.BlockSpec((1, deep, units), lambda i: (0, early(i), 0)),
            pl.BlockSpec((1, units, deep), lambda i: (0, 0, late(i))),
        ],
        out_specs=pl.BlockSpec((count, deep), lambda i: (0, late(i))),
        scratch_shapes=[pltpu.VMEM((count, units), F32)] * 2 + [pltpu.VMEM((count, units), BF16)],
        compiler_params=params(32),
    )(rows, w_gate, w_up, w_down)


def down_kernel(hidden, w_down, mate, out):
    out[...] = (dot(hidden[...], w_down[0]) + mate[...].astype(F32)).astype(BF16)


def down_rows(hidden, w_down, mate, steps=4):
    count, width = mate.shape
    units = hidden.shape[1]
    deep = width // steps
    return pl.pallas_call(
        down_kernel,
        grid=(steps,),
        out_shape=jax.ShapeDtypeStruct((count, width), BF16),
        in_specs=[
            pl.BlockSpec((count, units), lambda i: (0, 0)),
            pl.BlockSpec((1, units, deep), lambda i: (0, 0, i)),
            pl.BlockSpec((count, deep), lambda i: (0, i)),
        ],
        out_specs=pl.BlockSpec((count, deep), lambda i: (0, i)),
        compiler_params=params(32),
    )(hidden, w_down, mate)


def combine_kernel(high, low, back, own, base, *outs):
    rows, width = own.shape
    wide = width // 4
    for i in range(4):
        at = slice(i * wide, (i + 1) * wide)
        piece = back[:, at]
        mix = dot(high[...], piece) + dot(low[...], piece)
        base[:, at] = own[:, at] + mix[:rows]
        for hop in range(1, NZ):
            outs[hop - 1][:, at] = mix[hop * rows : (hop + 1) * rows].astype(BF16)


def combine(high, low, back, own):
    rows, width = own.shape
    return pl.pallas_call(
        combine_kernel,
        out_shape=(jax.ShapeDtypeStruct((rows, width), F32),)
        + (jax.ShapeDtypeStruct((rows, width), BF16),) * (NZ - 1),
        in_specs=[VMEM] * 4,
        out_specs=(VMEM,) * NZ,
        compiler_params=params(32),
    )(high, low, back, own)


def on_device(context, proj_weight, norm_gain, expert_ids, gate_values, w_gate, w_up, w_down):
    zi, xli, ci = (lax.axis_index(a).astype(jnp.int32) for a in ("z", "xl", "c"))
    n_spread = lax.axis_size(SPREAD)
    n_plane = lax.axis_size(PLANE)
    rows = expert_ids.shape[0]

    high = lax.reduce_precision(gate_values, exponent_bits=8, mantissa_bits=7)
    note = jnp.concatenate([expert_ids.astype(F32), high, gate_values - high], axis=1)
    note = jnp.pad(note, ((0, 0), (0, LANES - 3 * TOPK)))

    other = swap(proj_weight, "xl")
    give, keep = project(jnp.stack([ci, xli]), gather_z(context), proj_weight, other, n_spread)
    got = swap(give, "c")
    partial = (keep + got.astype(F32)).astype(BF16)
    partial = lax.all_to_all(partial, SPREAD, 0, 0, tiled=True)

    place = zi.reshape(1)
    part = settle(place, partial, note)
    sent, own, high, low = place_rows(place, gather_z(part), norm_gain, n_plane)
    width = sent.shape[1]
    mine = lax.all_to_all(sent.reshape(n_plane, -1, width), PLANE, 0, 0, tiled=True)
    mine = mine.reshape(-1, width)

    theirs = swap(mine, "c")
    hidden = hidden_rows(mine, w_gate, w_up)
    from_mate = swap(expert_rows(theirs, w_gate, w_up, w_down), "c")
    summed = down_rows(hidden, w_down, from_mate)
    back = lax.all_to_all(summed.reshape(n_plane, -1, width), PLANE, 0, 0, tiled=True)

    base, *blocks = combine(high, low, back.reshape(-1, width), own)
    total = base
    for hop in (4, 1, 7, 2, 6, 3, 5):
        total += fetch(blocks[hop - 1], -hop).astype(F32)
    return total.astype(BF16)


def solution(mesh):
    fine = Mesh(mesh.devices.reshape(SIZES), FINE)
    both = EXPERT + TENSOR
    return jax.shard_map(
        on_device,
        mesh=fine,
        in_specs=(
            P(EXPERT, TENSOR),
            P(TENSOR, EXPERT),
            P(),
            P(both, None),
            P(both, None),
            P(both, None, None),
            P(both, None, None),
            P(both, None, None),
        ),
        out_specs=P(both, None),
        check_vma=False,
    )
```

time: 205 us -> 175 us (0.85)
  blocking collectives: 30.3 us -> 61.8 us
  matrix products: 26.6 us -> 0 us
  local copies, waits for them, and re-layouts: 25.7 us -> 3.77 us
  waiting for transfers between devices: 51.3 us -> 31.1 us
  Pallas kernels: 0 us -> 15.3 us
  other arithmetic: 8.39 us -> 1.85 us
    all_to_all x1 -> x2, blocking collectives: 30.3 us -> 61.8 us  [the longest x1 31.5 us: on_device(): lax.all_to_all(summed.reshape(n_plane, -1, width), PLANE, 0, 0, tiled=True)]
    all_to_all x2 -> x1, waiting for transfers between devices: 36.7 us -> 8.92 us  [on_device(): partial = lax.all_to_all(partial, SPREAD, 0, 0, tiled=True)]
    dot_general x9 -> x0, matrix products: 26.6 us -> none  [the longest x1 7.04 us: on_device(): jnp.dot(mine_hidden, w_down[0], preferred_element_type=jnp.float32)]
    pallas_call x0 -> x7, Pallas kernels: none -> 15.3 us  [the longest x1 5.47 us: expert_rows(): pl.pallas_call(functools.partial(expert_kernel, steps), grid=(2 * steps,)...]
    unnamed x58 -> x18, local copies, waits for them, and re-layouts: 17.5 us -> 3.77 us
    all_to_all x2 -> x1, starting transfers between devices: 13.1 us -> 7.7 us  [on_device(): partial = lax.all_to_all(partial, SPREAD, 0, 0, tiled=True)]
    ppermute x21, waiting for transfers between devices: 10.4 us -> 15.3 us  [fetch(): return lax.ppermute(x, 'z', [((i + hop) % NZ, i) for i in range(NZ)])]
    ppermute x21, starting transfers between devices: 45.2 us -> 49.7 us  [fetch(): return lax.ppermute(x, 'z', [((i + hop) % NZ, i) for i in range(NZ)])]
  transfers between devices with their start and end apart: 27 -> 26, of which waited for: 9 -> 12; matrix products, arithmetic and copies ran while one was open for 12% -> 0% of each run, Pallas kernels for 0% -> 2%
where the time goes in v3:
time: 175 us; the launch traced here: 172 us
  blocking collectives  61.8 us (35%)
  starting transfers between devices  58.5 us (33%)
  waiting for transfers between devices  31.1 us (18%)
  Pallas kernels  15.3 us (9%)
  local copies, waits for them, and re-layouts  3.77 us (2%)
  other arithmetic  1.85 us (1%)
    ppermute x21, starting transfers between devices, fetch(): return lax.ppermute(x, 'z', [((i + hop) % NZ, i) for i in range(NZ)])  49.7 us
    all_to_all x1, blocking collectives, on_device(): lax.all_to_all(summed.reshape(n_plane, -1, width), PLANE, 0, 0, tiled=True)  31.5 us
    all_to_all x1, blocking collectives, on_device(): lax.all_to_all(sent.reshape(n_plane, -1, width), PLANE, 0, 0, tiled=True)  30.2 us
    ppermute x21, waiting for transfers between devices, fetch(): return lax.ppermute(x, 'z', [((i + hop) % NZ, i) for i in range(NZ)])  15.3 us
    all_to_all x1, waiting for transfers between devices, on_device(): partial = lax.all_to_all(partial, SPREAD, 0, 0, tiled=True)  8.92 us
    all_to_all x1, starting transfers between devices, on_device(): partial = lax.all_to_all(partial, SPREAD, 0, 0, tiled=True)  7.7 us
    ppermute x4, waiting for transfers between devices, swap(): return lax.ppermute(x, axis, [(0, 1), (1, 0)])  6.93 us
    pallas_call x1, Pallas kernels, expert_rows(): pl.pallas_call(functools.partial(expert_kernel, steps), grid=(2 * steps,)...  5.47 us
  transfers between devices with their start and end apart: 26, of which 12 were waited for; matrix products, arithmetic and copies ran while one was open for 0% of the time, Pallas kernels for 2%

profile of v3, /device:TPU:6, one launch (start us, length us, event | category | flops | bytes accessed | tf_op | source)
XLA Modules:
  0.0 172.5 jit_solution(12924108896996147881)
XLA Ops:
  0.0 5.9 %collective-permute-start = (bf16[128,512]{1,0:T(8,128)(2,1)}, bf16[128,512]{1,0:T(8,128)(2,1)S(1)}, u32[]{:S(2)}, u32[]{:S(2)}) collective-permute-start(bf16[128,512]{1,0:T(8,128)(2,1)} %refs_0_.1), channel_id=1, source_target_pairs={{32,0},{64,32},{96,64},{128,96},{160,128},{192,160},{224,192},{0,2... | collective-permute-start | bytes 393224 | tf_op jit(solution)/shard_map/ppermute | solution.py:34
  6.7 2.2 %collective-permute-done.refs_1_ = bf16[128,512]{1,0:T(8,128)(2,1)S(1)} collective-permute-done((bf16[128,512]{1,0:T(8,128)(2,1)}, bf16[128,512]{1,0:T(8,128)(2,1)S(1)}, u32[]{:S(2)}, u32[]{:S(2)}) %collective-permute-start) | collective-permute-done | bytes 131104 | tf_op jit(solution)/shard_map/ppermute | solution.py:34
  8.9 2.8 %collective-permute-start.2 = (bf16[128,512]{1,0:T(8,128)(2,1)S(1)}, bf16[128,512]{1,0:T(8,128)(2,1)S(1)}, u32[]{:S(2)}, u32[]{:S(2)}) collective-permute-start(bf16[128,512]{1,0:T(8,128)(2,1)S(1)} %collective-permute-done.refs_1_), channel_id=1, source_target_pairs={{64,0},{96,32},{128,64},{160,96},{192,128},{224,160},{0,192},{32,2... | collective-permute-start | bytes 393224 | tf_op jit(solution)/shard_map/ppermute | solution.py:34
  16.0 2.1 %collective-permute-done.2.refs_3_ = bf16[128,512]{1,0:T(8,128)(2,1)S(1)} collective-permute-done((bf16[128,512]{1,0:T(8,128)(2,1)S(1)}, bf16[128,512]{1,0:T(8,128)(2,1)S(1)}, u32[]{:S(2)}, u32[]{:S(2)}) %collective-permute-start.2) | collective-permute-done | bytes 131104 | tf_op jit(solution)/shard_map/ppermute | solution.py:34
  18.1 6.1 %collective-permute-start.3 = (bf16[128,512]{1,0:T(8,128)(2,1)S(1)}, bf16[128,512]{1,0:T(8,128)(2,1)S(1)}, u32[]{:S(2)}, u32[]{:S(2)}) collective-permute-start(bf16[128,512]{1,0:T(8,128)(2,1)S(1)} %collective-permute-done.2.refs_3_), channel_id=1, source_target_pairs={{32,0},{64,32},{96,64},{128,96},{160,128},{192,160},{224,192},{0,2... | collective-permute-start | bytes 393224 | tf_op jit(solution)/shard_map/ppermute | solution.py:34
  24.2 3.5 %collective-permute-done.5.refs_5_ = bf16[128,512]{1,0:T(8,128)(2,1)S(1)} collective-permute-done((bf16[128,512]{1,0:T(8,128)(2,1)S(1)}, bf16[128,512]{1,0:T(8,128)(2,1)S(1)}, u32[]{:S(2)}, u32[]{:S(2)}) %collective-permute-start.5) | collective-permute-done | bytes 131104 | tf_op jit(solution)/shard_map/ppermute | solution.py:34
  31.0 1.9 %collective-permute-done.8 = bf16[8,64,512]{2,1,0:T(8,128)(2,1)S(1)} collective-permute-done((bf16[8,64,512]{2,1,0:T(8,128)(2,1)S(1)}, bf16[8,64,512]{2,1,0:T(8,128)(2,1)S(1)}, u32[]{:S(2)}, u32[]{:S(2)}) %collective-permute-start.8) | collective-permute-done | bytes 524320 | tf_op jit(solution)/shard_map/ppermute | solution.py:30
  33.8 7.7 %all-to-all-start = ((bf16[8,64,512]{2,1,0:T(8,128)(2,1)}), bf16[8,64,512]{2,1,0:T(8,128)(2,1)}, u32[]{:S(2)}, u32[]{:S(2)}) async-start(bf16[8,64,512]{2,1,0:T(8,128)(2,1)} %add_convert_fusion), calls=%async_computation | async-start | bytes 1048576 | tf_op jit(solution)/shard_map/all_to_all | solution.py:335
  41.7 8.9 %all-to-all-done.parts = bf16[8,64,512]{2,1,0:T(8,128)(2,1)} async-done(((bf16[8,64,512]{2,1,0:T(8,128)(2,1)}), bf16[8,64,512]{2,1,0:T(8,128)(2,1)}, u32[]{:S(2)}, u32[]{:S(2)}) %all-to-all-start) | async-done | bytes 524320 | tf_op jit(solution)/shard_map/all_to_all | solution.py:335
  51.7 2.7 %collective-permute-start.9 = (bf16[80,512]{1,0:T(8,128)(2,1)S(1)}, bf16[80,512]{1,0:T(8,128)(2,1)S(1)}, u32[]{:S(2)}, u32[]{:S(2)}) collective-permute-start(bf16[80,512]{1,0:T(8,128)(2,1)S(1)} %shard_map.83.refs_0_), channel_id=1, source_target_pairs={{32,0},{64,32},{96,64},{128,96},{160,128},{192,160},{224,192},{0,2... | collective-permute-start | bytes 245768 | tf_op jit(solution)/shard_map/ppermute | solution.py:34
  54.4 2.1 %collective-permute-done.9.refs_1_ = bf16[80,512]{1,0:T(8,128)(2,1)S(1)} collective-permute-done((bf16[80,512]{1,0:T(8,128)(2,1)S(1)}, bf16[80,512]{1,0:T(8,128)(2,1)S(1)}, u32[]{:S(2)}, u32[]{:S(2)}) %collective-permute-start.9) | collective-permute-done | bytes 81952 | tf_op jit(solution)/shard_map/ppermute | solution.py:34
  59.4 3.0 %collective-permute-start.10 = (bf16[80,512]{1,0:T(8,128)(2,1)S(1)}, bf16[80,512]{1,0:T(8,128)(2,1)S(1)}, u32[]{:S(2)}, u32[]{:S(2)}) collective-permute-start(bf16[80,512]{1,0:T(8,128)(2,1)S(1)} %shard_map.83.refs_0_), channel_id=1, source_target_pairs={{64,0},{96,32},{128,64},{160,96},{192,128},{224,160},{0,192},{32,2... | collective-permute-start | bytes 245768 | tf_op jit(solution)/shard_map/ppermute | solution.py:34
  62.5 5.8 %collective-permute-start.12 = (bf16[80,512]{1,0:T(8,128)(2,1)S(1)}, bf16[80,512]{1,0:T(8,128)(2,1)S(1)}, u32[]{:S(2)}, u32[]{:S(2)}) collective-permute-start(bf16[80,512]{1,0:T(8,128)(2,1)S(1)} %collective-permute-done.11.refs_3_), channel_id=1, source_target_pairs={{32,0},{64,32},{96,64},{128,96},{160,128},{192,160},{224,192},{0,2... | collective-permute-start | bytes 245768 | tf_op jit(solution)/shard_map/ppermute | solution.py:34
  71.5 30.2 %all_to_all.15 = bf16[16,16,4096]{2,1,0:T(8,128)(2,1)S(1)} all-to-all(bf16[16,16,4096]{2,1,0:T(8,128)(2,1)S(1)} %bitcast.12), channel_id=1, replica_groups=mesh['z'=8,'xl'=2,'xh'=2,'y'=4,'c'=2] {'xl','xh','y'}, dimensions={0} | all-to-all | bytes 4194304 | tf_op jit(solution)/shard_map/all_to_all | solution.py:341
  101.8 4.2 %collective-permute-done.16.rows = bf16[256,4096]{1,0:T(8,128)(2,1)S(1)} collective-permute-done((bf16[256,4096]{1,0:T(8,128)(2,1)S(1)}, bf16[256,4096]{1,0:T(8,128)(2,1)S(1)}, u32[]{:S(2)}, u32[]{:S(2)}) %collective-permute-start.16) | collective-permute-done | bytes 2097184 | tf_op jit(solution)/shard_map/ppermute | solution.py:30
  107.8 5.5 %shard_map.86 = bf16[256,4096]{1,0:T(8,128)(2,1)S(1)} custom-call(bf16[256,4096]{1,0:T(8,128)(2,1)S(1)} %collective-permute-done.16.rows, bf16[1,4096,384]{2,1,0:T(8,128)(2,1)S(1)} %copy-done.1, bf16[1,4096,384]{2,1,0:T(8,128)(2,1)S(1)} %copy-done.2, bf16[1,384,4096]{2,1,0:T(8,128)(2,1)S(1)} %copy-done), custom_call_target="tpu_custom_call" | custom-call | tf_op jit(solution)/shard_map/pallas_call | solution.py:259
  113.5 3.1 %shard_map.85.hidden = bf16[256,384]{1,0:T(8,128)(2,1)S(1)} custom-call(bf16[256,4096]{1,0:T(8,128)(2,1)S(1)} %bitcast.11, bf16[1,4096,384]{2,1,0:T(8,128)(2,1)S(1)} %copy-done.1, bf16[1,4096,384]{2,1,0:T(8,128)(2,1)S(1)} %copy-done.3), custom_call_target="tpu_custom_call" | custom-call | tf_op jit(solution)/shard_map/pallas_call | solution.py:225
  117.6 2.3 %shard_map.87 = bf16[256,4096]{1,0:T(8,128)(2,1)S(1)} custom-call(bf16[256,384]{1,0:T(8,128)(2,1)S(1)} %shard_map.85.hidden, bf16[1,384,4096]{2,1,0:T(8,128)(2,1)S(1)} %copy-done, bf16[256,4096]{1,0:T(8,128)(2,1)S(1)} %collective-permute-done.17.mate), custom_call_target="tpu_custom_call" | custom-call | tf_op jit(solution)/shard_map/pallas_call | solution.py:283
  119.8 31.5 %all_to_all.16 = bf16[16,16,4096]{2,1,0:T(8,128)(2,1)S(1)} all-to-all(bf16[16,16,4096]{2,1,0:T(8,128)(2,1)S(1)} %bitcast.8), channel_id=1, replica_groups=mesh['z'=8,'xl'=2,'xh'=2,'y'=4,'c'=2] {'xl','xh','y'}, dimensions={0} | all-to-all | bytes 4194304 | tf_op jit(solution)/shard_map/all_to_all | solution.py:348
  152.2 3.7 %collective-permute-start.18 = (bf16[8,4096]{1,0:T(8,128)(2,1)S(1)}, bf16[8,4096]{1,0:T(8,128)(2,1)S(1)}, u32[]{:S(2)}, u32[]{:S(2)}) collective-permute-start(bf16[8,4096]{1,0:T(8,128)(2,1)S(1)} %get-tuple-element.26), channel_id=1, source_target_pairs={{128,0},{160,32},{192,64},{224,96},{0,128},{32,160},{64,192},{96,2... | collective-permute-start | bytes 196616 | tf_op jit(solution)/shard_map/ppermute | solution.py:34
  159.5 3.9 %collective-permute-start.22 = (bf16[8,4096]{1,0:T(8,128)(2,1)S(1)}, bf16[8,4096]{1,0:T(8,128)(2,1)S(1)}, u32[]{:S(2)}, u32[]{:S(2)}) collective-permute-start(bf16[8,4096]{1,0:T(8,128)(2,1)S(1)} %get-tuple-element.30), channel_id=1, source_target_pairs={{64,0},{96,32},{128,64},{160,96},{192,128},{224,160},{0,192},{32,2... | collective-permute-start | bytes 196616 | tf_op jit(solution)/shard_map/ppermute | solution.py:34
  163.4 2.1 %collective-permute-start.23 = (bf16[8,4096]{1,0:T(8,128)(2,1)S(1)}, bf16[8,4096]{1,0:T(8,128)(2,1)S(1)}, u32[]{:S(2)}, u32[]{:S(2)}) collective-permute-start(bf16[8,4096]{1,0:T(8,128)(2,1)S(1)} %get-tuple-element.31), channel_id=1, source_target_pairs={{160,0},{192,32},{224,64},{0,96},{32,128},{64,160},{96,192},{128,2... | collective-permute-start | bytes 196616 | tf_op jit(solution)/shard_map/ppermute | solution.py:34
  165.5 2.9 %collective-permute-start.24 = (bf16[8,4096]{1,0:T(8,128)(2,1)S(1)}, bf16[8,4096]{1,0:T(8,128)(2,1)S(1)}, u32[]{:S(2)}, u32[]{:S(2)}) collective-permute-start(bf16[8,4096]{1,0:T(8,128)(2,1)S(1)} %get-tuple-element.32), channel_id=1, source_target_pairs={{96,0},{128,32},{160,64},{192,96},{224,128},{0,160},{32,192},{64,2... | collective-permute-start | bytes 196616 | tf_op jit(solution)/shard_map/ppermute | solution.py:34
  168.5 3.3 %collective-permute-done.23 = bf16[8,4096]{1,0:T(8,128)(2,1)S(1)} collective-permute-done((bf16[8,4096]{1,0:T(8,128)(2,1)S(1)}, bf16[8,4096]{1,0:T(8,128)(2,1)S(1)}, u32[]{:S(2)}, u32[]{:S(2)}) %collective-permute-start.23) | collective-permute-done | bytes 65568 | tf_op jit(solution)/shard_map/ppermute | solution.py:34
  (61 shorter events, 25.0 us)
Async XLA Ops:
  0.0 8.9 %collective-permute-start = (bf16[128,512]{1,0:T(8,128)(2,1)}, bf16[128,512]{1,0:T(8,128)(2,1)S(1)}, u32[]{:S(2)}, u32[]{:S(2)}) collective-permute-start(bf16[128,512]{1,0:T(8,128)(2,1)} %refs_0_.1), channel_id=1, source_target_pairs={{32,0},{64,32},{96,64},{128,96},{160,128},{192,160},{224,192},{0,2... | collective-permute-start | bytes 393224 | tf_op jit(solution)/shard_map/ppermute | solution.py:34
  5.9 8.8 %collective-permute-start.4 = (bf16[128,512]{1,0:T(8,128)(2,1)}, bf16[128,512]{1,0:T(8,128)(2,1)S(1)}, u32[]{:S(2)}, u32[]{:S(2)}) collective-permute-start(bf16[128,512]{1,0:T(8,128)(2,1)} %refs_0_.1), channel_id=1, source_target_pairs={{224,0},{0,32},{32,64},{64,96},{96,128},{128,160},{160,192},{192,2... | collective-permute-start | bytes 393224 | tf_op jit(solution)/shard_map/ppermute | solution.py:34
  5.9 21.8 %collective-permute-start.7 = (bf16[512,256]{1,0:T(8,128)(2,1)}, bf16[512,256]{1,0:T(8,128)(2,1)S(1)}, u32[]{:S(2)}, u32[]{:S(2)}) collective-permute-start(bf16[512,256]{1,0:T(8,128)(2,1)} %refs_8_.1), channel_id=1, source_target_pairs={{0,16},{16,0},{1,17},{17,1},{2,18},{18,2},{3,19},{19,3},{4,20},{20... | collective-permute-start | bytes 786440 | tf_op jit(solution)/shard_map/ppermute | solution.py:30
  8.9 9.1 %collective-permute-start.2 = (bf16[128,512]{1,0:T(8,128)(2,1)S(1)}, bf16[128,512]{1,0:T(8,128)(2,1)S(1)}, u32[]{:S(2)}, u32[]{:S(2)}) collective-permute-start(bf16[128,512]{1,0:T(8,128)(2,1)S(1)} %collective-permute-done.refs_1_), channel_id=1, source_target_pairs={{64,0},{96,32},{128,64},{160,96},{192,128},{224,160},{0,192},{32,2... | collective-permute-start | bytes 393224 | tf_op jit(solution)/shard_map/ppermute | solution.py:34
  11.7 12.5 %collective-permute-start.1 = (bf16[128,512]{1,0:T(8,128)(2,1)}, bf16[128,512]{1,0:T(8,128)(2,1)S(1)}, u32[]{:S(2)}, u32[]{:S(2)}) collective-permute-start(bf16[128,512]{1,0:T(8,128)(2,1)} %refs_0_.1), channel_id=1, source_target_pairs={{64,0},{96,32},{128,64},{160,96},{192,128},{224,160},{0,192},{32,2... | collective-permute-start | bytes 393224 | tf_op jit(solution)/shard_map/ppermute | solution.py:34
  13.2 11.0 %collective-permute-start.6 = (bf16[128,512]{1,0:T(8,128)(2,1)}, bf16[128,512]{1,0:T(8,128)(2,1)S(1)}, u32[]{:S(2)}, u32[]{:S(2)}) collective-permute-start(bf16[128,512]{1,0:T(8,128)(2,1)} %refs_0_.1), channel_id=1, source_target_pairs={{192,0},{224,32},{0,64},{32,96},{64,128},{96,160},{128,192},{160,2... | collective-permute-start | bytes 393224 | tf_op jit(solution)/shard_map/ppermute | solution.py:34
  14.7 13.0 %collective-permute-start.5 = (bf16[128,512]{1,0:T(8,128)(2,1)S(1)}, bf16[128,512]{1,0:T(8,128)(2,1)S(1)}, u32[]{:S(2)}, u32[]{:S(2)}) collective-permute-start(bf16[128,512]{1,0:T(8,128)(2,1)S(1)} %collective-permute-done.4.refs_7_), channel_id=1, source_target_pairs={{192,0},{224,32},{0,64},{32,96},{64,128},{96,160},{128,192},{160,2... | collective-permute-start | bytes 393224 | tf_op jit(solution)/shard_map/ppermute | solution.py:34
  18.1 9.7 %collective-permute-start.3 = (bf16[128,512]{1,0:T(8,128)(2,1)S(1)}, bf16[128,512]{1,0:T(8,128)(2,1)S(1)}, u32[]{:S(2)}, u32[]{:S(2)}) collective-permute-start(bf16[128,512]{1,0:T(8,128)(2,1)S(1)} %collective-permute-done.2.refs_3_), channel_id=1, source_target_pairs={{32,0},{64,32},{96,64},{128,96},{160,128},{192,160},{224,192},{0,2... | collective-permute-start | bytes 393224 | tf_op jit(solution)/shard_map/ppermute | solution.py:34
  33.8 16.7 %all-to-all-start = ((bf16[8,64,512]{2,1,0:T(8,128)(2,1)}), bf16[8,64,512]{2,1,0:T(8,128)(2,1)}, u32[]{:S(2)}, u32[]{:S(2)}) async-start(bf16[8,64,512]{2,1,0:T(8,128)(2,1)} %add_convert_fusion), calls=%async_computation | async-start | bytes 1048576 | tf_op jit(solution)/shard_map/all_to_all | solution.py:335
  51.7 4.7 %collective-permute-start.9 = (bf16[80,512]{1,0:T(8,128)(2,1)S(1)}, bf16[80,512]{1,0:T(8,128)(2,1)S(1)}, u32[]{:S(2)}, u32[]{:S(2)}) collective-permute-start(bf16[80,512]{1,0:T(8,128)(2,1)S(1)} %shard_map.83.refs_0_), channel_id=1, source_target_pairs={{32,0},{64,32},{96,64},{128,96},{160,128},{192,160},{224,192},{0,2... | collective-permute-start | bytes 245768 | tf_op jit(solution)/shard_map/ppermute | solution.py:34
  54.4 8.0 %collective-permute-start.13 = (bf16[80,512]{1,0:T(8,128)(2,1)S(1)}, bf16[80,512]{1,0:T(8,128)(2,1)S(1)}, u32[]{:S(2)}, u32[]{:S(2)}) collective-permute-start(bf16[80,512]{1,0:T(8,128)(2,1)S(1)} %shard_map.83.refs_0_), channel_id=1, source_target_pairs={{224,0},{0,32},{32,64},{64,96},{96,128},{128,160},{160,192},{192,2... | collective-permute-start | bytes 245768 | tf_op jit(solution)/shard_map/ppermute | solution.py:34
  56.4 6.0 %collective-permute-start.11 = (bf16[80,512]{1,0:T(8,128)(2,1)S(1)}, bf16[80,512]{1,0:T(8,128)(2,1)S(1)}, u32[]{:S(2)}, u32[]{:S(2)}) collective-permute-start(bf16[80,512]{1,0:T(8,128)(2,1)S(1)} %collective-permute-done.9.refs_1_), channel_id=1, source_target_pairs={{64,0},{96,32},{128,64},{160,96},{192,128},{224,160},{0,192},{32,2... | collective-permute-start | bytes 245768 | tf_op jit(solution)/shard_map/ppermute | solution.py:34
  58.3 10.1 %collective-permute-start.15 = (bf16[80,512]{1,0:T(8,128)(2,1)S(1)}, bf16[80,512]{1,0:T(8,128)(2,1)S(1)}, u32[]{:S(2)}, u32[]{:S(2)}) collective-permute-start(bf16[80,512]{1,0:T(8,128)(2,1)S(1)} %shard_map.83.refs_0_), channel_id=1, source_target_pairs={{192,0},{224,32},{0,64},{32,96},{64,128},{96,160},{128,192},{160,2... | collective-permute-start | bytes 245768 | tf_op jit(solution)/shard_map/ppermute | solution.py:34
  59.4 9.0 %collective-permute-start.10 = (bf16[80,512]{1,0:T(8,128)(2,1)S(1)}, bf16[80,512]{1,0:T(8,128)(2,1)S(1)}, u32[]{:S(2)}, u32[]{:S(2)}) collective-permute-start(bf16[80,512]{1,0:T(8,128)(2,1)S(1)} %shard_map.83.refs_0_), channel_id=1, source_target_pairs={{64,0},{96,32},{128,64},{160,96},{192,128},{224,160},{0,192},{32,2... | collective-permute-start | bytes 245768 | tf_op jit(solution)/shard_map/ppermute | solution.py:34
  62.4 6.9 %collective-permute-start.14 = (bf16[80,512]{1,0:T(8,128)(2,1)S(1)}, bf16[80,512]{1,0:T(8,128)(2,1)S(1)}, u32[]{:S(2)}, u32[]{:S(2)}) collective-permute-start(bf16[80,512]{1,0:T(8,128)(2,1)S(1)} %collective-permute-done.13.refs_7_), channel_id=1, source_target_pairs={{192,0},{224,32},{0,64},{32,96},{64,128},{96,160},{128,192},{160,2... | collective-permute-start | bytes 245768 | tf_op jit(solution)/shard_map/ppermute | solution.py:34
  62.5 7.9 %collective-permute-start.12 = (bf16[80,512]{1,0:T(8,128)(2,1)S(1)}, bf16[80,512]{1,0:T(8,128)(2,1)S(1)}, u32[]{:S(2)}, u32[]{:S(2)}) collective-permute-start(bf16[80,512]{1,0:T(8,128)(2,1)S(1)} %collective-permute-done.11.refs_3_), channel_id=1, source_target_pairs={{32,0},{64,32},{96,64},{128,96},{160,128},{192,160},{224,192},{0,2... | collective-permute-start | bytes 245768 | tf_op jit(solution)/shard_map/ppermute | solution.py:34
  113.3 4.2 %collective-permute-start.17 = (bf16[256,4096]{1,0:T(8,128)(2,1)S(1)}, bf16[256,4096]{1,0:T(8,128)(2,1)S(1)}, u32[]{:S(2)}, u32[]{:S(2)}) collective-permute-start(bf16[256,4096]{1,0:T(8,128)(2,1)S(1)} %shard_map.86), channel_id=1, source_target_pairs={{0,1},{1,0},{2,3},{3,2},{4,5},{5,4},{6,7},{7,6},{8,9},{9,8},{10,11... | collective-permute-start | bytes 6291464 | tf_op jit(solution)/shard_map/ppermute | solution.py:30
  152.2 11.2 %collective-permute-start.18 = (bf16[8,4096]{1,0:T(8,128)(2,1)S(1)}, bf16[8,4096]{1,0:T(8,128)(2,1)S(1)}, u32[]{:S(2)}, u32[]{:S(2)}) collective-permute-start(bf16[8,4096]{1,0:T(8,128)(2,1)S(1)} %get-tuple-element.26), channel_id=1, source_target_pairs={{128,0},{160,32},{192,64},{224,96},{0,128},{32,160},{64,192},{96,2... | collective-permute-start | bytes 196616 | tf_op jit(solution)/shard_map/ppermute | solution.py:34
  155.9 9.6 %collective-permute-start.19 = (bf16[8,4096]{1,0:T(8,128)(2,1)S(1)}, bf16[8,4096]{1,0:T(8,128)(2,1)S(1)}, u32[]{:S(2)}, u32[]{:S(2)}) collective-permute-start(bf16[8,4096]{1,0:T(8,128)(2,1)S(1)} %get-tuple-element.27), channel_id=1, source_target_pairs={{224,0},{0,32},{32,64},{64,96},{96,128},{128,160},{160,192},{192,2... | collective-permute-start | bytes 196616 | tf_op jit(solution)/shard_map/ppermute | solution.py:34
  157.6 10.9 %collective-permute-start.20 = (bf16[8,4096]{1,0:T(8,128)(2,1)S(1)}, bf16[8,4096]{1,0:T(8,128)(2,1)S(1)}, u32[]{:S(2)}, u32[]{:S(2)}) collective-permute-start(bf16[8,4096]{1,0:T(8,128)(2,1)S(1)} %get-tuple-element.28), channel_id=1, source_target_pairs={{32,0},{64,32},{96,64},{128,96},{160,128},{192,160},{224,192},{0,2... | collective-permute-start | bytes 196616 | tf_op jit(solution)/shard_map/ppermute | solution.py:34
  159.3 9.2 %collective-permute-start.21 = (bf16[8,4096]{1,0:T(8,128)(2,1)S(1)}, bf16[8,4096]{1,0:T(8,128)(2,1)S(1)}, u32[]{:S(2)}, u32[]{:S(2)}) collective-permute-start(bf16[8,4096]{1,0:T(8,128)(2,1)S(1)} %get-tuple-element.29), channel_id=1, source_target_pairs={{192,0},{224,32},{0,64},{32,96},{64,128},{96,160},{128,192},{160,2... | collective-permute-start | bytes 196616 | tf_op jit(solution)/shard_map/ppermute | solution.py:34
  159.5 8.9 %collective-permute-start.22 = (bf16[8,4096]{1,0:T(8,128)(2,1)S(1)}, bf16[8,4096]{1,0:T(8,128)(2,1)S(1)}, u32[]{:S(2)}, u32[]{:S(2)}) collective-permute-start(bf16[8,4096]{1,0:T(8,128)(2,1)S(1)} %get-tuple-element.30), channel_id=1, source_target_pairs={{64,0},{96,32},{128,64},{160,96},{192,128},{224,160},{0,192},{32,2... | collective-permute-start | bytes 196616 | tf_op jit(solution)/shard_map/ppermute | solution.py:34
  163.4 8.3 %collective-permute-start.23 = (bf16[8,4096]{1,0:T(8,128)(2,1)S(1)}, bf16[8,4096]{1,0:T(8,128)(2,1)S(1)}, u32[]{:S(2)}, u32[]{:S(2)}) collective-permute-start(bf16[8,4096]{1,0:T(8,128)(2,1)S(1)} %get-tuple-element.31), channel_id=1, source_target_pairs={{160,0},{192,32},{224,64},{0,96},{32,128},{64,160},{96,192},{128,2... | collective-permute-start | bytes 196616 | tf_op jit(solution)/shard_map/ppermute | solution.py:34
  165.5 6.2 %collective-permute-start.24 = (bf16[8,4096]{1,0:T(8,128)(2,1)S(1)}, bf16[8,4096]{1,0:T(8,128)(2,1)S(1)}, u32[]{:S(2)}, u32[]{:S(2)}) collective-permute-start(bf16[8,4096]{1,0:T(8,128)(2,1)S(1)} %get-tuple-element.32), channel_id=1, source_target_pairs={{96,0},{128,32},{160,64},{192,96},{224,128},{0,160},{32,192},{64,2... | collective-permute-start | bytes 196616 | tf_op jit(solution)/shard_map/ppermute | solution.py:34
  (11 other events, 191.0 us)

commit v4 on v3

--- a/solution.py
+++ b/solution.py
@@ -1,5 +1,3 @@
-import functools
-
 import jax
 import jax.numpy as jnp
 from jax import lax
@@ -50,17 +48,35 @@
     return jnp.dot(a, b, preferred_element_type=F32)
 
 
-def project_kernel(place, *refs):
-    blocks, (own, other, give, keep, rhs, held) = refs[:NZ], refs[NZ:]
-    core, xl = place[0], place[1]
+def stage_kernel(place, own, other, context, rhs, held):
+    xl = place[1]
     cols = own.shape[1]
     rhs[:, pl.ds(pl.multiple_of(xl * cols, LANES), cols)] = own[...]
     rhs[:, pl.ds(pl.multiple_of((1 - xl) * cols, LANES), cols)] = other[...]
+    held[...] = context[...]
+
+
+def stage(place, own, other, context):
+    return pl.pallas_call(
+        stage_kernel,
+        out_shape=(
+            jax.ShapeDtypeStruct((own.shape[0], 2 * own.shape[1]), BF16),
+            jax.ShapeDtypeStruct(context.shape, BF16),
+        ),
+        in_specs=[SMEM] + [VMEM] * 3,
+        out_specs=(VMEM, VMEM),
+        compiler_params=params(16),
+    )(place, own, other, context)
+
+
+def project_kernel(place, *refs):
+    blocks, (rhs, give, keep, held) = refs[:NZ], refs[NZ:]
+    core = place[0]
     lhs = jnp.concatenate([b[...] for b in blocks], axis=0)
     total = dot(lhs, rhs[...])
     spread = give.shape[0]
     rows = lhs.shape[0] // (NZ * spread * 2)
-    total = total.reshape(NZ, spread, 2, rows, 2 * cols)
+    total = total.reshape(NZ, spread, 2, rows, rhs.shape[1])
     for k in range(NZ):
         at = slice(k * rows, (k + 1) * rows)
         first, second = total[k, :, 0], total[k, :, 1]
@@ -69,20 +85,17 @@
     give[...] = held[...].astype(BF16)
 
 
-def project(place, blocks, own, other, spread):
+def project(place, blocks, rhs, spread):
     rows = blocks[0].shape[0] // (2 * spread)
-    shape = (spread, NZ * rows, 2 * own.shape[1])
+    shape = (spread, NZ * rows, rhs.shape[1])
     return pl.pallas_call(
         project_kernel,
         out_shape=(jax.ShapeDtypeStruct(shape, BF16), jax.ShapeDtypeStruct(shape, F32)),
-        in_specs=[SMEM] + [VMEM] * (NZ + 2),
+        in_specs=[SMEM] + [VMEM] * (NZ + 1),
         out_specs=(VMEM, VMEM),
-        scratch_shapes=[
-            pltpu.VMEM((own.shape[0], 2 * own.shape[1]), BF16),
-            pltpu.VMEM(shape, F32),
-        ],
+        scratch_shapes=[pltpu.VMEM(shape, F32)],
         compiler_params=params(32),
-    )(place, *blocks, own, other)
+    )(place, *blocks, rhs)
 
 
 def settle_kernel(place, parts, note, out, held):
@@ -193,105 +206,29 @@
     )(place, *blocks, gain.reshape(1, width))
 
 
-def hidden_step(step, steps, rows, w_gate, w_up, gate_acc, up_acc):
-    @pl.when(step == 0)
-    def _():
-        gate_acc[...] = dot(rows[...], w_gate[0])
-        up_acc[...] = dot(rows[...], w_up[0])
-
-    @pl.when((step > 0) & (step < steps))
-    def _():
-        gate_acc[...] += dot(rows[...], w_gate[0])
-        up_acc[...] += dot(rows[...], w_up[0])
-
-
-def hidden_of(gate_acc, up_acc):
-    return (jax.nn.silu(gate_acc[...]) * up_acc[...]).astype(BF16)
-
-
-def hidden_kernel(steps, rows, w_gate, w_up, out, gate_acc, up_acc):
-    step = pl.program_id(0)
-    hidden_step(step, steps, rows, w_gate, w_up, gate_acc, up_acc)
-
-    @pl.when(step == steps - 1)
-    def _():
-        out[...] = hidden_of(gate_acc, up_acc)
-
-
-def hidden_rows(rows, w_gate, w_up, steps=4):
-    count, width = rows.shape
-    units = w_gate.shape[2]
-    deep = width // steps
-    return pl.pallas_call(
-        functools.partial(hidden_kernel, steps),
-        grid=(steps,),
-        out_shape=jax.ShapeDtypeStruct((count, units), BF16),
-        in_specs=[
-            pl.BlockSpec((count, deep), lambda i: (0, i)),
-            pl.BlockSpec((1, deep, units), lambda i: (0, i, 0)),
-            pl.BlockSpec((1, deep, units), lambda i: (0, i, 0)),
-        ],
-        out_specs=pl.BlockSpec((count, units), lambda i: (0, 0)),
-        scratch_shapes=[pltpu.VMEM((count, units), F32)] * 2,
-        compiler_params=params(32),
-    )(rows, w_gate, w_up)
-
-
-def expert_kernel(steps, rows, w_gate, w_up, w_down, out, gate_acc, up_acc, hidden):
-    step = pl.program_id(0)
-    hidden_step(step, steps, rows, w_gate, w_up, gate_acc, up_acc)
-
-    @pl.when(step == steps)
-    def _():
-        hidden[...] = hidden_of(gate_acc, up_acc)
-
-    @pl.when(step >= steps)
-    def _():
-        out[...] = dot(hidden[...], w_down[0]).astype(BF16)
-
-
-def expert_rows(rows, w_gate, w_up, w_down, steps=4):
-    count, width = rows.shape
-    units = w_gate.shape[2]
-    deep = width // steps
-    early = lambda i: jnp.minimum(i, steps - 1)
-    late = lambda i: jnp.maximum(i - steps, 0)
-    return pl.pallas_call(
-        functools.partial(expert_kernel, steps),
-        grid=(2 * steps,),
-        out_shape=jax.ShapeDtypeStruct((count, width), BF16),
-        in_specs=[
-            pl.BlockSpec((count, deep), lambda i: (0, early(i))),
-            pl.BlockSpec((1, deep, units), lambda i: (0, early(i), 0)),
-            pl.BlockSpec((1, deep, units), lambda i: (0, early(i), 0)),
-            pl.BlockSpec((1, units, deep), lambda i: (0, 0, late(i))),
-        ],
-        out_specs=pl.BlockSpec((count, deep), lambda i: (0, late(i))),
-        scratch_shapes=[pltpu.VMEM((count, units), F32)] * 2 + [pltpu.VMEM((count, units), BF16)],
+def expert_kernel(rows, w_gate, w_up, w_down, out):
+    width = rows.shape[1]
+    deep = width // 4
+    gate_act = up_act = 0.0
+    for i in range(4):
+        at = slice(i * deep, (i + 1) * deep)
+        piece = rows[:, at]
+        gate_act += dot(piece, w_gate[0, at, :])
+        up_act += dot(piece, w_up[0, at, :])
+    hidden = (jax.nn.silu(gate_act) * up_act).astype(BF16)
+    for i in range(4):
+        at = slice(i * deep, (i + 1) * deep)
+        out[:, at] = dot(hidden, w_down[0, :, at]).astype(BF16)
+
+
+def expert_rows(rows, w_gate, w_up, w_down):
+    return pl.pallas_call(
+        expert_kernel,
+        out_shape=jax.ShapeDtypeStruct(rows.shape, BF16),
+        in_specs=[VMEM] * 4,
+        out_specs=VMEM,
         compiler_params=params(32),
     )(rows, w_gate, w_up, w_down)
-
-
-def down_kernel(hidden, w_down, mate, out):
-    out[...] = (dot(hidden[...], w_down[0]) + mate[...].astype(F32)).astype(BF16)
-
-
-def down_rows(hidden, w_down, mate, steps=4):
-    count, width = mate.shape
-    units = hidden.shape[1]
-    deep = width // steps
-    return pl.pallas_call(
-        down_kernel,
-        grid=(steps,),
-        out_shape=jax.ShapeDtypeStruct((count, width), BF16),
-        in_specs=[
-            pl.BlockSpec((count, units), lambda i: (0, 0)),
-            pl.BlockSpec((1, units, deep), lambda i: (0, 0, i)),
-            pl.BlockSpec((count, deep), lambda i: (0, i)),
-        ],
-        out_specs=pl.BlockSpec((count, deep), lambda i: (0, i)),
-        compiler_params=params(32),
-    )(hidden, w_down, mate)
 
 
 def combine_kernel(high, low, back, own, base, *outs):
@@ -328,10 +265,12 @@
     note = jnp.concatenate([expert_ids.astype(F32), high, gate_values - high], axis=1)
     note = jnp.pad(note, ((0, 0), (0, LANES - 3 * TOPK)))
 
-    other = swap(proj_weight, "xl")
-    give, keep = project(jnp.stack([ci, xli]), gather_z(context), proj_weight, other, n_spread)
+    spot = jnp.stack([ci, xli])
+    rhs, held = stage(spot, proj_weight, swap(proj_weight, "xl"), context)
+    give, keep = project(spot, [held] + gather_z(context)[1:], rhs, n_spread)
     got = swap(give, "c")
     partial = (keep + got.astype(F32)).astype(BF16)
+    partial, note = lax.optimization_barrier((partial, note))
     partial = lax.all_to_all(partial, SPREAD, 0, 0, tiled=True)
 
     place = zi.reshape(1)
@@ -342,9 +281,9 @@
     mine = mine.reshape(-1, width)
 
     theirs = swap(mine, "c")
-    hidden = hidden_rows(mine, w_gate, w_up)
+    mine_out = expert_rows(mine, w_gate, w_up, w_down)
     from_mate = swap(expert_rows(theirs, w_gate, w_up, w_down), "c")
-    summed = down_rows(hidden, w_down, from_mate)
+    summed = (mine_out.astype(F32) + from_mate.astype(F32)).astype(BF16)
     back = lax.all_to_all(summed.reshape(n_plane, -1, width), PLANE, 0, 0, tiled=True)
 
     base, *blocks = combine(high, low, back.reshape(-1, width), own)

time: 175 us -> 169 us (0.966)
  Pallas kernels: 15.3 us -> 12 us
  waiting for transfers between devices: 31.1 us -> 28.2 us
    pallas_call x3, Pallas kernels: 10.9 us -> 7.6 us  [the longest x2 7.01 us: expert_rows(): pl.pallas_call(expert_kernel, out_shape=jax.ShapeDtypeStruct(rows.shape,...]
    ppermute x21, waiting for transfers between devices: 15.3 us -> 12.8 us  [fetch(): return lax.ppermute(x, 'z', [((i + hop) % NZ, i) for i in range(NZ)])]
    unnamed x18 -> x16, local copies, waits for them, and re-layouts: 3.77 us -> 3.77 us
where the time goes in v4:
time: 169 us; the launch traced here: 167 us
  blocking collectives  61.8 us (37%)
  starting transfers between devices  58.5 us (35%)
  waiting for transfers between devices  28.2 us (17%)
  Pallas kernels  12 us (7%)
  local copies, waits for them, and re-layouts  3.77 us (2%)
  other arithmetic  2.61 us (2%)
    ppermute x21, starting transfers between devices, fetch(): return lax.ppermute(x, 'z', [((i + hop) % NZ, i) for i in range(NZ)])  49.7 us
    all_to_all x1, blocking collectives, on_device(): lax.all_to_all(summed.reshape(n_plane, -1, width), PLANE, 0, 0, tiled=True)  31.5 us
    all_to_all x1, blocking collectives, on_device(): lax.all_to_all(sent.reshape(n_plane, -1, width), PLANE, 0, 0, tiled=True)  30.2 us
    ppermute x21, waiting for transfers between devices, fetch(): return lax.ppermute(x, 'z', [((i + hop) % NZ, i) for i in range(NZ)])  12.8 us
    all_to_all x1, waiting for transfers between devices, on_device(): partial = lax.all_to_all(partial, SPREAD, 0, 0, tiled=True)  9.03 us
    all_to_all x1, starting transfers between devices, on_device(): partial = lax.all_to_all(partial, SPREAD, 0, 0, tiled=True)  7.69 us
    pallas_call x2, Pallas kernels, expert_rows(): pl.pallas_call(expert_kernel, out_shape=jax.ShapeDtypeStruct(rows.shape,...  7.01 us
    ppermute x4, waiting for transfers between devices, swap(): return lax.ppermute(x, axis, [(0, 1), (1, 0)])  6.44 us
  transfers between devices with their start and end apart: 26, of which 12 were waited for; matrix products, arithmetic and copies ran while one was open for 0% of the time, Pallas kernels for 2%

profile of v4, /device:TPU:6, one launch (start us, length us, event | category | flops | bytes accessed | tf_op | source)
XLA Modules:
  0.0 167.1 jit_solution(17778796794755584663)
XLA Ops:
  0.0 5.9 %collective-permute-start.1 = (bf16[128,512]{1,0:T(8,128)(2,1)}, bf16[128,512]{1,0:T(8,128)(2,1)S(1)}, u32[]{:S(2)}, u32[]{:S(2)}) collective-permute-start(bf16[128,512]{1,0:T(8,128)(2,1)} %context.1), channel_id=1, source_target_pairs={{32,0},{64,32},{96,64},{128,96},{160,128},{192,160},{224,192},{0,2... | collective-permute-start | bytes 393224 | tf_op jit(solution)/shard_map/ppermute | solution.py:32
  6.7 2.2 %collective-permute-done.1.refs_1_ = bf16[128,512]{1,0:T(8,128)(2,1)S(1)} collective-permute-done((bf16[128,512]{1,0:T(8,128)(2,1)}, bf16[128,512]{1,0:T(8,128)(2,1)S(1)}, u32[]{:S(2)}, u32[]{:S(2)}) %collective-permute-start.1) | collective-permute-done | bytes 131104 | tf_op jit(solution)/shard_map/ppermute | solution.py:32
  8.9 2.8 %collective-permute-start.3 = (bf16[128,512]{1,0:T(8,128)(2,1)S(1)}, bf16[128,512]{1,0:T(8,128)(2,1)S(1)}, u32[]{:S(2)}, u32[]{:S(2)}) collective-permute-start(bf16[128,512]{1,0:T(8,128)(2,1)S(1)} %collective-permute-done.1.refs_1_), channel_id=1, source_target_pairs={{64,0},{96,32},{128,64},{160,96},{192,128},{224,160},{0,192},{32,2... | collective-permute-start | bytes 393224 | tf_op jit(solution)/shard_map/ppermute | solution.py:32
  16.0 2.1 %collective-permute-done.3.refs_3_ = bf16[128,512]{1,0:T(8,128)(2,1)S(1)} collective-permute-done((bf16[128,512]{1,0:T(8,128)(2,1)S(1)}, bf16[128,512]{1,0:T(8,128)(2,1)S(1)}, u32[]{:S(2)}, u32[]{:S(2)}) %collective-permute-start.3) | collective-permute-done | bytes 131104 | tf_op jit(solution)/shard_map/ppermute | solution.py:32
  18.1 6.1 %collective-permute-start.4 = (bf16[128,512]{1,0:T(8,128)(2,1)S(1)}, bf16[128,512]{1,0:T(8,128)(2,1)S(1)}, u32[]{:S(2)}, u32[]{:S(2)}) collective-permute-start(bf16[128,512]{1,0:T(8,128)(2,1)S(1)} %collective-permute-done.3.refs_3_), channel_id=1, source_target_pairs={{32,0},{64,32},{96,64},{128,96},{160,128},{192,160},{224,192},{0,2... | collective-permute-start | bytes 393224 | tf_op jit(solution)/shard_map/ppermute | solution.py:32
  29.2 1.8 %collective-permute-done.8 = bf16[8,64,512]{2,1,0:T(8,128)(2,1)S(1)} collective-permute-done((bf16[8,64,512]{2,1,0:T(8,128)(2,1)S(1)}, bf16[8,64,512]{2,1,0:T(8,128)(2,1)S(1)}, u32[]{:S(2)}, u32[]{:S(2)}) %collective-permute-start.8) | collective-permute-done | bytes 524320 | tf_op jit(solution)/shard_map/ppermute | solution.py:28
  32.0 7.7 %all-to-all-start = ((bf16[8,64,512]{2,1,0:T(8,128)(2,1)}), bf16[8,64,512]{2,1,0:T(8,128)(2,1)}, u32[]{:S(2)}, u32[]{:S(2)}) async-start(bf16[8,64,512]{2,1,0:T(8,128)(2,1)} %add_convert_fusion.1), calls=%async_computation | async-start | bytes 1048576 | tf_op jit(solution)/shard_map/all_to_all | solution.py:274
  39.6 9.0 %all-to-all-done.parts = bf16[8,64,512]{2,1,0:T(8,128)(2,1)} async-done(((bf16[8,64,512]{2,1,0:T(8,128)(2,1)}), bf16[8,64,512]{2,1,0:T(8,128)(2,1)}, u32[]{:S(2)}, u32[]{:S(2)}) %all-to-all-start) | async-done | bytes 524320 | tf_op jit(solution)/shard_map/all_to_all | solution.py:274
  49.8 2.7 %collective-permute-start.9 = (bf16[80,512]{1,0:T(8,128)(2,1)S(1)}, bf16[80,512]{1,0:T(8,128)(2,1)S(1)}, u32[]{:S(2)}, u32[]{:S(2)}) collective-permute-start(bf16[80,512]{1,0:T(8,128)(2,1)S(1)} %shard_map.84.refs_0_), channel_id=1, source_target_pairs={{32,0},{64,32},{96,64},{128,96},{160,128},{192,160},{224,192},{0,2... | collective-permute-start | bytes 245768 | tf_op jit(solution)/shard_map/ppermute | solution.py:32
  52.5 2.1 %collective-permute-done.9.refs_1_ = bf16[80,512]{1,0:T(8,128)(2,1)S(1)} collective-permute-done((bf16[80,512]{1,0:T(8,128)(2,1)S(1)}, bf16[80,512]{1,0:T(8,128)(2,1)S(1)}, u32[]{:S(2)}, u32[]{:S(2)}) %collective-permute-start.9) | collective-permute-done | bytes 81952 | tf_op jit(solution)/shard_map/ppermute | solution.py:32
  54.5 1.8 %collective-permute-start.11 = (bf16[80,512]{1,0:T(8,128)(2,1)S(1)}, bf16[80,512]{1,0:T(8,128)(2,1)S(1)}, u32[]{:S(2)}, u32[]{:S(2)}) collective-permute-start(bf16[80,512]{1,0:T(8,128)(2,1)S(1)} %collective-permute-done.9.refs_1_), channel_id=1, source_target_pairs={{64,0},{96,32},{128,64},{160,96},{192,128},{224,160},{0,192},{32,2... | collective-permute-start | bytes 245768 | tf_op jit(solution)/shard_map/ppermute | solution.py:32
  57.5 3.0 %collective-permute-start.10 = (bf16[80,512]{1,0:T(8,128)(2,1)S(1)}, bf16[80,512]{1,0:T(8,128)(2,1)S(1)}, u32[]{:S(2)}, u32[]{:S(2)}) collective-permute-start(bf16[80,512]{1,0:T(8,128)(2,1)S(1)} %shard_map.84.refs_0_), channel_id=1, source_target_pairs={{64,0},{96,32},{128,64},{160,96},{192,128},{224,160},{0,192},{32,2... | collective-permute-start | bytes 245768 | tf_op jit(solution)/shard_map/ppermute | solution.py:32
  60.6 5.8 %collective-permute-start.12 = (bf16[80,512]{1,0:T(8,128)(2,1)S(1)}, bf16[80,512]{1,0:T(8,128)(2,1)S(1)}, u32[]{:S(2)}, u32[]{:S(2)}) collective-permute-start(bf16[80,512]{1,0:T(8,128)(2,1)S(1)} %collective-permute-done.11.refs_3_), channel_id=1, source_target_pairs={{32,0},{64,32},{96,64},{128,96},{160,128},{192,160},{224,192},{0,2... | collective-permute-start | bytes 245768 | tf_op jit(solution)/shard_map/ppermute | solution.py:32
  69.7 30.2 %all_to_all.15 = bf16[16,16,4096]{2,1,0:T(8,128)(2,1)S(1)} all-to-all(bf16[16,16,4096]{2,1,0:T(8,128)(2,1)S(1)} %bitcast.11), channel_id=1, replica_groups=mesh['z'=8,'xl'=2,'xh'=2,'y'=4,'c'=2] {'xl','xh','y'}, dimensions={0} | all-to-all | bytes 4194304 | tf_op jit(solution)/shard_map/all_to_all | solution.py:280
  99.9 4.2 %collective-permute-done.16.rows = bf16[256,4096]{1,0:T(8,128)(2,1)S(1)} collective-permute-done((bf16[256,4096]{1,0:T(8,128)(2,1)S(1)}, bf16[256,4096]{1,0:T(8,128)(2,1)S(1)}, u32[]{:S(2)}, u32[]{:S(2)}) %collective-permute-start.16) | collective-permute-done | bytes 2097184 | tf_op jit(solution)/shard_map/ppermute | solution.py:28
  104.0 1.9 %copy-done.2 = bf16[1,384,4096]{2,1,0:T(8,128)(2,1)S(1)} copy-done((bf16[1,384,4096]{2,1,0:T(8,128)(2,1)S(1)}, bf16[1,384,4096]{2,1,0:T(8,128)(2,1)}, u32[]{:S(2)}) %copy-start.2) | copy-done | bytes 3145752
  105.9 3.5 %shard_map.87 = bf16[256,4096]{1,0:T(8,128)(2,1)S(1)} custom-call(bf16[256,4096]{1,0:T(8,128)(2,1)S(1)} %collective-permute-done.16.rows, bf16[1,4096,384]{2,1,0:T(8,128)(2,1)S(1)} %copy-done, bf16[1,4096,384]{2,1,0:T(8,128)(2,1)S(1)} %copy-done.1, bf16[1,384,4096]{2,1,0:T(8,128)(2,1)S(1)} %copy-done.2), custom_call_target="tpu_custom_call" | custom-call | tf_op jit(solution)/shard_map/pallas_call | solution.py:225
  109.7 3.5 %shard_map.86 = bf16[256,4096]{1,0:T(8,128)(2,1)S(1)} custom-call(bf16[256,4096]{1,0:T(8,128)(2,1)S(1)} %bitcast.10, bf16[1,4096,384]{2,1,0:T(8,128)(2,1)S(1)} %copy-done, bf16[1,4096,384]{2,1,0:T(8,128)(2,1)S(1)} %copy-done.1, bf16[1,384,4096]{2,1,0:T(8,128)(2,1)S(1)} %copy-done.2), custom_call_target="tpu_custom_call" | custom-call | tf_op jit(solution)/shard_map/pallas_call | solution.py:225
  114.5 31.5 %all_to_all.16 = bf16[16,16,4096]{2,1,0:T(8,128)(2,1)S(1)} all-to-all(bf16[16,16,4096]{2,1,0:T(8,128)(2,1)S(1)} %bitcast.13), channel_id=1, replica_groups=mesh['z'=8,'xl'=2,'xh'=2,'y'=4,'c'=2] {'xl','xh','y'}, dimensions={0} | all-to-all | bytes 4194304 | tf_op jit(solution)/shard_map/all_to_all | solution.py:287
  146.9 3.7 %collective-permute-start.18 = (bf16[8,4096]{1,0:T(8,128)(2,1)S(1)}, bf16[8,4096]{1,0:T(8,128)(2,1)S(1)}, u32[]{:S(2)}, u32[]{:S(2)}) collective-permute-start(bf16[8,4096]{1,0:T(8,128)(2,1)S(1)} %get-tuple-element.34), channel_id=1, source_target_pairs={{128,0},{160,32},{192,64},{224,96},{0,128},{32,160},{64,192},{96,2... | collective-permute-start | bytes 196616 | tf_op jit(solution)/shard_map/ppermute | solution.py:32
  154.2 3.9 %collective-permute-start.22 = (bf16[8,4096]{1,0:T(8,128)(2,1)S(1)}, bf16[8,4096]{1,0:T(8,128)(2,1)S(1)}, u32[]{:S(2)}, u32[]{:S(2)}) collective-permute-start(bf16[8,4096]{1,0:T(8,128)(2,1)S(1)} %get-tuple-element.38), channel_id=1, source_target_pairs={{64,0},{96,32},{128,64},{160,96},{192,128},{224,160},{0,192},{32,2... | collective-permute-start | bytes 196616 | tf_op jit(solution)/shard_map/ppermute | solution.py:32
  158.1 2.1 %collective-permute-start.23 = (bf16[8,4096]{1,0:T(8,128)(2,1)S(1)}, bf16[8,4096]{1,0:T(8,128)(2,1)S(1)}, u32[]{:S(2)}, u32[]{:S(2)}) collective-permute-start(bf16[8,4096]{1,0:T(8,128)(2,1)S(1)} %get-tuple-element.39), channel_id=1, source_target_pairs={{160,0},{192,32},{224,64},{0,96},{32,128},{64,160},{96,192},{128,2... | collective-permute-start | bytes 196616 | tf_op jit(solution)/shard_map/ppermute | solution.py:32
  160.2 2.9 %collective-permute-start.24 = (bf16[8,4096]{1,0:T(8,128)(2,1)S(1)}, bf16[8,4096]{1,0:T(8,128)(2,1)S(1)}, u32[]{:S(2)}, u32[]{:S(2)}) collective-permute-start(bf16[8,4096]{1,0:T(8,128)(2,1)S(1)} %get-tuple-element.40), channel_id=1, source_target_pairs={{96,0},{128,32},{160,64},{192,96},{224,128},{0,160},{32,192},{64,2... | collective-permute-start | bytes 196616 | tf_op jit(solution)/shard_map/ppermute | solution.py:32
  163.1 3.2 %collective-permute-done.23 = bf16[8,4096]{1,0:T(8,128)(2,1)S(1)} collective-permute-done((bf16[8,4096]{1,0:T(8,128)(2,1)S(1)}, bf16[8,4096]{1,0:T(8,128)(2,1)S(1)}, u32[]{:S(2)}, u32[]{:S(2)}) %collective-permute-start.23) | collective-permute-done | bytes 65568 | tf_op jit(solution)/shard_map/ppermute | solution.py:32
  (60 shorter events, 23.3 us)
Async XLA Ops:
  0.0 8.9 %collective-permute-start.1 = (bf16[128,512]{1,0:T(8,128)(2,1)}, bf16[128,512]{1,0:T(8,128)(2,1)S(1)}, u32[]{:S(2)}, u32[]{:S(2)}) collective-permute-start(bf16[128,512]{1,0:T(8,128)(2,1)} %context.1), channel_id=1, source_target_pairs={{32,0},{64,32},{96,64},{128,96},{160,128},{192,160},{224,192},{0,2... | collective-permute-start | bytes 393224 | tf_op jit(solution)/shard_map/ppermute | solution.py:32
  5.9 18.3 %collective-permute-start = (bf16[512,256]{1,0:T(8,128)(2,1)}, bf16[512,256]{1,0:T(8,128)(2,1)S(1)}, u32[]{:S(2)}, u32[]{:S(2)}) collective-permute-start(bf16[512,256]{1,0:T(8,128)(2,1)} %own.1), channel_id=1, source_target_pairs={{0,16},{16,0},{1,17},{17,1},{2,18},{18,2},{3,19},{19,3},{4,20},{20... | collective-permute-start | bytes 786440 | tf_op jit(solution)/shard_map/ppermute | solution.py:28
  6.7 8.0 %collective-permute-start.5 = (bf16[128,512]{1,0:T(8,128)(2,1)}, bf16[128,512]{1,0:T(8,128)(2,1)S(1)}, u32[]{:S(2)}, u32[]{:S(2)}) collective-permute-start(bf16[128,512]{1,0:T(8,128)(2,1)} %context.1), channel_id=1, source_target_pairs={{224,0},{0,32},{32,64},{64,96},{96,128},{128,160},{160,192},{192,2... | collective-permute-start | bytes 393224 | tf_op jit(solution)/shard_map/ppermute | solution.py:32
  8.9 9.1 %collective-permute-start.3 = (bf16[128,512]{1,0:T(8,128)(2,1)S(1)}, bf16[128,512]{1,0:T(8,128)(2,1)S(1)}, u32[]{:S(2)}, u32[]{:S(2)}) collective-permute-start(bf16[128,512]{1,0:T(8,128)(2,1)S(1)} %collective-permute-done.1.refs_1_), channel_id=1, source_target_pairs={{64,0},{96,32},{128,64},{160,96},{192,128},{224,160},{0,192},{32,2... | collective-permute-start | bytes 393224 | tf_op jit(solution)/shard_map/ppermute | solution.py:32
  11.8 14.9 %collective-permute-start.2 = (bf16[128,512]{1,0:T(8,128)(2,1)}, bf16[128,512]{1,0:T(8,128)(2,1)S(1)}, u32[]{:S(2)}, u32[]{:S(2)}) collective-permute-start(bf16[128,512]{1,0:T(8,128)(2,1)} %context.1), channel_id=1, source_target_pairs={{64,0},{96,32},{128,64},{160,96},{192,128},{224,160},{0,192},{32,2... | collective-permute-start | bytes 393224 | tf_op jit(solution)/shard_map/ppermute | solution.py:32
  13.2 13.5 %collective-permute-start.7 = (bf16[128,512]{1,0:T(8,128)(2,1)}, bf16[128,512]{1,0:T(8,128)(2,1)S(1)}, u32[]{:S(2)}, u32[]{:S(2)}) collective-permute-start(bf16[128,512]{1,0:T(8,128)(2,1)} %context.1), channel_id=1, source_target_pairs={{192,0},{224,32},{0,64},{32,96},{64,128},{96,160},{128,192},{160,2... | collective-permute-start | bytes 393224 | tf_op jit(solution)/shard_map/ppermute | solution.py:32
  14.7 13.0 %collective-permute-start.6 = (bf16[128,512]{1,0:T(8,128)(2,1)S(1)}, bf16[128,512]{1,0:T(8,128)(2,1)S(1)}, u32[]{:S(2)}, u32[]{:S(2)}) collective-permute-start(bf16[128,512]{1,0:T(8,128)(2,1)S(1)} %collective-permute-done.5.refs_7_), channel_id=1, source_target_pairs={{192,0},{224,32},{0,64},{32,96},{64,128},{96,160},{128,192},{160,2... | collective-permute-start | bytes 393224 | tf_op jit(solution)/shard_map/ppermute | solution.py:32
  18.1 9.6 %collective-permute-start.4 = (bf16[128,512]{1,0:T(8,128)(2,1)S(1)}, bf16[128,512]{1,0:T(8,128)(2,1)S(1)}, u32[]{:S(2)}, u32[]{:S(2)}) collective-permute-start(bf16[128,512]{1,0:T(8,128)(2,1)S(1)} %collective-permute-done.3.refs_3_), channel_id=1, source_target_pairs={{32,0},{64,32},{96,64},{128,96},{160,128},{192,160},{224,192},{0,2... | collective-permute-start | bytes 393224 | tf_op jit(solution)/shard_map/ppermute | solution.py:32
  32.0 16.7 %all-to-all-start = ((bf16[8,64,512]{2,1,0:T(8,128)(2,1)}), bf16[8,64,512]{2,1,0:T(8,128)(2,1)}, u32[]{:S(2)}, u32[]{:S(2)}) async-start(bf16[8,64,512]{2,1,0:T(8,128)(2,1)} %add_convert_fusion.1), calls=%async_computation | async-start | bytes 1048576 | tf_op jit(solution)/shard_map/all_to_all | solution.py:274
  49.8 4.7 %collective-permute-start.9 = (bf16[80,512]{1,0:T(8,128)(2,1)S(1)}, bf16[80,512]{1,0:T(8,128)(2,1)S(1)}, u32[]{:S(2)}, u32[]{:S(2)}) collective-permute-start(bf16[80,512]{1,0:T(8,128)(2,1)S(1)} %shard_map.84.refs_0_), channel_id=1, source_target_pairs={{32,0},{64,32},{96,64},{128,96},{160,128},{192,160},{224,192},{0,2... | collective-permute-start | bytes 245768 | tf_op jit(solution)/shard_map/ppermute | solution.py:32
  52.5 8.0 %collective-permute-start.13 = (bf16[80,512]{1,0:T(8,128)(2,1)S(1)}, bf16[80,512]{1,0:T(8,128)(2,1)S(1)}, u32[]{:S(2)}, u32[]{:S(2)}) collective-permute-start(bf16[80,512]{1,0:T(8,128)(2,1)S(1)} %shard_map.84.refs_0_), channel_id=1, source_target_pairs={{224,0},{0,32},{32,64},{64,96},{96,128},{128,160},{160,192},{192,2... | collective-permute-start | bytes 245768 | tf_op jit(solution)/shard_map/ppermute | solution.py:32
  54.5 6.0 %collective-permute-start.11 = (bf16[80,512]{1,0:T(8,128)(2,1)S(1)}, bf16[80,512]{1,0:T(8,128)(2,1)S(1)}, u32[]{:S(2)}, u32[]{:S(2)}) collective-permute-start(bf16[80,512]{1,0:T(8,128)(2,1)S(1)} %collective-permute-done.9.refs_1_), channel_id=1, source_target_pairs={{64,0},{96,32},{128,64},{160,96},{192,128},{224,160},{0,192},{32,2... | collective-permute-start | bytes 245768 | tf_op jit(solution)/shard_map/ppermute | solution.py:32
  56.4 10.1 %collective-permute-start.15 = (bf16[80,512]{1,0:T(8,128)(2,1)S(1)}, bf16[80,512]{1,0:T(8,128)(2,1)S(1)}, u32[]{:S(2)}, u32[]{:S(2)}) collective-permute-start(bf16[80,512]{1,0:T(8,128)(2,1)S(1)} %shard_map.84.refs_0_), channel_id=1, source_target_pairs={{192,0},{224,32},{0,64},{32,96},{64,128},{96,160},{128,192},{160,2... | collective-permute-start | bytes 245768 | tf_op jit(solution)/shard_map/ppermute | solution.py:32
  57.5 9.0 %collective-permute-start.10 = (bf16[80,512]{1,0:T(8,128)(2,1)S(1)}, bf16[80,512]{1,0:T(8,128)(2,1)S(1)}, u32[]{:S(2)}, u32[]{:S(2)}) collective-permute-start(bf16[80,512]{1,0:T(8,128)(2,1)S(1)} %shard_map.84.refs_0_), channel_id=1, source_target_pairs={{64,0},{96,32},{128,64},{160,96},{192,128},{224,160},{0,192},{32,2... | collective-permute-start | bytes 245768 | tf_op jit(solution)/shard_map/ppermute | solution.py:32
  60.5 6.9 %collective-permute-start.14 = (bf16[80,512]{1,0:T(8,128)(2,1)S(1)}, bf16[80,512]{1,0:T(8,128)(2,1)S(1)}, u32[]{:S(2)}, u32[]{:S(2)}) collective-permute-start(bf16[80,512]{1,0:T(8,128)(2,1)S(1)} %collective-permute-done.13.refs_7_), channel_id=1, source_target_pairs={{192,0},{224,32},{0,64},{32,96},{64,128},{96,160},{128,192},{160,2... | collective-permute-start | bytes 245768 | tf_op jit(solution)/shard_map/ppermute | solution.py:32
  60.6 7.9 %collective-permute-start.12 = (bf16[80,512]{1,0:T(8,128)(2,1)S(1)}, bf16[80,512]{1,0:T(8,128)(2,1)S(1)}, u32[]{:S(2)}, u32[]{:S(2)}) collective-permute-start(bf16[80,512]{1,0:T(8,128)(2,1)S(1)} %collective-permute-done.11.refs_3_), channel_id=1, source_target_pairs={{32,0},{64,32},{96,64},{128,96},{160,128},{192,160},{224,192},{0,2... | collective-permute-start | bytes 245768 | tf_op jit(solution)/shard_map/ppermute | solution.py:32
  109.4 4.2 %collective-permute-start.17 = (bf16[256,4096]{1,0:T(8,128)(2,1)S(1)}, bf16[256,4096]{1,0:T(8,128)(2,1)S(1)}, u32[]{:S(2)}, u32[]{:S(2)}) collective-permute-start(bf16[256,4096]{1,0:T(8,128)(2,1)S(1)} %shard_map.87), channel_id=1, source_target_pairs={{0,1},{1,0},{2,3},{3,2},{4,5},{5,4},{6,7},{7,6},{8,9},{9,8},{10,11... | collective-permute-start | bytes 6291464 | tf_op jit(solution)/shard_map/ppermute | solution.py:28
  146.9 11.2 %collective-permute-start.18 = (bf16[8,4096]{1,0:T(8,128)(2,1)S(1)}, bf16[8,4096]{1,0:T(8,128)(2,1)S(1)}, u32[]{:S(2)}, u32[]{:S(2)}) collective-permute-start(bf16[8,4096]{1,0:T(8,128)(2,1)S(1)} %get-tuple-element.34), channel_id=1, source_target_pairs={{128,0},{160,32},{192,64},{224,96},{0,128},{32,160},{64,192},{96,2... | collective-permute-start | bytes 196616 | tf_op jit(solution)/shard_map/ppermute | solution.py:32
  150.5 9.6 %collective-permute-start.19 = (bf16[8,4096]{1,0:T(8,128)(2,1)S(1)}, bf16[8,4096]{1,0:T(8,128)(2,1)S(1)}, u32[]{:S(2)}, u32[]{:S(2)}) collective-permute-start(bf16[8,4096]{1,0:T(8,128)(2,1)S(1)} %get-tuple-element.35), channel_id=1, source_target_pairs={{224,0},{0,32},{32,64},{64,96},{96,128},{128,160},{160,192},{192,2... | collective-permute-start | bytes 196616 | tf_op jit(solution)/shard_map/ppermute | solution.py:32
  152.2 10.9 %collective-permute-start.20 = (bf16[8,4096]{1,0:T(8,128)(2,1)S(1)}, bf16[8,4096]{1,0:T(8,128)(2,1)S(1)}, u32[]{:S(2)}, u32[]{:S(2)}) collective-permute-start(bf16[8,4096]{1,0:T(8,128)(2,1)S(1)} %get-tuple-element.36), channel_id=1, source_target_pairs={{32,0},{64,32},{96,64},{128,96},{160,128},{192,160},{224,192},{0,2... | collective-permute-start | bytes 196616 | tf_op jit(solution)/shard_map/ppermute | solution.py:32
  153.9 9.2 %collective-permute-start.21 = (bf16[8,4096]{1,0:T(8,128)(2,1)S(1)}, bf16[8,4096]{1,0:T(8,128)(2,1)S(1)}, u32[]{:S(2)}, u32[]{:S(2)}) collective-permute-start(bf16[8,4096]{1,0:T(8,128)(2,1)S(1)} %get-tuple-element.37), channel_id=1, source_target_pairs={{192,0},{224,32},{0,64},{32,96},{64,128},{96,160},{128,192},{160,2... | collective-permute-start | bytes 196616 | tf_op jit(solution)/shard_map/ppermute | solution.py:32
  154.2 8.9 %collective-permute-start.22 = (bf16[8,4096]{1,0:T(8,128)(2,1)S(1)}, bf16[8,4096]{1,0:T(8,128)(2,1)S(1)}, u32[]{:S(2)}, u32[]{:S(2)}) collective-permute-start(bf16[8,4096]{1,0:T(8,128)(2,1)S(1)} %get-tuple-element.38), channel_id=1, source_target_pairs={{64,0},{96,32},{128,64},{160,96},{192,128},{224,160},{0,192},{32,2... | collective-permute-start | bytes 196616 | tf_op jit(solution)/shard_map/ppermute | solution.py:32
  158.1 8.3 %collective-permute-start.23 = (bf16[8,4096]{1,0:T(8,128)(2,1)S(1)}, bf16[8,4096]{1,0:T(8,128)(2,1)S(1)}, u32[]{:S(2)}, u32[]{:S(2)}) collective-permute-start(bf16[8,4096]{1,0:T(8,128)(2,1)S(1)} %get-tuple-element.39), channel_id=1, source_target_pairs={{160,0},{192,32},{224,64},{0,96},{32,128},{64,160},{96,192},{128,2... | collective-permute-start | bytes 196616 | tf_op jit(solution)/shard_map/ppermute | solution.py:32
  160.2 6.2 %collective-permute-start.24 = (bf16[8,4096]{1,0:T(8,128)(2,1)S(1)}, bf16[8,4096]{1,0:T(8,128)(2,1)S(1)}, u32[]{:S(2)}, u32[]{:S(2)}) collective-permute-start(bf16[8,4096]{1,0:T(8,128)(2,1)S(1)} %get-tuple-element.40), channel_id=1, source_target_pairs={{96,0},{128,32},{160,64},{192,96},{224,128},{0,160},{32,192},{64,2... | collective-permute-start | bytes 196616 | tf_op jit(solution)/shard_map/ppermute | solution.py:32
  (10 other events, 214.1 us)

commit v5 on v4

--- a/solution.py
+++ b/solution.py
@@ -1,3 +1,5 @@
+import functools
+
 import jax
 import jax.numpy as jnp
 from jax import lax
@@ -33,10 +35,10 @@
 
 
 def gather_z(x):
+    up2, dn2 = fetch(x, 2), fetch(x, -2)
     up1, dn1 = fetch(x, 1), fetch(x, -1)
-    up2, dn2 = fetch(x, 2), fetch(x, -2)
-    up3, dn3 = fetch(up1, 2), fetch(dn1, -2)
-    far = fetch(up3, 1)
+    up3, dn3 = fetch(up2, 1), fetch(dn2, -1)
+    far = fetch(up2, 2)
     return [x, up1, up2, up3, far, dn3, dn2, dn1]
 
 
@@ -49,7 +51,7 @@
 
 
 def stage_kernel(place, own, other, context, rhs, held):
-    xl = place[1]
+    xl = place[0]
     cols = own.shape[1]
     rhs[:, pl.ds(pl.multiple_of(xl * cols, LANES), cols)] = own[...]
     rhs[:, pl.ds(pl.multiple_of((1 - xl) * cols, LANES), cols)] = other[...]
@@ -69,33 +71,29 @@
     )(place, own, other, context)
 
 
-def project_kernel(place, *refs):
-    blocks, (rhs, give, keep, held) = refs[:NZ], refs[NZ:]
-    core = place[0]
+def project_kernel(*refs):
+    blocks, (rhs, out, held) = refs[:NZ], refs[NZ:]
     lhs = jnp.concatenate([b[...] for b in blocks], axis=0)
     total = dot(lhs, rhs[...])
-    spread = give.shape[0]
-    rows = lhs.shape[0] // (NZ * spread * 2)
-    total = total.reshape(NZ, spread, 2, rows, rhs.shape[1])
+    peers = out.shape[0]
+    rows = out.shape[1] // NZ
+    total = total.reshape(NZ, peers, rows, rhs.shape[1])
     for k in range(NZ):
-        at = slice(k * rows, (k + 1) * rows)
-        first, second = total[k, :, 0], total[k, :, 1]
-        keep[:, at, :] = jnp.where(core == 0, first, second)
-        held[:, at, :] = jnp.where(core == 0, second, first)
-    give[...] = held[...].astype(BF16)
-
-
-def project(place, blocks, rhs, spread):
-    rows = blocks[0].shape[0] // (2 * spread)
-    shape = (spread, NZ * rows, rhs.shape[1])
+        held[:, k * rows : (k + 1) * rows, :] = total[k]
+    out[...] = held[...].astype(BF16)
+
+
+def project(blocks, rhs, peers):
+    rows = blocks[0].shape[0] // peers
+    shape = (peers, NZ * rows, rhs.shape[1])
     return pl.pallas_call(
         project_kernel,
-        out_shape=(jax.ShapeDtypeStruct(shape, BF16), jax.ShapeDtypeStruct(shape, F32)),
-        in_specs=[SMEM] + [VMEM] * (NZ + 1),
-        out_specs=(VMEM, VMEM),
+        out_shape=jax.ShapeDtypeStruct(shape, BF16),
+        in_specs=[VMEM] * (NZ + 1),
+        out_specs=VMEM,
         scratch_shapes=[pltpu.VMEM(shape, F32)],
         compiler_params=params(32),
-    )(place, *blocks, rhs)
+    )(*blocks, rhs)
 
 
 def settle_kernel(place, parts, note, out, held):
@@ -126,7 +124,7 @@
 
 
 def place_kernel(place, *refs):
-    blocks, (gain, sent, own, high, low, stream, notes, mass) = refs[:NZ], refs[NZ:]
+    blocks, (gain, sent, own, high, low, stream, notes) = refs[:NZ], refs[NZ:]
     z = place[0]
     tokens, width = stream.shape
     rows, wide = tokens // NZ, width // NZ
@@ -157,16 +155,9 @@
     rank = dot(jnp.where(earlier, 1.0, 0.0).astype(BF16), match.astype(BF16))
     slot = (token // rows) * CAP + rank.astype(jnp.int32)
     placed = (match > 0.5) & (slot == lane % slots) & (rank < CAP - 0.5)
-    mass[...] = jnp.where(placed, gate, 0.0)
     spots = jnp.transpose(jnp.where(placed, 1.0, 0.0)).astype(BF16)
 
-    weight = jnp.concatenate(
-        [
-            mass[pl.ds(pl.multiple_of(lax.rem(z + hop, NZ) * rows, rows), rows), :]
-            for hop in range(NZ)
-        ],
-        axis=0,
-    )
+    weight = jnp.where(placed, gate, 0.0)
     top = weight.astype(BF16)
     high[...] = top
     low[...] = (weight - top.astype(F32)).astype(BF16)
@@ -200,97 +191,111 @@
         scratch_shapes=[
             pltpu.VMEM((tokens, width), F32),
             pltpu.VMEM((tokens, LANES), F32),
-            pltpu.VMEM((tokens, lanes), F32),
         ],
         compiler_params=params(32),
     )(place, *blocks, gain.reshape(1, width))
 
 
-def expert_kernel(rows, w_gate, w_up, w_down, out):
-    width = rows.shape[1]
+def expert_kernel(first, rows, w_gate, w_up, w_down, out, down, arrived):
+    copy = pltpu.make_async_copy(w_down, down, arrived)
+    copy.start()
+    count, width = out.shape
     deep = width // 4
     gate_act = up_act = 0.0
     for i in range(4):
         at = slice(i * deep, (i + 1) * deep)
-        piece = rows[:, at]
+        piece = rows[first : first + count, at]
         gate_act += dot(piece, w_gate[0, at, :])
         up_act += dot(piece, w_up[0, at, :])
     hidden = (jax.nn.silu(gate_act) * up_act).astype(BF16)
+    copy.wait()
     for i in range(4):
         at = slice(i * deep, (i + 1) * deep)
-        out[:, at] = dot(hidden, w_down[0, :, at]).astype(BF16)
-
-
-def expert_rows(rows, w_gate, w_up, w_down):
-    return pl.pallas_call(
-        expert_kernel,
-        out_shape=jax.ShapeDtypeStruct(rows.shape, BF16),
-        in_specs=[VMEM] * 4,
-        out_specs=VMEM,
+        out[:, at] = dot(hidden, down[0, :, at]).astype(BF16)
+
+
+def expert_rows(rows, first, count, w_gate, w_up, w_down):
+    return pl.pallas_call(
+        functools.partial(expert_kernel, first),
+        out_shape=jax.ShapeDtypeStruct((count, rows.shape[1]), BF16),
+        in_specs=[VMEM] * 3 + [pl.BlockSpec(memory_space=pl.ANY)],
+        out_specs=VMEM,
+        scratch_shapes=[pltpu.VMEM(w_down.shape, BF16), pltpu.SemaphoreType.DMA],
         compiler_params=params(32),
     )(rows, w_gate, w_up, w_down)
 
 
-def combine_kernel(high, low, back, own, base, *outs):
-    rows, width = own.shape
+def add_kernel(mine, *refs):
+    parts, out = refs[:-1], refs[-1]
+    count = parts[0].shape[0]
+    for i, part in enumerate(parts):
+        at = slice(i * count, (i + 1) * count)
+        out[at, :] = (mine[at, :].astype(F32) + part[...].astype(F32)).astype(BF16)
+
+
+def add_rows(mine, parts):
+    return pl.pallas_call(
+        add_kernel,
+        out_shape=jax.ShapeDtypeStruct(mine.shape, BF16),
+        in_specs=[VMEM] * (1 + len(parts)),
+        out_specs=VMEM,
+        compiler_params=params(32),
+    )(mine, *parts)
+
+
+def combine_kernel(high, low, back, out):
+    width = back.shape[1]
     wide = width // 4
     for i in range(4):
         at = slice(i * wide, (i + 1) * wide)
         piece = back[:, at]
-        mix = dot(high[...], piece) + dot(low[...], piece)
-        base[:, at] = own[:, at] + mix[:rows]
-        for hop in range(1, NZ):
-            outs[hop - 1][:, at] = mix[hop * rows : (hop + 1) * rows].astype(BF16)
-
-
-def combine(high, low, back, own):
-    rows, width = own.shape
+        out[:, at] = (dot(high[...], piece) + dot(low[...], piece)).astype(BF16)
+
+
+def combine(high, low, back):
     return pl.pallas_call(
         combine_kernel,
-        out_shape=(jax.ShapeDtypeStruct((rows, width), F32),)
-        + (jax.ShapeDtypeStruct((rows, width), BF16),) * (NZ - 1),
-        in_specs=[VMEM] * 4,
-        out_specs=(VMEM,) * NZ,
-        compiler_params=params(32),
-    )(high, low, back, own)
+        out_shape=jax.ShapeDtypeStruct((high.shape[0], back.shape[1]), BF16),
+        in_specs=[VMEM] * 3,
+        out_specs=VMEM,
+        compiler_params=params(32),
+    )(high, low, back)
 
 
 def on_device(context, proj_weight, norm_gain, expert_ids, gate_values, w_gate, w_up, w_down):
-    zi, xli, ci = (lax.axis_index(a).astype(jnp.int32) for a in ("z", "xl", "c"))
-    n_spread = lax.axis_size(SPREAD)
+    zi, xli = (lax.axis_index(a).astype(jnp.int32) for a in ("z", "xl"))
+    n_tensor = lax.axis_size(TENSOR)
     n_plane = lax.axis_size(PLANE)
-    rows = expert_ids.shape[0]
 
     high = lax.reduce_precision(gate_values, exponent_bits=8, mantissa_bits=7)
     note = jnp.concatenate([expert_ids.astype(F32), high, gate_values - high], axis=1)
     note = jnp.pad(note, ((0, 0), (0, LANES - 3 * TOPK)))
 
-    spot = jnp.stack([ci, xli])
-    rhs, held = stage(spot, proj_weight, swap(proj_weight, "xl"), context)
-    give, keep = project(spot, [held] + gather_z(context)[1:], rhs, n_spread)
-    got = swap(give, "c")
-    partial = (keep + got.astype(F32)).astype(BF16)
-    partial, note = lax.optimization_barrier((partial, note))
-    partial = lax.all_to_all(partial, SPREAD, 0, 0, tiled=True)
-
     place = zi.reshape(1)
+    rhs, held = stage(xli.reshape(1), proj_weight, swap(proj_weight, "xl"), context)
+    partial = project([held] + gather_z(context)[1:], rhs, n_tensor)
+    partial, note, place = lax.optimization_barrier((partial, note, place))
+    partial = lax.all_to_all(partial, TENSOR, 0, 0, tiled=True)
+
     part = settle(place, partial, note)
     sent, own, high, low = place_rows(place, gather_z(part), norm_gain, n_plane)
     width = sent.shape[1]
     mine = lax.all_to_all(sent.reshape(n_plane, -1, width), PLANE, 0, 0, tiled=True)
     mine = mine.reshape(-1, width)
 
+    weights = (w_gate, w_up, w_down)
     theirs = swap(mine, "c")
-    mine_out = expert_rows(mine, w_gate, w_up, w_down)
-    from_mate = swap(expert_rows(theirs, w_gate, w_up, w_down), "c")
-    summed = (mine_out.astype(F32) + from_mate.astype(F32)).astype(BF16)
-    back = lax.all_to_all(summed.reshape(n_plane, -1, width), PLANE, 0, 0, tiled=True)
-
-    base, *blocks = combine(high, low, back.reshape(-1, width), own)
-    total = base
-    for hop in (4, 1, 7, 2, 6, 3, 5):
-        total += fetch(blocks[hop - 1], -hop).astype(F32)
-    return total.astype(BF16)
+    count = mine.shape[0]
+    mine_out = expert_rows(mine, 0, count, *weights)
+    theirs, mine_out = lax.optimization_barrier((theirs, mine_out))
+    half = count // 2
+    parts = [swap(expert_rows(theirs, at, half, *weights), "c") for at in (0, half)]
+    summed = add_rows(mine_out, parts).reshape(n_plane, -1, width)
+    back = lax.all_to_all(summed, PLANE, 0, 0, tiled=True).reshape(-1, width)
+
+    mixture = combine(high, low, back).reshape(NZ, -1, width)
+    home = lax.all_to_all(mixture, "z", 0, 0, tiled=True)
+    return (own + jnp.sum(home.astype(F32), axis=0)).astype(BF16)
 
 
 def solution(mesh):

time: 169 us -> 168 us (level); the launches traced: 167 us -> 168 us
  blocking collectives: 61.8 us -> 109 us
  starting transfers between devices: 58.5 us -> 31.7 us
  waiting for transfers between devices: 28.2 us -> 10.7 us
  local copies, waits for them, and re-layouts: 3.77 us -> 1.88 us
    all_to_all x1 -> x3, blocking collectives: 31.5 us -> 76.8 us  [the longest x1 31.6 us: on_device(): back = lax.all_to_all(summed, PLANE, 0, 0, tiled=True).reshape(-1, width)]
    ppermute x21 -> x14, starting transfers between devices: 49.7 us -> 30.3 us  [fetch(): return lax.ppermute(x, 'z', [((i + hop) % NZ, i) for i in range(NZ)])]
    all_to_all x1 -> x0, waiting for transfers between devices: 9.03 us -> none  [on_device(): partial = lax.all_to_all(partial, SPREAD, 0, 0, tiled=True)]
    all_to_all x1 -> x0, starting transfers between devices: 7.69 us -> none  [on_device(): partial = lax.all_to_all(partial, SPREAD, 0, 0, tiled=True)]
    ppermute x21 -> x14, waiting for transfers between devices: 12.8 us -> 6.78 us  [fetch(): return lax.ppermute(x, 'z', [((i + hop) % NZ, i) for i in range(NZ)])]
    all_to_all x1, blocking collectives: 30.2 us -> 32.7 us  [on_device(): lax.all_to_all(sent.reshape(n_plane, -1, width), PLANE, 0, 0, tiled=True)]
    ppermute x4, waiting for transfers between devices: 6.44 us -> 3.94 us  [swap(): return lax.ppermute(x, axis, [(0, 1), (1, 0)])]
    unnamed x16 -> x12, local copies, waits for them, and re-layouts: 3.77 us -> 1.88 us
  transfers between devices with their start and end apart: 26 -> 18, of which waited for: 12 -> 7; matrix products, arithmetic and copies ran while one was open for 0% -> 1% of each run, Pallas kernels for 2% -> 2%
where the time goes in v5:
time: 168 us
  blocking collectives  109 us (65%)
  starting transfers between devices  31.7 us (19%)
  Pallas kernels  11.7 us (7%)
  waiting for transfers between devices  10.7 us (6%)
  other arithmetic  2.17 us (1%)
  local copies, waits for them, and re-layouts  1.88 us (1%)
    all_to_all x1, blocking collectives, on_device(): lax.all_to_all(sent.reshape(n_plane, -1, width), PLANE, 0, 0, tiled=True)  32.7 us
    all_to_all x1, blocking collectives, on_device(): back = lax.all_to_all(summed, PLANE, 0, 0, tiled=True).reshape(-1, width)  31.6 us
    ppermute x14, starting transfers between devices, fetch(): return lax.ppermute(x, 'z', [((i + hop) % NZ, i) for i in range(NZ)])  30.3 us
    all_to_all x1, blocking collectives, on_device(): partial = lax.all_to_all(partial, TENSOR, 0, 0, tiled=True)  22.6 us
    all_to_all x1, blocking collectives, on_device(): home = lax.all_to_all(mixture, 'z', 0, 0, tiled=True)  22.5 us
    pallas_call x3, Pallas kernels, expert_rows(): pl.pallas_call(functools.partial(expert_kernel, first), out_shape=jax.Sha...  8.26 us
    ppermute x14, waiting for transfers between devices, fetch(): return lax.ppermute(x, 'z', [((i + hop) % NZ, i) for i in range(NZ)])  6.78 us
    ppermute x4, waiting for transfers between devices, swap(): return lax.ppermute(x, axis, [(0, 1), (1, 0)])  3.94 us
  transfers between devices with their start and end apart: 18, of which 7 were waited for; matrix products, arithmetic and copies ran while one was open for 1% of the time, Pallas kernels for 2%

profile of v5, /device:TPU:6, one launch (start us, length us, event | category | flops | bytes accessed | tf_op | source)
XLA Modules:
  0.0 167.8 jit_solution(9542744241448590446)
XLA Ops:
  0.8 6.3 %collective-permute-start.2 = (bf16[128,512]{1,0:T(8,128)(2,1)}, bf16[128,512]{1,0:T(8,128)(2,1)S(1)}, u32[]{:S(2)}, u32[]{:S(2)}) collective-permute-start(bf16[128,512]{1,0:T(8,128)(2,1)} %context.1), channel_id=1, source_target_pairs={{64,0},{96,32},{128,64},{160,96},{192,128},{224,160},{0,192},{32,2... | collective-permute-start | bytes 393224 | tf_op jit(solution)/shard_map/ppermute | solution.py:34
  7.1 3.7 %collective-permute-start.1 = (bf16[128,512]{1,0:T(8,128)(2,1)}, bf16[128,512]{1,0:T(8,128)(2,1)S(1)}, u32[]{:S(2)}, u32[]{:S(2)}) collective-permute-start(bf16[128,512]{1,0:T(8,128)(2,1)} %context.1), channel_id=1, source_target_pairs={{32,0},{64,32},{96,64},{128,96},{160,128},{192,160},{224,192},{0,2... | collective-permute-start | bytes 393224 | tf_op jit(solution)/shard_map/ppermute | solution.py:34
  10.8 2.7 %collective-permute-done.2.refs_2_ = bf16[128,512]{1,0:T(8,128)(2,1)S(1)} collective-permute-done((bf16[128,512]{1,0:T(8,128)(2,1)}, bf16[128,512]{1,0:T(8,128)(2,1)S(1)}, u32[]{:S(2)}, u32[]{:S(2)}) %collective-permute-start.2) | collective-permute-done | bytes 131104 | tf_op jit(solution)/shard_map/ppermute | solution.py:34
  13.5 4.6 %collective-permute-start.4 = (bf16[128,512]{1,0:T(8,128)(2,1)S(1)}, bf16[128,512]{1,0:T(8,128)(2,1)S(1)}, u32[]{:S(2)}, u32[]{:S(2)}) collective-permute-start(bf16[128,512]{1,0:T(8,128)(2,1)S(1)} %collective-permute-done.2.refs_2_), channel_id=1, source_target_pairs={{64,0},{96,32},{128,64},{160,96},{192,128},{224,160},{0,192},{32,2... | collective-permute-start | bytes 393224 | tf_op jit(solution)/shard_map/ppermute | solution.py:34
  18.2 2.0 %collective-permute-start.6 = (bf16[128,512]{1,0:T(8,128)(2,1)S(1)}, bf16[128,512]{1,0:T(8,128)(2,1)S(1)}, u32[]{:S(2)}, u32[]{:S(2)}) collective-permute-start(bf16[128,512]{1,0:T(8,128)(2,1)S(1)} %collective-permute-done.5.refs_6_), channel_id=1, source_target_pairs={{224,0},{0,32},{32,64},{64,96},{96,128},{128,160},{160,192},{192,2... | collective-permute-start | bytes 393224 | tf_op jit(solution)/shard_map/ppermute | solution.py:34
  21.6 0.9 copy-done.3
  23.6 1.2 collective-permute-done.3.refs_3_
  25.5 22.6 %all_to_all.20.parts = bf16[16,64,512]{2,1,0:T(8,128)(2,1)S(1)} all-to-all(bf16[16,64,512]{2,1,0:T(8,128)(2,1)S(1)} %shard_map.83), channel_id=1, replica_groups=mesh['z'=8,'xl'=2,'xh'=2,'y'=4,'c'=2] {'xh','y','c'}, dimensions={0} | all-to-all | bytes 2097152 | tf_op jit(solution)/shard_map/all_to_all | solution.py:278
  48.9 3.7 %collective-permute-start.9 = (bf16[80,512]{1,0:T(8,128)(2,1)S(1)}, bf16[80,512]{1,0:T(8,128)(2,1)S(1)}, u32[]{:S(2)}, u32[]{:S(2)}) collective-permute-start(bf16[80,512]{1,0:T(8,128)(2,1)S(1)} %shard_map.84.refs_0_), channel_id=1, source_target_pairs={{64,0},{96,32},{128,64},{160,96},{192,128},{224,160},{0,192},{32,2... | collective-permute-start | bytes 245768 | tf_op jit(solution)/shard_map/ppermute | solution.py:34
  52.9 2.9 %collective-permute-start.8 = (bf16[80,512]{1,0:T(8,128)(2,1)S(1)}, bf16[80,512]{1,0:T(8,128)(2,1)S(1)}, u32[]{:S(2)}, u32[]{:S(2)}) collective-permute-start(bf16[80,512]{1,0:T(8,128)(2,1)S(1)} %shard_map.84.refs_0_), channel_id=1, source_target_pairs={{32,0},{64,32},{96,64},{128,96},{160,128},{192,160},{224,192},{0,2... | collective-permute-start | bytes 245768 | tf_op jit(solution)/shard_map/ppermute | solution.py:34
  55.8 1.3 collective-permute-start.13
  57.1 3.4 %collective-permute-start.11 = (bf16[80,512]{1,0:T(8,128)(2,1)S(1)}, bf16[80,512]{1,0:T(8,128)(2,1)S(1)}, u32[]{:S(2)}, u32[]{:S(2)}) collective-permute-start(bf16[80,512]{1,0:T(8,128)(2,1)S(1)} %collective-permute-done.9.refs_2_), channel_id=1, source_target_pairs={{64,0},{96,32},{128,64},{160,96},{192,128},{224,160},{0,192},{32,2... | collective-permute-start | bytes 245768 | tf_op jit(solution)/shard_map/ppermute | solution.py:34
  60.4 1.6 collective-permute-start.10
  62.0 1.4 collective-permute-done.11.refs_4_
  63.4 1.5 collective-permute-done.10.refs_3_
  64.9 1.2 shard_map.85
  66.1 32.7 %all_to_all.21 = bf16[16,16,4096]{2,1,0:T(8,128)(2,1)S(1)} all-to-all(bf16[16,16,4096]{2,1,0:T(8,128)(2,1)S(1)} %bitcast.12), channel_id=1, replica_groups=mesh['z'=8,'xl'=2,'xh'=2,'y'=4,'c'=2] {'xl','xh','y'}, dimensions={0} | all-to-all | bytes 4194304 | tf_op jit(solution)/shard_map/all_to_all | solution.py:283
  98.8 3.8 %shard_map.86.mine = bf16[256,4096]{1,0:T(8,128)(2,1)S(1)} custom-call(bf16[256,4096]{1,0:T(8,128)(2,1)S(1)} %bitcast.11, bf16[1,4096,384]{2,1,0:T(8,128)(2,1)S(1)} %copy-done, bf16[1,4096,384]{2,1,0:T(8,128)(2,1)S(1)} %copy-done.1, bf16[1,384,4096]{2,1,0:T(8,128)(2,1)S(1)} %copy-done.2), custom_call_target="tpu_custom_call" | custom-call | tf_op jit(solution)/shard_map/pallas_call | solution.py:218
  103.0 2.2 %shard_map.88 = bf16[128,4096]{1,0:T(8,128)(2,1)S(1)} custom-call(bf16[256,4096]{1,0:T(8,128)(2,1)S(1)} %collective-permute-done.15.rows, bf16[1,4096,384]{2,1,0:T(8,128)(2,1)S(1)} %copy-done, bf16[1,4096,384]{2,1,0:T(8,128)(2,1)S(1)} %copy-done.1, bf16[1,384,4096]{2,1,0:T(8,128)(2,1)S(1)} %copy-done.2), custom_call_target="tpu_custom_call" | custom-call | tf_op jit(solution)/shard_map/pallas_call | solution.py:218
  105.2 2.2 %shard_map.87 = bf16[128,4096]{1,0:T(8,128)(2,1)S(1)} custom-call(bf16[256,4096]{1,0:T(8,128)(2,1)S(1)} %collective-permute-done.15.rows, bf16[1,4096,384]{2,1,0:T(8,128)(2,1)S(1)} %copy-done, bf16[1,4096,384]{2,1,0:T(8,128)(2,1)S(1)} %copy-done.1, bf16[1,384,4096]{2,1,0:T(8,128)(2,1)S(1)} %copy-done.2), custom_call_target="tpu_custom_call" | custom-call | tf_op jit(solution)/shard_map/pallas_call | solution.py:218
  108.0 2.1 %collective-permute-done.16.refs_0_ = bf16[128,4096]{1,0:T(8,128)(2,1)S(1)} collective-permute-done((bf16[128,4096]{1,0:T(8,128)(2,1)S(1)}, bf16[128,4096]{1,0:T(8,128)(2,1)S(1)}, u32[]{:S(2)}, u32[]{:S(2)}) %collective-permute-start.16) | collective-permute-done | bytes 1048608 | tf_op jit(solution)/shard_map/ppermute | solution.py:30
  110.1 1.5 collective-permute-done.17.refs_1_
  112.1 31.6 %all_to_all.22 = bf16[16,16,4096]{2,1,0:T(8,128)(2,1)S(1)} all-to-all(bf16[16,16,4096]{2,1,0:T(8,128)(2,1)S(1)} %bitcast.8), channel_id=1, replica_groups=mesh['z'=8,'xl'=2,'xh'=2,'y'=4,'c'=2] {'xl','xh','y'}, dimensions={0} | all-to-all | bytes 4194304 | tf_op jit(solution)/shard_map/all_to_all | solution.py:294
  144.6 22.5 %all_to_all.23 = bf16[8,8,4096]{2,1,0:T(8,128)(2,1)S(1)} all-to-all(bf16[8,8,4096]{2,1,0:T(8,128)(2,1)S(1)} %bitcast.13), channel_id=1, replica_groups=mesh['z'=8,'xl'=2,'xh'=2,'y'=4,'c'=2] {'z'}, dimensions={0} | all-to-all | bytes 1048576 | tf_op jit(solution)/shard_map/all_to_all | solution.py:297
  (42 shorter events, 8.0 us)
Async XLA Ops:
  0.0 18.2 %collective-permute-start = (bf16[512,256]{1,0:T(8,128)(2,1)}, bf16[512,256]{1,0:T(8,128)(2,1)S(1)}, u32[]{:S(2)}, u32[]{:S(2)}) collective-permute-start(bf16[512,256]{1,0:T(8,128)(2,1)} %own.1), channel_id=1, source_target_pairs={{0,16},{16,0},{1,17},{17,1},{2,18},{18,2},{3,19},{19,3},{4,20},{20... | collective-permute-start | bytes 786440 | tf_op jit(solution)/shard_map/ppermute | solution.py:30
  0.8 12.7 %collective-permute-start.2 = (bf16[128,512]{1,0:T(8,128)(2,1)}, bf16[128,512]{1,0:T(8,128)(2,1)S(1)}, u32[]{:S(2)}, u32[]{:S(2)}) collective-permute-start(bf16[128,512]{1,0:T(8,128)(2,1)} %context.1), channel_id=1, source_target_pairs={{64,0},{96,32},{128,64},{160,96},{192,128},{224,160},{0,192},{32,2... | collective-permute-start | bytes 393224 | tf_op jit(solution)/shard_map/ppermute | solution.py:34
  7.1 11.0 %collective-permute-start.5 = (bf16[128,512]{1,0:T(8,128)(2,1)}, bf16[128,512]{1,0:T(8,128)(2,1)S(1)}, u32[]{:S(2)}, u32[]{:S(2)}) collective-permute-start(bf16[128,512]{1,0:T(8,128)(2,1)} %context.1), channel_id=1, source_target_pairs={{192,0},{224,32},{0,64},{32,96},{64,128},{96,160},{128,192},{160,2... | collective-permute-start | bytes 393224 | tf_op jit(solution)/shard_map/ppermute | solution.py:34
  7.1 16.4 %collective-permute-start.1 = (bf16[128,512]{1,0:T(8,128)(2,1)}, bf16[128,512]{1,0:T(8,128)(2,1)S(1)}, u32[]{:S(2)}, u32[]{:S(2)}) collective-permute-start(bf16[128,512]{1,0:T(8,128)(2,1)} %context.1), channel_id=1, source_target_pairs={{32,0},{64,32},{96,64},{128,96},{160,128},{192,160},{224,192},{0,2... | collective-permute-start | bytes 393224 | tf_op jit(solution)/shard_map/ppermute | solution.py:34
  10.8 12.7 %collective-permute-start.7 = (bf16[128,512]{1,0:T(8,128)(2,1)}, bf16[128,512]{1,0:T(8,128)(2,1)S(1)}, u32[]{:S(2)}, u32[]{:S(2)}) collective-permute-start(bf16[128,512]{1,0:T(8,128)(2,1)} %context.1), channel_id=1, source_target_pairs={{224,0},{0,32},{32,64},{64,96},{96,128},{128,160},{160,192},{192,2... | collective-permute-start | bytes 393224 | tf_op jit(solution)/shard_map/ppermute | solution.py:34
  13.5 10.1 %collective-permute-start.4 = (bf16[128,512]{1,0:T(8,128)(2,1)S(1)}, bf16[128,512]{1,0:T(8,128)(2,1)S(1)}, u32[]{:S(2)}, u32[]{:S(2)}) collective-permute-start(bf16[128,512]{1,0:T(8,128)(2,1)S(1)} %collective-permute-done.2.refs_2_), channel_id=1, source_target_pairs={{64,0},{96,32},{128,64},{160,96},{192,128},{224,160},{0,192},{32,2... | collective-permute-start | bytes 393224 | tf_op jit(solution)/shard_map/ppermute | solution.py:34
  18.2 6.6 %collective-permute-start.3 = (bf16[128,512]{1,0:T(8,128)(2,1)S(1)}, bf16[128,512]{1,0:T(8,128)(2,1)S(1)}, u32[]{:S(2)}, u32[]{:S(2)}) collective-permute-start(bf16[128,512]{1,0:T(8,128)(2,1)S(1)} %collective-permute-done.2.refs_2_), channel_id=1, source_target_pairs={{32,0},{64,32},{96,64},{128,96},{160,128},{192,160},{224,192},{0,2... | collective-permute-start | bytes 393224 | tf_op jit(solution)/shard_map/ppermute | solution.py:34
  18.2 6.6 %collective-permute-start.6 = (bf16[128,512]{1,0:T(8,128)(2,1)S(1)}, bf16[128,512]{1,0:T(8,128)(2,1)S(1)}, u32[]{:S(2)}, u32[]{:S(2)}) collective-permute-start(bf16[128,512]{1,0:T(8,128)(2,1)S(1)} %collective-permute-done.5.refs_6_), channel_id=1, source_target_pairs={{224,0},{0,32},{32,64},{64,96},{96,128},{128,160},{160,192},{192,2... | collective-permute-start | bytes 393224 | tf_op jit(solution)/shard_map/ppermute | solution.py:34
  21.6 1.0 copy-start.3
  22.6 0.9 copy-start.4
  24.8 74.0 %copy-start.2 = (bf16[1,384,4096]{2,1,0:T(8,128)(2,1)S(1)}, bf16[1,384,4096]{2,1,0:T(8,128)(2,1)}, u32[]{:S(2)}) copy-start(bf16[1,384,4096]{2,1,0:T(8,128)(2,1)} %w_down.5) | copy-start | bytes 9437188
  25.5 39.4 %copy-start.5 = (f32[4096]{0:T(1024)S(1)}, f32[4096]{0:T(1024)}, u32[]{:S(2)}) copy-start(f32[4096]{0:T(1024)} %param.10) | copy-start | bytes 49156
  25.5 73.3 %copy-start.1 = (bf16[1,4096,384]{2,1,0:T(8,128)(2,1)S(1)}, bf16[1,4096,384]{2,1,0:T(8,128)(2,1)}, u32[]{:S(2)}) copy-start(bf16[1,4096,384]{2,1,0:T(8,128)(2,1)} %w_up.5) | copy-start | bytes 9437188
  48.3 7.5 %collective-permute-start.12 = (bf16[80,512]{1,0:T(8,128)(2,1)S(1)}, bf16[80,512]{1,0:T(8,128)(2,1)S(1)}, u32[]{:S(2)}, u32[]{:S(2)}) collective-permute-start(bf16[80,512]{1,0:T(8,128)(2,1)S(1)} %shard_map.84.refs_0_), channel_id=1, source_target_pairs={{192,0},{224,32},{0,64},{32,96},{64,128},{96,160},{128,192},{160,2... | collective-permute-start | bytes 245768 | tf_op jit(solution)/shard_map/ppermute | solution.py:34
  48.9 8.2 %collective-permute-start.9 = (bf16[80,512]{1,0:T(8,128)(2,1)S(1)}, bf16[80,512]{1,0:T(8,128)(2,1)S(1)}, u32[]{:S(2)}, u32[]{:S(2)}) collective-permute-start(bf16[80,512]{1,0:T(8,128)(2,1)S(1)} %shard_map.84.refs_0_), channel_id=1, source_target_pairs={{64,0},{96,32},{128,64},{160,96},{192,128},{224,160},{0,192},{32,2... | collective-permute-start | bytes 245768 | tf_op jit(solution)/shard_map/ppermute | solution.py:34
  52.6 9.5 %collective-permute-start.14 = (bf16[80,512]{1,0:T(8,128)(2,1)S(1)}, bf16[80,512]{1,0:T(8,128)(2,1)S(1)}, u32[]{:S(2)}, u32[]{:S(2)}) collective-permute-start(bf16[80,512]{1,0:T(8,128)(2,1)S(1)} %shard_map.84.refs_0_), channel_id=1, source_target_pairs={{224,0},{0,32},{32,64},{64,96},{96,128},{128,160},{160,192},{192,2... | collective-permute-start | bytes 245768 | tf_op jit(solution)/shard_map/ppermute | solution.py:34
  52.9 9.1 %collective-permute-start.8 = (bf16[80,512]{1,0:T(8,128)(2,1)S(1)}, bf16[80,512]{1,0:T(8,128)(2,1)S(1)}, u32[]{:S(2)}, u32[]{:S(2)}) collective-permute-start(bf16[80,512]{1,0:T(8,128)(2,1)S(1)} %shard_map.84.refs_0_), channel_id=1, source_target_pairs={{32,0},{64,32},{96,64},{128,96},{160,128},{192,160},{224,192},{0,2... | collective-permute-start | bytes 245768 | tf_op jit(solution)/shard_map/ppermute | solution.py:34
  55.8 6.2 %collective-permute-start.13 = (bf16[80,512]{1,0:T(8,128)(2,1)S(1)}, bf16[80,512]{1,0:T(8,128)(2,1)S(1)}, u32[]{:S(2)}, u32[]{:S(2)}) collective-permute-start(bf16[80,512]{1,0:T(8,128)(2,1)S(1)} %collective-permute-done.12.refs_6_), channel_id=1, source_target_pairs={{224,0},{0,32},{32,64},{64,96},{96,128},{128,160},{160,192},{192,2... | collective-permute-start | bytes 245768 | tf_op jit(solution)/shard_map/ppermute | solution.py:34
  57.1 6.3 %collective-permute-start.11 = (bf16[80,512]{1,0:T(8,128)(2,1)S(1)}, bf16[80,512]{1,0:T(8,128)(2,1)S(1)}, u32[]{:S(2)}, u32[]{:S(2)}) collective-permute-start(bf16[80,512]{1,0:T(8,128)(2,1)S(1)} %collective-permute-done.9.refs_2_), channel_id=1, source_target_pairs={{64,0},{96,32},{128,64},{160,96},{192,128},{224,160},{0,192},{32,2... | collective-permute-start | bytes 245768 | tf_op jit(solution)/shard_map/ppermute | solution.py:34
  60.4 4.4 %collective-permute-start.10 = (bf16[80,512]{1,0:T(8,128)(2,1)S(1)}, bf16[80,512]{1,0:T(8,128)(2,1)S(1)}, u32[]{:S(2)}, u32[]{:S(2)}) collective-permute-start(bf16[80,512]{1,0:T(8,128)(2,1)S(1)} %collective-permute-done.9.refs_2_), channel_id=1, source_target_pairs={{32,0},{64,32},{96,64},{128,96},{160,128},{192,160},{224,192},{0,2... | collective-permute-start | bytes 245768 | tf_op jit(solution)/shard_map/ppermute | solution.py:34
  66.1 32.8 %copy-start = (bf16[1,4096,384]{2,1,0:T(8,128)(2,1)S(1)}, bf16[1,4096,384]{2,1,0:T(8,128)(2,1)}, u32[]{:S(2)}) copy-start(bf16[1,4096,384]{2,1,0:T(8,128)(2,1)} %w_gate.5) | copy-start | bytes 9437188
  98.8 4.2 %collective-permute-start.15 = (bf16[256,4096]{1,0:T(8,128)(2,1)S(1)}, bf16[256,4096]{1,0:T(8,128)(2,1)S(1)}, u32[]{:S(2)}, u32[]{:S(2)}) collective-permute-start(bf16[256,4096]{1,0:T(8,128)(2,1)S(1)} %bitcast.10), channel_id=1, source_target_pairs={{0,1},{1,0},{2,3},{3,2},{4,5},{5,4},{6,7},{7,6},{8,9},{9,8},{10,11... | collective-permute-start | bytes 6291464 | tf_op jit(solution)/shard_map/ppermute | solution.py:30
  107.4 2.7 %collective-permute-start.16 = (bf16[128,4096]{1,0:T(8,128)(2,1)S(1)}, bf16[128,4096]{1,0:T(8,128)(2,1)S(1)}, u32[]{:S(2)}, u32[]{:S(2)}) collective-permute-start(bf16[128,4096]{1,0:T(8,128)(2,1)S(1)} %shard_map.87), channel_id=1, source_target_pairs={{0,1},{1,0},{2,3},{3,2},{4,5},{5,4},{6,7},{7,6},{8,9},{9,8},{10,11... | collective-permute-start | bytes 3145736 | tf_op jit(solution)/shard_map/ppermute | solution.py:30
  107.7 3.9 %collective-permute-start.17 = (bf16[128,4096]{1,0:T(8,128)(2,1)S(1)}, bf16[128,4096]{1,0:T(8,128)(2,1)S(1)}, u32[]{:S(2)}, u32[]{:S(2)}) collective-permute-start(bf16[128,4096]{1,0:T(8,128)(2,1)S(1)} %shard_map.88), channel_id=1, source_target_pairs={{0,1},{1,0},{2,3},{3,2},{4,5},{5,4},{6,7},{7,6},{8,9},{9,8},{10,11... | collective-permute-start | bytes 3145736 | tf_op jit(solution)/shard_map/ppermute | solution.py:30

commit v6 on v4

--- a/solution.py
+++ b/solution.py
@@ -1,3 +1,5 @@
+import functools
+
 import jax
 import jax.numpy as jnp
 from jax import lax
@@ -33,10 +35,10 @@
 
 
 def gather_z(x):
+    up2, dn2 = fetch(x, 2), fetch(x, -2)
     up1, dn1 = fetch(x, 1), fetch(x, -1)
-    up2, dn2 = fetch(x, 2), fetch(x, -2)
-    up3, dn3 = fetch(up1, 2), fetch(dn1, -2)
-    far = fetch(up3, 1)
+    up3, dn3 = fetch(up2, 1), fetch(dn2, -1)
+    far = fetch(up2, 2)
     return [x, up1, up2, up3, far, dn3, dn2, dn1]
 
 
@@ -49,7 +51,7 @@
 
 
 def stage_kernel(place, own, other, context, rhs, held):
-    xl = place[1]
+    xl = place[0]
     cols = own.shape[1]
     rhs[:, pl.ds(pl.multiple_of(xl * cols, LANES), cols)] = own[...]
     rhs[:, pl.ds(pl.multiple_of((1 - xl) * cols, LANES), cols)] = other[...]
@@ -71,11 +73,11 @@
 
 def project_kernel(place, *refs):
     blocks, (rhs, give, keep, held) = refs[:NZ], refs[NZ:]
-    core = place[0]
+    core = place[1]
     lhs = jnp.concatenate([b[...] for b in blocks], axis=0)
     total = dot(lhs, rhs[...])
     spread = give.shape[0]
-    rows = lhs.shape[0] // (NZ * spread * 2)
+    rows = give.shape[1] // NZ
     total = total.reshape(NZ, spread, 2, rows, rhs.shape[1])
     for k in range(NZ):
         at = slice(k * rows, (k + 1) * rows)
@@ -96,6 +98,20 @@
         scratch_shapes=[pltpu.VMEM(shape, F32)],
         compiler_params=params(32),
     )(place, *blocks, rhs)
+
+
+def join_kernel(keep, got, out):
+    out[...] = (keep[...] + got[...].astype(F32)).astype(BF16)
+
+
+def join(keep, got):
+    return pl.pallas_call(
+        join_kernel,
+        out_shape=jax.ShapeDtypeStruct(keep.shape, BF16),
+        in_specs=[VMEM] * 2,
+        out_specs=VMEM,
+        compiler_params=params(16),
+    )(keep, got)
 
 
 def settle_kernel(place, parts, note, out, held):
@@ -157,8 +173,9 @@
     rank = dot(jnp.where(earlier, 1.0, 0.0).astype(BF16), match.astype(BF16))
     slot = (token // rows) * CAP + rank.astype(jnp.int32)
     placed = (match > 0.5) & (slot == lane % slots) & (rank < CAP - 0.5)
+    spots = jnp.transpose(jnp.where(placed, 1.0, 0.0)).astype(BF16)
+
     mass[...] = jnp.where(placed, gate, 0.0)
-    spots = jnp.transpose(jnp.where(placed, 1.0, 0.0)).astype(BF16)
 
     weight = jnp.concatenate(
         [
@@ -206,29 +223,56 @@
     )(place, *blocks, gain.reshape(1, width))
 
 
-def expert_kernel(rows, w_gate, w_up, w_down, out):
-    width = rows.shape[1]
+def expert_kernel(first, rows, w_gate, w_up, w_down, out, down, arrived):
+    copy = pltpu.make_async_copy(w_down, down, arrived)
+    copy.start()
+    count, width = out.shape
     deep = width // 4
     gate_act = up_act = 0.0
     for i in range(4):
         at = slice(i * deep, (i + 1) * deep)
-        piece = rows[:, at]
+        piece = rows[first : first + count, at]
         gate_act += dot(piece, w_gate[0, at, :])
         up_act += dot(piece, w_up[0, at, :])
     hidden = (jax.nn.silu(gate_act) * up_act).astype(BF16)
+    copy.wait()
     for i in range(4):
         at = slice(i * deep, (i + 1) * deep)
-        out[:, at] = dot(hidden, w_down[0, :, at]).astype(BF16)
-
-
-def expert_rows(rows, w_gate, w_up, w_down):
-    return pl.pallas_call(
-        expert_kernel,
-        out_shape=jax.ShapeDtypeStruct(rows.shape, BF16),
-        in_specs=[VMEM] * 4,
+        out[:, at] = dot(hidden, down[0, :, at]).astype(BF16)
+
+
+def expert_rows(rows, first, count, w_gate, w_up, w_down):
+    return pl.pallas_call(
+        functools.partial(expert_kernel, first),
+        out_shape=jax.ShapeDtypeStruct((count, rows.shape[1]), BF16),
+        in_specs=[VMEM] * 3 + [pl.BlockSpec(memory_space=pl.ANY)],
         out_specs=VMEM,
-        compiler_params=params(32),
+        scratch_shapes=[pltpu.VMEM(w_down.shape, BF16), pltpu.SemaphoreType.DMA],
+        compiler_params=params(32),
+        cost_estimate=pl.CostEstimate(
+            flops=6 * count * w_down.shape[1] * w_down.shape[2],
+            bytes_accessed=6 * w_down.size + 4 * count * rows.shape[1],
+            transcendentals=count * w_down.shape[1],
+        ),
     )(rows, w_gate, w_up, w_down)
+
+
+def add_kernel(mine, *refs):
+    parts, out = refs[:-1], refs[-1]
+    count = parts[0].shape[0]
+    for i, part in enumerate(parts):
+        at = slice(i * count, (i + 1) * count)
+        out[at, :] = (mine[at, :].astype(F32) + part[...].astype(F32)).astype(BF16)
+
+
+def add_rows(mine, parts):
+    return pl.pallas_call(
+        add_kernel,
+        out_shape=jax.ShapeDtypeStruct(mine.shape, BF16),
+        in_specs=[VMEM] * (1 + len(parts)),
+        out_specs=VMEM,
+        compiler_params=params(32),
+    )(mine, *parts)
 
 
 def combine_kernel(high, low, back, own, base, *outs):
@@ -259,36 +303,37 @@
     zi, xli, ci = (lax.axis_index(a).astype(jnp.int32) for a in ("z", "xl", "c"))
     n_spread = lax.axis_size(SPREAD)
     n_plane = lax.axis_size(PLANE)
-    rows = expert_ids.shape[0]
 
     high = lax.reduce_precision(gate_values, exponent_bits=8, mantissa_bits=7)
     note = jnp.concatenate([expert_ids.astype(F32), high, gate_values - high], axis=1)
     note = jnp.pad(note, ((0, 0), (0, LANES - 3 * TOPK)))
 
-    spot = jnp.stack([ci, xli])
+    place = zi.reshape(1)
+    spot = jnp.stack([xli, ci])
     rhs, held = stage(spot, proj_weight, swap(proj_weight, "xl"), context)
     give, keep = project(spot, [held] + gather_z(context)[1:], rhs, n_spread)
-    got = swap(give, "c")
-    partial = (keep + got.astype(F32)).astype(BF16)
-    partial, note = lax.optimization_barrier((partial, note))
+    partial = join(keep, swap(give, "c"))
+    partial, note, place = lax.optimization_barrier((partial, note, place))
     partial = lax.all_to_all(partial, SPREAD, 0, 0, tiled=True)
 
-    place = zi.reshape(1)
     part = settle(place, partial, note)
     sent, own, high, low = place_rows(place, gather_z(part), norm_gain, n_plane)
     width = sent.shape[1]
     mine = lax.all_to_all(sent.reshape(n_plane, -1, width), PLANE, 0, 0, tiled=True)
     mine = mine.reshape(-1, width)
 
+    weights = (w_gate, w_up, w_down)
     theirs = swap(mine, "c")
-    mine_out = expert_rows(mine, w_gate, w_up, w_down)
-    from_mate = swap(expert_rows(theirs, w_gate, w_up, w_down), "c")
-    summed = (mine_out.astype(F32) + from_mate.astype(F32)).astype(BF16)
-    back = lax.all_to_all(summed.reshape(n_plane, -1, width), PLANE, 0, 0, tiled=True)
-
-    base, *blocks = combine(high, low, back.reshape(-1, width), own)
-    total = base
-    for hop in (4, 1, 7, 2, 6, 3, 5):
+    count = mine.shape[0]
+    mine_out = expert_rows(mine, 0, count, *weights)
+    theirs, mine_out = lax.optimization_barrier((theirs, mine_out))
+    half = count // 2
+    parts = [swap(expert_rows(theirs, at, half, *weights), "c") for at in (0, half)]
+    summed = add_rows(mine_out, parts).reshape(n_plane, -1, width)
+    back = lax.all_to_all(summed, PLANE, 0, 0, tiled=True).reshape(-1, width)
+
+    total, *blocks = combine(high, low, back, own)
+    for hop in (2, 6, 3, 5, 4, 1, 7):
         total += fetch(blocks[hop - 1], -hop).astype(F32)
     return total.astype(BF16)
 

time: 169 us -> 168 us (level)
  blocking collectives: 61.8 us -> 78 us
  starting transfers between devices: 58.5 us -> 45.3 us
  waiting for transfers between devices: 28.2 us -> 16.6 us
  local copies, waits for them, and re-layouts: 3.77 us -> 10.3 us
  Pallas kernels: 12 us -> 14.6 us
    all_to_all x1 -> x2, blocking collectives: 31.5 us -> 48.1 us  [the longest x1 31.7 us: on_device(): back = lax.all_to_all(summed, PLANE, 0, 0, tiled=True).reshape(-1, width)]
    all_to_all x1 -> x0, waiting for transfers between devices: 9.03 us -> none  [on_device(): partial = lax.all_to_all(partial, SPREAD, 0, 0, tiled=True)]
    all_to_all x1 -> x0, starting transfers between devices: 7.69 us -> none  [on_device(): partial = lax.all_to_all(partial, SPREAD, 0, 0, tiled=True)]
    unnamed x16 -> x32, local copies, waits for them, and re-layouts: 3.77 us -> 10.3 us
    ppermute x21, starting transfers between devices: 49.7 us -> 43.8 us  [fetch(): return lax.ppermute(x, 'z', [((i + hop) % NZ, i) for i in range(NZ)])]
    pallas_call x2 -> x5, Pallas kernels: 7.01 us -> 9.86 us  [the longest x3 8.26 us: expert_rows(): pl.pallas_call(functools.partial(expert_kernel, first), out_shape=jax.Sha...]
    convert_element_type x2 -> x0, other arithmetic: 1.75 us -> none  [the longest x1 0.98 us: on_device(): partial = (keep + got.astype(F32)).astype(BF16)]
    ppermute x4 -> x5, waiting for transfers between devices: 6.44 us -> 4.73 us  [swap(): return lax.ppermute(x, axis, [(0, 1), (1, 0)])]
  transfers between devices with their start and end apart: 26 -> 26, of which waited for: 12 -> 12; matrix products, arithmetic and copies ran while one was open for 0% -> 1% of each run, Pallas kernels for 2% -> 3%
where the time goes in v6:
time: 168 us; the launch traced here: 167 us
  blocking collectives  78 us (46%)
  starting transfers between devices  45.3 us (27%)
  waiting for transfers between devices  16.6 us (10%)
  Pallas kernels  14.6 us (9%)
  local copies, waits for them, and re-layouts  10.3 us (6%)
  other arithmetic  2.23 us (1%)
    ppermute x21, starting transfers between devices, fetch(): return lax.ppermute(x, 'z', [((i + hop) % NZ, i) for i in range(NZ)])  43.8 us
    all_to_all x1, blocking collectives, on_device(): back = lax.all_to_all(summed, PLANE, 0, 0, tiled=True).reshape(-1, width)  31.7 us
    all_to_all x1, blocking collectives, on_device(): lax.all_to_all(sent.reshape(n_plane, -1, width), PLANE, 0, 0, tiled=True)  29.9 us
    all_to_all x1, blocking collectives, on_device(): partial = lax.all_to_all(partial, SPREAD, 0, 0, tiled=True)  16.4 us
    ppermute x21, waiting for transfers between devices, fetch(): return lax.ppermute(x, 'z', [((i + hop) % NZ, i) for i in range(NZ)])  11.8 us
    unnamed x32, local copies, waits for them, and re-layouts  10.3 us
    pallas_call x3, Pallas kernels, expert_rows(): pl.pallas_call(functools.partial(expert_kernel, first), out_shape=jax.Sha...  8.26 us
    ppermute x5, waiting for transfers between devices, swap(): return lax.ppermute(x, axis, [(0, 1), (1, 0)])  4.73 us
  transfers between devices with their start and end apart: 26, of which 12 were waited for; matrix products, arithmetic and copies ran while one was open for 1% of the time, Pallas kernels for 3%

profile of v6, /device:TPU:6, one launch (start us, length us, event | category | flops | bytes accessed | tf_op | source)
XLA Modules:
  0.0 167.1 jit_solution(12631586095408135180)
XLA Ops:
  0.8 6.3 %collective-permute-start.2 = (bf16[128,512]{1,0:T(8,128)(2,1)}, bf16[128,512]{1,0:T(8,128)(2,1)S(1)}, u32[]{:S(2)}, u32[]{:S(2)}) collective-permute-start(bf16[128,512]{1,0:T(8,128)(2,1)} %context.1), channel_id=1, source_target_pairs={{64,0},{96,32},{128,64},{160,96},{192,128},{224,160},{0,192},{32,2... | collective-permute-start | bytes 393224 | tf_op jit(solution)/shard_map/ppermute | solution.py:34
  7.1 3.7 %collective-permute-start.1 = (bf16[128,512]{1,0:T(8,128)(2,1)}, bf16[128,512]{1,0:T(8,128)(2,1)S(1)}, u32[]{:S(2)}, u32[]{:S(2)}) collective-permute-start(bf16[128,512]{1,0:T(8,128)(2,1)} %context.1), channel_id=1, source_target_pairs={{32,0},{64,32},{96,64},{128,96},{160,128},{192,160},{224,192},{0,2... | collective-permute-start | bytes 393224 | tf_op jit(solution)/shard_map/ppermute | solution.py:34
  10.8 2.7 %collective-permute-done.2.refs_2_ = bf16[128,512]{1,0:T(8,128)(2,1)S(1)} collective-permute-done((bf16[128,512]{1,0:T(8,128)(2,1)}, bf16[128,512]{1,0:T(8,128)(2,1)S(1)}, u32[]{:S(2)}, u32[]{:S(2)}) %collective-permute-start.2) | collective-permute-done | bytes 131104 | tf_op jit(solution)/shard_map/ppermute | solution.py:34
  13.5 4.6 %collective-permute-start.4 = (bf16[128,512]{1,0:T(8,128)(2,1)S(1)}, bf16[128,512]{1,0:T(8,128)(2,1)S(1)}, u32[]{:S(2)}, u32[]{:S(2)}) collective-permute-start(bf16[128,512]{1,0:T(8,128)(2,1)S(1)} %collective-permute-done.2.refs_2_), channel_id=1, source_target_pairs={{64,0},{96,32},{128,64},{160,96},{192,128},{224,160},{0,192},{32,2... | collective-permute-start | bytes 393224 | tf_op jit(solution)/shard_map/ppermute | solution.py:34
  18.2 2.0 %collective-permute-start.6 = (bf16[128,512]{1,0:T(8,128)(2,1)S(1)}, bf16[128,512]{1,0:T(8,128)(2,1)S(1)}, u32[]{:S(2)}, u32[]{:S(2)}) collective-permute-start(bf16[128,512]{1,0:T(8,128)(2,1)S(1)} %collective-permute-done.5.refs_6_), channel_id=1, source_target_pairs={{224,0},{0,32},{32,64},{64,96},{96,128},{128,160},{160,192},{192,2... | collective-permute-start | bytes 393224 | tf_op jit(solution)/shard_map/ppermute | solution.py:34
  29.7 2.0 %shard_map.83 = (bf16[8,64,512]{2,1,0:T(8,128)(2,1)}, f32[8,64,512]{2,1,0:T(8,128)S(1)}) custom-call(s32[2]{0:T(128)S(1)} %pad_add_fusion.place, bf16[128,512]{1,0:T(8,128)(2,1)S(1)} %get-tuple-element.26.refs_0_, bf16[128,512]{1,0:T(8,128)(2,1)S(1)} %collective-permute-done.1.refs_1_, bf16[128,512]{1,0:T(8,128)(2,1)S(1)} %collective-permute-done.2.refs_2_, ...), custom_call_target="tpu_custom_call" | custom-call | tf_op jit(solution)/shard_map/pallas_call | solution.py:93
  37.4 16.4 %all_to_all.15.parts = bf16[8,64,512]{2,1,0:T(8,128)(2,1)S(1)} all-to-all(bf16[8,64,512]{2,1,0:T(8,128)(2,1)S(1)} %shard_map.84), channel_id=1, replica_groups=mesh['z'=8,'xl'=2,'xh'=2,'y'=4,'c'=2] {'xh','y'}, dimensions={0} | all-to-all | bytes 1048576 | tf_op jit(solution)/shard_map/all_to_all | solution.py:317
  55.1 3.0 %collective-permute-start.10 = (bf16[80,512]{1,0:T(8,128)(2,1)S(1)}, bf16[80,512]{1,0:T(8,128)(2,1)S(1)}, u32[]{:S(2)}, u32[]{:S(2)}) collective-permute-start(bf16[80,512]{1,0:T(8,128)(2,1)S(1)} %shard_map.85.refs_0_), channel_id=1, source_target_pairs={{64,0},{96,32},{128,64},{160,96},{192,128},{224,160},{0,192},{32,2... | collective-permute-start | bytes 245768 | tf_op jit(solution)/shard_map/ppermute | solution.py:34
  58.3 3.1 %collective-permute-start.9 = (bf16[80,512]{1,0:T(8,128)(2,1)S(1)}, bf16[80,512]{1,0:T(8,128)(2,1)S(1)}, u32[]{:S(2)}, u32[]{:S(2)}) collective-permute-start(bf16[80,512]{1,0:T(8,128)(2,1)S(1)} %shard_map.85.refs_0_), channel_id=1, source_target_pairs={{32,0},{64,32},{96,64},{128,96},{160,128},{192,160},{224,192},{0,2... | collective-permute-start | bytes 245768 | tf_op jit(solution)/shard_map/ppermute | solution.py:34
  62.7 3.6 %collective-permute-start.12 = (bf16[80,512]{1,0:T(8,128)(2,1)S(1)}, bf16[80,512]{1,0:T(8,128)(2,1)S(1)}, u32[]{:S(2)}, u32[]{:S(2)}) collective-permute-start(bf16[80,512]{1,0:T(8,128)(2,1)S(1)} %collective-permute-done.10.refs_2_), channel_id=1, source_target_pairs={{64,0},{96,32},{128,64},{160,96},{192,128},{224,160},{0,192},{32,2... | collective-permute-start | bytes 245768 | tf_op jit(solution)/shard_map/ppermute | solution.py:34
  66.4 2.0 %collective-permute-done.14.refs_5_ = bf16[80,512]{1,0:T(8,128)(2,1)S(1)} collective-permute-done((bf16[80,512]{1,0:T(8,128)(2,1)S(1)}, bf16[80,512]{1,0:T(8,128)(2,1)S(1)}, u32[]{:S(2)}, u32[]{:S(2)}) %collective-permute-start.14) | collective-permute-done | bytes 81952 | tf_op jit(solution)/shard_map/ppermute | solution.py:34
  69.2 1.6 collective-permute-done.11.refs_3_
  72.0 29.9 %all_to_all.16 = bf16[16,16,4096]{2,1,0:T(8,128)(2,1)S(1)} all-to-all(bf16[16,16,4096]{2,1,0:T(8,128)(2,1)S(1)} %bitcast.12), channel_id=1, replica_groups=mesh['z'=8,'xl'=2,'xh'=2,'y'=4,'c'=2] {'xl','xh','y'}, dimensions={0} | all-to-all | bytes 4194304 | tf_op jit(solution)/shard_map/all_to_all | solution.py:322
  101.9 3.8 %shard_map.87.mine = bf16[256,4096]{1,0:T(8,128)(2,1)S(1)} custom-call(bf16[256,4096]{1,0:T(8,128)(2,1)S(1)} %bitcast.11, bf16[1,4096,384]{2,1,0:T(8,128)(2,1)S(1)} %copy-done, bf16[1,4096,384]{2,1,0:T(8,128)(2,1)S(1)} %copy-done.1, bf16[1,384,4096]{2,1,0:T(8,128)(2,1)S(1)} %copy-done.2), custom_call_target="tpu_custom_call" | custom-call | flops 2415919104 | bytes 13631488 | tf_op jit(solution)/shard_map/pallas_call | solution.py:245
  106.0 2.2 %shard_map.89 = bf16[128,4096]{1,0:T(8,128)(2,1)S(1)} custom-call(bf16[256,4096]{1,0:T(8,128)(2,1)S(1)} %collective-permute-done.16.rows, bf16[1,4096,384]{2,1,0:T(8,128)(2,1)S(1)} %copy-done, bf16[1,4096,384]{2,1,0:T(8,128)(2,1)S(1)} %copy-done.1, bf16[1,384,4096]{2,1,0:T(8,128)(2,1)S(1)} %copy-done.2), custom_call_target="tpu_custom_call" | custom-call | flops 1207959552 | bytes 11534336 | tf_op jit(solution)/shard_map/pallas_call | solution.py:245
  108.2 2.2 %shard_map.88 = bf16[128,4096]{1,0:T(8,128)(2,1)S(1)} custom-call(bf16[256,4096]{1,0:T(8,128)(2,1)S(1)} %collective-permute-done.16.rows, bf16[1,4096,384]{2,1,0:T(8,128)(2,1)S(1)} %copy-done, bf16[1,4096,384]{2,1,0:T(8,128)(2,1)S(1)} %copy-done.1, bf16[1,384,4096]{2,1,0:T(8,128)(2,1)S(1)} %copy-done.2), custom_call_target="tpu_custom_call" | custom-call | flops 1207959552 | bytes 11534336 | tf_op jit(solution)/shard_map/pallas_call | solution.py:245
  111.0 2.1 %collective-permute-done.17.refs_0_ = bf16[128,4096]{1,0:T(8,128)(2,1)S(1)} collective-permute-done((bf16[128,4096]{1,0:T(8,128)(2,1)S(1)}, bf16[128,4096]{1,0:T(8,128)(2,1)S(1)}, u32[]{:S(2)}, u32[]{:S(2)}) %collective-permute-start.17) | collective-permute-done | bytes 1048608 | tf_op jit(solution)/shard_map/ppermute | solution.py:30
  113.2 1.5 collective-permute-done.18.refs_1_
  115.1 31.7 %all_to_all.17 = bf16[16,16,4096]{2,1,0:T(8,128)(2,1)S(1)} all-to-all(bf16[16,16,4096]{2,1,0:T(8,128)(2,1)S(1)} %bitcast.8), channel_id=1, replica_groups=mesh['z'=8,'xl'=2,'xh'=2,'y'=4,'c'=2] {'xl','xh','y'}, dimensions={0} | all-to-all | bytes 4194304 | tf_op jit(solution)/shard_map/all_to_all | solution.py:333
  148.0 4.1 %collective-permute-start.20 = (bf16[8,4096]{1,0:T(8,128)(2,1)S(1)}, bf16[8,4096]{1,0:T(8,128)(2,1)S(1)}, u32[]{:S(2)}, u32[]{:S(2)}) collective-permute-start(bf16[8,4096]{1,0:T(8,128)(2,1)S(1)} %get-tuple-element.41), channel_id=1, source_target_pairs={{64,0},{96,32},{128,64},{160,96},{192,128},{224,160},{0,192},{32,2... | collective-permute-start | bytes 196616 | tf_op jit(solution)/shard_map/ppermute | solution.py:34
  152.5 4.7 %collective-permute-start.22 = (bf16[8,4096]{1,0:T(8,128)(2,1)S(1)}, bf16[8,4096]{1,0:T(8,128)(2,1)S(1)}, u32[]{:S(2)}, u32[]{:S(2)}) collective-permute-start(bf16[8,4096]{1,0:T(8,128)(2,1)S(1)} %get-tuple-element.43), channel_id=1, source_target_pairs={{96,0},{128,32},{160,64},{192,96},{224,128},{0,160},{32,192},{64,2... | collective-permute-start | bytes 196616 | tf_op jit(solution)/shard_map/ppermute | solution.py:34
  157.2 3.4 %collective-permute-start.23 = (bf16[8,4096]{1,0:T(8,128)(2,1)S(1)}, bf16[8,4096]{1,0:T(8,128)(2,1)S(1)}, u32[]{:S(2)}, u32[]{:S(2)}) collective-permute-start(bf16[8,4096]{1,0:T(8,128)(2,1)S(1)} %get-tuple-element.44), channel_id=1, source_target_pairs={{128,0},{160,32},{192,64},{224,96},{0,128},{32,160},{64,192},{96,2... | collective-permute-start | bytes 196616 | tf_op jit(solution)/shard_map/ppermute | solution.py:34
  160.6 3.2 %collective-permute-start.25 = (bf16[8,4096]{1,0:T(8,128)(2,1)S(1)}, bf16[8,4096]{1,0:T(8,128)(2,1)S(1)}, u32[]{:S(2)}, u32[]{:S(2)}) collective-permute-start(bf16[8,4096]{1,0:T(8,128)(2,1)S(1)} %get-tuple-element.46), channel_id=1, source_target_pairs={{32,0},{64,32},{96,64},{128,96},{160,128},{192,160},{224,192},{0,2... | collective-permute-start | bytes 196616 | tf_op jit(solution)/shard_map/ppermute | solution.py:34
  163.8 2.0 %collective-permute-done.23 = bf16[8,4096]{1,0:T(8,128)(2,1)S(1)} collective-permute-done((bf16[8,4096]{1,0:T(8,128)(2,1)S(1)}, bf16[8,4096]{1,0:T(8,128)(2,1)S(1)}, u32[]{:S(2)}, u32[]{:S(2)}) %collective-permute-start.23) | collective-permute-done | bytes 65568 | tf_op jit(solution)/shard_map/ppermute | solution.py:34
  (78 shorter events, 24.9 us)
Async XLA Ops:
  0.0 18.2 %collective-permute-start = (bf16[512,256]{1,0:T(8,128)(2,1)}, bf16[512,256]{1,0:T(8,128)(2,1)S(1)}, u32[]{:S(2)}, u32[]{:S(2)}) collective-permute-start(bf16[512,256]{1,0:T(8,128)(2,1)} %own.1), channel_id=1, source_target_pairs={{0,16},{16,0},{1,17},{17,1},{2,18},{18,2},{3,19},{19,3},{4,20},{20... | collective-permute-start | bytes 786440 | tf_op jit(solution)/shard_map/ppermute | solution.py:30
  0.8 12.7 %collective-permute-start.2 = (bf16[128,512]{1,0:T(8,128)(2,1)}, bf16[128,512]{1,0:T(8,128)(2,1)S(1)}, u32[]{:S(2)}, u32[]{:S(2)}) collective-permute-start(bf16[128,512]{1,0:T(8,128)(2,1)} %context.1), channel_id=1, source_target_pairs={{64,0},{96,32},{128,64},{160,96},{192,128},{224,160},{0,192},{32,2... | collective-permute-start | bytes 393224 | tf_op jit(solution)/shard_map/ppermute | solution.py:34
  7.1 11.0 %collective-permute-start.5 = (bf16[128,512]{1,0:T(8,128)(2,1)}, bf16[128,512]{1,0:T(8,128)(2,1)S(1)}, u32[]{:S(2)}, u32[]{:S(2)}) collective-permute-start(bf16[128,512]{1,0:T(8,128)(2,1)} %context.1), channel_id=1, source_target_pairs={{192,0},{224,32},{0,64},{32,96},{64,128},{96,160},{128,192},{160,2... | collective-permute-start | bytes 393224 | tf_op jit(solution)/shard_map/ppermute | solution.py:34
  7.1 15.6 %collective-permute-start.1 = (bf16[128,512]{1,0:T(8,128)(2,1)}, bf16[128,512]{1,0:T(8,128)(2,1)S(1)}, u32[]{:S(2)}, u32[]{:S(2)}) collective-permute-start(bf16[128,512]{1,0:T(8,128)(2,1)} %context.1), channel_id=1, source_target_pairs={{32,0},{64,32},{96,64},{128,96},{160,128},{192,160},{224,192},{0,2... | collective-permute-start | bytes 393224 | tf_op jit(solution)/shard_map/ppermute | solution.py:34
  10.8 11.9 %collective-permute-start.7 = (bf16[128,512]{1,0:T(8,128)(2,1)}, bf16[128,512]{1,0:T(8,128)(2,1)S(1)}, u32[]{:S(2)}, u32[]{:S(2)}) collective-permute-start(bf16[128,512]{1,0:T(8,128)(2,1)} %context.1), channel_id=1, source_target_pairs={{224,0},{0,32},{32,64},{64,96},{96,128},{128,160},{160,192},{192,2... | collective-permute-start | bytes 393224 | tf_op jit(solution)/shard_map/ppermute | solution.py:34
  13.5 9.9 %collective-permute-start.4 = (bf16[128,512]{1,0:T(8,128)(2,1)S(1)}, bf16[128,512]{1,0:T(8,128)(2,1)S(1)}, u32[]{:S(2)}, u32[]{:S(2)}) collective-permute-start(bf16[128,512]{1,0:T(8,128)(2,1)S(1)} %collective-permute-done.2.refs_2_), channel_id=1, source_target_pairs={{64,0},{96,32},{128,64},{160,96},{192,128},{224,160},{0,192},{32,2... | collective-permute-start | bytes 393224 | tf_op jit(solution)/shard_map/ppermute | solution.py:34
  18.2 6.6 %collective-permute-start.3 = (bf16[128,512]{1,0:T(8,128)(2,1)S(1)}, bf16[128,512]{1,0:T(8,128)(2,1)S(1)}, u32[]{:S(2)}, u32[]{:S(2)}) collective-permute-start(bf16[128,512]{1,0:T(8,128)(2,1)S(1)} %collective-permute-done.2.refs_2_), channel_id=1, source_target_pairs={{32,0},{64,32},{96,64},{128,96},{160,128},{192,160},{224,192},{0,2... | collective-permute-start | bytes 393224 | tf_op jit(solution)/shard_map/ppermute | solution.py:34
  18.2 7.3 %collective-permute-start.6 = (bf16[128,512]{1,0:T(8,128)(2,1)S(1)}, bf16[128,512]{1,0:T(8,128)(2,1)S(1)}, u32[]{:S(2)}, u32[]{:S(2)}) collective-permute-start(bf16[128,512]{1,0:T(8,128)(2,1)S(1)} %collective-permute-done.5.refs_6_), channel_id=1, source_target_pairs={{224,0},{0,32},{32,64},{64,96},{96,128},{128,160},{160,192},{192,2... | collective-permute-start | bytes 393224 | tf_op jit(solution)/shard_map/ppermute | solution.py:34
  53.9 8.8 %collective-permute-start.13 = (bf16[80,512]{1,0:T(8,128)(2,1)S(1)}, bf16[80,512]{1,0:T(8,128)(2,1)S(1)}, u32[]{:S(2)}, u32[]{:S(2)}) collective-permute-start(bf16[80,512]{1,0:T(8,128)(2,1)S(1)} %shard_map.85.refs_0_), channel_id=1, source_target_pairs={{192,0},{224,32},{0,64},{32,96},{64,128},{96,160},{128,192},{160,2... | collective-permute-start | bytes 245768 | tf_op jit(solution)/shard_map/ppermute | solution.py:34
  55.1 7.6 %collective-permute-start.10 = (bf16[80,512]{1,0:T(8,128)(2,1)S(1)}, bf16[80,512]{1,0:T(8,128)(2,1)S(1)}, u32[]{:S(2)}, u32[]{:S(2)}) collective-permute-start(bf16[80,512]{1,0:T(8,128)(2,1)S(1)} %shard_map.85.refs_0_), channel_id=1, source_target_pairs={{64,0},{96,32},{128,64},{160,96},{192,128},{224,160},{0,192},{32,2... | collective-permute-start | bytes 245768 | tf_op jit(solution)/shard_map/ppermute | solution.py:34
  58.1 8.2 %collective-permute-start.15 = (bf16[80,512]{1,0:T(8,128)(2,1)S(1)}, bf16[80,512]{1,0:T(8,128)(2,1)S(1)}, u32[]{:S(2)}, u32[]{:S(2)}) collective-permute-start(bf16[80,512]{1,0:T(8,128)(2,1)S(1)} %shard_map.85.refs_0_), channel_id=1, source_target_pairs={{224,0},{0,32},{32,64},{64,96},{96,128},{128,160},{160,192},{192,2... | collective-permute-start | bytes 245768 | tf_op jit(solution)/shard_map/ppermute | solution.py:34
  58.3 8.1 %collective-permute-start.9 = (bf16[80,512]{1,0:T(8,128)(2,1)S(1)}, bf16[80,512]{1,0:T(8,128)(2,1)S(1)}, u32[]{:S(2)}, u32[]{:S(2)}) collective-permute-start(bf16[80,512]{1,0:T(8,128)(2,1)S(1)} %shard_map.85.refs_0_), channel_id=1, source_target_pairs={{32,0},{64,32},{96,64},{128,96},{160,128},{192,160},{224,192},{0,2... | collective-permute-start | bytes 245768 | tf_op jit(solution)/shard_map/ppermute | solution.py:34
  62.7 5.7 %collective-permute-start.14 = (bf16[80,512]{1,0:T(8,128)(2,1)S(1)}, bf16[80,512]{1,0:T(8,128)(2,1)S(1)}, u32[]{:S(2)}, u32[]{:S(2)}) collective-permute-start(bf16[80,512]{1,0:T(8,128)(2,1)S(1)} %collective-permute-done.13.refs_6_), channel_id=1, source_target_pairs={{224,0},{0,32},{32,64},{64,96},{96,128},{128,160},{160,192},{192,2... | collective-permute-start | bytes 245768 | tf_op jit(solution)/shard_map/ppermute | solution.py:34
  62.7 6.5 %collective-permute-start.12 = (bf16[80,512]{1,0:T(8,128)(2,1)S(1)}, bf16[80,512]{1,0:T(8,128)(2,1)S(1)}, u32[]{:S(2)}, u32[]{:S(2)}) collective-permute-start(bf16[80,512]{1,0:T(8,128)(2,1)S(1)} %collective-permute-done.10.refs_2_), channel_id=1, source_target_pairs={{64,0},{96,32},{128,64},{160,96},{192,128},{224,160},{0,192},{32,2... | collective-permute-start | bytes 245768 | tf_op jit(solution)/shard_map/ppermute | solution.py:34
  66.3 4.4 %collective-permute-start.11 = (bf16[80,512]{1,0:T(8,128)(2,1)S(1)}, bf16[80,512]{1,0:T(8,128)(2,1)S(1)}, u32[]{:S(2)}, u32[]{:S(2)}) collective-permute-start(bf16[80,512]{1,0:T(8,128)(2,1)S(1)} %collective-permute-done.10.refs_2_), channel_id=1, source_target_pairs={{32,0},{64,32},{96,64},{128,96},{160,128},{192,160},{224,192},{0,2... | collective-permute-start | bytes 245768 | tf_op jit(solution)/shard_map/ppermute | solution.py:34
  101.8 4.2 %collective-permute-start.16 = (bf16[256,4096]{1,0:T(8,128)(2,1)S(1)}, bf16[256,4096]{1,0:T(8,128)(2,1)S(1)}, u32[]{:S(2)}, u32[]{:S(2)}) collective-permute-start(bf16[256,4096]{1,0:T(8,128)(2,1)S(1)} %bitcast.10), channel_id=1, source_target_pairs={{0,1},{1,0},{2,3},{3,2},{4,5},{5,4},{6,7},{7,6},{8,9},{9,8},{10,11... | collective-permute-start | bytes 6291464 | tf_op jit(solution)/shard_map/ppermute | solution.py:30
  110.7 3.9 %collective-permute-start.18 = (bf16[128,4096]{1,0:T(8,128)(2,1)S(1)}, bf16[128,4096]{1,0:T(8,128)(2,1)S(1)}, u32[]{:S(2)}, u32[]{:S(2)}) collective-permute-start(bf16[128,4096]{1,0:T(8,128)(2,1)S(1)} %shard_map.89), channel_id=1, source_target_pairs={{0,1},{1,0},{2,3},{3,2},{4,5},{5,4},{6,7},{7,6},{8,9},{9,8},{10,11... | collective-permute-start | bytes 3145736 | tf_op jit(solution)/shard_map/ppermute | solution.py:30
  147.7 12.9 %collective-permute-start.19 = (bf16[8,4096]{1,0:T(8,128)(2,1)S(1)}, bf16[8,4096]{1,0:T(8,128)(2,1)S(1)}, u32[]{:S(2)}, u32[]{:S(2)}) collective-permute-start(bf16[8,4096]{1,0:T(8,128)(2,1)S(1)} %get-tuple-element.40), channel_id=1, source_target_pairs={{192,0},{224,32},{0,64},{32,96},{64,128},{96,160},{128,192},{160,2... | collective-permute-start | bytes 196616 | tf_op jit(solution)/shard_map/ppermute | solution.py:34
  148.0 12.6 %collective-permute-start.20 = (bf16[8,4096]{1,0:T(8,128)(2,1)S(1)}, bf16[8,4096]{1,0:T(8,128)(2,1)S(1)}, u32[]{:S(2)}, u32[]{:S(2)}) collective-permute-start(bf16[8,4096]{1,0:T(8,128)(2,1)S(1)} %get-tuple-element.41), channel_id=1, source_target_pairs={{64,0},{96,32},{128,64},{160,96},{192,128},{224,160},{0,192},{32,2... | collective-permute-start | bytes 196616 | tf_op jit(solution)/shard_map/ppermute | solution.py:34
  152.1 11.7 %collective-permute-start.21 = (bf16[8,4096]{1,0:T(8,128)(2,1)S(1)}, bf16[8,4096]{1,0:T(8,128)(2,1)S(1)}, u32[]{:S(2)}, u32[]{:S(2)}) collective-permute-start(bf16[8,4096]{1,0:T(8,128)(2,1)S(1)} %get-tuple-element.42), channel_id=1, source_target_pairs={{160,0},{192,32},{224,64},{0,96},{32,128},{64,160},{96,192},{128,2... | collective-permute-start | bytes 196616 | tf_op jit(solution)/shard_map/ppermute | solution.py:34
  152.5 11.3 %collective-permute-start.22 = (bf16[8,4096]{1,0:T(8,128)(2,1)S(1)}, bf16[8,4096]{1,0:T(8,128)(2,1)S(1)}, u32[]{:S(2)}, u32[]{:S(2)}) collective-permute-start(bf16[8,4096]{1,0:T(8,128)(2,1)S(1)} %get-tuple-element.43), channel_id=1, source_target_pairs={{96,0},{128,32},{160,64},{192,96},{224,128},{0,160},{32,192},{64,2... | collective-permute-start | bytes 196616 | tf_op jit(solution)/shard_map/ppermute | solution.py:34
  157.2 8.7 %collective-permute-start.23 = (bf16[8,4096]{1,0:T(8,128)(2,1)S(1)}, bf16[8,4096]{1,0:T(8,128)(2,1)S(1)}, u32[]{:S(2)}, u32[]{:S(2)}) collective-permute-start(bf16[8,4096]{1,0:T(8,128)(2,1)S(1)} %get-tuple-element.44), channel_id=1, source_target_pairs={{128,0},{160,32},{192,64},{224,96},{0,128},{32,160},{64,192},{96,2... | collective-permute-start | bytes 196616 | tf_op jit(solution)/shard_map/ppermute | solution.py:34
  160.6 5.8 %collective-permute-start.24 = (bf16[8,4096]{1,0:T(8,128)(2,1)S(1)}, bf16[8,4096]{1,0:T(8,128)(2,1)S(1)}, u32[]{:S(2)}, u32[]{:S(2)}) collective-permute-start(bf16[8,4096]{1,0:T(8,128)(2,1)S(1)} %get-tuple-element.45), channel_id=1, source_target_pairs={{224,0},{0,32},{32,64},{64,96},{96,128},{128,160},{160,192},{192,2... | collective-permute-start | bytes 196616 | tf_op jit(solution)/shard_map/ppermute | solution.py:34
  160.6 5.8 %collective-permute-start.25 = (bf16[8,4096]{1,0:T(8,128)(2,1)S(1)}, bf16[8,4096]{1,0:T(8,128)(2,1)S(1)}, u32[]{:S(2)}, u32[]{:S(2)}) collective-permute-start(bf16[8,4096]{1,0:T(8,128)(2,1)S(1)} %get-tuple-element.46), channel_id=1, source_target_pairs={{32,0},{64,32},{96,64},{128,96},{160,128},{192,160},{224,192},{0,2... | collective-permute-start | bytes 196616 | tf_op jit(solution)/shard_map/ppermute | solution.py:34
  (18 other events, 230.4 us)

commit v7 on v6

--- a/solution.py
+++ b/solution.py
@@ -50,8 +50,12 @@
     return jnp.dot(a, b, preferred_element_type=F32)
 
 
+def where(place):
+    return lax.div(place[0], 4), lax.rem(lax.div(place[0], 2), 2), lax.rem(place[0], 2)
+
+
 def stage_kernel(place, own, other, context, rhs, held):
-    xl = place[0]
+    _, xl, _ = where(place)
     cols = own.shape[1]
     rhs[:, pl.ds(pl.multiple_of(xl * cols, LANES), cols)] = own[...]
     rhs[:, pl.ds(pl.multiple_of((1 - xl) * cols, LANES), cols)] = other[...]
@@ -73,7 +77,7 @@
 
 def project_kernel(place, *refs):
     blocks, (rhs, give, keep, held) = refs[:NZ], refs[NZ:]
-    core = place[1]
+    _, _, core = where(place)
     lhs = jnp.concatenate([b[...] for b in blocks], axis=0)
     total = dot(lhs, rhs[...])
     spread = give.shape[0]
@@ -114,45 +118,52 @@
     )(keep, got)
 
 
-def settle_kernel(place, parts, note, out, held):
-    z = place[0]
+def settle_kernel(place, parts, ids, gates, out, held):
+    z, _, _ = where(place)
     tokens = parts.shape[1]
     rows = tokens // NZ
     total = parts[0].astype(F32)
     for i in range(1, parts.shape[0]):
         total += parts[i].astype(F32)
-    held[tokens:, :] = jnp.zeros((held.shape[0] - tokens, held.shape[1]), F32)
-    held[tokens : tokens + rows, :LANES] = note[...]
     for k in range(NZ):
         at = pl.multiple_of(lax.rem(z + k, NZ) * rows, rows)
         held[pl.ds(at, rows), :] = total[k * rows : (k + 1) * rows]
+    named = ids[...].astype(F32)
+    high = gates[...].astype(BF16).astype(F32)
+    low = gates[...] - high
+    lane = lax.broadcasted_iota(jnp.int32, (rows, held.shape[1]), 1)
+    note = jnp.zeros((rows, held.shape[1]), F32)
+    for i, part in enumerate((named, high, low)):
+        for k in range(TOPK):
+            note = jnp.where(lane == i * TOPK + k, part[:, k : k + 1], note)
+    held[tokens:, :] = note
     out[...] = held[...].astype(BF16)
 
 
-def settle(place, parts, note):
-    shape = (parts.shape[1] + 16, parts.shape[2])
+def settle(place, parts, ids, gates):
+    shape = (parts.shape[1] + ids.shape[0], parts.shape[2])
     return pl.pallas_call(
         settle_kernel,
         out_shape=jax.ShapeDtypeStruct(shape, BF16),
-        in_specs=[SMEM, VMEM, VMEM],
+        in_specs=[SMEM, VMEM, VMEM, VMEM],
         out_specs=VMEM,
         scratch_shapes=[pltpu.VMEM(shape, F32)],
         compiler_params=params(16),
-    )(place, parts, note)
+    )(place, parts, ids, gates)
 
 
 def place_kernel(place, *refs):
     blocks, (gain, sent, own, high, low, stream, notes, mass) = refs[:NZ], refs[NZ:]
-    z = place[0]
+    z, _, _ = where(place)
     tokens, width = stream.shape
     rows, wide = tokens // NZ, width // NZ
     lanes = sent.shape[0]
     for hop in range(NZ):
         there = lax.rem(z + hop, NZ)
         at = pl.multiple_of(there * wide, LANES)
-        stream[:, pl.ds(at, wide)] = blocks[hop][:tokens, :].astype(F32)
-        note = blocks[hop][tokens:, :LANES].astype(F32)
-        notes[pl.ds(pl.multiple_of(there * rows, rows), rows), :] = note[:rows]
+        block = blocks[hop][...].astype(F32)
+        stream[:, pl.ds(at, wide)] = block[:tokens]
+        notes[pl.ds(pl.multiple_of(there * rows, rows), rows), :] = block[tokens:, :LANES]
     own[...] = stream[pl.ds(pl.multiple_of(z * rows, rows), rows), :]
 
     slots = NZ * CAP
@@ -200,9 +211,9 @@
 
 
 def place_rows(place, blocks, gain, plane):
-    tokens = blocks[0].shape[0] - 16
+    rows = blocks[0].shape[0] // (NZ + 1)
+    tokens = NZ * rows
     width = NZ * blocks[0].shape[1]
-    rows = tokens // NZ
     lanes = plane * NZ * CAP
     return pl.pallas_call(
         place_kernel,
@@ -257,22 +268,24 @@
     )(rows, w_gate, w_up, w_down)
 
 
-def add_kernel(mine, *refs):
-    parts, out = refs[:-1], refs[-1]
-    count = parts[0].shape[0]
-    for i, part in enumerate(parts):
-        at = slice(i * count, (i + 1) * count)
-        out[at, :] = (mine[at, :].astype(F32) + part[...].astype(F32)).astype(BF16)
-
-
-def add_rows(mine, parts):
-    return pl.pallas_call(
-        add_kernel,
-        out_shape=jax.ShapeDtypeStruct(mine.shape, BF16),
-        in_specs=[VMEM] * (1 + len(parts)),
+def add_kernel(first, mine, part, *refs):
+    out = refs[-1]
+    count = part.shape[0]
+    if len(refs) > 1:
+        out[:first, :] = refs[0][...]
+    total = mine[first : first + count, :].astype(F32) + part[...].astype(F32)
+    out[first:, :] = total.astype(BF16)
+
+
+def add_rows(mine, part, *before):
+    first = before[0].shape[0] if before else 0
+    return pl.pallas_call(
+        functools.partial(add_kernel, first),
+        out_shape=jax.ShapeDtypeStruct((first + part.shape[0], mine.shape[1]), BF16),
+        in_specs=[VMEM] * (2 + len(before)),
         out_specs=VMEM,
         compiler_params=params(32),
-    )(mine, *parts)
+    )(mine, part, *before)
 
 
 def combine_kernel(high, low, back, own, base, *outs):
@@ -301,22 +314,16 @@
 
 def on_device(context, proj_weight, norm_gain, expert_ids, gate_values, w_gate, w_up, w_down):
     zi, xli, ci = (lax.axis_index(a).astype(jnp.int32) for a in ("z", "xl", "c"))
+    place = (4 * zi + 2 * xli + ci).reshape(1)
     n_spread = lax.axis_size(SPREAD)
     n_plane = lax.axis_size(PLANE)
 
-    high = lax.reduce_precision(gate_values, exponent_bits=8, mantissa_bits=7)
-    note = jnp.concatenate([expert_ids.astype(F32), high, gate_values - high], axis=1)
-    note = jnp.pad(note, ((0, 0), (0, LANES - 3 * TOPK)))
-
-    place = zi.reshape(1)
-    spot = jnp.stack([xli, ci])
-    rhs, held = stage(spot, proj_weight, swap(proj_weight, "xl"), context)
-    give, keep = project(spot, [held] + gather_z(context)[1:], rhs, n_spread)
+    rhs, held = stage(place, proj_weight, swap(proj_weight, "xl"), context)
+    give, keep = project(place, [held] + gather_z(context)[1:], rhs, n_spread)
     partial = join(keep, swap(give, "c"))
-    partial, note, place = lax.optimization_barrier((partial, note, place))
     partial = lax.all_to_all(partial, SPREAD, 0, 0, tiled=True)
 
-    part = settle(place, partial, note)
+    part = settle(place, partial, expert_ids, gate_values)
     sent, own, high, low = place_rows(place, gather_z(part), norm_gain, n_plane)
     width = sent.shape[1]
     mine = lax.all_to_all(sent.reshape(n_plane, -1, width), PLANE, 0, 0, tiled=True)
@@ -328,8 +335,8 @@
     mine_out = expert_rows(mine, 0, count, *weights)
     theirs, mine_out = lax.optimization_barrier((theirs, mine_out))
     half = count // 2
-    parts = [swap(expert_rows(theirs, at, half, *weights), "c") for at in (0, half)]
-    summed = add_rows(mine_out, parts).reshape(n_plane, -1, width)
+    top, bottom = (swap(expert_rows(theirs, at, half, *weights), "c") for at in (0, half))
+    summed = add_rows(mine_out, bottom, add_rows(mine_out, top)).reshape(n_plane, -1, width)
     back = lax.all_to_all(summed, PLANE, 0, 0, tiled=True).reshape(-1, width)
 
     total, *blocks = combine(high, low, back, own)

time: 168 us -> 155 us (0.923)
  local copies, waits for them, and re-layouts: 10.3 us -> 1.88 us
  Pallas kernels: 14.6 us -> 11.8 us
    unnamed x32 -> x16, local copies, waits for them, and re-layouts: 10.3 us -> 1.88 us
  transfers between devices with their start and end apart: 26 -> 26, of which waited for: 12 -> 12; matrix products, arithmetic and copies ran while one was open for 1% -> 0% of each run, Pallas kernels for 3% -> 4%
where the time goes in v7:
time: 155 us
  blocking collectives  77.6 us (50%)
  starting transfers between devices  45.6 us (29%)
  waiting for transfers between devices  17.1 us (11%)
  Pallas kernels  11.8 us (8%)
  local copies, waits for them, and re-layouts  1.88 us (1%)
    ppermute x21, starting transfers between devices, fetch(): return lax.ppermute(x, 'z', [((i + hop) % NZ, i) for i in range(NZ)])  44 us
    all_to_all x1, blocking collectives, on_device(): back = lax.all_to_all(summed, PLANE, 0, 0, tiled=True).reshape(-1, width)  31.7 us
    all_to_all x1, blocking collectives, on_device(): lax.all_to_all(sent.reshape(n_plane, -1, width), PLANE, 0, 0, tiled=True)  29.4 us
    all_to_all x1, blocking collectives, on_device(): partial = lax.all_to_all(partial, SPREAD, 0, 0, tiled=True)  16.4 us
    ppermute x21, waiting for transfers between devices, fetch(): return lax.ppermute(x, 'z', [((i + hop) % NZ, i) for i in range(NZ)])  12.8 us
    pallas_call x3, Pallas kernels, expert_rows(): pl.pallas_call(functools.partial(expert_kernel, first), out_shape=jax.Sha...  8.25 us
    ppermute x5, waiting for transfers between devices, swap(): return lax.ppermute(x, axis, [(0, 1), (1, 0)])  4.32 us
  transfers between devices with their start and end apart: 26, of which 12 were waited for; matrix products, arithmetic and copies ran while one was open for 0% of the time, Pallas kernels for 4%

profile of v7, /device:TPU:6, one launch (start us, length us, event | category | flops | bytes accessed | tf_op | source)
XLA Modules:
  0.0 154.8 jit_solution(3228883923521124587)
XLA Ops:
  0.8 6.3 %collective-permute-start.2 = (bf16[128,512]{1,0:T(8,128)(2,1)}, bf16[128,512]{1,0:T(8,128)(2,1)S(1)}, u32[]{:S(2)}, u32[]{:S(2)}) collective-permute-start(bf16[128,512]{1,0:T(8,128)(2,1)} %context.1), channel_id=1, source_target_pairs={{64,0},{96,32},{128,64},{160,96},{192,128},{224,160},{0,192},{32,2... | collective-permute-start | bytes 393224 | tf_op jit(solution)/shard_map/ppermute | solution.py:34
  7.1 3.7 %collective-permute-start.1 = (bf16[128,512]{1,0:T(8,128)(2,1)}, bf16[128,512]{1,0:T(8,128)(2,1)S(1)}, u32[]{:S(2)}, u32[]{:S(2)}) collective-permute-start(bf16[128,512]{1,0:T(8,128)(2,1)} %context.1), channel_id=1, source_target_pairs={{32,0},{64,32},{96,64},{128,96},{160,128},{192,160},{224,192},{0,2... | collective-permute-start | bytes 393224 | tf_op jit(solution)/shard_map/ppermute | solution.py:34
  10.8 2.7 %collective-permute-done.2.refs_2_ = bf16[128,512]{1,0:T(8,128)(2,1)S(1)} collective-permute-done((bf16[128,512]{1,0:T(8,128)(2,1)}, bf16[128,512]{1,0:T(8,128)(2,1)S(1)}, u32[]{:S(2)}, u32[]{:S(2)}) %collective-permute-start.2) | collective-permute-done | bytes 131104 | tf_op jit(solution)/shard_map/ppermute | solution.py:34
  13.5 4.6 %collective-permute-start.4 = (bf16[128,512]{1,0:T(8,128)(2,1)S(1)}, bf16[128,512]{1,0:T(8,128)(2,1)S(1)}, u32[]{:S(2)}, u32[]{:S(2)}) collective-permute-start(bf16[128,512]{1,0:T(8,128)(2,1)S(1)} %collective-permute-done.2.refs_2_), channel_id=1, source_target_pairs={{64,0},{96,32},{128,64},{160,96},{192,128},{224,160},{0,192},{32,2... | collective-permute-start | bytes 393224 | tf_op jit(solution)/shard_map/ppermute | solution.py:34
  18.2 2.0 %collective-permute-start.6 = (bf16[128,512]{1,0:T(8,128)(2,1)S(1)}, bf16[128,512]{1,0:T(8,128)(2,1)S(1)}, u32[]{:S(2)}, u32[]{:S(2)}) collective-permute-start(bf16[128,512]{1,0:T(8,128)(2,1)S(1)} %collective-permute-done.5.refs_6_), channel_id=1, source_target_pairs={{224,0},{0,32},{32,64},{64,96},{96,128},{128,160},{160,192},{192,2... | collective-permute-start | bytes 393224 | tf_op jit(solution)/shard_map/ppermute | solution.py:34
  22.5 2.3 %collective-permute-done.3.refs_3_ = bf16[128,512]{1,0:T(8,128)(2,1)S(1)} collective-permute-done((bf16[128,512]{1,0:T(8,128)(2,1)S(1)}, bf16[128,512]{1,0:T(8,128)(2,1)S(1)}, u32[]{:S(2)}, u32[]{:S(2)}) %collective-permute-start.3) | collective-permute-done | bytes 131104 | tf_op jit(solution)/shard_map/ppermute | solution.py:34
  25.6 1.9 %collective-permute-done.8.got = bf16[8,64,512]{2,1,0:T(8,128)(2,1)S(1)} collective-permute-done((bf16[8,64,512]{2,1,0:T(8,128)(2,1)S(1)}, bf16[8,64,512]{2,1,0:T(8,128)(2,1)S(1)}, u32[]{:S(2)}, u32[]{:S(2)}) %collective-permute-start.8) | collective-permute-done | bytes 524320 | tf_op jit(solution)/shard_map/ppermute | solution.py:30
  27.7 16.4 %all_to_all.15.parts = bf16[8,64,512]{2,1,0:T(8,128)(2,1)S(1)} all-to-all(bf16[8,64,512]{2,1,0:T(8,128)(2,1)S(1)} %shard_map.84), channel_id=1, replica_groups=mesh['z'=8,'xl'=2,'xh'=2,'y'=4,'c'=2] {'xh','y'}, dimensions={0} | all-to-all | bytes 1048576 | tf_op jit(solution)/shard_map/all_to_all | solution.py:324
  44.8 3.7 %collective-permute-start.10 = (bf16[72,512]{1,0:T(8,128)(2,1)S(1)}, bf16[72,512]{1,0:T(8,128)(2,1)S(1)}, u32[]{:S(2)}, u32[]{:S(2)}) collective-permute-start(bf16[72,512]{1,0:T(8,128)(2,1)S(1)} %shard_map.85.refs_0_), channel_id=1, source_target_pairs={{64,0},{96,32},{128,64},{160,96},{192,128},{224,160},{0,192},{32,2... | collective-permute-start | bytes 221192 | tf_op jit(solution)/shard_map/ppermute | solution.py:34
  48.8 2.9 %collective-permute-start.9 = (bf16[72,512]{1,0:T(8,128)(2,1)S(1)}, bf16[72,512]{1,0:T(8,128)(2,1)S(1)}, u32[]{:S(2)}, u32[]{:S(2)}) collective-permute-start(bf16[72,512]{1,0:T(8,128)(2,1)S(1)} %shard_map.85.refs_0_), channel_id=1, source_target_pairs={{32,0},{64,32},{96,64},{128,96},{160,128},{192,160},{224,192},{0,2... | collective-permute-start | bytes 221192 | tf_op jit(solution)/shard_map/ppermute | solution.py:34
  51.8 4.5 %collective-permute-start.12 = (bf16[72,512]{1,0:T(8,128)(2,1)S(1)}, bf16[72,512]{1,0:T(8,128)(2,1)S(1)}, u32[]{:S(2)}, u32[]{:S(2)}) collective-permute-start(bf16[72,512]{1,0:T(8,128)(2,1)S(1)} %collective-permute-done.10.refs_2_), channel_id=1, source_target_pairs={{64,0},{96,32},{128,64},{160,96},{192,128},{224,160},{0,192},{32,2... | collective-permute-start | bytes 221192 | tf_op jit(solution)/shard_map/ppermute | solution.py:34
  57.4 1.3 collective-permute-done.12.refs_4_
  58.7 2.0 %collective-permute-done.11.refs_3_ = bf16[72,512]{1,0:T(8,128)(2,1)S(1)} collective-permute-done((bf16[72,512]{1,0:T(8,128)(2,1)S(1)}, bf16[72,512]{1,0:T(8,128)(2,1)S(1)}, u32[]{:S(2)}, u32[]{:S(2)}) %collective-permute-start.11) | collective-permute-done | bytes 73760 | tf_op jit(solution)/shard_map/ppermute | solution.py:34
  61.8 29.4 %all_to_all.16 = bf16[16,16,4096]{2,1,0:T(8,128)(2,1)S(1)} all-to-all(bf16[16,16,4096]{2,1,0:T(8,128)(2,1)S(1)} %bitcast.10), channel_id=1, replica_groups=mesh['z'=8,'xl'=2,'xh'=2,'y'=4,'c'=2] {'xl','xh','y'}, dimensions={0} | all-to-all | bytes 4194304 | tf_op jit(solution)/shard_map/all_to_all | solution.py:329
  91.3 3.8 %shard_map.87.mine = bf16[256,4096]{1,0:T(8,128)(2,1)S(1)} custom-call(bf16[256,4096]{1,0:T(8,128)(2,1)S(1)} %bitcast.9, bf16[1,4096,384]{2,1,0:T(8,128)(2,1)S(1)} %copy-done, bf16[1,4096,384]{2,1,0:T(8,128)(2,1)S(1)} %copy-done.1, bf16[1,384,4096]{2,1,0:T(8,128)(2,1)S(1)} %copy-done.2), custom_call_target="tpu_custom_call" | custom-call | flops 2415919104 | bytes 13631488 | tf_op jit(solution)/shard_map/pallas_call | solution.py:256
  95.4 2.2 %shard_map.89 = bf16[128,4096]{1,0:T(8,128)(2,1)S(1)} custom-call(bf16[256,4096]{1,0:T(8,128)(2,1)S(1)} %collective-permute-done.16.rows, bf16[1,4096,384]{2,1,0:T(8,128)(2,1)S(1)} %copy-done, bf16[1,4096,384]{2,1,0:T(8,128)(2,1)S(1)} %copy-done.1, bf16[1,384,4096]{2,1,0:T(8,128)(2,1)S(1)} %copy-done.2), custom_call_target="tpu_custom_call" | custom-call | flops 1207959552 | bytes 11534336 | tf_op jit(solution)/shard_map/pallas_call | solution.py:256
  97.9 2.2 %shard_map.88 = bf16[128,4096]{1,0:T(8,128)(2,1)S(1)} custom-call(bf16[256,4096]{1,0:T(8,128)(2,1)S(1)} %collective-permute-done.16.rows, bf16[1,4096,384]{2,1,0:T(8,128)(2,1)S(1)} %copy-done, bf16[1,4096,384]{2,1,0:T(8,128)(2,1)S(1)} %copy-done.1, bf16[1,384,4096]{2,1,0:T(8,128)(2,1)S(1)} %copy-done.2), custom_call_target="tpu_custom_call" | custom-call | flops 1207959552 | bytes 11534336 | tf_op jit(solution)/shard_map/pallas_call | solution.py:256
  100.8 2.1 %collective-permute-done.17.part = bf16[128,4096]{1,0:T(8,128)(2,1)S(1)} collective-permute-done((bf16[128,4096]{1,0:T(8,128)(2,1)S(1)}, bf16[128,4096]{1,0:T(8,128)(2,1)S(1)}, u32[]{:S(2)}, u32[]{:S(2)}) %collective-permute-start.17) | collective-permute-done | bytes 1048608 | tf_op jit(solution)/shard_map/ppermute | solution.py:30
  103.2 31.7 %all_to_all.17 = bf16[16,16,4096]{2,1,0:T(8,128)(2,1)S(1)} all-to-all(bf16[16,16,4096]{2,1,0:T(8,128)(2,1)S(1)} %bitcast.6), channel_id=1, replica_groups=mesh['z'=8,'xl'=2,'xh'=2,'y'=4,'c'=2] {'xl','xh','y'}, dimensions={0} | all-to-all | bytes 4194304 | tf_op jit(solution)/shard_map/all_to_all | solution.py:340
  136.2 4.1 %collective-permute-start.20 = (bf16[8,4096]{1,0:T(8,128)(2,1)S(1)}, bf16[8,4096]{1,0:T(8,128)(2,1)S(1)}, u32[]{:S(2)}, u32[]{:S(2)}) collective-permute-start(bf16[8,4096]{1,0:T(8,128)(2,1)S(1)} %get-tuple-element.35), channel_id=1, source_target_pairs={{64,0},{96,32},{128,64},{160,96},{192,128},{224,160},{0,192},{32,2... | collective-permute-start | bytes 196616 | tf_op jit(solution)/shard_map/ppermute | solution.py:34
  140.7 4.6 %collective-permute-start.22 = (bf16[8,4096]{1,0:T(8,128)(2,1)S(1)}, bf16[8,4096]{1,0:T(8,128)(2,1)S(1)}, u32[]{:S(2)}, u32[]{:S(2)}) collective-permute-start(bf16[8,4096]{1,0:T(8,128)(2,1)S(1)} %get-tuple-element.37), channel_id=1, source_target_pairs={{96,0},{128,32},{160,64},{192,96},{224,128},{0,160},{32,192},{64,2... | collective-permute-start | bytes 196616 | tf_op jit(solution)/shard_map/ppermute | solution.py:34
  145.3 2.7 %collective-permute-start.23 = (bf16[8,4096]{1,0:T(8,128)(2,1)S(1)}, bf16[8,4096]{1,0:T(8,128)(2,1)S(1)}, u32[]{:S(2)}, u32[]{:S(2)}) collective-permute-start(bf16[8,4096]{1,0:T(8,128)(2,1)S(1)} %get-tuple-element.38), channel_id=1, source_target_pairs={{128,0},{160,32},{192,64},{224,96},{0,128},{32,160},{64,192},{96,2... | collective-permute-start | bytes 196616 | tf_op jit(solution)/shard_map/ppermute | solution.py:34
  148.5 2.7 %collective-permute-start.25 = (bf16[8,4096]{1,0:T(8,128)(2,1)S(1)}, bf16[8,4096]{1,0:T(8,128)(2,1)S(1)}, u32[]{:S(2)}, u32[]{:S(2)}) collective-permute-start(bf16[8,4096]{1,0:T(8,128)(2,1)S(1)} %get-tuple-element.40), channel_id=1, source_target_pairs={{32,0},{64,32},{96,64},{128,96},{160,128},{192,160},{224,192},{0,2... | collective-permute-start | bytes 196616 | tf_op jit(solution)/shard_map/ppermute | solution.py:34
  151.2 2.3 %collective-permute-done.23 = bf16[8,4096]{1,0:T(8,128)(2,1)S(1)} collective-permute-done((bf16[8,4096]{1,0:T(8,128)(2,1)S(1)}, bf16[8,4096]{1,0:T(8,128)(2,1)S(1)}, u32[]{:S(2)}, u32[]{:S(2)}) %collective-permute-start.23) | collective-permute-done | bytes 65568 | tf_op jit(solution)/shard_map/ppermute | solution.py:34
  (59 shorter events, 12.5 us)
Async XLA Ops:
  0.0 18.2 %collective-permute-start = (bf16[512,256]{1,0:T(8,128)(2,1)}, bf16[512,256]{1,0:T(8,128)(2,1)S(1)}, u32[]{:S(2)}, u32[]{:S(2)}) collective-permute-start(bf16[512,256]{1,0:T(8,128)(2,1)} %own.1), channel_id=1, source_target_pairs={{0,16},{16,0},{1,17},{17,1},{2,18},{18,2},{3,19},{19,3},{4,20},{20... | collective-permute-start | bytes 786440 | tf_op jit(solution)/shard_map/ppermute | solution.py:30
  0.8 12.7 %collective-permute-start.2 = (bf16[128,512]{1,0:T(8,128)(2,1)}, bf16[128,512]{1,0:T(8,128)(2,1)S(1)}, u32[]{:S(2)}, u32[]{:S(2)}) collective-permute-start(bf16[128,512]{1,0:T(8,128)(2,1)} %context.1), channel_id=1, source_target_pairs={{64,0},{96,32},{128,64},{160,96},{192,128},{224,160},{0,192},{32,2... | collective-permute-start | bytes 393224 | tf_op jit(solution)/shard_map/ppermute | solution.py:34
  7.1 11.0 %collective-permute-start.5 = (bf16[128,512]{1,0:T(8,128)(2,1)}, bf16[128,512]{1,0:T(8,128)(2,1)S(1)}, u32[]{:S(2)}, u32[]{:S(2)}) collective-permute-start(bf16[128,512]{1,0:T(8,128)(2,1)} %context.1), channel_id=1, source_target_pairs={{192,0},{224,32},{0,64},{32,96},{64,128},{96,160},{128,192},{160,2... | collective-permute-start | bytes 393224 | tf_op jit(solution)/shard_map/ppermute | solution.py:34
  7.1 15.0 %collective-permute-start.1 = (bf16[128,512]{1,0:T(8,128)(2,1)}, bf16[128,512]{1,0:T(8,128)(2,1)S(1)}, u32[]{:S(2)}, u32[]{:S(2)}) collective-permute-start(bf16[128,512]{1,0:T(8,128)(2,1)} %context.1), channel_id=1, source_target_pairs={{32,0},{64,32},{96,64},{128,96},{160,128},{192,160},{224,192},{0,2... | collective-permute-start | bytes 393224 | tf_op jit(solution)/shard_map/ppermute | solution.py:34
  10.8 11.3 %collective-permute-start.7 = (bf16[128,512]{1,0:T(8,128)(2,1)}, bf16[128,512]{1,0:T(8,128)(2,1)S(1)}, u32[]{:S(2)}, u32[]{:S(2)}) collective-permute-start(bf16[128,512]{1,0:T(8,128)(2,1)} %context.1), channel_id=1, source_target_pairs={{224,0},{0,32},{32,64},{64,96},{96,128},{128,160},{160,192},{192,2... | collective-permute-start | bytes 393224 | tf_op jit(solution)/shard_map/ppermute | solution.py:34
  13.5 9.0 %collective-permute-start.4 = (bf16[128,512]{1,0:T(8,128)(2,1)S(1)}, bf16[128,512]{1,0:T(8,128)(2,1)S(1)}, u32[]{:S(2)}, u32[]{:S(2)}) collective-permute-start(bf16[128,512]{1,0:T(8,128)(2,1)S(1)} %collective-permute-done.2.refs_2_), channel_id=1, source_target_pairs={{64,0},{96,32},{128,64},{160,96},{192,128},{224,160},{0,192},{32,2... | collective-permute-start | bytes 393224 | tf_op jit(solution)/shard_map/ppermute | solution.py:34
  18.2 6.6 %collective-permute-start.3 = (bf16[128,512]{1,0:T(8,128)(2,1)S(1)}, bf16[128,512]{1,0:T(8,128)(2,1)S(1)}, u32[]{:S(2)}, u32[]{:S(2)}) collective-permute-start(bf16[128,512]{1,0:T(8,128)(2,1)S(1)} %collective-permute-done.2.refs_2_), channel_id=1, source_target_pairs={{32,0},{64,32},{96,64},{128,96},{160,128},{192,160},{224,192},{0,2... | collective-permute-start | bytes 393224 | tf_op jit(solution)/shard_map/ppermute | solution.py:34
  18.2 6.6 %collective-permute-start.6 = (bf16[128,512]{1,0:T(8,128)(2,1)S(1)}, bf16[128,512]{1,0:T(8,128)(2,1)S(1)}, u32[]{:S(2)}, u32[]{:S(2)}) collective-permute-start(bf16[128,512]{1,0:T(8,128)(2,1)S(1)} %collective-permute-done.5.refs_6_), channel_id=1, source_target_pairs={{224,0},{0,32},{32,64},{64,96},{96,128},{128,160},{160,192},{192,2... | collective-permute-start | bytes 393224 | tf_op jit(solution)/shard_map/ppermute | solution.py:34
  44.2 7.6 %collective-permute-start.13 = (bf16[72,512]{1,0:T(8,128)(2,1)S(1)}, bf16[72,512]{1,0:T(8,128)(2,1)S(1)}, u32[]{:S(2)}, u32[]{:S(2)}) collective-permute-start(bf16[72,512]{1,0:T(8,128)(2,1)S(1)} %shard_map.85.refs_0_), channel_id=1, source_target_pairs={{192,0},{224,32},{0,64},{32,96},{64,128},{96,160},{128,192},{160,2... | collective-permute-start | bytes 221192 | tf_op jit(solution)/shard_map/ppermute | solution.py:34
  44.8 7.1 %collective-permute-start.10 = (bf16[72,512]{1,0:T(8,128)(2,1)S(1)}, bf16[72,512]{1,0:T(8,128)(2,1)S(1)}, u32[]{:S(2)}, u32[]{:S(2)}) collective-permute-start(bf16[72,512]{1,0:T(8,128)(2,1)S(1)} %shard_map.85.refs_0_), channel_id=1, source_target_pairs={{64,0},{96,32},{128,64},{160,96},{192,128},{224,160},{0,192},{32,2... | collective-permute-start | bytes 221192 | tf_op jit(solution)/shard_map/ppermute | solution.py:34
  48.4 7.9 %collective-permute-start.15 = (bf16[72,512]{1,0:T(8,128)(2,1)S(1)}, bf16[72,512]{1,0:T(8,128)(2,1)S(1)}, u32[]{:S(2)}, u32[]{:S(2)}) collective-permute-start(bf16[72,512]{1,0:T(8,128)(2,1)S(1)} %shard_map.85.refs_0_), channel_id=1, source_target_pairs={{224,0},{0,32},{32,64},{64,96},{96,128},{128,160},{160,192},{192,2... | collective-permute-start | bytes 221192 | tf_op jit(solution)/shard_map/ppermute | solution.py:34
  48.8 7.6 %collective-permute-start.9 = (bf16[72,512]{1,0:T(8,128)(2,1)S(1)}, bf16[72,512]{1,0:T(8,128)(2,1)S(1)}, u32[]{:S(2)}, u32[]{:S(2)}) collective-permute-start(bf16[72,512]{1,0:T(8,128)(2,1)S(1)} %shard_map.85.refs_0_), channel_id=1, source_target_pairs={{32,0},{64,32},{96,64},{128,96},{160,128},{192,160},{224,192},{0,2... | collective-permute-start | bytes 221192 | tf_op jit(solution)/shard_map/ppermute | solution.py:34
  51.8 5.6 %collective-permute-start.14 = (bf16[72,512]{1,0:T(8,128)(2,1)S(1)}, bf16[72,512]{1,0:T(8,128)(2,1)S(1)}, u32[]{:S(2)}, u32[]{:S(2)}) collective-permute-start(bf16[72,512]{1,0:T(8,128)(2,1)S(1)} %collective-permute-done.13.refs_6_), channel_id=1, source_target_pairs={{224,0},{0,32},{32,64},{64,96},{96,128},{128,160},{160,192},{192,2... | collective-permute-start | bytes 221192 | tf_op jit(solution)/shard_map/ppermute | solution.py:34
  51.8 6.8 %collective-permute-start.12 = (bf16[72,512]{1,0:T(8,128)(2,1)S(1)}, bf16[72,512]{1,0:T(8,128)(2,1)S(1)}, u32[]{:S(2)}, u32[]{:S(2)}) collective-permute-start(bf16[72,512]{1,0:T(8,128)(2,1)S(1)} %collective-permute-done.10.refs_2_), channel_id=1, source_target_pairs={{64,0},{96,32},{128,64},{160,96},{192,128},{224,160},{0,192},{32,2... | collective-permute-start | bytes 221192 | tf_op jit(solution)/shard_map/ppermute | solution.py:34
  56.3 4.4 %collective-permute-start.11 = (bf16[72,512]{1,0:T(8,128)(2,1)S(1)}, bf16[72,512]{1,0:T(8,128)(2,1)S(1)}, u32[]{:S(2)}, u32[]{:S(2)}) collective-permute-start(bf16[72,512]{1,0:T(8,128)(2,1)S(1)} %collective-permute-done.10.refs_2_), channel_id=1, source_target_pairs={{32,0},{64,32},{96,64},{128,96},{160,128},{192,160},{224,192},{0,2... | collective-permute-start | bytes 221192 | tf_op jit(solution)/shard_map/ppermute | solution.py:34
  91.2 4.2 %collective-permute-start.16 = (bf16[256,4096]{1,0:T(8,128)(2,1)S(1)}, bf16[256,4096]{1,0:T(8,128)(2,1)S(1)}, u32[]{:S(2)}, u32[]{:S(2)}) collective-permute-start(bf16[256,4096]{1,0:T(8,128)(2,1)S(1)} %bitcast.8), channel_id=1, source_target_pairs={{0,1},{1,0},{2,3},{3,2},{4,5},{5,4},{6,7},{7,6},{8,9},{9,8},{10,11... | collective-permute-start | bytes 6291464 | tf_op jit(solution)/shard_map/ppermute | solution.py:30
  97.6 2.9 %collective-permute-start.18 = (bf16[128,4096]{1,0:T(8,128)(2,1)S(1)}, bf16[128,4096]{1,0:T(8,128)(2,1)S(1)}, u32[]{:S(2)}, u32[]{:S(2)}) collective-permute-start(bf16[128,4096]{1,0:T(8,128)(2,1)S(1)} %shard_map.89), channel_id=1, source_target_pairs={{0,1},{1,0},{2,3},{3,2},{4,5},{5,4},{6,7},{7,6},{8,9},{9,8},{10,11... | collective-permute-start | bytes 3145736 | tf_op jit(solution)/shard_map/ppermute | solution.py:30
  135.8 12.2 %collective-permute-start.19 = (bf16[8,4096]{1,0:T(8,128)(2,1)S(1)}, bf16[8,4096]{1,0:T(8,128)(2,1)S(1)}, u32[]{:S(2)}, u32[]{:S(2)}) collective-permute-start(bf16[8,4096]{1,0:T(8,128)(2,1)S(1)} %get-tuple-element.34), channel_id=1, source_target_pairs={{192,0},{224,32},{0,64},{32,96},{64,128},{96,160},{128,192},{160,2... | collective-permute-start | bytes 196616 | tf_op jit(solution)/shard_map/ppermute | solution.py:34
  136.2 12.3 %collective-permute-start.20 = (bf16[8,4096]{1,0:T(8,128)(2,1)S(1)}, bf16[8,4096]{1,0:T(8,128)(2,1)S(1)}, u32[]{:S(2)}, u32[]{:S(2)}) collective-permute-start(bf16[8,4096]{1,0:T(8,128)(2,1)S(1)} %get-tuple-element.35), channel_id=1, source_target_pairs={{64,0},{96,32},{128,64},{160,96},{192,128},{224,160},{0,192},{32,2... | collective-permute-start | bytes 196616 | tf_op jit(solution)/shard_map/ppermute | solution.py:34
  140.2 11.0 %collective-permute-start.21 = (bf16[8,4096]{1,0:T(8,128)(2,1)S(1)}, bf16[8,4096]{1,0:T(8,128)(2,1)S(1)}, u32[]{:S(2)}, u32[]{:S(2)}) collective-permute-start(bf16[8,4096]{1,0:T(8,128)(2,1)S(1)} %get-tuple-element.36), channel_id=1, source_target_pairs={{160,0},{192,32},{224,64},{0,96},{32,128},{64,160},{96,192},{128,2... | collective-permute-start | bytes 196616 | tf_op jit(solution)/shard_map/ppermute | solution.py:34
  140.7 10.5 %collective-permute-start.22 = (bf16[8,4096]{1,0:T(8,128)(2,1)S(1)}, bf16[8,4096]{1,0:T(8,128)(2,1)S(1)}, u32[]{:S(2)}, u32[]{:S(2)}) collective-permute-start(bf16[8,4096]{1,0:T(8,128)(2,1)S(1)} %get-tuple-element.37), channel_id=1, source_target_pairs={{96,0},{128,32},{160,64},{192,96},{224,128},{0,160},{32,192},{64,2... | collective-permute-start | bytes 196616 | tf_op jit(solution)/shard_map/ppermute | solution.py:34
  145.3 8.2 %collective-permute-start.23 = (bf16[8,4096]{1,0:T(8,128)(2,1)S(1)}, bf16[8,4096]{1,0:T(8,128)(2,1)S(1)}, u32[]{:S(2)}, u32[]{:S(2)}) collective-permute-start(bf16[8,4096]{1,0:T(8,128)(2,1)S(1)} %get-tuple-element.38), channel_id=1, source_target_pairs={{128,0},{160,32},{192,64},{224,96},{0,128},{32,160},{64,192},{96,2... | collective-permute-start | bytes 196616 | tf_op jit(solution)/shard_map/ppermute | solution.py:34
  148.0 6.2 %collective-permute-start.24 = (bf16[8,4096]{1,0:T(8,128)(2,1)S(1)}, bf16[8,4096]{1,0:T(8,128)(2,1)S(1)}, u32[]{:S(2)}, u32[]{:S(2)}) collective-permute-start(bf16[8,4096]{1,0:T(8,128)(2,1)S(1)} %get-tuple-element.39), channel_id=1, source_target_pairs={{224,0},{0,32},{32,64},{64,96},{96,128},{128,160},{160,192},{192,2... | collective-permute-start | bytes 196616 | tf_op jit(solution)/shard_map/ppermute | solution.py:34
  148.5 5.7 %collective-permute-start.25 = (bf16[8,4096]{1,0:T(8,128)(2,1)S(1)}, bf16[8,4096]{1,0:T(8,128)(2,1)S(1)}, u32[]{:S(2)}, u32[]{:S(2)}) collective-permute-start(bf16[8,4096]{1,0:T(8,128)(2,1)S(1)} %get-tuple-element.40), channel_id=1, source_target_pairs={{32,0},{64,32},{96,64},{128,96},{160,128},{192,160},{224,192},{0,2... | collective-permute-start | bytes 196616 | tf_op jit(solution)/shard_map/ppermute | solution.py:34
  (10 other events, 239.8 us)

commit v8 on v7

--- a/solution.py
+++ b/solution.py
@@ -13,13 +13,14 @@
 LANES = 128
 F32, BF16 = jnp.float32, jnp.bfloat16
 
-FINE = ("z", "xl", "xh", "y", "c")
-SIZES = (8, 2, 2, 4, 2)
-EXPERT = ("z", "xl")
+FINE = ("zh", "zl", "xl", "xh", "y", "c")
+SIZES = (4, 2, 2, 2, 4, 2)
+EXPERT = ("zh", "zl", "xl")
 TENSOR = ("xh", "y", "c")
 SPREAD = ("xh", "y")
-PLANE = ("xl", "xh", "y")
-NZ = 8
+PEERS = ("zl", "y", "xh", "xl")
+RING = ("zh", "zl")
+NZ, NH = 8, 4
 MIB = 1 << 20
 
 VMEM = pl.BlockSpec(memory_space=pltpu.VMEM)
@@ -30,8 +31,12 @@
     return lax.ppermute(x, axis, [(0, 1), (1, 0)])
 
 
-def fetch(x, hop):
-    return lax.ppermute(x, "z", [((i + hop) % NZ, i) for i in range(NZ)])
+def fetch(x, hop, axis=RING, size=NZ):
+    return lax.ppermute(x, axis, [((i + hop) % size, i) for i in range(size)])
+
+
+def fetch_pair(x, hop):
+    return fetch(x, hop, "zh", NH)
 
 
 def gather_z(x):
@@ -50,12 +55,12 @@
     return jnp.dot(a, b, preferred_element_type=F32)
 
 
-def where(place):
+def where_am_i(place):
     return lax.div(place[0], 4), lax.rem(lax.div(place[0], 2), 2), lax.rem(place[0], 2)
 
 
 def stage_kernel(place, own, other, context, rhs, held):
-    _, xl, _ = where(place)
+    _, xl, _ = where_am_i(place)
     cols = own.shape[1]
     rhs[:, pl.ds(pl.multiple_of(xl * cols, LANES), cols)] = own[...]
     rhs[:, pl.ds(pl.multiple_of((1 - xl) * cols, LANES), cols)] = other[...]
@@ -77,7 +82,7 @@
 
 def project_kernel(place, *refs):
     blocks, (rhs, give, keep, held) = refs[:NZ], refs[NZ:]
-    _, _, core = where(place)
+    _, _, core = where_am_i(place)
     lhs = jnp.concatenate([b[...] for b in blocks], axis=0)
     total = dot(lhs, rhs[...])
     spread = give.shape[0]
@@ -118,16 +123,41 @@
     )(keep, got)
 
 
-def settle_kernel(place, parts, ids, gates, out, held):
-    z, _, _ = where(place)
-    tokens = parts.shape[1]
-    rows = tokens // NZ
+def settle_kernel(place, parts, mine, give, held):
+    z, _, _ = where_am_i(place)
+    rows = parts.shape[1] // NZ
     total = parts[0].astype(F32)
     for i in range(1, parts.shape[0]):
         total += parts[i].astype(F32)
     for k in range(NZ):
         at = pl.multiple_of(lax.rem(z + k, NZ) * rows, rows)
         held[pl.ds(at, rows), :] = total[k * rows : (k + 1) * rows]
+    for out, parity in ((mine, lax.rem(z, 2)), (give, 1 - lax.rem(z, 2))):
+        out[...] = jnp.concatenate(
+            [held[pl.ds(pl.multiple_of((2 * i + parity) * rows, rows), rows), :] for i in range(NH)],
+            axis=0,
+        ).astype(BF16)
+
+
+def settle(place, parts):
+    shape = (parts.shape[1] // 2, parts.shape[2])
+    return pl.pallas_call(
+        settle_kernel,
+        out_shape=(jax.ShapeDtypeStruct(shape, BF16),) * 2,
+        in_specs=[SMEM, VMEM],
+        out_specs=(VMEM, VMEM),
+        scratch_shapes=[pltpu.VMEM(parts.shape[1:], F32)],
+        compiler_params=params(16),
+    )(place, parts)
+
+
+def pack_kernel(place, mine, got, ids, gates, out, held):
+    z, _, _ = where_am_i(place)
+    tokens, cols = mine.shape
+    rows = ids.shape[0]
+    parity = lax.rem(z, 2)
+    held[:tokens, pl.ds(pl.multiple_of(parity * cols, LANES), cols)] = mine[...].astype(F32)
+    held[:tokens, pl.ds(pl.multiple_of((1 - parity) * cols, LANES), cols)] = got[...].astype(F32)
     named = ids[...].astype(F32)
     high = gates[...].astype(BF16).astype(F32)
     low = gates[...] - high
@@ -140,36 +170,39 @@
     out[...] = held[...].astype(BF16)
 
 
-def settle(place, parts, ids, gates):
-    shape = (parts.shape[1] + ids.shape[0], parts.shape[2])
-    return pl.pallas_call(
-        settle_kernel,
+def pack(place, mine, got, ids, gates):
+    shape = (mine.shape[0] + ids.shape[0], 2 * mine.shape[1])
+    return pl.pallas_call(
+        pack_kernel,
         out_shape=jax.ShapeDtypeStruct(shape, BF16),
-        in_specs=[SMEM, VMEM, VMEM, VMEM],
+        in_specs=[SMEM] + [VMEM] * 4,
         out_specs=VMEM,
         scratch_shapes=[pltpu.VMEM(shape, F32)],
         compiler_params=params(16),
-    )(place, parts, ids, gates)
+    )(place, mine, got, ids, gates)
 
 
 def place_kernel(place, *refs):
-    blocks, (gain, sent, own, high, low, stream, notes, mass) = refs[:NZ], refs[NZ:]
-    z, _, _ = where(place)
+    blocks, (gain, sent, own, high, low, stream, notes, mass) = refs[:NH], refs[NH:]
+    z, _, _ = where_am_i(place)
+    pair = lax.div(z, 2)
     tokens, width = stream.shape
-    rows, wide = tokens // NZ, width // NZ
+    rows, wide = tokens // NH, width // NH
     lanes = sent.shape[0]
-    for hop in range(NZ):
-        there = lax.rem(z + hop, NZ)
+    for hop in range(NH):
+        there = lax.rem(pair + hop, NH)
         at = pl.multiple_of(there * wide, LANES)
         block = blocks[hop][...].astype(F32)
         stream[:, pl.ds(at, wide)] = block[:tokens]
         notes[pl.ds(pl.multiple_of(there * rows, rows), rows), :] = block[tokens:, :LANES]
-    own[...] = stream[pl.ds(pl.multiple_of(z * rows, rows), rows), :]
-
-    slots = NZ * CAP
+    own[...] = stream[pl.ds(pl.multiple_of(pair * rows, rows), rows), :]
+
+    slots = NH * CAP
     lane = lax.broadcasted_iota(jnp.int32, (tokens, lanes), 1)
     token = lax.broadcasted_iota(jnp.int32, (tokens, lanes), 0)
-    label = (z * (lanes // (2 * slots)) + lane // (2 * slots)).astype(F32)
+    peer = lane // slots
+    xl, xh, y, zl = peer % 2, (peer // 2) % 2, (peer // 4) % 4, peer // 16
+    label = (((pair * 2 + zl) * 2 + xl) * 4 + xh * 2 + y // 2).astype(F32)
     listed = notes[...]
     match = jnp.zeros((tokens, lanes), F32)
     gate = jnp.zeros((tokens, lanes), F32)
@@ -184,14 +217,13 @@
     rank = dot(jnp.where(earlier, 1.0, 0.0).astype(BF16), match.astype(BF16))
     slot = (token // rows) * CAP + rank.astype(jnp.int32)
     placed = (match > 0.5) & (slot == lane % slots) & (rank < CAP - 0.5)
+    mass[...] = jnp.where(placed, gate, 0.0)
     spots = jnp.transpose(jnp.where(placed, 1.0, 0.0)).astype(BF16)
-
-    mass[...] = jnp.where(placed, gate, 0.0)
 
     weight = jnp.concatenate(
         [
-            mass[pl.ds(pl.multiple_of(lax.rem(z + hop, NZ) * rows, rows), rows), :]
-            for hop in range(NZ)
+            mass[pl.ds(pl.multiple_of(lax.rem(pair + hop, NH) * rows, rows), rows), :]
+            for hop in range(NH)
         ],
         axis=0,
     )
@@ -200,21 +232,21 @@
     low[...] = (weight - top.astype(F32)).astype(BF16)
 
     square = jnp.zeros((tokens, 1), F32)
-    for hop in range(NZ):
-        part = stream[:, hop * wide : (hop + 1) * wide]
+    for i in range(NH):
+        part = stream[:, i * wide : (i + 1) * wide]
         square += jnp.sum(part * part, axis=-1, keepdims=True)
     scale = lax.rsqrt(square / width + 1e-06)
-    for hop in range(NZ):
-        at = slice(hop * wide, (hop + 1) * wide)
+    for i in range(NH):
+        at = slice(i * wide, (i + 1) * wide)
         normed = (stream[:, at] * scale * gain[:, at]).astype(BF16)
         sent[:, at] = dot(spots, normed).astype(BF16)
 
 
-def place_rows(place, blocks, gain, plane):
-    rows = blocks[0].shape[0] // (NZ + 1)
-    tokens = NZ * rows
-    width = NZ * blocks[0].shape[1]
-    lanes = plane * NZ * CAP
+def place_rows(place, blocks, gain, peers):
+    rows = blocks[0].shape[0] // (NH + 1)
+    tokens = NH * rows
+    width = NH * blocks[0].shape[1]
+    lanes = peers * NH * CAP
     return pl.pallas_call(
         place_kernel,
         out_shape=(
@@ -223,7 +255,7 @@
             jax.ShapeDtypeStruct((tokens, lanes), BF16),
             jax.ShapeDtypeStruct((tokens, lanes), BF16),
         ),
-        in_specs=[SMEM] + [VMEM] * (NZ + 1),
+        in_specs=[SMEM] + [VMEM] * (NH + 1),
         out_specs=(VMEM,) * 4,
         scratch_shapes=[
             pltpu.VMEM((tokens, width), F32),
@@ -296,7 +328,7 @@
         piece = back[:, at]
         mix = dot(high[...], piece) + dot(low[...], piece)
         base[:, at] = own[:, at] + mix[:rows]
-        for hop in range(1, NZ):
+        for hop in range(1, NH):
             outs[hop - 1][:, at] = mix[hop * rows : (hop + 1) * rows].astype(BF16)
 
 
@@ -305,28 +337,30 @@
     return pl.pallas_call(
         combine_kernel,
         out_shape=(jax.ShapeDtypeStruct((rows, width), F32),)
-        + (jax.ShapeDtypeStruct((rows, width), BF16),) * (NZ - 1),
+        + (jax.ShapeDtypeStruct((rows, width), BF16),) * (NH - 1),
         in_specs=[VMEM] * 4,
-        out_specs=(VMEM,) * NZ,
+        out_specs=(VMEM,) * NH,
         compiler_params=params(32),
     )(high, low, back, own)
 
 
 def on_device(context, proj_weight, norm_gain, expert_ids, gate_values, w_gate, w_up, w_down):
-    zi, xli, ci = (lax.axis_index(a).astype(jnp.int32) for a in ("z", "xl", "c"))
+    zi, xli, ci = (lax.axis_index(a).astype(jnp.int32) for a in (RING, "xl", "c"))
     place = (4 * zi + 2 * xli + ci).reshape(1)
     n_spread = lax.axis_size(SPREAD)
-    n_plane = lax.axis_size(PLANE)
+    n_peers = lax.axis_size(PEERS)
 
     rhs, held = stage(place, proj_weight, swap(proj_weight, "xl"), context)
     give, keep = project(place, [held] + gather_z(context)[1:], rhs, n_spread)
     partial = join(keep, swap(give, "c"))
     partial = lax.all_to_all(partial, SPREAD, 0, 0, tiled=True)
 
-    part = settle(place, partial, expert_ids, gate_values)
-    sent, own, high, low = place_rows(place, gather_z(part), norm_gain, n_plane)
+    part, give = settle(place, partial)
+    part = pack(place, part, swap(give, "zl"), expert_ids, gate_values)
+    far, up, dn = fetch_pair(part, 2), fetch_pair(part, 1), fetch_pair(part, -1)
+    sent, own, high, low = place_rows(place, [part, up, far, dn], norm_gain, n_peers)
     width = sent.shape[1]
-    mine = lax.all_to_all(sent.reshape(n_plane, -1, width), PLANE, 0, 0, tiled=True)
+    mine = lax.all_to_all(sent.reshape(n_peers, -1, width), PEERS, 0, 0, tiled=True)
     mine = mine.reshape(-1, width)
 
     weights = (w_gate, w_up, w_down)
@@ -336,12 +370,12 @@
     theirs, mine_out = lax.optimization_barrier((theirs, mine_out))
     half = count // 2
     top, bottom = (swap(expert_rows(theirs, at, half, *weights), "c") for at in (0, half))
-    summed = add_rows(mine_out, bottom, add_rows(mine_out, top)).reshape(n_plane, -1, width)
-    back = lax.all_to_all(summed, PLANE, 0, 0, tiled=True).reshape(-1, width)
+    summed = add_rows(mine_out, bottom, add_rows(mine_out, top)).reshape(n_peers, -1, width)
+    back = lax.all_to_all(summed, PEERS, 0, 0, tiled=True).reshape(-1, width)
 
     total, *blocks = combine(high, low, back, own)
-    for hop in (2, 6, 3, 5, 4, 1, 7):
-        total += fetch(blocks[hop - 1], -hop).astype(F32)
+    for hop in (2, 1, 3):
+        total += fetch_pair(blocks[hop - 1], -hop).astype(F32)
     return total.astype(BF16)
 
 

time: 155 us -> 152 us (0.981)
  starting transfers between devices: 45.6 us -> 31 us
  waiting for transfers between devices: 17.1 us -> 25.5 us
  blocking collectives: 77.6 us -> 81.1 us
    ppermute x21 -> x13, starting transfers between devices: 44 us -> 28.9 us  [fetch(): return lax.ppermute(x, axis, [((i + hop) % size, i) for i in range(size)])]
    ppermute x21 -> x13, waiting for transfers between devices: 12.8 us -> 17.7 us  [fetch(): return lax.ppermute(x, axis, [((i + hop) % size, i) for i in range(size)])]
    ppermute x5 -> x6, waiting for transfers between devices: 4.32 us -> 7.88 us  [swap(): return lax.ppermute(x, axis, [(0, 1), (1, 0)])]
    all_to_all x2, blocking collectives: 61.1 us -> 64.6 us  [the longest x1 32.9 us: on_device(): back = lax.all_to_all(summed, PEERS, 0, 0, tiled=True).reshape(-1, width)]
  transfers between devices with their start and end apart: 26 -> 19, of which waited for: 12 -> 12; matrix products, arithmetic and copies ran while one was open for 0% -> 0% of each run, Pallas kernels for 4% -> 4%
where the time goes in v8:
time: 152 us
  blocking collectives  81.1 us (53%)
  starting transfers between devices  31 us (20%)
  waiting for transfers between devices  25.5 us (17%)
  Pallas kernels  11.7 us (8%)
  local copies, waits for them, and re-layouts  1.89 us (1%)
    all_to_all x1, blocking collectives, on_device(): back = lax.all_to_all(summed, PEERS, 0, 0, tiled=True).reshape(-1, width)  32.9 us
    all_to_all x1, blocking collectives, on_device(): lax.all_to_all(sent.reshape(n_peers, -1, width), PEERS, 0, 0, tiled=True)  31.7 us
    ppermute x13, starting transfers between devices, fetch(): return lax.ppermute(x, axis, [((i + hop) % size, i) for i in range(size)])  28.9 us
    ppermute x13, waiting for transfers between devices, fetch(): return lax.ppermute(x, axis, [((i + hop) % size, i) for i in range(size)])  17.7 us
    all_to_all x1, blocking collectives, on_device(): partial = lax.all_to_all(partial, SPREAD, 0, 0, tiled=True)  16.4 us
    pallas_call x3, Pallas kernels, expert_rows(): pl.pallas_call(functools.partial(expert_kernel, first), out_shape=jax.Sha...  8.25 us
    ppermute x6, waiting for transfers between devices, swap(): return lax.ppermute(x, axis, [(0, 1), (1, 0)])  7.88 us
  transfers between devices with their start and end apart: 19, of which 12 were waited for; matrix products, arithmetic and copies ran while one was open for 0% of the time, Pallas kernels for 4%

profile of v8, /device:TPU:6, one launch (start us, length us, event | category | flops | bytes accessed | tf_op | source)
XLA Modules:
  0.0 152.0 jit_solution(10899358163128956505)
XLA Ops:
  0.8 6.3 %collective-permute-start.2 = (bf16[128,512]{1,0:T(8,128)(2,1)}, bf16[128,512]{1,0:T(8,128)(2,1)S(1)}, u32[]{:S(2)}, u32[]{:S(2)}) collective-permute-start(bf16[128,512]{1,0:T(8,128)(2,1)} %context.1), channel_id=1, source_target_pairs={{64,0},{96,32},{128,64},{160,96},{192,128},{224,160},{0,192},{32,2... | collective-permute-start | bytes 393224 | tf_op jit(solution)/shard_map/ppermute | solution.py:35
  7.1 3.7 %collective-permute-start.1 = (bf16[128,512]{1,0:T(8,128)(2,1)}, bf16[128,512]{1,0:T(8,128)(2,1)S(1)}, u32[]{:S(2)}, u32[]{:S(2)}) collective-permute-start(bf16[128,512]{1,0:T(8,128)(2,1)} %context.1), channel_id=1, source_target_pairs={{32,0},{64,32},{96,64},{128,96},{160,128},{192,160},{224,192},{0,2... | collective-permute-start | bytes 393224 | tf_op jit(solution)/shard_map/ppermute | solution.py:35
  10.8 2.7 %collective-permute-done.2.refs_2_ = bf16[128,512]{1,0:T(8,128)(2,1)S(1)} collective-permute-done((bf16[128,512]{1,0:T(8,128)(2,1)}, bf16[128,512]{1,0:T(8,128)(2,1)S(1)}, u32[]{:S(2)}, u32[]{:S(2)}) %collective-permute-start.2) | collective-permute-done | bytes 131104 | tf_op jit(solution)/shard_map/ppermute | solution.py:35
  13.5 4.6 %collective-permute-start.4 = (bf16[128,512]{1,0:T(8,128)(2,1)S(1)}, bf16[128,512]{1,0:T(8,128)(2,1)S(1)}, u32[]{:S(2)}, u32[]{:S(2)}) collective-permute-start(bf16[128,512]{1,0:T(8,128)(2,1)S(1)} %collective-permute-done.2.refs_2_), channel_id=1, source_target_pairs={{64,0},{96,32},{128,64},{160,96},{192,128},{224,160},{0,192},{32,2... | collective-permute-start | bytes 393224 | tf_op jit(solution)/shard_map/ppermute | solution.py:35
  18.2 2.0 %collective-permute-start.6 = (bf16[128,512]{1,0:T(8,128)(2,1)S(1)}, bf16[128,512]{1,0:T(8,128)(2,1)S(1)}, u32[]{:S(2)}, u32[]{:S(2)}) collective-permute-start(bf16[128,512]{1,0:T(8,128)(2,1)S(1)} %collective-permute-done.5.refs_6_), channel_id=1, source_target_pairs={{224,0},{0,32},{32,64},{64,96},{96,128},{128,160},{160,192},{192,2... | collective-permute-start | bytes 393224 | tf_op jit(solution)/shard_map/ppermute | solution.py:35
  22.5 2.3 %collective-permute-done.3.refs_3_ = bf16[128,512]{1,0:T(8,128)(2,1)S(1)} collective-permute-done((bf16[128,512]{1,0:T(8,128)(2,1)S(1)}, bf16[128,512]{1,0:T(8,128)(2,1)S(1)}, u32[]{:S(2)}, u32[]{:S(2)}) %collective-permute-start.3) | collective-permute-done | bytes 131104 | tf_op jit(solution)/shard_map/ppermute | solution.py:35
  25.7 1.9 %collective-permute-done.8.got = bf16[8,64,512]{2,1,0:T(8,128)(2,1)S(1)} collective-permute-done((bf16[8,64,512]{2,1,0:T(8,128)(2,1)S(1)}, bf16[8,64,512]{2,1,0:T(8,128)(2,1)S(1)}, u32[]{:S(2)}, u32[]{:S(2)}) %collective-permute-start.8) | collective-permute-done | bytes 524320 | tf_op jit(solution)/shard_map/ppermute | solution.py:31
  27.7 16.4 %all_to_all.15.parts = bf16[8,64,512]{2,1,0:T(8,128)(2,1)S(1)} all-to-all(bf16[8,64,512]{2,1,0:T(8,128)(2,1)S(1)} %shard_map.84), channel_id=1, replica_groups=mesh['zh'=4,'zl'=2,'xl'=2,'xh'=2,'y'=4,'c'=2] {'xh','y'}, dimensions={0} | all-to-all | bytes 1048576 | tf_op jit(solution)/shard_map/all_to_all | solution.py:356
  44.6 3.6 %collective-permute-done.9.got = bf16[32,512]{1,0:T(8,128)(2,1)S(1)} collective-permute-done((bf16[32,512]{1,0:T(8,128)(2,1)S(1)}, bf16[32,512]{1,0:T(8,128)(2,1)S(1)}, u32[]{:S(2)}, u32[]{:S(2)}) %collective-permute-start.9) | collective-permute-done | bytes 32800 | tf_op jit(solution)/shard_map/ppermute | solution.py:31
  48.8 4.2 %collective-permute-start.11 = (bf16[40,1024]{1,0:T(8,128)(2,1)S(1)}, bf16[40,1024]{1,0:T(8,128)(2,1)S(1)}, u32[]{:S(2)}, u32[]{:S(2)}) collective-permute-start(bf16[40,1024]{1,0:T(8,128)(2,1)S(1)} %shard_map.86.refs_0_), channel_id=1, source_target_pairs={{128,0},{192,64},{0,128},{64,192},{129,1},{193,65},{1,129},{65,193... | collective-permute-start | bytes 245768 | tf_op jit(solution)/shard_map/ppermute | solution.py:35
  53.0 1.5 %collective-permute-start.10 = (bf16[40,1024]{1,0:T(8,128)(2,1)S(1)}, bf16[40,1024]{1,0:T(8,128)(2,1)S(1)}, u32[]{:S(2)}, u32[]{:S(2)}) collective-permute-start(bf16[40,1024]{1,0:T(8,128)(2,1)S(1)} %shard_map.86.refs_0_), channel_id=1, source_target_pairs={{64,0},{128,64},{192,128},{0,192},{65,1},{129,65},{193,129},{1,193... | collective-permute-start | bytes 245768 | tf_op jit(solution)/shard_map/ppermute | solution.py:35
  54.5 1.7 %collective-permute-done.12.refs_3_ = bf16[40,1024]{1,0:T(8,128)(2,1)S(1)} collective-permute-done((bf16[40,1024]{1,0:T(8,128)(2,1)S(1)}, bf16[40,1024]{1,0:T(8,128)(2,1)S(1)}, u32[]{:S(2)}, u32[]{:S(2)}) %collective-permute-start.12) | collective-permute-done | bytes 81952 | tf_op jit(solution)/shard_map/ppermute | solution.py:35
  56.2 1.2 collective-permute-done.11.refs_2_
  57.4 2.7 %collective-permute-done.10.refs_1_ = bf16[40,1024]{1,0:T(8,128)(2,1)S(1)} collective-permute-done((bf16[40,1024]{1,0:T(8,128)(2,1)S(1)}, bf16[40,1024]{1,0:T(8,128)(2,1)S(1)}, u32[]{:S(2)}, u32[]{:S(2)}) %collective-permute-start.10) | collective-permute-done | bytes 81952 | tf_op jit(solution)/shard_map/ppermute | solution.py:35
  61.1 31.7 %all_to_all.16 = bf16[32,8,4096]{2,1,0:T(8,128)(2,1)S(1)} all-to-all(bf16[32,8,4096]{2,1,0:T(8,128)(2,1)S(1)} %bitcast.10), channel_id=1, replica_groups=mesh['zh'=4,'zl'=2,'xl'=2,'xh'=2,'y'=4,'c'=2] {'zl','y','xh','xl'}, dimensions={0} | all-to-all | bytes 4194304 | tf_op jit(solution)/shard_map/all_to_all | solution.py:363
  92.9 3.8 %shard_map.88.mine = bf16[256,4096]{1,0:T(8,128)(2,1)S(1)} custom-call(bf16[256,4096]{1,0:T(8,128)(2,1)S(1)} %bitcast.9, bf16[1,4096,384]{2,1,0:T(8,128)(2,1)S(1)} %copy-done, bf16[1,4096,384]{2,1,0:T(8,128)(2,1)S(1)} %copy-done.1, bf16[1,384,4096]{2,1,0:T(8,128)(2,1)S(1)} %copy-done.2), custom_call_target="tpu_custom_call" | custom-call | flops 2415919104 | bytes 13631488 | tf_op jit(solution)/shard_map/pallas_call | solution.py:288
  97.0 2.2 %shard_map.90 = bf16[128,4096]{1,0:T(8,128)(2,1)S(1)} custom-call(bf16[256,4096]{1,0:T(8,128)(2,1)S(1)} %collective-permute-done.13.rows, bf16[1,4096,384]{2,1,0:T(8,128)(2,1)S(1)} %copy-done, bf16[1,4096,384]{2,1,0:T(8,128)(2,1)S(1)} %copy-done.1, bf16[1,384,4096]{2,1,0:T(8,128)(2,1)S(1)} %copy-done.2), custom_call_target="tpu_custom_call" | custom-call | flops 1207959552 | bytes 11534336 | tf_op jit(solution)/shard_map/pallas_call | solution.py:288
  99.5 2.2 %shard_map.89 = bf16[128,4096]{1,0:T(8,128)(2,1)S(1)} custom-call(bf16[256,4096]{1,0:T(8,128)(2,1)S(1)} %collective-permute-done.13.rows, bf16[1,4096,384]{2,1,0:T(8,128)(2,1)S(1)} %copy-done, bf16[1,4096,384]{2,1,0:T(8,128)(2,1)S(1)} %copy-done.1, bf16[1,384,4096]{2,1,0:T(8,128)(2,1)S(1)} %copy-done.2), custom_call_target="tpu_custom_call" | custom-call | flops 1207959552 | bytes 11534336 | tf_op jit(solution)/shard_map/pallas_call | solution.py:288
  102.4 2.1 %collective-permute-done.14.part = bf16[128,4096]{1,0:T(8,128)(2,1)S(1)} collective-permute-done((bf16[128,4096]{1,0:T(8,128)(2,1)S(1)}, bf16[128,4096]{1,0:T(8,128)(2,1)S(1)}, u32[]{:S(2)}, u32[]{:S(2)}) %collective-permute-start.14) | collective-permute-done | bytes 1048608 | tf_op jit(solution)/shard_map/ppermute | solution.py:31
  104.8 32.9 %all_to_all.17 = bf16[32,8,4096]{2,1,0:T(8,128)(2,1)S(1)} all-to-all(bf16[32,8,4096]{2,1,0:T(8,128)(2,1)S(1)} %bitcast.6), channel_id=1, replica_groups=mesh['zh'=4,'zl'=2,'xl'=2,'xh'=2,'y'=4,'c'=2] {'zl','y','xh','xl'}, dimensions={0} | all-to-all | bytes 4194304 | tf_op jit(solution)/shard_map/all_to_all | solution.py:374
  138.5 1.8 %collective-permute-start.16 = (bf16[8,4096]{1,0:T(8,128)(2,1)S(1)}, bf16[8,4096]{1,0:T(8,128)(2,1)S(1)}, u32[]{:S(2)}, u32[]{:S(2)}) collective-permute-start(bf16[8,4096]{1,0:T(8,128)(2,1)S(1)} %get-tuple-element.34), channel_id=1, source_target_pairs={{128,0},{192,64},{0,128},{64,192},{129,1},{193,65},{1,129},{65,193... | collective-permute-start | bytes 196616 | tf_op jit(solution)/shard_map/ppermute | solution.py:35
  140.4 4.2 %collective-permute-start.17 = (bf16[8,4096]{1,0:T(8,128)(2,1)S(1)}, bf16[8,4096]{1,0:T(8,128)(2,1)S(1)}, u32[]{:S(2)}, u32[]{:S(2)}) collective-permute-start(bf16[8,4096]{1,0:T(8,128)(2,1)S(1)} %get-tuple-element.35), channel_id=1, source_target_pairs={{192,0},{0,64},{64,128},{128,192},{193,1},{1,65},{65,129},{129,193... | collective-permute-start | bytes 196616 | tf_op jit(solution)/shard_map/ppermute | solution.py:35
  144.6 3.0 %collective-permute-done.16 = bf16[8,4096]{1,0:T(8,128)(2,1)S(1)} collective-permute-done((bf16[8,4096]{1,0:T(8,128)(2,1)S(1)}, bf16[8,4096]{1,0:T(8,128)(2,1)S(1)}, u32[]{:S(2)}, u32[]{:S(2)}) %collective-permute-start.16) | collective-permute-done | bytes 65568 | tf_op jit(solution)/shard_map/ppermute | solution.py:35
  147.6 3.8 %collective-permute-done.18 = bf16[8,4096]{1,0:T(8,128)(2,1)S(1)} collective-permute-done((bf16[8,4096]{1,0:T(8,128)(2,1)S(1)}, bf16[8,4096]{1,0:T(8,128)(2,1)S(1)}, u32[]{:S(2)}, u32[]{:S(2)}) %collective-permute-start.18) | collective-permute-done | bytes 65568 | tf_op jit(solution)/shard_map/ppermute | solution.py:35
  (46 shorter events, 9.3 us)
Async XLA Ops:
  0.0 18.2 %collective-permute-start = (bf16[512,256]{1,0:T(8,128)(2,1)}, bf16[512,256]{1,0:T(8,128)(2,1)S(1)}, u32[]{:S(2)}, u32[]{:S(2)}) collective-permute-start(bf16[512,256]{1,0:T(8,128)(2,1)} %own.1), channel_id=1, source_target_pairs={{0,16},{16,0},{1,17},{17,1},{2,18},{18,2},{3,19},{19,3},{4,20},{20... | collective-permute-start | bytes 786440 | tf_op jit(solution)/shard_map/ppermute | solution.py:31
  0.8 12.7 %collective-permute-start.2 = (bf16[128,512]{1,0:T(8,128)(2,1)}, bf16[128,512]{1,0:T(8,128)(2,1)S(1)}, u32[]{:S(2)}, u32[]{:S(2)}) collective-permute-start(bf16[128,512]{1,0:T(8,128)(2,1)} %context.1), channel_id=1, source_target_pairs={{64,0},{96,32},{128,64},{160,96},{192,128},{224,160},{0,192},{32,2... | collective-permute-start | bytes 393224 | tf_op jit(solution)/shard_map/ppermute | solution.py:35
  7.1 11.0 %collective-permute-start.5 = (bf16[128,512]{1,0:T(8,128)(2,1)}, bf16[128,512]{1,0:T(8,128)(2,1)S(1)}, u32[]{:S(2)}, u32[]{:S(2)}) collective-permute-start(bf16[128,512]{1,0:T(8,128)(2,1)} %context.1), channel_id=1, source_target_pairs={{192,0},{224,32},{0,64},{32,96},{64,128},{96,160},{128,192},{160,2... | collective-permute-start | bytes 393224 | tf_op jit(solution)/shard_map/ppermute | solution.py:35
  7.1 15.0 %collective-permute-start.1 = (bf16[128,512]{1,0:T(8,128)(2,1)}, bf16[128,512]{1,0:T(8,128)(2,1)S(1)}, u32[]{:S(2)}, u32[]{:S(2)}) collective-permute-start(bf16[128,512]{1,0:T(8,128)(2,1)} %context.1), channel_id=1, source_target_pairs={{32,0},{64,32},{96,64},{128,96},{160,128},{192,160},{224,192},{0,2... | collective-permute-start | bytes 393224 | tf_op jit(solution)/shard_map/ppermute | solution.py:35
  10.8 11.3 %collective-permute-start.7 = (bf16[128,512]{1,0:T(8,128)(2,1)}, bf16[128,512]{1,0:T(8,128)(2,1)S(1)}, u32[]{:S(2)}, u32[]{:S(2)}) collective-permute-start(bf16[128,512]{1,0:T(8,128)(2,1)} %context.1), channel_id=1, source_target_pairs={{224,0},{0,32},{32,64},{64,96},{96,128},{128,160},{160,192},{192,2... | collective-permute-start | bytes 393224 | tf_op jit(solution)/shard_map/ppermute | solution.py:35
  13.5 9.0 %collective-permute-start.4 = (bf16[128,512]{1,0:T(8,128)(2,1)S(1)}, bf16[128,512]{1,0:T(8,128)(2,1)S(1)}, u32[]{:S(2)}, u32[]{:S(2)}) collective-permute-start(bf16[128,512]{1,0:T(8,128)(2,1)S(1)} %collective-permute-done.2.refs_2_), channel_id=1, source_target_pairs={{64,0},{96,32},{128,64},{160,96},{192,128},{224,160},{0,192},{32,2... | collective-permute-start | bytes 393224 | tf_op jit(solution)/shard_map/ppermute | solution.py:35
  18.2 6.6 %collective-permute-start.3 = (bf16[128,512]{1,0:T(8,128)(2,1)S(1)}, bf16[128,512]{1,0:T(8,128)(2,1)S(1)}, u32[]{:S(2)}, u32[]{:S(2)}) collective-permute-start(bf16[128,512]{1,0:T(8,128)(2,1)S(1)} %collective-permute-done.2.refs_2_), channel_id=1, source_target_pairs={{32,0},{64,32},{96,64},{128,96},{160,128},{192,160},{224,192},{0,2... | collective-permute-start | bytes 393224 | tf_op jit(solution)/shard_map/ppermute | solution.py:35
  18.2 6.6 %collective-permute-start.6 = (bf16[128,512]{1,0:T(8,128)(2,1)S(1)}, bf16[128,512]{1,0:T(8,128)(2,1)S(1)}, u32[]{:S(2)}, u32[]{:S(2)}) collective-permute-start(bf16[128,512]{1,0:T(8,128)(2,1)S(1)} %collective-permute-done.5.refs_6_), channel_id=1, source_target_pairs={{224,0},{0,32},{32,64},{64,96},{96,128},{128,160},{160,192},{192,2... | collective-permute-start | bytes 393224 | tf_op jit(solution)/shard_map/ppermute | solution.py:35
  24.8 68.1 %copy-start.2 = (bf16[1,384,4096]{2,1,0:T(8,128)(2,1)S(1)}, bf16[1,384,4096]{2,1,0:T(8,128)(2,1)}, u32[]{:S(2)}) copy-start(bf16[1,384,4096]{2,1,0:T(8,128)(2,1)} %w_down.5) | copy-start | bytes 9437188
  25.5 22.7 %copy-start.6 = (s32[8,8]{1,0:T(8,128)S(1)}, s32[8,8]{1,0:T(8,128)}, u32[]{:S(2)}) copy-start(s32[8,8]{1,0:T(8,128)} %ids.1) | copy-start | bytes 772
  25.5 34.5 %copy-start.5 = (f32[4096]{0:T(1024)S(1)}, f32[4096]{0:T(1024)}, u32[]{:S(2)}) copy-start(f32[4096]{0:T(1024)} %param.10) | copy-start | bytes 49156
  25.6 2.0 %collective-permute-start.8 = (bf16[8,64,512]{2,1,0:T(8,128)(2,1)S(1)}, bf16[8,64,512]{2,1,0:T(8,128)(2,1)S(1)}, u32[]{:S(2)}, u32[]{:S(2)}) collective-permute-start(bf16[8,64,512]{2,1,0:T(8,128)(2,1)S(1)} %get-tuple-element.24), channel_id=1, source_target_pairs={{0,1},{1,0},{2,3},{3,2},{4,5},{5,4},{6,7},{7,6},{8,9},{9,8},{10,11... | collective-permute-start | bytes 1572872 | tf_op jit(solution)/shard_map/ppermute | solution.py:31
  27.6 65.3 %copy-start.1 = (bf16[1,4096,384]{2,1,0:T(8,128)(2,1)S(1)}, bf16[1,4096,384]{2,1,0:T(8,128)(2,1)}, u32[]{:S(2)}) copy-start(bf16[1,4096,384]{2,1,0:T(8,128)(2,1)} %w_up.5) | copy-start | bytes 9437188
  44.2 4.0 %collective-permute-start.9 = (bf16[32,512]{1,0:T(8,128)(2,1)S(1)}, bf16[32,512]{1,0:T(8,128)(2,1)S(1)}, u32[]{:S(2)}, u32[]{:S(2)}) collective-permute-start(bf16[32,512]{1,0:T(8,128)(2,1)S(1)} %get-tuple-element.26), channel_id=1, source_target_pairs={{0,32},{32,0},{1,33},{33,1},{2,34},{34,2},{3,35},{35,3},{4,36},{36... | collective-permute-start | bytes 98312 | tf_op jit(solution)/shard_map/ppermute | solution.py:31
  48.3 7.9 %collective-permute-start.12 = (bf16[40,1024]{1,0:T(8,128)(2,1)S(1)}, bf16[40,1024]{1,0:T(8,128)(2,1)S(1)}, u32[]{:S(2)}, u32[]{:S(2)}) collective-permute-start(bf16[40,1024]{1,0:T(8,128)(2,1)S(1)} %shard_map.86.refs_0_), channel_id=1, source_target_pairs={{192,0},{0,64},{64,128},{128,192},{193,1},{1,65},{65,129},{129,193... | collective-permute-start | bytes 245768 | tf_op jit(solution)/shard_map/ppermute | solution.py:35
  48.8 8.6 %collective-permute-start.11 = (bf16[40,1024]{1,0:T(8,128)(2,1)S(1)}, bf16[40,1024]{1,0:T(8,128)(2,1)S(1)}, u32[]{:S(2)}, u32[]{:S(2)}) collective-permute-start(bf16[40,1024]{1,0:T(8,128)(2,1)S(1)} %shard_map.86.refs_0_), channel_id=1, source_target_pairs={{128,0},{192,64},{0,128},{64,192},{129,1},{193,65},{1,129},{65,193... | collective-permute-start | bytes 245768 | tf_op jit(solution)/shard_map/ppermute | solution.py:35
  53.0 7.1 %collective-permute-start.10 = (bf16[40,1024]{1,0:T(8,128)(2,1)S(1)}, bf16[40,1024]{1,0:T(8,128)(2,1)S(1)}, u32[]{:S(2)}, u32[]{:S(2)}) collective-permute-start(bf16[40,1024]{1,0:T(8,128)(2,1)S(1)} %shard_map.86.refs_0_), channel_id=1, source_target_pairs={{64,0},{128,64},{192,128},{0,192},{65,1},{129,65},{193,129},{1,193... | collective-permute-start | bytes 245768 | tf_op jit(solution)/shard_map/ppermute | solution.py:35
  61.1 31.7 %copy-start = (bf16[1,4096,384]{2,1,0:T(8,128)(2,1)S(1)}, bf16[1,4096,384]{2,1,0:T(8,128)(2,1)}, u32[]{:S(2)}) copy-start(bf16[1,4096,384]{2,1,0:T(8,128)(2,1)} %w_gate.5) | copy-start | bytes 9437188
  92.9 4.2 %collective-permute-start.13 = (bf16[256,4096]{1,0:T(8,128)(2,1)S(1)}, bf16[256,4096]{1,0:T(8,128)(2,1)S(1)}, u32[]{:S(2)}, u32[]{:S(2)}) collective-permute-start(bf16[256,4096]{1,0:T(8,128)(2,1)S(1)} %bitcast.8), channel_id=1, source_target_pairs={{0,1},{1,0},{2,3},{3,2},{4,5},{5,4},{6,7},{7,6},{8,9},{9,8},{10,11... | collective-permute-start | bytes 6291464 | tf_op jit(solution)/shard_map/ppermute | solution.py:31
  99.2 2.9 %collective-permute-start.15 = (bf16[128,4096]{1,0:T(8,128)(2,1)S(1)}, bf16[128,4096]{1,0:T(8,128)(2,1)S(1)}, u32[]{:S(2)}, u32[]{:S(2)}) collective-permute-start(bf16[128,4096]{1,0:T(8,128)(2,1)S(1)} %shard_map.90), channel_id=1, source_target_pairs={{0,1},{1,0},{2,3},{3,2},{4,5},{5,4},{6,7},{7,6},{8,9},{9,8},{10,11... | collective-permute-start | bytes 3145736 | tf_op jit(solution)/shard_map/ppermute | solution.py:31
  101.7 2.7 %collective-permute-start.14 = (bf16[128,4096]{1,0:T(8,128)(2,1)S(1)}, bf16[128,4096]{1,0:T(8,128)(2,1)S(1)}, u32[]{:S(2)}, u32[]{:S(2)}) collective-permute-start(bf16[128,4096]{1,0:T(8,128)(2,1)S(1)} %shard_map.89), channel_id=1, source_target_pairs={{0,1},{1,0},{2,3},{3,2},{4,5},{5,4},{6,7},{7,6},{8,9},{9,8},{10,11... | collective-permute-start | bytes 3145736 | tf_op jit(solution)/shard_map/ppermute | solution.py:31
  138.5 9.0 %collective-permute-start.16 = (bf16[8,4096]{1,0:T(8,128)(2,1)S(1)}, bf16[8,4096]{1,0:T(8,128)(2,1)S(1)}, u32[]{:S(2)}, u32[]{:S(2)}) collective-permute-start(bf16[8,4096]{1,0:T(8,128)(2,1)S(1)} %get-tuple-element.34), channel_id=1, source_target_pairs={{128,0},{192,64},{0,128},{64,192},{129,1},{193,65},{1,129},{65,193... | collective-permute-start | bytes 196616 | tf_op jit(solution)/shard_map/ppermute | solution.py:35
  140.4 7.2 %collective-permute-start.17 = (bf16[8,4096]{1,0:T(8,128)(2,1)S(1)}, bf16[8,4096]{1,0:T(8,128)(2,1)S(1)}, u32[]{:S(2)}, u32[]{:S(2)}) collective-permute-start(bf16[8,4096]{1,0:T(8,128)(2,1)S(1)} %get-tuple-element.35), channel_id=1, source_target_pairs={{192,0},{0,64},{64,128},{128,192},{193,1},{1,65},{65,129},{129,193... | collective-permute-start | bytes 196616 | tf_op jit(solution)/shard_map/ppermute | solution.py:35
  144.6 6.8 %collective-permute-start.18 = (bf16[8,4096]{1,0:T(8,128)(2,1)S(1)}, bf16[8,4096]{1,0:T(8,128)(2,1)S(1)}, u32[]{:S(2)}, u32[]{:S(2)}) collective-permute-start(bf16[8,4096]{1,0:T(8,128)(2,1)S(1)} %get-tuple-element.36), channel_id=1, source_target_pairs={{64,0},{128,64},{192,128},{0,192},{65,1},{129,65},{193,129},{1,193... | collective-permute-start | bytes 196616 | tf_op jit(solution)/shard_map/ppermute | solution.py:35
  (3 other events, 24.5 us)

commit v9 on v7

--- a/solution.py
+++ b/solution.py
@@ -10,16 +10,19 @@
 
 TOPK = 8
 CAP = 2
+ROWS = 8
 LANES = 128
 F32, BF16 = jnp.float32, jnp.bfloat16
 
-FINE = ("z", "xl", "xh", "y", "c")
-SIZES = (8, 2, 2, 4, 2)
-EXPERT = ("z", "xl")
+FINE = ("zh", "zl", "xl", "xh", "y", "c")
+SIZES = (4, 2, 2, 2, 4, 2)
+EXPERT = ("zh", "zl", "xl")
 TENSOR = ("xh", "y", "c")
 SPREAD = ("xh", "y")
-PLANE = ("xl", "xh", "y")
-NZ = 8
+PLANE = ("y", "xh", "xl")
+PEERS = ("y", "xh", "xl", "zl")
+RING = ("zh", "zl")
+NZ, NH = 8, 4
 MIB = 1 << 20
 
 VMEM = pl.BlockSpec(memory_space=pltpu.VMEM)
@@ -30,8 +33,12 @@
     return lax.ppermute(x, axis, [(0, 1), (1, 0)])
 
 
-def fetch(x, hop):
-    return lax.ppermute(x, "z", [((i + hop) % NZ, i) for i in range(NZ)])
+def fetch(x, hop, axis=RING, size=NZ):
+    return lax.ppermute(x, axis, [((i + hop) % size, i) for i in range(size)])
+
+
+def fetch_pair(x, hop):
+    return fetch(x, hop, "zh", NH)
 
 
 def gather_z(x):
@@ -50,12 +57,12 @@
     return jnp.dot(a, b, preferred_element_type=F32)
 
 
-def where(place):
+def where_am_i(place):
     return lax.div(place[0], 4), lax.rem(lax.div(place[0], 2), 2), lax.rem(place[0], 2)
 
 
 def stage_kernel(place, own, other, context, rhs, held):
-    _, xl, _ = where(place)
+    _, xl, _ = where_am_i(place)
     cols = own.shape[1]
     rhs[:, pl.ds(pl.multiple_of(xl * cols, LANES), cols)] = own[...]
     rhs[:, pl.ds(pl.multiple_of((1 - xl) * cols, LANES), cols)] = other[...]
@@ -77,7 +84,7 @@
 
 def project_kernel(place, *refs):
     blocks, (rhs, give, keep, held) = refs[:NZ], refs[NZ:]
-    _, _, core = where(place)
+    _, _, core = where_am_i(place)
     lhs = jnp.concatenate([b[...] for b in blocks], axis=0)
     total = dot(lhs, rhs[...])
     spread = give.shape[0]
@@ -119,7 +126,7 @@
 
 
 def settle_kernel(place, parts, ids, gates, out, held):
-    z, _, _ = where(place)
+    z, _, _ = where_am_i(place)
     tokens = parts.shape[1]
     rows = tokens // NZ
     total = parts[0].astype(F32)
@@ -152,11 +159,29 @@
     )(place, parts, ids, gates)
 
 
+def routed(listed, label, spot):
+    tokens, rows = listed.shape[0], ROWS
+    match = jnp.zeros(label.shape, F32)
+    gate = jnp.zeros(label.shape, F32)
+    for k in range(TOPK):
+        hit = listed[:, k : k + 1] == label.astype(F32)
+        value = listed[:, TOPK + k : TOPK + k + 1] + listed[:, 2 * TOPK + k : 2 * TOPK + k + 1]
+        match += jnp.where(hit, 1.0, 0.0)
+        gate += jnp.where(hit, value, 0.0)
+    before = lax.broadcasted_iota(jnp.int32, (tokens, tokens), 1)
+    after = lax.broadcasted_iota(jnp.int32, (tokens, tokens), 0)
+    earlier = (before // rows == after // rows) & (before < after)
+    rank = dot(jnp.where(earlier, 1.0, 0.0).astype(BF16), match.astype(BF16))
+    placed = (match > 0.5) & (rank.astype(jnp.int32) == spot)
+    return placed, gate
+
+
 def place_kernel(place, *refs):
-    blocks, (gain, sent, own, high, low, stream, notes, mass) = refs[:NZ], refs[NZ:]
-    z, _, _ = where(place)
+    blocks, (gain, sent, own, high, low, stream, notes) = refs[:NZ], refs[NZ:]
+    z, _, _ = where_am_i(place)
+    pair, parity = lax.div(z, 2), lax.rem(z, 2)
     tokens, width = stream.shape
-    rows, wide = tokens // NZ, width // NZ
+    rows, wide = ROWS, width // NZ
     lanes = sent.shape[0]
     for hop in range(NZ):
         there = lax.rem(z + hop, NZ)
@@ -166,69 +191,58 @@
         notes[pl.ds(pl.multiple_of(there * rows, rows), rows), :] = block[tokens:, :LANES]
     own[...] = stream[pl.ds(pl.multiple_of(z * rows, rows), rows), :]
 
-    slots = NZ * CAP
     lane = lax.broadcasted_iota(jnp.int32, (tokens, lanes), 1)
-    token = lax.broadcasted_iota(jnp.int32, (tokens, lanes), 0)
-    label = (z * (lanes // (2 * slots)) + lane // (2 * slots)).astype(F32)
-    listed = notes[...]
-    match = jnp.zeros((tokens, lanes), F32)
-    gate = jnp.zeros((tokens, lanes), F32)
-    for k in range(TOPK):
-        hit = listed[:, k : k + 1] == label
-        value = listed[:, TOPK + k : TOPK + k + 1] + listed[:, 2 * TOPK + k : 2 * TOPK + k + 1]
-        match += jnp.where(hit, 1.0, 0.0)
-        gate += jnp.where(hit, value, 0.0)
-    before = lax.broadcasted_iota(jnp.int32, (tokens, tokens), 1)
-    after = lax.broadcasted_iota(jnp.int32, (tokens, tokens), 0)
-    earlier = (before // rows == after // rows) & (before < after)
-    rank = dot(jnp.where(earlier, 1.0, 0.0).astype(BF16), match.astype(BF16))
-    slot = (token // rows) * CAP + rank.astype(jnp.int32)
-    placed = (match > 0.5) & (slot == lane % slots) & (rank < CAP - 0.5)
+    from_z = lax.broadcasted_iota(jnp.int32, (tokens, lanes), 0) // rows
+    slot, device = lane % (NZ * CAP), lane // (NZ * CAP)
+    label = (z * 2 + device % 2) * 4 + (device // 2) % 2 * 2 + device // 8
+    spot = slot - (from_z % 2) * (NH * CAP) - (from_z // 2) * CAP
+    placed, _ = routed(notes[...], label, spot)
     spots = jnp.transpose(jnp.where(placed, 1.0, 0.0)).astype(BF16)
 
-    mass[...] = jnp.where(placed, gate, 0.0)
-
-    weight = jnp.concatenate(
-        [
-            mass[pl.ds(pl.multiple_of(lax.rem(z + hop, NZ) * rows, rows), rows), :]
-            for hop in range(NZ)
-        ],
+    half = tokens // 2
+    near = [lax.rem(pair + hop, NH) for hop in range(NH)]
+    listed = jnp.concatenate(
+        [notes[pl.ds(pl.multiple_of((2 * n + parity) * rows, rows), rows), :] for n in near],
         axis=0,
     )
+    lane = lax.broadcasted_iota(jnp.int32, (half, lanes), 1)
+    hop = lax.broadcasted_iota(jnp.int32, (half, lanes), 0) // rows
+    slot, peer = lane % (NH * CAP), lane // (NH * CAP)
+    label = ((pair * 2 + peer % 2) * 2 + (peer // 2) % 2) * 4 + (peer // 4) % 2 * 2 + peer // 16
+    placed, gate = routed(listed, label, slot - ((pair + hop) % NH) * CAP)
+    weight = jnp.where(placed, gate, 0.0)
     top = weight.astype(BF16)
     high[...] = top
     low[...] = (weight - top.astype(F32)).astype(BF16)
 
     square = jnp.zeros((tokens, 1), F32)
-    for hop in range(NZ):
-        part = stream[:, hop * wide : (hop + 1) * wide]
+    for i in range(NZ):
+        part = stream[:, i * wide : (i + 1) * wide]
         square += jnp.sum(part * part, axis=-1, keepdims=True)
     scale = lax.rsqrt(square / width + 1e-06)
-    for hop in range(NZ):
-        at = slice(hop * wide, (hop + 1) * wide)
+    for i in range(NZ):
+        at = slice(i * wide, (i + 1) * wide)
         normed = (stream[:, at] * scale * gain[:, at]).astype(BF16)
         sent[:, at] = dot(spots, normed).astype(BF16)
 
 
 def place_rows(place, blocks, gain, plane):
-    rows = blocks[0].shape[0] // (NZ + 1)
-    tokens = NZ * rows
+    tokens = NZ * ROWS
     width = NZ * blocks[0].shape[1]
     lanes = plane * NZ * CAP
     return pl.pallas_call(
         place_kernel,
         out_shape=(
             jax.ShapeDtypeStruct((lanes, width), BF16),
-            jax.ShapeDtypeStruct((rows, width), F32),
-            jax.ShapeDtypeStruct((tokens, lanes), BF16),
-            jax.ShapeDtypeStruct((tokens, lanes), BF16),
+            jax.ShapeDtypeStruct((ROWS, width), F32),
+            jax.ShapeDtypeStruct((tokens // 2, lanes), BF16),
+            jax.ShapeDtypeStruct((tokens // 2, lanes), BF16),
         ),
         in_specs=[SMEM] + [VMEM] * (NZ + 1),
         out_specs=(VMEM,) * 4,
         scratch_shapes=[
             pltpu.VMEM((tokens, width), F32),
             pltpu.VMEM((tokens, LANES), F32),
-            pltpu.VMEM((tokens, lanes), F32),
         ],
         compiler_params=params(32),
     )(place, *blocks, gain.reshape(1, width))
@@ -296,7 +310,7 @@
         piece = back[:, at]
         mix = dot(high[...], piece) + dot(low[...], piece)
         base[:, at] = own[:, at] + mix[:rows]
-        for hop in range(1, NZ):
+        for hop in range(1, NH):
             outs[hop - 1][:, at] = mix[hop * rows : (hop + 1) * rows].astype(BF16)
 
 
@@ -305,18 +319,18 @@
     return pl.pallas_call(
         combine_kernel,
         out_shape=(jax.ShapeDtypeStruct((rows, width), F32),)
-        + (jax.ShapeDtypeStruct((rows, width), BF16),) * (NZ - 1),
+        + (jax.ShapeDtypeStruct((rows, width), BF16),) * (NH - 1),
         in_specs=[VMEM] * 4,
-        out_specs=(VMEM,) * NZ,
+        out_specs=(VMEM,) * NH,
         compiler_params=params(32),
     )(high, low, back, own)
 
 
 def on_device(context, proj_weight, norm_gain, expert_ids, gate_values, w_gate, w_up, w_down):
-    zi, xli, ci = (lax.axis_index(a).astype(jnp.int32) for a in ("z", "xl", "c"))
+    zi, xli, ci = (lax.axis_index(a).astype(jnp.int32) for a in (RING, "xl", "c"))
     place = (4 * zi + 2 * xli + ci).reshape(1)
     n_spread = lax.axis_size(SPREAD)
-    n_plane = lax.axis_size(PLANE)
+    n_plane, n_peers = lax.axis_size(PLANE), lax.axis_size(PEERS)
 
     rhs, held = stage(place, proj_weight, swap(proj_weight, "xl"), context)
     give, keep = project(place, [held] + gather_z(context)[1:], rhs, n_spread)
@@ -336,12 +350,12 @@
     theirs, mine_out = lax.optimization_barrier((theirs, mine_out))
     half = count // 2
     top, bottom = (swap(expert_rows(theirs, at, half, *weights), "c") for at in (0, half))
-    summed = add_rows(mine_out, bottom, add_rows(mine_out, top)).reshape(n_plane, -1, width)
-    back = lax.all_to_all(summed, PLANE, 0, 0, tiled=True).reshape(-1, width)
+    summed = add_rows(mine_out, bottom, add_rows(mine_out, top)).reshape(n_peers, -1, width)
+    back = lax.all_to_all(summed, PEERS, 0, 0, tiled=True).reshape(-1, width)
 
     total, *blocks = combine(high, low, back, own)
-    for hop in (2, 6, 3, 5, 4, 1, 7):
-        total += fetch(blocks[hop - 1], -hop).astype(F32)
+    for hop in (2, 1, 3):
+        total += fetch_pair(blocks[hop - 1], -hop).astype(F32)
     return total.astype(BF16)
 
 

time: 155 us -> 150 us (0.968); the launches traced: 155 us -> 148 us
  starting transfers between devices: 45.6 us -> 37.1 us
  waiting for transfers between devices: 17.1 us -> 18.7 us
    ppermute x21 -> x17, starting transfers between devices: 44 us -> 35.5 us  [fetch(): return lax.ppermute(x, axis, [((i + hop) % size, i) for i in range(size)])]
    ppermute x21 -> x17, waiting for transfers between devices: 12.8 us -> 14.4 us  [fetch(): return lax.ppermute(x, axis, [((i + hop) % size, i) for i in range(size)])]
  transfers between devices with their start and end apart: 26 -> 22, of which waited for: 12 -> 13; matrix products, arithmetic and copies ran while one was open for 0% -> 0% of each run, Pallas kernels for 4% -> 4%
where the time goes in v9:
time: 150 us; the launch traced here: 148 us
  blocking collectives  77.7 us (52%)
  starting transfers between devices  37.1 us (25%)
  waiting for transfers between devices  18.7 us (12%)
  Pallas kernels  11.9 us (8%)
  local copies, waits for them, and re-layouts  1.88 us (1%)
    ppermute x17, starting transfers between devices, fetch(): return lax.ppermute(x, axis, [((i + hop) % size, i) for i in range(size)])  35.5 us
    all_to_all x1, blocking collectives, on_device(): back = lax.all_to_all(summed, PEERS, 0, 0, tiled=True).reshape(-1, width)  32.7 us
    all_to_all x1, blocking collectives, on_device(): lax.all_to_all(sent.reshape(n_plane, -1, width), PLANE, 0, 0, tiled=True)  28.5 us
    all_to_all x1, blocking collectives, on_device(): partial = lax.all_to_all(partial, SPREAD, 0, 0, tiled=True)  16.4 us
    ppermute x17, waiting for transfers between devices, fetch(): return lax.ppermute(x, axis, [((i + hop) % size, i) for i in range(size)])  14.4 us
    pallas_call x3, Pallas kernels, expert_rows(): pl.pallas_call(functools.partial(expert_kernel, first), out_shape=jax.Sha...  8.25 us
    ppermute x5, waiting for transfers between devices, swap(): return lax.ppermute(x, axis, [(0, 1), (1, 0)])  4.32 us
  transfers between devices with their start and end apart: 22, of which 13 were waited for; matrix products, arithmetic and copies ran while one was open for 0% of the time, Pallas kernels for 4%

profile of v9, /device:TPU:6, one launch (start us, length us, event | category | flops | bytes accessed | tf_op | source)
XLA Modules:
  0.0 148.1 jit_solution(7717483579233715150)
XLA Ops:
  0.8 6.3 %collective-permute-start.2 = (bf16[128,512]{1,0:T(8,128)(2,1)}, bf16[128,512]{1,0:T(8,128)(2,1)S(1)}, u32[]{:S(2)}, u32[]{:S(2)}) collective-permute-start(bf16[128,512]{1,0:T(8,128)(2,1)} %context.1), channel_id=1, source_target_pairs={{64,0},{96,32},{128,64},{160,96},{192,128},{224,160},{0,192},{32,2... | collective-permute-start | bytes 393224 | tf_op jit(solution)/shard_map/ppermute | solution.py:37
  7.1 3.7 %collective-permute-start.1 = (bf16[128,512]{1,0:T(8,128)(2,1)}, bf16[128,512]{1,0:T(8,128)(2,1)S(1)}, u32[]{:S(2)}, u32[]{:S(2)}) collective-permute-start(bf16[128,512]{1,0:T(8,128)(2,1)} %context.1), channel_id=1, source_target_pairs={{32,0},{64,32},{96,64},{128,96},{160,128},{192,160},{224,192},{0,2... | collective-permute-start | bytes 393224 | tf_op jit(solution)/shard_map/ppermute | solution.py:37
  10.8 2.7 %collective-permute-done.2.refs_2_ = bf16[128,512]{1,0:T(8,128)(2,1)S(1)} collective-permute-done((bf16[128,512]{1,0:T(8,128)(2,1)}, bf16[128,512]{1,0:T(8,128)(2,1)S(1)}, u32[]{:S(2)}, u32[]{:S(2)}) %collective-permute-start.2) | collective-permute-done | bytes 131104 | tf_op jit(solution)/shard_map/ppermute | solution.py:37
  13.5 4.6 %collective-permute-start.4 = (bf16[128,512]{1,0:T(8,128)(2,1)S(1)}, bf16[128,512]{1,0:T(8,128)(2,1)S(1)}, u32[]{:S(2)}, u32[]{:S(2)}) collective-permute-start(bf16[128,512]{1,0:T(8,128)(2,1)S(1)} %collective-permute-done.2.refs_2_), channel_id=1, source_target_pairs={{64,0},{96,32},{128,64},{160,96},{192,128},{224,160},{0,192},{32,2... | collective-permute-start | bytes 393224 | tf_op jit(solution)/shard_map/ppermute | solution.py:37
  18.2 2.0 %collective-permute-start.6 = (bf16[128,512]{1,0:T(8,128)(2,1)S(1)}, bf16[128,512]{1,0:T(8,128)(2,1)S(1)}, u32[]{:S(2)}, u32[]{:S(2)}) collective-permute-start(bf16[128,512]{1,0:T(8,128)(2,1)S(1)} %collective-permute-done.5.refs_6_), channel_id=1, source_target_pairs={{224,0},{0,32},{32,64},{64,96},{96,128},{128,160},{160,192},{192,2... | collective-permute-start | bytes 393224 | tf_op jit(solution)/shard_map/ppermute | solution.py:37
  22.5 2.3 %collective-permute-done.3.refs_3_ = bf16[128,512]{1,0:T(8,128)(2,1)S(1)} collective-permute-done((bf16[128,512]{1,0:T(8,128)(2,1)S(1)}, bf16[128,512]{1,0:T(8,128)(2,1)S(1)}, u32[]{:S(2)}, u32[]{:S(2)}) %collective-permute-start.3) | collective-permute-done | bytes 131104 | tf_op jit(solution)/shard_map/ppermute | solution.py:37
  25.6 1.9 %collective-permute-done.8.got = bf16[8,64,512]{2,1,0:T(8,128)(2,1)S(1)} collective-permute-done((bf16[8,64,512]{2,1,0:T(8,128)(2,1)S(1)}, bf16[8,64,512]{2,1,0:T(8,128)(2,1)S(1)}, u32[]{:S(2)}, u32[]{:S(2)}) %collective-permute-start.8) | collective-permute-done | bytes 524320 | tf_op jit(solution)/shard_map/ppermute | solution.py:33
  27.7 16.4 %all_to_all.15.parts = bf16[8,64,512]{2,1,0:T(8,128)(2,1)S(1)} all-to-all(bf16[8,64,512]{2,1,0:T(8,128)(2,1)S(1)} %shard_map.84), channel_id=1, replica_groups=mesh['zh'=4,'zl'=2,'xl'=2,'xh'=2,'y'=4,'c'=2] {'xh','y'}, dimensions={0} | all-to-all | bytes 1048576 | tf_op jit(solution)/shard_map/all_to_all | solution.py:338
  44.8 3.7 %collective-permute-start.10 = (bf16[72,512]{1,0:T(8,128)(2,1)S(1)}, bf16[72,512]{1,0:T(8,128)(2,1)S(1)}, u32[]{:S(2)}, u32[]{:S(2)}) collective-permute-start(bf16[72,512]{1,0:T(8,128)(2,1)S(1)} %shard_map.85.refs_0_), channel_id=1, source_target_pairs={{64,0},{96,32},{128,64},{160,96},{192,128},{224,160},{0,192},{32,2... | collective-permute-start | bytes 221192 | tf_op jit(solution)/shard_map/ppermute | solution.py:37
  48.8 2.9 %collective-permute-start.9 = (bf16[72,512]{1,0:T(8,128)(2,1)S(1)}, bf16[72,512]{1,0:T(8,128)(2,1)S(1)}, u32[]{:S(2)}, u32[]{:S(2)}) collective-permute-start(bf16[72,512]{1,0:T(8,128)(2,1)S(1)} %shard_map.85.refs_0_), channel_id=1, source_target_pairs={{32,0},{64,32},{96,64},{128,96},{160,128},{192,160},{224,192},{0,2... | collective-permute-start | bytes 221192 | tf_op jit(solution)/shard_map/ppermute | solution.py:37
  51.8 4.5 %collective-permute-start.12 = (bf16[72,512]{1,0:T(8,128)(2,1)S(1)}, bf16[72,512]{1,0:T(8,128)(2,1)S(1)}, u32[]{:S(2)}, u32[]{:S(2)}) collective-permute-start(bf16[72,512]{1,0:T(8,128)(2,1)S(1)} %collective-permute-done.10.refs_2_), channel_id=1, source_target_pairs={{64,0},{96,32},{128,64},{160,96},{192,128},{224,160},{0,192},{32,2... | collective-permute-start | bytes 221192 | tf_op jit(solution)/shard_map/ppermute | solution.py:37
  57.4 1.3 collective-permute-done.12.refs_4_
  58.7 2.0 %collective-permute-done.11.refs_3_ = bf16[72,512]{1,0:T(8,128)(2,1)S(1)} collective-permute-done((bf16[72,512]{1,0:T(8,128)(2,1)S(1)}, bf16[72,512]{1,0:T(8,128)(2,1)S(1)}, u32[]{:S(2)}, u32[]{:S(2)}) %collective-permute-start.11) | collective-permute-done | bytes 73760 | tf_op jit(solution)/shard_map/ppermute | solution.py:37
  61.9 28.5 %all_to_all.16 = bf16[16,16,4096]{2,1,0:T(8,128)(2,1)S(1)} all-to-all(bf16[16,16,4096]{2,1,0:T(8,128)(2,1)S(1)} %bitcast.10), channel_id=1, replica_groups=mesh['zh'=4,'zl'=2,'xl'=2,'xh'=2,'y'=4,'c'=2] {'y','xh','xl'}, dimensions={0} | all-to-all | bytes 4194304 | tf_op jit(solution)/shard_map/all_to_all | solution.py:343
  90.5 3.8 %shard_map.87.mine = bf16[256,4096]{1,0:T(8,128)(2,1)S(1)} custom-call(bf16[256,4096]{1,0:T(8,128)(2,1)S(1)} %bitcast.9, bf16[1,4096,384]{2,1,0:T(8,128)(2,1)S(1)} %copy-done, bf16[1,4096,384]{2,1,0:T(8,128)(2,1)S(1)} %copy-done.1, bf16[1,384,4096]{2,1,0:T(8,128)(2,1)S(1)} %copy-done.2), custom_call_target="tpu_custom_call" | custom-call | flops 2415919104 | bytes 13631488 | tf_op jit(solution)/shard_map/pallas_call | solution.py:270
  94.6 2.2 %shard_map.89 = bf16[128,4096]{1,0:T(8,128)(2,1)S(1)} custom-call(bf16[256,4096]{1,0:T(8,128)(2,1)S(1)} %collective-permute-done.16.rows, bf16[1,4096,384]{2,1,0:T(8,128)(2,1)S(1)} %copy-done, bf16[1,4096,384]{2,1,0:T(8,128)(2,1)S(1)} %copy-done.1, bf16[1,384,4096]{2,1,0:T(8,128)(2,1)S(1)} %copy-done.2), custom_call_target="tpu_custom_call" | custom-call | flops 1207959552 | bytes 11534336 | tf_op jit(solution)/shard_map/pallas_call | solution.py:270
  97.1 2.2 %shard_map.88 = bf16[128,4096]{1,0:T(8,128)(2,1)S(1)} custom-call(bf16[256,4096]{1,0:T(8,128)(2,1)S(1)} %collective-permute-done.16.rows, bf16[1,4096,384]{2,1,0:T(8,128)(2,1)S(1)} %copy-done, bf16[1,4096,384]{2,1,0:T(8,128)(2,1)S(1)} %copy-done.1, bf16[1,384,4096]{2,1,0:T(8,128)(2,1)S(1)} %copy-done.2), custom_call_target="tpu_custom_call" | custom-call | flops 1207959552 | bytes 11534336 | tf_op jit(solution)/shard_map/pallas_call | solution.py:270
  100.0 2.1 %collective-permute-done.17.part = bf16[128,4096]{1,0:T(8,128)(2,1)S(1)} collective-permute-done((bf16[128,4096]{1,0:T(8,128)(2,1)S(1)}, bf16[128,4096]{1,0:T(8,128)(2,1)S(1)}, u32[]{:S(2)}, u32[]{:S(2)}) %collective-permute-start.17) | collective-permute-done | bytes 1048608 | tf_op jit(solution)/shard_map/ppermute | solution.py:33
  102.4 32.7 %all_to_all.17 = bf16[32,8,4096]{2,1,0:T(8,128)(2,1)S(1)} all-to-all(bf16[32,8,4096]{2,1,0:T(8,128)(2,1)S(1)} %bitcast.6), channel_id=1, replica_groups=mesh['zh'=4,'zl'=2,'xl'=2,'xh'=2,'y'=4,'c'=2] {'y','xh','xl','zl'}, dimensions={0} | all-to-all | bytes 4194304 | tf_op jit(solution)/shard_map/all_to_all | solution.py:354
  135.9 2.8 %collective-permute-start.19 = (bf16[8,4096]{1,0:T(8,128)(2,1)S(1)}, bf16[8,4096]{1,0:T(8,128)(2,1)S(1)}, u32[]{:S(2)}, u32[]{:S(2)}) collective-permute-start(bf16[8,4096]{1,0:T(8,128)(2,1)S(1)} %get-tuple-element.30), channel_id=1, source_target_pairs={{128,0},{192,64},{0,128},{64,192},{129,1},{193,65},{1,129},{65,193... | collective-permute-start | bytes 196616 | tf_op jit(solution)/shard_map/ppermute | solution.py:37
  138.7 2.9 %collective-permute-start.20 = (bf16[8,4096]{1,0:T(8,128)(2,1)S(1)}, bf16[8,4096]{1,0:T(8,128)(2,1)S(1)}, u32[]{:S(2)}, u32[]{:S(2)}) collective-permute-start(bf16[8,4096]{1,0:T(8,128)(2,1)S(1)} %get-tuple-element.31), channel_id=1, source_target_pairs={{192,0},{0,64},{64,128},{128,192},{193,1},{1,65},{65,129},{129,193... | collective-permute-start | bytes 196616 | tf_op jit(solution)/shard_map/ppermute | solution.py:37
  142.8 1.7 %collective-permute-done.19 = bf16[8,4096]{1,0:T(8,128)(2,1)S(1)} collective-permute-done((bf16[8,4096]{1,0:T(8,128)(2,1)S(1)}, bf16[8,4096]{1,0:T(8,128)(2,1)S(1)}, u32[]{:S(2)}, u32[]{:S(2)}) %collective-permute-start.19) | collective-permute-done | bytes 65568 | tf_op jit(solution)/shard_map/ppermute | solution.py:37
  144.5 1.5 %collective-permute-done.20 = bf16[8,4096]{1,0:T(8,128)(2,1)S(1)} collective-permute-done((bf16[8,4096]{1,0:T(8,128)(2,1)S(1)}, bf16[8,4096]{1,0:T(8,128)(2,1)S(1)}, u32[]{:S(2)}, u32[]{:S(2)}) %collective-permute-start.20) | collective-permute-done | bytes 65568 | tf_op jit(solution)/shard_map/ppermute | solution.py:37
  146.0 1.4 collective-permute-done.21
  (51 shorter events, 11.7 us)
Async XLA Ops:
  0.0 18.2 %collective-permute-start = (bf16[512,256]{1,0:T(8,128)(2,1)}, bf16[512,256]{1,0:T(8,128)(2,1)S(1)}, u32[]{:S(2)}, u32[]{:S(2)}) collective-permute-start(bf16[512,256]{1,0:T(8,128)(2,1)} %own.1), channel_id=1, source_target_pairs={{0,16},{16,0},{1,17},{17,1},{2,18},{18,2},{3,19},{19,3},{4,20},{20... | collective-permute-start | bytes 786440 | tf_op jit(solution)/shard_map/ppermute | solution.py:33
  0.8 12.7 %collective-permute-start.2 = (bf16[128,512]{1,0:T(8,128)(2,1)}, bf16[128,512]{1,0:T(8,128)(2,1)S(1)}, u32[]{:S(2)}, u32[]{:S(2)}) collective-permute-start(bf16[128,512]{1,0:T(8,128)(2,1)} %context.1), channel_id=1, source_target_pairs={{64,0},{96,32},{128,64},{160,96},{192,128},{224,160},{0,192},{32,2... | collective-permute-start | bytes 393224 | tf_op jit(solution)/shard_map/ppermute | solution.py:37
  7.1 11.0 %collective-permute-start.5 = (bf16[128,512]{1,0:T(8,128)(2,1)}, bf16[128,512]{1,0:T(8,128)(2,1)S(1)}, u32[]{:S(2)}, u32[]{:S(2)}) collective-permute-start(bf16[128,512]{1,0:T(8,128)(2,1)} %context.1), channel_id=1, source_target_pairs={{192,0},{224,32},{0,64},{32,96},{64,128},{96,160},{128,192},{160,2... | collective-permute-start | bytes 393224 | tf_op jit(solution)/shard_map/ppermute | solution.py:37
  7.1 15.0 %collective-permute-start.1 = (bf16[128,512]{1,0:T(8,128)(2,1)}, bf16[128,512]{1,0:T(8,128)(2,1)S(1)}, u32[]{:S(2)}, u32[]{:S(2)}) collective-permute-start(bf16[128,512]{1,0:T(8,128)(2,1)} %context.1), channel_id=1, source_target_pairs={{32,0},{64,32},{96,64},{128,96},{160,128},{192,160},{224,192},{0,2... | collective-permute-start | bytes 393224 | tf_op jit(solution)/shard_map/ppermute | solution.py:37
  10.8 11.3 %collective-permute-start.7 = (bf16[128,512]{1,0:T(8,128)(2,1)}, bf16[128,512]{1,0:T(8,128)(2,1)S(1)}, u32[]{:S(2)}, u32[]{:S(2)}) collective-permute-start(bf16[128,512]{1,0:T(8,128)(2,1)} %context.1), channel_id=1, source_target_pairs={{224,0},{0,32},{32,64},{64,96},{96,128},{128,160},{160,192},{192,2... | collective-permute-start | bytes 393224 | tf_op jit(solution)/shard_map/ppermute | solution.py:37
  13.5 9.0 %collective-permute-start.4 = (bf16[128,512]{1,0:T(8,128)(2,1)S(1)}, bf16[128,512]{1,0:T(8,128)(2,1)S(1)}, u32[]{:S(2)}, u32[]{:S(2)}) collective-permute-start(bf16[128,512]{1,0:T(8,128)(2,1)S(1)} %collective-permute-done.2.refs_2_), channel_id=1, source_target_pairs={{64,0},{96,32},{128,64},{160,96},{192,128},{224,160},{0,192},{32,2... | collective-permute-start | bytes 393224 | tf_op jit(solution)/shard_map/ppermute | solution.py:37
  18.2 6.6 %collective-permute-start.3 = (bf16[128,512]{1,0:T(8,128)(2,1)S(1)}, bf16[128,512]{1,0:T(8,128)(2,1)S(1)}, u32[]{:S(2)}, u32[]{:S(2)}) collective-permute-start(bf16[128,512]{1,0:T(8,128)(2,1)S(1)} %collective-permute-done.2.refs_2_), channel_id=1, source_target_pairs={{32,0},{64,32},{96,64},{128,96},{160,128},{192,160},{224,192},{0,2... | collective-permute-start | bytes 393224 | tf_op jit(solution)/shard_map/ppermute | solution.py:37
  18.2 6.6 %collective-permute-start.6 = (bf16[128,512]{1,0:T(8,128)(2,1)S(1)}, bf16[128,512]{1,0:T(8,128)(2,1)S(1)}, u32[]{:S(2)}, u32[]{:S(2)}) collective-permute-start(bf16[128,512]{1,0:T(8,128)(2,1)S(1)} %collective-permute-done.5.refs_6_), channel_id=1, source_target_pairs={{224,0},{0,32},{32,64},{64,96},{96,128},{128,160},{160,192},{192,2... | collective-permute-start | bytes 393224 | tf_op jit(solution)/shard_map/ppermute | solution.py:37
  24.8 65.6 %copy-start.2 = (bf16[1,384,4096]{2,1,0:T(8,128)(2,1)S(1)}, bf16[1,384,4096]{2,1,0:T(8,128)(2,1)}, u32[]{:S(2)}) copy-start(bf16[1,384,4096]{2,1,0:T(8,128)(2,1)} %w_down.5) | copy-start | bytes 9437188
  25.5 2.0 %collective-permute-start.8 = (bf16[8,64,512]{2,1,0:T(8,128)(2,1)S(1)}, bf16[8,64,512]{2,1,0:T(8,128)(2,1)S(1)}, u32[]{:S(2)}, u32[]{:S(2)}) collective-permute-start(bf16[8,64,512]{2,1,0:T(8,128)(2,1)S(1)} %get-tuple-element.22), channel_id=1, source_target_pairs={{0,1},{1,0},{2,3},{3,2},{4,5},{5,4},{6,7},{7,6},{8,9},{9,8},{10,11... | collective-permute-start | bytes 1572872 | tf_op jit(solution)/shard_map/ppermute | solution.py:33
  27.6 62.8 %copy-start.1 = (bf16[1,4096,384]{2,1,0:T(8,128)(2,1)S(1)}, bf16[1,4096,384]{2,1,0:T(8,128)(2,1)}, u32[]{:S(2)}) copy-start(bf16[1,4096,384]{2,1,0:T(8,128)(2,1)} %w_up.5) | copy-start | bytes 9437188
  44.2 7.6 %collective-permute-start.13 = (bf16[72,512]{1,0:T(8,128)(2,1)S(1)}, bf16[72,512]{1,0:T(8,128)(2,1)S(1)}, u32[]{:S(2)}, u32[]{:S(2)}) collective-permute-start(bf16[72,512]{1,0:T(8,128)(2,1)S(1)} %shard_map.85.refs_0_), channel_id=1, source_target_pairs={{192,0},{224,32},{0,64},{32,96},{64,128},{96,160},{128,192},{160,2... | collective-permute-start | bytes 221192 | tf_op jit(solution)/shard_map/ppermute | solution.py:37
  44.8 7.1 %collective-permute-start.10 = (bf16[72,512]{1,0:T(8,128)(2,1)S(1)}, bf16[72,512]{1,0:T(8,128)(2,1)S(1)}, u32[]{:S(2)}, u32[]{:S(2)}) collective-permute-start(bf16[72,512]{1,0:T(8,128)(2,1)S(1)} %shard_map.85.refs_0_), channel_id=1, source_target_pairs={{64,0},{96,32},{128,64},{160,96},{192,128},{224,160},{0,192},{32,2... | collective-permute-start | bytes 221192 | tf_op jit(solution)/shard_map/ppermute | solution.py:37
  48.4 7.9 %collective-permute-start.15 = (bf16[72,512]{1,0:T(8,128)(2,1)S(1)}, bf16[72,512]{1,0:T(8,128)(2,1)S(1)}, u32[]{:S(2)}, u32[]{:S(2)}) collective-permute-start(bf16[72,512]{1,0:T(8,128)(2,1)S(1)} %shard_map.85.refs_0_), channel_id=1, source_target_pairs={{224,0},{0,32},{32,64},{64,96},{96,128},{128,160},{160,192},{192,2... | collective-permute-start | bytes 221192 | tf_op jit(solution)/shard_map/ppermute | solution.py:37
  48.8 7.6 %collective-permute-start.9 = (bf16[72,512]{1,0:T(8,128)(2,1)S(1)}, bf16[72,512]{1,0:T(8,128)(2,1)S(1)}, u32[]{:S(2)}, u32[]{:S(2)}) collective-permute-start(bf16[72,512]{1,0:T(8,128)(2,1)S(1)} %shard_map.85.refs_0_), channel_id=1, source_target_pairs={{32,0},{64,32},{96,64},{128,96},{160,128},{192,160},{224,192},{0,2... | collective-permute-start | bytes 221192 | tf_op jit(solution)/shard_map/ppermute | solution.py:37
  51.8 5.6 %collective-permute-start.14 = (bf16[72,512]{1,0:T(8,128)(2,1)S(1)}, bf16[72,512]{1,0:T(8,128)(2,1)S(1)}, u32[]{:S(2)}, u32[]{:S(2)}) collective-permute-start(bf16[72,512]{1,0:T(8,128)(2,1)S(1)} %collective-permute-done.13.refs_6_), channel_id=1, source_target_pairs={{224,0},{0,32},{32,64},{64,96},{96,128},{128,160},{160,192},{192,2... | collective-permute-start | bytes 221192 | tf_op jit(solution)/shard_map/ppermute | solution.py:37
  51.8 6.8 %collective-permute-start.12 = (bf16[72,512]{1,0:T(8,128)(2,1)S(1)}, bf16[72,512]{1,0:T(8,128)(2,1)S(1)}, u32[]{:S(2)}, u32[]{:S(2)}) collective-permute-start(bf16[72,512]{1,0:T(8,128)(2,1)S(1)} %collective-permute-done.10.refs_2_), channel_id=1, source_target_pairs={{64,0},{96,32},{128,64},{160,96},{192,128},{224,160},{0,192},{32,2... | collective-permute-start | bytes 221192 | tf_op jit(solution)/shard_map/ppermute | solution.py:37
  56.3 4.4 %collective-permute-start.11 = (bf16[72,512]{1,0:T(8,128)(2,1)S(1)}, bf16[72,512]{1,0:T(8,128)(2,1)S(1)}, u32[]{:S(2)}, u32[]{:S(2)}) collective-permute-start(bf16[72,512]{1,0:T(8,128)(2,1)S(1)} %collective-permute-done.10.refs_2_), channel_id=1, source_target_pairs={{32,0},{64,32},{96,64},{128,96},{160,128},{192,160},{224,192},{0,2... | collective-permute-start | bytes 221192 | tf_op jit(solution)/shard_map/ppermute | solution.py:37
  90.4 4.2 %collective-permute-start.16 = (bf16[256,4096]{1,0:T(8,128)(2,1)S(1)}, bf16[256,4096]{1,0:T(8,128)(2,1)S(1)}, u32[]{:S(2)}, u32[]{:S(2)}) collective-permute-start(bf16[256,4096]{1,0:T(8,128)(2,1)S(1)} %bitcast.8), channel_id=1, source_target_pairs={{0,1},{1,0},{2,3},{3,2},{4,5},{5,4},{6,7},{7,6},{8,9},{9,8},{10,11... | collective-permute-start | bytes 6291464 | tf_op jit(solution)/shard_map/ppermute | solution.py:33
  96.8 2.9 %collective-permute-start.18 = (bf16[128,4096]{1,0:T(8,128)(2,1)S(1)}, bf16[128,4096]{1,0:T(8,128)(2,1)S(1)}, u32[]{:S(2)}, u32[]{:S(2)}) collective-permute-start(bf16[128,4096]{1,0:T(8,128)(2,1)S(1)} %shard_map.89), channel_id=1, source_target_pairs={{0,1},{1,0},{2,3},{3,2},{4,5},{5,4},{6,7},{7,6},{8,9},{9,8},{10,11... | collective-permute-start | bytes 3145736 | tf_op jit(solution)/shard_map/ppermute | solution.py:33
  99.3 2.7 %collective-permute-start.17 = (bf16[128,4096]{1,0:T(8,128)(2,1)S(1)}, bf16[128,4096]{1,0:T(8,128)(2,1)S(1)}, u32[]{:S(2)}, u32[]{:S(2)}) collective-permute-start(bf16[128,4096]{1,0:T(8,128)(2,1)S(1)} %shard_map.88), channel_id=1, source_target_pairs={{0,1},{1,0},{2,3},{3,2},{4,5},{5,4},{6,7},{7,6},{8,9},{9,8},{10,11... | collective-permute-start | bytes 3145736 | tf_op jit(solution)/shard_map/ppermute | solution.py:33
  135.9 8.6 %collective-permute-start.19 = (bf16[8,4096]{1,0:T(8,128)(2,1)S(1)}, bf16[8,4096]{1,0:T(8,128)(2,1)S(1)}, u32[]{:S(2)}, u32[]{:S(2)}) collective-permute-start(bf16[8,4096]{1,0:T(8,128)(2,1)S(1)} %get-tuple-element.30), channel_id=1, source_target_pairs={{128,0},{192,64},{0,128},{64,192},{129,1},{193,65},{1,129},{65,193... | collective-permute-start | bytes 196616 | tf_op jit(solution)/shard_map/ppermute | solution.py:37
  138.7 7.3 %collective-permute-start.20 = (bf16[8,4096]{1,0:T(8,128)(2,1)S(1)}, bf16[8,4096]{1,0:T(8,128)(2,1)S(1)}, u32[]{:S(2)}, u32[]{:S(2)}) collective-permute-start(bf16[8,4096]{1,0:T(8,128)(2,1)S(1)} %get-tuple-element.31), channel_id=1, source_target_pairs={{192,0},{0,64},{64,128},{128,192},{193,1},{1,65},{65,129},{129,193... | collective-permute-start | bytes 196616 | tf_op jit(solution)/shard_map/ppermute | solution.py:37
  141.6 5.7 %collective-permute-start.21 = (bf16[8,4096]{1,0:T(8,128)(2,1)S(1)}, bf16[8,4096]{1,0:T(8,128)(2,1)S(1)}, u32[]{:S(2)}, u32[]{:S(2)}) collective-permute-start(bf16[8,4096]{1,0:T(8,128)(2,1)S(1)} %get-tuple-element.32), channel_id=1, source_target_pairs={{64,0},{128,64},{192,128},{0,192},{65,1},{129,65},{193,129},{1,193... | collective-permute-start | bytes 196616 | tf_op jit(solution)/shard_map/ppermute | solution.py:37
  (6 other events, 104.1 us)

commit v10 on v9

--- a/solution.py
+++ b/solution.py
@@ -19,8 +19,8 @@
 EXPERT = ("zh", "zl", "xl")
 TENSOR = ("xh", "y", "c")
 SPREAD = ("xh", "y")
-PLANE = ("y", "xh", "xl")
-PEERS = ("y", "xh", "xl", "zl")
+PLANE = ("y", "xl", "xh")
+PEERS = ("y", "xl", "xh", "zl")
 RING = ("zh", "zl")
 NZ, NH = 8, 4
 MIB = 1 << 20
@@ -159,6 +159,19 @@
     )(place, parts, ids, gates)
 
 
+def coords(index, axes):
+    found = {}
+    for axis in reversed(axes):
+        size = SIZES[FINE.index(axis)]
+        found[axis] = index % size
+        index = index // size
+    return found
+
+
+def label_of(z, at):
+    return (z * 2 + at["xl"]) * 4 + at["xh"] * 2 + at["y"] // 2
+
+
 def routed(listed, label, spot):
     tokens, rows = listed.shape[0], ROWS
     match = jnp.zeros(label.shape, F32)
@@ -194,7 +207,7 @@
     lane = lax.broadcasted_iota(jnp.int32, (tokens, lanes), 1)
     from_z = lax.broadcasted_iota(jnp.int32, (tokens, lanes), 0) // rows
     slot, device = lane % (NZ * CAP), lane // (NZ * CAP)
-    label = (z * 2 + device % 2) * 4 + (device // 2) % 2 * 2 + device // 8
+    label = label_of(z, coords(device, PLANE))
     spot = slot - (from_z % 2) * (NH * CAP) - (from_z // 2) * CAP
     placed, _ = routed(notes[...], label, spot)
     spots = jnp.transpose(jnp.where(placed, 1.0, 0.0)).astype(BF16)
@@ -208,7 +221,8 @@
     lane = lax.broadcasted_iota(jnp.int32, (half, lanes), 1)
     hop = lax.broadcasted_iota(jnp.int32, (half, lanes), 0) // rows
     slot, peer = lane % (NH * CAP), lane // (NH * CAP)
-    label = ((pair * 2 + peer % 2) * 2 + (peer // 2) % 2) * 4 + (peer // 4) % 2 * 2 + peer // 16
+    at = coords(peer, PEERS)
+    label = label_of(pair * 2 + at["zl"], at)
     placed, gate = routed(listed, label, slot - ((pair + hop) % NH) * CAP)
     weight = jnp.where(placed, gate, 0.0)
     top = weight.astype(BF16)

time: 150 us -> 149 us (level); the launches traced: 148 us -> 149 us
  no operation moved by 1% of the time
where the time goes in v10:
time: 149 us
  blocking collectives  78.3 us (53%)
  starting transfers between devices  37.3 us (25%)
  waiting for transfers between devices  18.7 us (13%)
  Pallas kernels  11.9 us (8%)
  local copies, waits for them, and re-layouts  1.88 us (1%)
    ppermute x17, starting transfers between devices, fetch(): return lax.ppermute(x, axis, [((i + hop) % size, i) for i in range(size)])  35.7 us
    all_to_all x1, blocking collectives, on_device(): back = lax.all_to_all(summed, PEERS, 0, 0, tiled=True).reshape(-1, width)  33.2 us
    all_to_all x1, blocking collectives, on_device(): lax.all_to_all(sent.reshape(n_plane, -1, width), PLANE, 0, 0, tiled=True)  28.7 us
    all_to_all x1, blocking collectives, on_device(): partial = lax.all_to_all(partial, SPREAD, 0, 0, tiled=True)  16.4 us
    ppermute x17, waiting for transfers between devices, fetch(): return lax.ppermute(x, axis, [((i + hop) % size, i) for i in range(size)])  14.4 us
    pallas_call x3, Pallas kernels, expert_rows(): pl.pallas_call(functools.partial(expert_kernel, first), out_shape=jax.Sha...  8.25 us
    ppermute x5, waiting for transfers between devices, swap(): return lax.ppermute(x, axis, [(0, 1), (1, 0)])  4.32 us
  transfers between devices with their start and end apart: 22, of which 13 were waited for; matrix products, arithmetic and copies ran while one was open for 0% of the time, Pallas kernels for 4%

profile of v10, /device:TPU:6, one launch (start us, length us, event | category | flops | bytes accessed | tf_op | source)
XLA Modules:
  0.0 148.9 jit_solution(10061029597758194176)
XLA Ops:
  0.8 6.3 %collective-permute-start.2 = (bf16[128,512]{1,0:T(8,128)(2,1)}, bf16[128,512]{1,0:T(8,128)(2,1)S(1)}, u32[]{:S(2)}, u32[]{:S(2)}) collective-permute-start(bf16[128,512]{1,0:T(8,128)(2,1)} %context.1), channel_id=1, source_target_pairs={{64,0},{96,32},{128,64},{160,96},{192,128},{224,160},{0,192},{32,2... | collective-permute-start | bytes 393224 | tf_op jit(solution)/shard_map/ppermute | solution.py:37
  7.1 3.7 %collective-permute-start.1 = (bf16[128,512]{1,0:T(8,128)(2,1)}, bf16[128,512]{1,0:T(8,128)(2,1)S(1)}, u32[]{:S(2)}, u32[]{:S(2)}) collective-permute-start(bf16[128,512]{1,0:T(8,128)(2,1)} %context.1), channel_id=1, source_target_pairs={{32,0},{64,32},{96,64},{128,96},{160,128},{192,160},{224,192},{0,2... | collective-permute-start | bytes 393224 | tf_op jit(solution)/shard_map/ppermute | solution.py:37
  10.8 2.7 %collective-permute-done.2.refs_2_ = bf16[128,512]{1,0:T(8,128)(2,1)S(1)} collective-permute-done((bf16[128,512]{1,0:T(8,128)(2,1)}, bf16[128,512]{1,0:T(8,128)(2,1)S(1)}, u32[]{:S(2)}, u32[]{:S(2)}) %collective-permute-start.2) | collective-permute-done | bytes 131104 | tf_op jit(solution)/shard_map/ppermute | solution.py:37
  13.5 4.6 %collective-permute-start.4 = (bf16[128,512]{1,0:T(8,128)(2,1)S(1)}, bf16[128,512]{1,0:T(8,128)(2,1)S(1)}, u32[]{:S(2)}, u32[]{:S(2)}) collective-permute-start(bf16[128,512]{1,0:T(8,128)(2,1)S(1)} %collective-permute-done.2.refs_2_), channel_id=1, source_target_pairs={{64,0},{96,32},{128,64},{160,96},{192,128},{224,160},{0,192},{32,2... | collective-permute-start | bytes 393224 | tf_op jit(solution)/shard_map/ppermute | solution.py:37
  18.2 2.0 %collective-permute-start.6 = (bf16[128,512]{1,0:T(8,128)(2,1)S(1)}, bf16[128,512]{1,0:T(8,128)(2,1)S(1)}, u32[]{:S(2)}, u32[]{:S(2)}) collective-permute-start(bf16[128,512]{1,0:T(8,128)(2,1)S(1)} %collective-permute-done.5.refs_6_), channel_id=1, source_target_pairs={{224,0},{0,32},{32,64},{64,96},{96,128},{128,160},{160,192},{192,2... | collective-permute-start | bytes 393224 | tf_op jit(solution)/shard_map/ppermute | solution.py:37
  22.5 2.3 %collective-permute-done.3.refs_3_ = bf16[128,512]{1,0:T(8,128)(2,1)S(1)} collective-permute-done((bf16[128,512]{1,0:T(8,128)(2,1)S(1)}, bf16[128,512]{1,0:T(8,128)(2,1)S(1)}, u32[]{:S(2)}, u32[]{:S(2)}) %collective-permute-start.3) | collective-permute-done | bytes 131104 | tf_op jit(solution)/shard_map/ppermute | solution.py:37
  25.6 1.9 %collective-permute-done.8.got = bf16[8,64,512]{2,1,0:T(8,128)(2,1)S(1)} collective-permute-done((bf16[8,64,512]{2,1,0:T(8,128)(2,1)S(1)}, bf16[8,64,512]{2,1,0:T(8,128)(2,1)S(1)}, u32[]{:S(2)}, u32[]{:S(2)}) %collective-permute-start.8) | collective-permute-done | bytes 524320 | tf_op jit(solution)/shard_map/ppermute | solution.py:33
  27.7 16.4 %all_to_all.15.parts = bf16[8,64,512]{2,1,0:T(8,128)(2,1)S(1)} all-to-all(bf16[8,64,512]{2,1,0:T(8,128)(2,1)S(1)} %shard_map.84), channel_id=1, replica_groups=mesh['zh'=4,'zl'=2,'xl'=2,'xh'=2,'y'=4,'c'=2] {'xh','y'}, dimensions={0} | all-to-all | bytes 1048576 | tf_op jit(solution)/shard_map/all_to_all | solution.py:352
  44.8 3.7 %collective-permute-start.10 = (bf16[72,512]{1,0:T(8,128)(2,1)S(1)}, bf16[72,512]{1,0:T(8,128)(2,1)S(1)}, u32[]{:S(2)}, u32[]{:S(2)}) collective-permute-start(bf16[72,512]{1,0:T(8,128)(2,1)S(1)} %shard_map.85.refs_0_), channel_id=1, source_target_pairs={{64,0},{96,32},{128,64},{160,96},{192,128},{224,160},{0,192},{32,2... | collective-permute-start | bytes 221192 | tf_op jit(solution)/shard_map/ppermute | solution.py:37
  48.8 2.9 %collective-permute-start.9 = (bf16[72,512]{1,0:T(8,128)(2,1)S(1)}, bf16[72,512]{1,0:T(8,128)(2,1)S(1)}, u32[]{:S(2)}, u32[]{:S(2)}) collective-permute-start(bf16[72,512]{1,0:T(8,128)(2,1)S(1)} %shard_map.85.refs_0_), channel_id=1, source_target_pairs={{32,0},{64,32},{96,64},{128,96},{160,128},{192,160},{224,192},{0,2... | collective-permute-start | bytes 221192 | tf_op jit(solution)/shard_map/ppermute | solution.py:37
  51.8 4.5 %collective-permute-start.12 = (bf16[72,512]{1,0:T(8,128)(2,1)S(1)}, bf16[72,512]{1,0:T(8,128)(2,1)S(1)}, u32[]{:S(2)}, u32[]{:S(2)}) collective-permute-start(bf16[72,512]{1,0:T(8,128)(2,1)S(1)} %collective-permute-done.10.refs_2_), channel_id=1, source_target_pairs={{64,0},{96,32},{128,64},{160,96},{192,128},{224,160},{0,192},{32,2... | collective-permute-start | bytes 221192 | tf_op jit(solution)/shard_map/ppermute | solution.py:37
  57.4 1.3 collective-permute-done.12.refs_4_
  58.7 2.0 %collective-permute-done.11.refs_3_ = bf16[72,512]{1,0:T(8,128)(2,1)S(1)} collective-permute-done((bf16[72,512]{1,0:T(8,128)(2,1)S(1)}, bf16[72,512]{1,0:T(8,128)(2,1)S(1)}, u32[]{:S(2)}, u32[]{:S(2)}) %collective-permute-start.11) | collective-permute-done | bytes 73760 | tf_op jit(solution)/shard_map/ppermute | solution.py:37
  61.9 28.7 %all_to_all.16 = bf16[16,16,4096]{2,1,0:T(8,128)(2,1)S(1)} all-to-all(bf16[16,16,4096]{2,1,0:T(8,128)(2,1)S(1)} %bitcast.10), channel_id=1, replica_groups=mesh['zh'=4,'zl'=2,'xl'=2,'xh'=2,'y'=4,'c'=2] {'y','xl','xh'}, dimensions={0} | all-to-all | bytes 4194304 | tf_op jit(solution)/shard_map/all_to_all | solution.py:357
  90.7 3.8 %shard_map.87.mine = bf16[256,4096]{1,0:T(8,128)(2,1)S(1)} custom-call(bf16[256,4096]{1,0:T(8,128)(2,1)S(1)} %bitcast.9, bf16[1,4096,384]{2,1,0:T(8,128)(2,1)S(1)} %copy-done, bf16[1,4096,384]{2,1,0:T(8,128)(2,1)S(1)} %copy-done.1, bf16[1,384,4096]{2,1,0:T(8,128)(2,1)S(1)} %copy-done.2), custom_call_target="tpu_custom_call" | custom-call | flops 2415919104 | bytes 13631488 | tf_op jit(solution)/shard_map/pallas_call | solution.py:284
  94.8 2.2 %shard_map.89 = bf16[128,4096]{1,0:T(8,128)(2,1)S(1)} custom-call(bf16[256,4096]{1,0:T(8,128)(2,1)S(1)} %collective-permute-done.16.rows, bf16[1,4096,384]{2,1,0:T(8,128)(2,1)S(1)} %copy-done, bf16[1,4096,384]{2,1,0:T(8,128)(2,1)S(1)} %copy-done.1, bf16[1,384,4096]{2,1,0:T(8,128)(2,1)S(1)} %copy-done.2), custom_call_target="tpu_custom_call" | custom-call | flops 1207959552 | bytes 11534336 | tf_op jit(solution)/shard_map/pallas_call | solution.py:284
  97.4 2.2 %shard_map.88 = bf16[128,4096]{1,0:T(8,128)(2,1)S(1)} custom-call(bf16[256,4096]{1,0:T(8,128)(2,1)S(1)} %collective-permute-done.16.rows, bf16[1,4096,384]{2,1,0:T(8,128)(2,1)S(1)} %copy-done, bf16[1,4096,384]{2,1,0:T(8,128)(2,1)S(1)} %copy-done.1, bf16[1,384,4096]{2,1,0:T(8,128)(2,1)S(1)} %copy-done.2), custom_call_target="tpu_custom_call" | custom-call | flops 1207959552 | bytes 11534336 | tf_op jit(solution)/shard_map/pallas_call | solution.py:284
  100.2 2.1 %collective-permute-done.17.part = bf16[128,4096]{1,0:T(8,128)(2,1)S(1)} collective-permute-done((bf16[128,4096]{1,0:T(8,128)(2,1)S(1)}, bf16[128,4096]{1,0:T(8,128)(2,1)S(1)}, u32[]{:S(2)}, u32[]{:S(2)}) %collective-permute-start.17) | collective-permute-done | bytes 1048608 | tf_op jit(solution)/shard_map/ppermute | solution.py:33
  102.6 33.2 %all_to_all.17 = bf16[32,8,4096]{2,1,0:T(8,128)(2,1)S(1)} all-to-all(bf16[32,8,4096]{2,1,0:T(8,128)(2,1)S(1)} %bitcast.6), channel_id=1, replica_groups=mesh['zh'=4,'zl'=2,'xl'=2,'xh'=2,'y'=4,'c'=2] {'y','xl','xh','zl'}, dimensions={0} | all-to-all | bytes 4194304 | tf_op jit(solution)/shard_map/all_to_all | solution.py:368
  136.6 3.0 %collective-permute-start.19 = (bf16[8,4096]{1,0:T(8,128)(2,1)S(1)}, bf16[8,4096]{1,0:T(8,128)(2,1)S(1)}, u32[]{:S(2)}, u32[]{:S(2)}) collective-permute-start(bf16[8,4096]{1,0:T(8,128)(2,1)S(1)} %get-tuple-element.30), channel_id=1, source_target_pairs={{128,0},{192,64},{0,128},{64,192},{129,1},{193,65},{1,129},{65,193... | collective-permute-start | bytes 196616 | tf_op jit(solution)/shard_map/ppermute | solution.py:37
  139.6 2.8 %collective-permute-start.20 = (bf16[8,4096]{1,0:T(8,128)(2,1)S(1)}, bf16[8,4096]{1,0:T(8,128)(2,1)S(1)}, u32[]{:S(2)}, u32[]{:S(2)}) collective-permute-start(bf16[8,4096]{1,0:T(8,128)(2,1)S(1)} %get-tuple-element.31), channel_id=1, source_target_pairs={{192,0},{0,64},{64,128},{128,192},{193,1},{1,65},{65,129},{129,193... | collective-permute-start | bytes 196616 | tf_op jit(solution)/shard_map/ppermute | solution.py:37
  142.4 1.4 collective-permute-start.21
  143.7 2.0 %collective-permute-done.19 = bf16[8,4096]{1,0:T(8,128)(2,1)S(1)} collective-permute-done((bf16[8,4096]{1,0:T(8,128)(2,1)S(1)}, bf16[8,4096]{1,0:T(8,128)(2,1)S(1)}, u32[]{:S(2)}, u32[]{:S(2)}) %collective-permute-start.19) | collective-permute-done | bytes 65568 | tf_op jit(solution)/shard_map/ppermute | solution.py:37
  145.7 1.5 collective-permute-done.20
  (51 shorter events, 11.6 us)
Async XLA Ops:
  0.0 18.2 %collective-permute-start = (bf16[512,256]{1,0:T(8,128)(2,1)}, bf16[512,256]{1,0:T(8,128)(2,1)S(1)}, u32[]{:S(2)}, u32[]{:S(2)}) collective-permute-start(bf16[512,256]{1,0:T(8,128)(2,1)} %own.1), channel_id=1, source_target_pairs={{0,16},{16,0},{1,17},{17,1},{2,18},{18,2},{3,19},{19,3},{4,20},{20... | collective-permute-start | bytes 786440 | tf_op jit(solution)/shard_map/ppermute | solution.py:33
  0.8 12.7 %collective-permute-start.2 = (bf16[128,512]{1,0:T(8,128)(2,1)}, bf16[128,512]{1,0:T(8,128)(2,1)S(1)}, u32[]{:S(2)}, u32[]{:S(2)}) collective-permute-start(bf16[128,512]{1,0:T(8,128)(2,1)} %context.1), channel_id=1, source_target_pairs={{64,0},{96,32},{128,64},{160,96},{192,128},{224,160},{0,192},{32,2... | collective-permute-start | bytes 393224 | tf_op jit(solution)/shard_map/ppermute | solution.py:37
  7.1 11.0 %collective-permute-start.5 = (bf16[128,512]{1,0:T(8,128)(2,1)}, bf16[128,512]{1,0:T(8,128)(2,1)S(1)}, u32[]{:S(2)}, u32[]{:S(2)}) collective-permute-start(bf16[128,512]{1,0:T(8,128)(2,1)} %context.1), channel_id=1, source_target_pairs={{192,0},{224,32},{0,64},{32,96},{64,128},{96,160},{128,192},{160,2... | collective-permute-start | bytes 393224 | tf_op jit(solution)/shard_map/ppermute | solution.py:37
  7.1 15.0 %collective-permute-start.1 = (bf16[128,512]{1,0:T(8,128)(2,1)}, bf16[128,512]{1,0:T(8,128)(2,1)S(1)}, u32[]{:S(2)}, u32[]{:S(2)}) collective-permute-start(bf16[128,512]{1,0:T(8,128)(2,1)} %context.1), channel_id=1, source_target_pairs={{32,0},{64,32},{96,64},{128,96},{160,128},{192,160},{224,192},{0,2... | collective-permute-start | bytes 393224 | tf_op jit(solution)/shard_map/ppermute | solution.py:37
  10.8 11.3 %collective-permute-start.7 = (bf16[128,512]{1,0:T(8,128)(2,1)}, bf16[128,512]{1,0:T(8,128)(2,1)S(1)}, u32[]{:S(2)}, u32[]{:S(2)}) collective-permute-start(bf16[128,512]{1,0:T(8,128)(2,1)} %context.1), channel_id=1, source_target_pairs={{224,0},{0,32},{32,64},{64,96},{96,128},{128,160},{160,192},{192,2... | collective-permute-start | bytes 393224 | tf_op jit(solution)/shard_map/ppermute | solution.py:37
  13.5 9.0 %collective-permute-start.4 = (bf16[128,512]{1,0:T(8,128)(2,1)S(1)}, bf16[128,512]{1,0:T(8,128)(2,1)S(1)}, u32[]{:S(2)}, u32[]{:S(2)}) collective-permute-start(bf16[128,512]{1,0:T(8,128)(2,1)S(1)} %collective-permute-done.2.refs_2_), channel_id=1, source_target_pairs={{64,0},{96,32},{128,64},{160,96},{192,128},{224,160},{0,192},{32,2... | collective-permute-start | bytes 393224 | tf_op jit(solution)/shard_map/ppermute | solution.py:37
  18.2 6.6 %collective-permute-start.3 = (bf16[128,512]{1,0:T(8,128)(2,1)S(1)}, bf16[128,512]{1,0:T(8,128)(2,1)S(1)}, u32[]{:S(2)}, u32[]{:S(2)}) collective-permute-start(bf16[128,512]{1,0:T(8,128)(2,1)S(1)} %collective-permute-done.2.refs_2_), channel_id=1, source_target_pairs={{32,0},{64,32},{96,64},{128,96},{160,128},{192,160},{224,192},{0,2... | collective-permute-start | bytes 393224 | tf_op jit(solution)/shard_map/ppermute | solution.py:37
  18.2 6.6 %collective-permute-start.6 = (bf16[128,512]{1,0:T(8,128)(2,1)S(1)}, bf16[128,512]{1,0:T(8,128)(2,1)S(1)}, u32[]{:S(2)}, u32[]{:S(2)}) collective-permute-start(bf16[128,512]{1,0:T(8,128)(2,1)S(1)} %collective-permute-done.5.refs_6_), channel_id=1, source_target_pairs={{224,0},{0,32},{32,64},{64,96},{96,128},{128,160},{160,192},{192,2... | collective-permute-start | bytes 393224 | tf_op jit(solution)/shard_map/ppermute | solution.py:37
  24.8 65.9 %copy-start.2 = (bf16[1,384,4096]{2,1,0:T(8,128)(2,1)S(1)}, bf16[1,384,4096]{2,1,0:T(8,128)(2,1)}, u32[]{:S(2)}) copy-start(bf16[1,384,4096]{2,1,0:T(8,128)(2,1)} %w_down.5) | copy-start | bytes 9437188
  25.5 2.0 %collective-permute-start.8 = (bf16[8,64,512]{2,1,0:T(8,128)(2,1)S(1)}, bf16[8,64,512]{2,1,0:T(8,128)(2,1)S(1)}, u32[]{:S(2)}, u32[]{:S(2)}) collective-permute-start(bf16[8,64,512]{2,1,0:T(8,128)(2,1)S(1)} %get-tuple-element.22), channel_id=1, source_target_pairs={{0,1},{1,0},{2,3},{3,2},{4,5},{5,4},{6,7},{7,6},{8,9},{9,8},{10,11... | collective-permute-start | bytes 1572872 | tf_op jit(solution)/shard_map/ppermute | solution.py:33
  27.6 63.0 %copy-start.1 = (bf16[1,4096,384]{2,1,0:T(8,128)(2,1)S(1)}, bf16[1,4096,384]{2,1,0:T(8,128)(2,1)}, u32[]{:S(2)}) copy-start(bf16[1,4096,384]{2,1,0:T(8,128)(2,1)} %w_up.5) | copy-start | bytes 9437188
  44.2 7.6 %collective-permute-start.13 = (bf16[72,512]{1,0:T(8,128)(2,1)S(1)}, bf16[72,512]{1,0:T(8,128)(2,1)S(1)}, u32[]{:S(2)}, u32[]{:S(2)}) collective-permute-start(bf16[72,512]{1,0:T(8,128)(2,1)S(1)} %shard_map.85.refs_0_), channel_id=1, source_target_pairs={{192,0},{224,32},{0,64},{32,96},{64,128},{96,160},{128,192},{160,2... | collective-permute-start | bytes 221192 | tf_op jit(solution)/shard_map/ppermute | solution.py:37
  44.8 7.1 %collective-permute-start.10 = (bf16[72,512]{1,0:T(8,128)(2,1)S(1)}, bf16[72,512]{1,0:T(8,128)(2,1)S(1)}, u32[]{:S(2)}, u32[]{:S(2)}) collective-permute-start(bf16[72,512]{1,0:T(8,128)(2,1)S(1)} %shard_map.85.refs_0_), channel_id=1, source_target_pairs={{64,0},{96,32},{128,64},{160,96},{192,128},{224,160},{0,192},{32,2... | collective-permute-start | bytes 221192 | tf_op jit(solution)/shard_map/ppermute | solution.py:37
  48.4 7.9 %collective-permute-start.15 = (bf16[72,512]{1,0:T(8,128)(2,1)S(1)}, bf16[72,512]{1,0:T(8,128)(2,1)S(1)}, u32[]{:S(2)}, u32[]{:S(2)}) collective-permute-start(bf16[72,512]{1,0:T(8,128)(2,1)S(1)} %shard_map.85.refs_0_), channel_id=1, source_target_pairs={{224,0},{0,32},{32,64},{64,96},{96,128},{128,160},{160,192},{192,2... | collective-permute-start | bytes 221192 | tf_op jit(solution)/shard_map/ppermute | solution.py:37
  48.8 7.6 %collective-permute-start.9 = (bf16[72,512]{1,0:T(8,128)(2,1)S(1)}, bf16[72,512]{1,0:T(8,128)(2,1)S(1)}, u32[]{:S(2)}, u32[]{:S(2)}) collective-permute-start(bf16[72,512]{1,0:T(8,128)(2,1)S(1)} %shard_map.85.refs_0_), channel_id=1, source_target_pairs={{32,0},{64,32},{96,64},{128,96},{160,128},{192,160},{224,192},{0,2... | collective-permute-start | bytes 221192 | tf_op jit(solution)/shard_map/ppermute | solution.py:37
  51.8 5.6 %collective-permute-start.14 = (bf16[72,512]{1,0:T(8,128)(2,1)S(1)}, bf16[72,512]{1,0:T(8,128)(2,1)S(1)}, u32[]{:S(2)}, u32[]{:S(2)}) collective-permute-start(bf16[72,512]{1,0:T(8,128)(2,1)S(1)} %collective-permute-done.13.refs_6_), channel_id=1, source_target_pairs={{224,0},{0,32},{32,64},{64,96},{96,128},{128,160},{160,192},{192,2... | collective-permute-start | bytes 221192 | tf_op jit(solution)/shard_map/ppermute | solution.py:37
  51.8 6.8 %collective-permute-start.12 = (bf16[72,512]{1,0:T(8,128)(2,1)S(1)}, bf16[72,512]{1,0:T(8,128)(2,1)S(1)}, u32[]{:S(2)}, u32[]{:S(2)}) collective-permute-start(bf16[72,512]{1,0:T(8,128)(2,1)S(1)} %collective-permute-done.10.refs_2_), channel_id=1, source_target_pairs={{64,0},{96,32},{128,64},{160,96},{192,128},{224,160},{0,192},{32,2... | collective-permute-start | bytes 221192 | tf_op jit(solution)/shard_map/ppermute | solution.py:37
  56.3 4.4 %collective-permute-start.11 = (bf16[72,512]{1,0:T(8,128)(2,1)S(1)}, bf16[72,512]{1,0:T(8,128)(2,1)S(1)}, u32[]{:S(2)}, u32[]{:S(2)}) collective-permute-start(bf16[72,512]{1,0:T(8,128)(2,1)S(1)} %collective-permute-done.10.refs_2_), channel_id=1, source_target_pairs={{32,0},{64,32},{96,64},{128,96},{160,128},{192,160},{224,192},{0,2... | collective-permute-start | bytes 221192 | tf_op jit(solution)/shard_map/ppermute | solution.py:37
  90.7 4.2 %collective-permute-start.16 = (bf16[256,4096]{1,0:T(8,128)(2,1)S(1)}, bf16[256,4096]{1,0:T(8,128)(2,1)S(1)}, u32[]{:S(2)}, u32[]{:S(2)}) collective-permute-start(bf16[256,4096]{1,0:T(8,128)(2,1)S(1)} %bitcast.8), channel_id=1, source_target_pairs={{0,1},{1,0},{2,3},{3,2},{4,5},{5,4},{6,7},{7,6},{8,9},{9,8},{10,11... | collective-permute-start | bytes 6291464 | tf_op jit(solution)/shard_map/ppermute | solution.py:33
  97.1 2.9 %collective-permute-start.18 = (bf16[128,4096]{1,0:T(8,128)(2,1)S(1)}, bf16[128,4096]{1,0:T(8,128)(2,1)S(1)}, u32[]{:S(2)}, u32[]{:S(2)}) collective-permute-start(bf16[128,4096]{1,0:T(8,128)(2,1)S(1)} %shard_map.89), channel_id=1, source_target_pairs={{0,1},{1,0},{2,3},{3,2},{4,5},{5,4},{6,7},{7,6},{8,9},{9,8},{10,11... | collective-permute-start | bytes 3145736 | tf_op jit(solution)/shard_map/ppermute | solution.py:33
  99.6 2.7 %collective-permute-start.17 = (bf16[128,4096]{1,0:T(8,128)(2,1)S(1)}, bf16[128,4096]{1,0:T(8,128)(2,1)S(1)}, u32[]{:S(2)}, u32[]{:S(2)}) collective-permute-start(bf16[128,4096]{1,0:T(8,128)(2,1)S(1)} %shard_map.88), channel_id=1, source_target_pairs={{0,1},{1,0},{2,3},{3,2},{4,5},{5,4},{6,7},{7,6},{8,9},{9,8},{10,11... | collective-permute-start | bytes 3145736 | tf_op jit(solution)/shard_map/ppermute | solution.py:33
  136.6 9.1 %collective-permute-start.19 = (bf16[8,4096]{1,0:T(8,128)(2,1)S(1)}, bf16[8,4096]{1,0:T(8,128)(2,1)S(1)}, u32[]{:S(2)}, u32[]{:S(2)}) collective-permute-start(bf16[8,4096]{1,0:T(8,128)(2,1)S(1)} %get-tuple-element.30), channel_id=1, source_target_pairs={{128,0},{192,64},{0,128},{64,192},{129,1},{193,65},{1,129},{65,193... | collective-permute-start | bytes 196616 | tf_op jit(solution)/shard_map/ppermute | solution.py:37
  139.6 7.6 %collective-permute-start.20 = (bf16[8,4096]{1,0:T(8,128)(2,1)S(1)}, bf16[8,4096]{1,0:T(8,128)(2,1)S(1)}, u32[]{:S(2)}, u32[]{:S(2)}) collective-permute-start(bf16[8,4096]{1,0:T(8,128)(2,1)S(1)} %get-tuple-element.31), channel_id=1, source_target_pairs={{192,0},{0,64},{64,128},{128,192},{193,1},{1,65},{65,129},{129,193... | collective-permute-start | bytes 196616 | tf_op jit(solution)/shard_map/ppermute | solution.py:37
  142.4 5.9 %collective-permute-start.21 = (bf16[8,4096]{1,0:T(8,128)(2,1)S(1)}, bf16[8,4096]{1,0:T(8,128)(2,1)S(1)}, u32[]{:S(2)}, u32[]{:S(2)}) collective-permute-start(bf16[8,4096]{1,0:T(8,128)(2,1)S(1)} %get-tuple-element.32), channel_id=1, source_target_pairs={{64,0},{128,64},{192,128},{0,192},{65,1},{129,65},{193,129},{1,193... | collective-permute-start | bytes 196616 | tf_op jit(solution)/shard_map/ppermute | solution.py:37
  (6 other events, 104.3 us)

commit v11 on v10

--- a/solution.py
+++ b/solution.py
@@ -262,31 +262,24 @@
     )(place, *blocks, gain.reshape(1, width))
 
 
-def expert_kernel(first, rows, w_gate, w_up, w_down, out, down, arrived):
-    copy = pltpu.make_async_copy(w_down, down, arrived)
-    copy.start()
+def expert_kernel(first, rows, w_gate, w_up, w_down, out):
     count, width = out.shape
     deep = width // 4
-    gate_act = up_act = 0.0
+    piece = rows[first : first + count, :]
+    gate_act = dot(piece, w_gate[0])
+    up_act = dot(piece, w_up[0])
+    hidden = (jax.nn.silu(gate_act) * up_act).astype(BF16)
     for i in range(4):
         at = slice(i * deep, (i + 1) * deep)
-        piece = rows[first : first + count, at]
-        gate_act += dot(piece, w_gate[0, at, :])
-        up_act += dot(piece, w_up[0, at, :])
-    hidden = (jax.nn.silu(gate_act) * up_act).astype(BF16)
-    copy.wait()
-    for i in range(4):
-        at = slice(i * deep, (i + 1) * deep)
-        out[:, at] = dot(hidden, down[0, :, at]).astype(BF16)
+        out[:, at] = dot(hidden, w_down[0, :, at]).astype(BF16)
 
 
 def expert_rows(rows, first, count, w_gate, w_up, w_down):
     return pl.pallas_call(
         functools.partial(expert_kernel, first),
         out_shape=jax.ShapeDtypeStruct((count, rows.shape[1]), BF16),
-        in_specs=[VMEM] * 3 + [pl.BlockSpec(memory_space=pl.ANY)],
+        in_specs=[VMEM] * 4,
         out_specs=VMEM,
-        scratch_shapes=[pltpu.VMEM(w_down.shape, BF16), pltpu.SemaphoreType.DMA],
         compiler_params=params(32),
         cost_estimate=pl.CostEstimate(
             flops=6 * count * w_down.shape[1] * w_down.shape[2],

time: 149 us -> 149 us (level)
  transfers between devices with their start and end apart: 22 -> 22, of which waited for: 13 -> 14; matrix products, arithmetic and copies ran while one was open for 0% -> 0% of each run, Pallas kernels for 4% -> 4%
where the time goes in v11:
time: 149 us
  blocking collectives  78.5 us (53%)
  starting transfers between devices  37.3 us (25%)
  waiting for transfers between devices  19.1 us (13%)
  Pallas kernels  10.9 us (7%)
  local copies, waits for them, and re-layouts  1.88 us (1%)
    ppermute x17, starting transfers between devices, fetch(): return lax.ppermute(x, axis, [((i + hop) % size, i) for i in range(size)])  35.7 us
    all_to_all x1, blocking collectives, on_device(): back = lax.all_to_all(summed, PEERS, 0, 0, tiled=True).reshape(-1, width)  33.3 us
    all_to_all x1, blocking collectives, on_device(): lax.all_to_all(sent.reshape(n_plane, -1, width), PLANE, 0, 0, tiled=True)  28.7 us
    all_to_all x1, blocking collectives, on_device(): partial = lax.all_to_all(partial, SPREAD, 0, 0, tiled=True)  16.4 us
    ppermute x17, waiting for transfers between devices, fetch(): return lax.ppermute(x, axis, [((i + hop) % size, i) for i in range(size)])  14.5 us
    pallas_call x3, Pallas kernels, expert_rows(): pl.pallas_call(functools.partial(expert_kernel, first), out_shape=jax.Sha...  7.32 us
    ppermute x5, waiting for transfers between devices, swap(): return lax.ppermute(x, axis, [(0, 1), (1, 0)])  4.57 us
  transfers between devices with their start and end apart: 22, of which 14 were waited for; matrix products, arithmetic and copies ran while one was open for 0% of the time, Pallas kernels for 4%

profile of v11, /device:TPU:6, one launch (start us, length us, event | category | flops | bytes accessed | tf_op | source)
XLA Modules:
  0.0 148.5 jit_solution(8280300516425597913)
XLA Ops:
  0.8 6.3 %collective-permute-start.2 = (bf16[128,512]{1,0:T(8,128)(2,1)}, bf16[128,512]{1,0:T(8,128)(2,1)S(1)}, u32[]{:S(2)}, u32[]{:S(2)}) collective-permute-start(bf16[128,512]{1,0:T(8,128)(2,1)} %context.1), channel_id=1, source_target_pairs={{64,0},{96,32},{128,64},{160,96},{192,128},{224,160},{0,192},{32,2... | collective-permute-start | bytes 393224 | tf_op jit(solution)/shard_map/ppermute | solution.py:37
  7.1 3.7 %collective-permute-start.1 = (bf16[128,512]{1,0:T(8,128)(2,1)}, bf16[128,512]{1,0:T(8,128)(2,1)S(1)}, u32[]{:S(2)}, u32[]{:S(2)}) collective-permute-start(bf16[128,512]{1,0:T(8,128)(2,1)} %context.1), channel_id=1, source_target_pairs={{32,0},{64,32},{96,64},{128,96},{160,128},{192,160},{224,192},{0,2... | collective-permute-start | bytes 393224 | tf_op jit(solution)/shard_map/ppermute | solution.py:37
  10.8 2.7 %collective-permute-done.2.refs_2_ = bf16[128,512]{1,0:T(8,128)(2,1)S(1)} collective-permute-done((bf16[128,512]{1,0:T(8,128)(2,1)}, bf16[128,512]{1,0:T(8,128)(2,1)S(1)}, u32[]{:S(2)}, u32[]{:S(2)}) %collective-permute-start.2) | collective-permute-done | bytes 131104 | tf_op jit(solution)/shard_map/ppermute | solution.py:37
  13.5 4.6 %collective-permute-start.4 = (bf16[128,512]{1,0:T(8,128)(2,1)S(1)}, bf16[128,512]{1,0:T(8,128)(2,1)S(1)}, u32[]{:S(2)}, u32[]{:S(2)}) collective-permute-start(bf16[128,512]{1,0:T(8,128)(2,1)S(1)} %collective-permute-done.2.refs_2_), channel_id=1, source_target_pairs={{64,0},{96,32},{128,64},{160,96},{192,128},{224,160},{0,192},{32,2... | collective-permute-start | bytes 393224 | tf_op jit(solution)/shard_map/ppermute | solution.py:37
  18.2 2.0 %collective-permute-start.6 = (bf16[128,512]{1,0:T(8,128)(2,1)S(1)}, bf16[128,512]{1,0:T(8,128)(2,1)S(1)}, u32[]{:S(2)}, u32[]{:S(2)}) collective-permute-start(bf16[128,512]{1,0:T(8,128)(2,1)S(1)} %collective-permute-done.5.refs_6_), channel_id=1, source_target_pairs={{224,0},{0,32},{32,64},{64,96},{96,128},{128,160},{160,192},{192,2... | collective-permute-start | bytes 393224 | tf_op jit(solution)/shard_map/ppermute | solution.py:37
  22.5 2.3 %collective-permute-done.3.refs_3_ = bf16[128,512]{1,0:T(8,128)(2,1)S(1)} collective-permute-done((bf16[128,512]{1,0:T(8,128)(2,1)S(1)}, bf16[128,512]{1,0:T(8,128)(2,1)S(1)}, u32[]{:S(2)}, u32[]{:S(2)}) %collective-permute-start.3) | collective-permute-done | bytes 131104 | tf_op jit(solution)/shard_map/ppermute | solution.py:37
  25.6 1.9 %collective-permute-done.8.got = bf16[8,64,512]{2,1,0:T(8,128)(2,1)S(1)} collective-permute-done((bf16[8,64,512]{2,1,0:T(8,128)(2,1)S(1)}, bf16[8,64,512]{2,1,0:T(8,128)(2,1)S(1)}, u32[]{:S(2)}, u32[]{:S(2)}) %collective-permute-start.8) | collective-permute-done | bytes 524320 | tf_op jit(solution)/shard_map/ppermute | solution.py:33
  27.7 16.4 %all_to_all.15.parts = bf16[8,64,512]{2,1,0:T(8,128)(2,1)S(1)} all-to-all(bf16[8,64,512]{2,1,0:T(8,128)(2,1)S(1)} %shard_map.84), channel_id=1, replica_groups=mesh['zh'=4,'zl'=2,'xl'=2,'xh'=2,'y'=4,'c'=2] {'xh','y'}, dimensions={0} | all-to-all | bytes 1048576 | tf_op jit(solution)/shard_map/all_to_all | solution.py:345
  44.8 3.7 %collective-permute-start.10 = (bf16[72,512]{1,0:T(8,128)(2,1)S(1)}, bf16[72,512]{1,0:T(8,128)(2,1)S(1)}, u32[]{:S(2)}, u32[]{:S(2)}) collective-permute-start(bf16[72,512]{1,0:T(8,128)(2,1)S(1)} %shard_map.85.refs_0_), channel_id=1, source_target_pairs={{64,0},{96,32},{128,64},{160,96},{192,128},{224,160},{0,192},{32,2... | collective-permute-start | bytes 221192 | tf_op jit(solution)/shard_map/ppermute | solution.py:37
  48.8 2.9 %collective-permute-start.9 = (bf16[72,512]{1,0:T(8,128)(2,1)S(1)}, bf16[72,512]{1,0:T(8,128)(2,1)S(1)}, u32[]{:S(2)}, u32[]{:S(2)}) collective-permute-start(bf16[72,512]{1,0:T(8,128)(2,1)S(1)} %shard_map.85.refs_0_), channel_id=1, source_target_pairs={{32,0},{64,32},{96,64},{128,96},{160,128},{192,160},{224,192},{0,2... | collective-permute-start | bytes 221192 | tf_op jit(solution)/shard_map/ppermute | solution.py:37
  51.8 4.5 %collective-permute-start.12 = (bf16[72,512]{1,0:T(8,128)(2,1)S(1)}, bf16[72,512]{1,0:T(8,128)(2,1)S(1)}, u32[]{:S(2)}, u32[]{:S(2)}) collective-permute-start(bf16[72,512]{1,0:T(8,128)(2,1)S(1)} %collective-permute-done.10.refs_2_), channel_id=1, source_target_pairs={{64,0},{96,32},{128,64},{160,96},{192,128},{224,160},{0,192},{32,2... | collective-permute-start | bytes 221192 | tf_op jit(solution)/shard_map/ppermute | solution.py:37
  58.7 2.0 %collective-permute-done.11.refs_3_ = bf16[72,512]{1,0:T(8,128)(2,1)S(1)} collective-permute-done((bf16[72,512]{1,0:T(8,128)(2,1)S(1)}, bf16[72,512]{1,0:T(8,128)(2,1)S(1)}, u32[]{:S(2)}, u32[]{:S(2)}) %collective-permute-start.11) | collective-permute-done | bytes 73760 | tf_op jit(solution)/shard_map/ppermute | solution.py:37
  61.9 28.7 %all_to_all.16 = bf16[16,16,4096]{2,1,0:T(8,128)(2,1)S(1)} all-to-all(bf16[16,16,4096]{2,1,0:T(8,128)(2,1)S(1)} %bitcast.10), channel_id=1, replica_groups=mesh['zh'=4,'zl'=2,'xl'=2,'xh'=2,'y'=4,'c'=2] {'y','xl','xh'}, dimensions={0} | all-to-all | bytes 4194304 | tf_op jit(solution)/shard_map/all_to_all | solution.py:350
  90.7 3.5 %shard_map.87.mine = bf16[256,4096]{1,0:T(8,128)(2,1)S(1)} custom-call(bf16[256,4096]{1,0:T(8,128)(2,1)S(1)} %bitcast.9, bf16[1,4096,384]{2,1,0:T(8,128)(2,1)S(1)} %copy-done, bf16[1,4096,384]{2,1,0:T(8,128)(2,1)S(1)} %copy-done.1, bf16[1,384,4096]{2,1,0:T(8,128)(2,1)S(1)} %copy-done.2), custom_call_target="tpu_custom_call" | custom-call | flops 2415919104 | bytes 13631488 | tf_op jit(solution)/shard_map/pallas_call | solution.py:278
  94.8 1.9 %shard_map.89 = bf16[128,4096]{1,0:T(8,128)(2,1)S(1)} custom-call(bf16[256,4096]{1,0:T(8,128)(2,1)S(1)} %collective-permute-done.16.rows, bf16[1,4096,384]{2,1,0:T(8,128)(2,1)S(1)} %copy-done, bf16[1,4096,384]{2,1,0:T(8,128)(2,1)S(1)} %copy-done.1, bf16[1,384,4096]{2,1,0:T(8,128)(2,1)S(1)} %copy-done.2), custom_call_target="tpu_custom_call" | custom-call | flops 1207959552 | bytes 11534336 | tf_op jit(solution)/shard_map/pallas_call | solution.py:278
  97.0 1.9 %shard_map.88 = bf16[128,4096]{1,0:T(8,128)(2,1)S(1)} custom-call(bf16[256,4096]{1,0:T(8,128)(2,1)S(1)} %collective-permute-done.16.rows, bf16[1,4096,384]{2,1,0:T(8,128)(2,1)S(1)} %copy-done, bf16[1,4096,384]{2,1,0:T(8,128)(2,1)S(1)} %copy-done.1, bf16[1,384,4096]{2,1,0:T(8,128)(2,1)S(1)} %copy-done.2), custom_call_target="tpu_custom_call" | custom-call | flops 1207959552 | bytes 11534336 | tf_op jit(solution)/shard_map/pallas_call | solution.py:278
  99.8 1.9 %collective-permute-done.17.part = bf16[128,4096]{1,0:T(8,128)(2,1)S(1)} collective-permute-done((bf16[128,4096]{1,0:T(8,128)(2,1)S(1)}, bf16[128,4096]{1,0:T(8,128)(2,1)S(1)}, u32[]{:S(2)}, u32[]{:S(2)}) %collective-permute-start.17) | collective-permute-done | bytes 1048608 | tf_op jit(solution)/shard_map/ppermute | solution.py:33
  102.0 33.3 %all_to_all.17 = bf16[32,8,4096]{2,1,0:T(8,128)(2,1)S(1)} all-to-all(bf16[32,8,4096]{2,1,0:T(8,128)(2,1)S(1)} %bitcast.6), channel_id=1, replica_groups=mesh['zh'=4,'zl'=2,'xl'=2,'xh'=2,'y'=4,'c'=2] {'y','xl','xh','zl'}, dimensions={0} | all-to-all | bytes 4194304 | tf_op jit(solution)/shard_map/all_to_all | solution.py:361
  136.1 3.0 %collective-permute-start.19 = (bf16[8,4096]{1,0:T(8,128)(2,1)S(1)}, bf16[8,4096]{1,0:T(8,128)(2,1)S(1)}, u32[]{:S(2)}, u32[]{:S(2)}) collective-permute-start(bf16[8,4096]{1,0:T(8,128)(2,1)S(1)} %get-tuple-element.30), channel_id=1, source_target_pairs={{128,0},{192,64},{0,128},{64,192},{129,1},{193,65},{1,129},{65,193... | collective-permute-start | bytes 196616 | tf_op jit(solution)/shard_map/ppermute | solution.py:37
  139.1 2.8 %collective-permute-start.20 = (bf16[8,4096]{1,0:T(8,128)(2,1)S(1)}, bf16[8,4096]{1,0:T(8,128)(2,1)S(1)}, u32[]{:S(2)}, u32[]{:S(2)}) collective-permute-start(bf16[8,4096]{1,0:T(8,128)(2,1)S(1)} %get-tuple-element.31), channel_id=1, source_target_pairs={{192,0},{0,64},{64,128},{128,192},{193,1},{1,65},{65,129},{129,193... | collective-permute-start | bytes 196616 | tf_op jit(solution)/shard_map/ppermute | solution.py:37
  141.9 1.3 collective-permute-start.21
  143.2 1.9 %collective-permute-done.19 = bf16[8,4096]{1,0:T(8,128)(2,1)S(1)} collective-permute-done((bf16[8,4096]{1,0:T(8,128)(2,1)S(1)}, bf16[8,4096]{1,0:T(8,128)(2,1)S(1)}, u32[]{:S(2)}, u32[]{:S(2)}) %collective-permute-start.19) | collective-permute-done | bytes 65568 | tf_op jit(solution)/shard_map/ppermute | solution.py:37
  145.1 1.4 collective-permute-done.20
  146.6 1.3 collective-permute-done.21
  (51 shorter events, 12.3 us)
Async XLA Ops:
  0.0 18.2 %collective-permute-start = (bf16[512,256]{1,0:T(8,128)(2,1)}, bf16[512,256]{1,0:T(8,128)(2,1)S(1)}, u32[]{:S(2)}, u32[]{:S(2)}) collective-permute-start(bf16[512,256]{1,0:T(8,128)(2,1)} %own.1), channel_id=1, source_target_pairs={{0,16},{16,0},{1,17},{17,1},{2,18},{18,2},{3,19},{19,3},{4,20},{20... | collective-permute-start | bytes 786440 | tf_op jit(solution)/shard_map/ppermute | solution.py:33
  0.8 12.7 %collective-permute-start.2 = (bf16[128,512]{1,0:T(8,128)(2,1)}, bf16[128,512]{1,0:T(8,128)(2,1)S(1)}, u32[]{:S(2)}, u32[]{:S(2)}) collective-permute-start(bf16[128,512]{1,0:T(8,128)(2,1)} %context.1), channel_id=1, source_target_pairs={{64,0},{96,32},{128,64},{160,96},{192,128},{224,160},{0,192},{32,2... | collective-permute-start | bytes 393224 | tf_op jit(solution)/shard_map/ppermute | solution.py:37
  7.1 11.0 %collective-permute-start.5 = (bf16[128,512]{1,0:T(8,128)(2,1)}, bf16[128,512]{1,0:T(8,128)(2,1)S(1)}, u32[]{:S(2)}, u32[]{:S(2)}) collective-permute-start(bf16[128,512]{1,0:T(8,128)(2,1)} %context.1), channel_id=1, source_target_pairs={{192,0},{224,32},{0,64},{32,96},{64,128},{96,160},{128,192},{160,2... | collective-permute-start | bytes 393224 | tf_op jit(solution)/shard_map/ppermute | solution.py:37
  7.1 15.0 %collective-permute-start.1 = (bf16[128,512]{1,0:T(8,128)(2,1)}, bf16[128,512]{1,0:T(8,128)(2,1)S(1)}, u32[]{:S(2)}, u32[]{:S(2)}) collective-permute-start(bf16[128,512]{1,0:T(8,128)(2,1)} %context.1), channel_id=1, source_target_pairs={{32,0},{64,32},{96,64},{128,96},{160,128},{192,160},{224,192},{0,2... | collective-permute-start | bytes 393224 | tf_op jit(solution)/shard_map/ppermute | solution.py:37
  10.8 11.3 %collective-permute-start.7 = (bf16[128,512]{1,0:T(8,128)(2,1)}, bf16[128,512]{1,0:T(8,128)(2,1)S(1)}, u32[]{:S(2)}, u32[]{:S(2)}) collective-permute-start(bf16[128,512]{1,0:T(8,128)(2,1)} %context.1), channel_id=1, source_target_pairs={{224,0},{0,32},{32,64},{64,96},{96,128},{128,160},{160,192},{192,2... | collective-permute-start | bytes 393224 | tf_op jit(solution)/shard_map/ppermute | solution.py:37
  13.5 9.0 %collective-permute-start.4 = (bf16[128,512]{1,0:T(8,128)(2,1)S(1)}, bf16[128,512]{1,0:T(8,128)(2,1)S(1)}, u32[]{:S(2)}, u32[]{:S(2)}) collective-permute-start(bf16[128,512]{1,0:T(8,128)(2,1)S(1)} %collective-permute-done.2.refs_2_), channel_id=1, source_target_pairs={{64,0},{96,32},{128,64},{160,96},{192,128},{224,160},{0,192},{32,2... | collective-permute-start | bytes 393224 | tf_op jit(solution)/shard_map/ppermute | solution.py:37
  18.2 6.6 %collective-permute-start.3 = (bf16[128,512]{1,0:T(8,128)(2,1)S(1)}, bf16[128,512]{1,0:T(8,128)(2,1)S(1)}, u32[]{:S(2)}, u32[]{:S(2)}) collective-permute-start(bf16[128,512]{1,0:T(8,128)(2,1)S(1)} %collective-permute-done.2.refs_2_), channel_id=1, source_target_pairs={{32,0},{64,32},{96,64},{128,96},{160,128},{192,160},{224,192},{0,2... | collective-permute-start | bytes 393224 | tf_op jit(solution)/shard_map/ppermute | solution.py:37
  18.2 6.6 %collective-permute-start.6 = (bf16[128,512]{1,0:T(8,128)(2,1)S(1)}, bf16[128,512]{1,0:T(8,128)(2,1)S(1)}, u32[]{:S(2)}, u32[]{:S(2)}) collective-permute-start(bf16[128,512]{1,0:T(8,128)(2,1)S(1)} %collective-permute-done.5.refs_6_), channel_id=1, source_target_pairs={{224,0},{0,32},{32,64},{64,96},{96,128},{128,160},{160,192},{192,2... | collective-permute-start | bytes 393224 | tf_op jit(solution)/shard_map/ppermute | solution.py:37
  24.8 65.9 %copy-start.2 = (bf16[1,384,4096]{2,1,0:T(8,128)(2,1)S(1)}, bf16[1,384,4096]{2,1,0:T(8,128)(2,1)}, u32[]{:S(2)}) copy-start(bf16[1,384,4096]{2,1,0:T(8,128)(2,1)} %w_down.5) | copy-start | bytes 9437188
  25.5 2.0 %collective-permute-start.8 = (bf16[8,64,512]{2,1,0:T(8,128)(2,1)S(1)}, bf16[8,64,512]{2,1,0:T(8,128)(2,1)S(1)}, u32[]{:S(2)}, u32[]{:S(2)}) collective-permute-start(bf16[8,64,512]{2,1,0:T(8,128)(2,1)S(1)} %get-tuple-element.22), channel_id=1, source_target_pairs={{0,1},{1,0},{2,3},{3,2},{4,5},{5,4},{6,7},{7,6},{8,9},{9,8},{10,11... | collective-permute-start | bytes 1572872 | tf_op jit(solution)/shard_map/ppermute | solution.py:33
  27.6 63.0 %copy-start.1 = (bf16[1,4096,384]{2,1,0:T(8,128)(2,1)S(1)}, bf16[1,4096,384]{2,1,0:T(8,128)(2,1)}, u32[]{:S(2)}) copy-start(bf16[1,4096,384]{2,1,0:T(8,128)(2,1)} %w_up.5) | copy-start | bytes 9437188
  44.2 7.6 %collective-permute-start.13 = (bf16[72,512]{1,0:T(8,128)(2,1)S(1)}, bf16[72,512]{1,0:T(8,128)(2,1)S(1)}, u32[]{:S(2)}, u32[]{:S(2)}) collective-permute-start(bf16[72,512]{1,0:T(8,128)(2,1)S(1)} %shard_map.85.refs_0_), channel_id=1, source_target_pairs={{192,0},{224,32},{0,64},{32,96},{64,128},{96,160},{128,192},{160,2... | collective-permute-start | bytes 221192 | tf_op jit(solution)/shard_map/ppermute | solution.py:37
  44.8 7.1 %collective-permute-start.10 = (bf16[72,512]{1,0:T(8,128)(2,1)S(1)}, bf16[72,512]{1,0:T(8,128)(2,1)S(1)}, u32[]{:S(2)}, u32[]{:S(2)}) collective-permute-start(bf16[72,512]{1,0:T(8,128)(2,1)S(1)} %shard_map.85.refs_0_), channel_id=1, source_target_pairs={{64,0},{96,32},{128,64},{160,96},{192,128},{224,160},{0,192},{32,2... | collective-permute-start | bytes 221192 | tf_op jit(solution)/shard_map/ppermute | solution.py:37
  48.4 7.9 %collective-permute-start.15 = (bf16[72,512]{1,0:T(8,128)(2,1)S(1)}, bf16[72,512]{1,0:T(8,128)(2,1)S(1)}, u32[]{:S(2)}, u32[]{:S(2)}) collective-permute-start(bf16[72,512]{1,0:T(8,128)(2,1)S(1)} %shard_map.85.refs_0_), channel_id=1, source_target_pairs={{224,0},{0,32},{32,64},{64,96},{96,128},{128,160},{160,192},{192,2... | collective-permute-start | bytes 221192 | tf_op jit(solution)/shard_map/ppermute | solution.py:37
  48.8 7.6 %collective-permute-start.9 = (bf16[72,512]{1,0:T(8,128)(2,1)S(1)}, bf16[72,512]{1,0:T(8,128)(2,1)S(1)}, u32[]{:S(2)}, u32[]{:S(2)}) collective-permute-start(bf16[72,512]{1,0:T(8,128)(2,1)S(1)} %shard_map.85.refs_0_), channel_id=1, source_target_pairs={{32,0},{64,32},{96,64},{128,96},{160,128},{192,160},{224,192},{0,2... | collective-permute-start | bytes 221192 | tf_op jit(solution)/shard_map/ppermute | solution.py:37
  51.8 5.6 %collective-permute-start.14 = (bf16[72,512]{1,0:T(8,128)(2,1)S(1)}, bf16[72,512]{1,0:T(8,128)(2,1)S(1)}, u32[]{:S(2)}, u32[]{:S(2)}) collective-permute-start(bf16[72,512]{1,0:T(8,128)(2,1)S(1)} %collective-permute-done.13.refs_6_), channel_id=1, source_target_pairs={{224,0},{0,32},{32,64},{64,96},{96,128},{128,160},{160,192},{192,2... | collective-permute-start | bytes 221192 | tf_op jit(solution)/shard_map/ppermute | solution.py:37
  51.8 6.8 %collective-permute-start.12 = (bf16[72,512]{1,0:T(8,128)(2,1)S(1)}, bf16[72,512]{1,0:T(8,128)(2,1)S(1)}, u32[]{:S(2)}, u32[]{:S(2)}) collective-permute-start(bf16[72,512]{1,0:T(8,128)(2,1)S(1)} %collective-permute-done.10.refs_2_), channel_id=1, source_target_pairs={{64,0},{96,32},{128,64},{160,96},{192,128},{224,160},{0,192},{32,2... | collective-permute-start | bytes 221192 | tf_op jit(solution)/shard_map/ppermute | solution.py:37
  56.3 4.4 %collective-permute-start.11 = (bf16[72,512]{1,0:T(8,128)(2,1)S(1)}, bf16[72,512]{1,0:T(8,128)(2,1)S(1)}, u32[]{:S(2)}, u32[]{:S(2)}) collective-permute-start(bf16[72,512]{1,0:T(8,128)(2,1)S(1)} %collective-permute-done.10.refs_2_), channel_id=1, source_target_pairs={{32,0},{64,32},{96,64},{128,96},{160,128},{192,160},{224,192},{0,2... | collective-permute-start | bytes 221192 | tf_op jit(solution)/shard_map/ppermute | solution.py:37
  90.7 4.2 %collective-permute-start.16 = (bf16[256,4096]{1,0:T(8,128)(2,1)S(1)}, bf16[256,4096]{1,0:T(8,128)(2,1)S(1)}, u32[]{:S(2)}, u32[]{:S(2)}) collective-permute-start(bf16[256,4096]{1,0:T(8,128)(2,1)S(1)} %bitcast.8), channel_id=1, source_target_pairs={{0,1},{1,0},{2,3},{3,2},{4,5},{5,4},{6,7},{7,6},{8,9},{9,8},{10,11... | collective-permute-start | bytes 6291464 | tf_op jit(solution)/shard_map/ppermute | solution.py:33
  96.8 2.7 %collective-permute-start.18 = (bf16[128,4096]{1,0:T(8,128)(2,1)S(1)}, bf16[128,4096]{1,0:T(8,128)(2,1)S(1)}, u32[]{:S(2)}, u32[]{:S(2)}) collective-permute-start(bf16[128,4096]{1,0:T(8,128)(2,1)S(1)} %shard_map.89), channel_id=1, source_target_pairs={{0,1},{1,0},{2,3},{3,2},{4,5},{5,4},{6,7},{7,6},{8,9},{9,8},{10,11... | collective-permute-start | bytes 3145736 | tf_op jit(solution)/shard_map/ppermute | solution.py:33
  98.9 2.8 %collective-permute-start.17 = (bf16[128,4096]{1,0:T(8,128)(2,1)S(1)}, bf16[128,4096]{1,0:T(8,128)(2,1)S(1)}, u32[]{:S(2)}, u32[]{:S(2)}) collective-permute-start(bf16[128,4096]{1,0:T(8,128)(2,1)S(1)} %shard_map.88), channel_id=1, source_target_pairs={{0,1},{1,0},{2,3},{3,2},{4,5},{5,4},{6,7},{7,6},{8,9},{9,8},{10,11... | collective-permute-start | bytes 3145736 | tf_op jit(solution)/shard_map/ppermute | solution.py:33
  136.1 9.1 %collective-permute-start.19 = (bf16[8,4096]{1,0:T(8,128)(2,1)S(1)}, bf16[8,4096]{1,0:T(8,128)(2,1)S(1)}, u32[]{:S(2)}, u32[]{:S(2)}) collective-permute-start(bf16[8,4096]{1,0:T(8,128)(2,1)S(1)} %get-tuple-element.30), channel_id=1, source_target_pairs={{128,0},{192,64},{0,128},{64,192},{129,1},{193,65},{1,129},{65,193... | collective-permute-start | bytes 196616 | tf_op jit(solution)/shard_map/ppermute | solution.py:37
  139.1 7.5 %collective-permute-start.20 = (bf16[8,4096]{1,0:T(8,128)(2,1)S(1)}, bf16[8,4096]{1,0:T(8,128)(2,1)S(1)}, u32[]{:S(2)}, u32[]{:S(2)}) collective-permute-start(bf16[8,4096]{1,0:T(8,128)(2,1)S(1)} %get-tuple-element.31), channel_id=1, source_target_pairs={{192,0},{0,64},{64,128},{128,192},{193,1},{1,65},{65,129},{129,193... | collective-permute-start | bytes 196616 | tf_op jit(solution)/shard_map/ppermute | solution.py:37
  141.9 6.0 %collective-permute-start.21 = (bf16[8,4096]{1,0:T(8,128)(2,1)S(1)}, bf16[8,4096]{1,0:T(8,128)(2,1)S(1)}, u32[]{:S(2)}, u32[]{:S(2)}) collective-permute-start(bf16[8,4096]{1,0:T(8,128)(2,1)S(1)} %get-tuple-element.32), channel_id=1, source_target_pairs={{64,0},{128,64},{192,128},{0,192},{65,1},{129,65},{193,129},{1,193... | collective-permute-start | bytes 196616 | tf_op jit(solution)/shard_map/ppermute | solution.py:37
  (6 other events, 104.3 us)

commit v12 on v11

--- a/solution.py
+++ b/solution.py
@@ -333,6 +333,24 @@
     )(high, low, back, own)
 
 
+def finish_kernel(base, *refs):
+    out = refs[-1]
+    total = base[...]
+    for part in refs[:-1]:
+        total += part[...].astype(F32)
+    out[...] = total.astype(BF16)
+
+
+def finish(base, parts):
+    return pl.pallas_call(
+        finish_kernel,
+        out_shape=jax.ShapeDtypeStruct(base.shape, BF16),
+        in_specs=[VMEM] * (1 + len(parts)),
+        out_specs=VMEM,
+        compiler_params=params(16),
+    )(base, *parts)
+
+
 def on_device(context, proj_weight, norm_gain, expert_ids, gate_values, w_gate, w_up, w_down):
     zi, xli, ci = (lax.axis_index(a).astype(jnp.int32) for a in (RING, "xl", "c"))
     place = (4 * zi + 2 * xli + ci).reshape(1)
@@ -360,10 +378,8 @@
     summed = add_rows(mine_out, bottom, add_rows(mine_out, top)).reshape(n_peers, -1, width)
     back = lax.all_to_all(summed, PEERS, 0, 0, tiled=True).reshape(-1, width)
 
-    total, *blocks = combine(high, low, back, own)
-    for hop in (2, 1, 3):
-        total += fetch_pair(blocks[hop - 1], -hop).astype(F32)
-    return total.astype(BF16)
+    base, *blocks = combine(high, low, back, own)
+    return finish(base, [fetch_pair(blocks[hop - 1], -hop) for hop in (2, 1, 3)])
 
 
 def solution(mesh):

time: 149 us -> 149 us (level)
  no operation moved by 1% of the time
where the time goes in v12:
time: 149 us
  blocking collectives  78.5 us (53%)
  starting transfers between devices  37.3 us (25%)
  waiting for transfers between devices  19.1 us (13%)
  Pallas kernels  11.6 us (8%)
  local copies, waits for them, and re-layouts  1.88 us (1%)
    ppermute x17, starting transfers between devices, fetch(): return lax.ppermute(x, axis, [((i + hop) % size, i) for i in range(size)])  35.7 us
    all_to_all x1, blocking collectives, on_device(): back = lax.all_to_all(summed, PEERS, 0, 0, tiled=True).reshape(-1, width)  33.3 us
    all_to_all x1, blocking collectives, on_device(): lax.all_to_all(sent.reshape(n_plane, -1, width), PLANE, 0, 0, tiled=True)  28.7 us
    all_to_all x1, blocking collectives, on_device(): partial = lax.all_to_all(partial, SPREAD, 0, 0, tiled=True)  16.4 us
    ppermute x17, waiting for transfers between devices, fetch(): return lax.ppermute(x, axis, [((i + hop) % size, i) for i in range(size)])  14.5 us
    pallas_call x3, Pallas kernels, expert_rows(): pl.pallas_call(functools.partial(expert_kernel, first), out_shape=jax.Sha...  7.32 us
    ppermute x5, waiting for transfers between devices, swap(): return lax.ppermute(x, axis, [(0, 1), (1, 0)])  4.57 us
  transfers between devices with their start and end apart: 22, of which 14 were waited for; matrix products, arithmetic and copies ran while one was open for 0% of the time, Pallas kernels for 4%

profile of v12, /device:TPU:6, one launch (start us, length us, event | category | flops | bytes accessed | tf_op | source)
XLA Modules:
  0.0 148.5 jit_solution(17941964536001251799)
XLA Ops:
  0.8 6.3 %collective-permute-start.2 = (bf16[128,512]{1,0:T(8,128)(2,1)}, bf16[128,512]{1,0:T(8,128)(2,1)S(1)}, u32[]{:S(2)}, u32[]{:S(2)}) collective-permute-start(bf16[128,512]{1,0:T(8,128)(2,1)} %context.1), channel_id=1, source_target_pairs={{64,0},{96,32},{128,64},{160,96},{192,128},{224,160},{0,192},{32,2... | collective-permute-start | bytes 393224 | tf_op jit(solution)/shard_map/ppermute | solution.py:37
  7.1 3.7 %collective-permute-start.1 = (bf16[128,512]{1,0:T(8,128)(2,1)}, bf16[128,512]{1,0:T(8,128)(2,1)S(1)}, u32[]{:S(2)}, u32[]{:S(2)}) collective-permute-start(bf16[128,512]{1,0:T(8,128)(2,1)} %context.1), channel_id=1, source_target_pairs={{32,0},{64,32},{96,64},{128,96},{160,128},{192,160},{224,192},{0,2... | collective-permute-start | bytes 393224 | tf_op jit(solution)/shard_map/ppermute | solution.py:37
  10.8 2.7 %collective-permute-done.2.refs_2_ = bf16[128,512]{1,0:T(8,128)(2,1)S(1)} collective-permute-done((bf16[128,512]{1,0:T(8,128)(2,1)}, bf16[128,512]{1,0:T(8,128)(2,1)S(1)}, u32[]{:S(2)}, u32[]{:S(2)}) %collective-permute-start.2) | collective-permute-done | bytes 131104 | tf_op jit(solution)/shard_map/ppermute | solution.py:37
  13.5 4.6 %collective-permute-start.4 = (bf16[128,512]{1,0:T(8,128)(2,1)S(1)}, bf16[128,512]{1,0:T(8,128)(2,1)S(1)}, u32[]{:S(2)}, u32[]{:S(2)}) collective-permute-start(bf16[128,512]{1,0:T(8,128)(2,1)S(1)} %collective-permute-done.2.refs_2_), channel_id=1, source_target_pairs={{64,0},{96,32},{128,64},{160,96},{192,128},{224,160},{0,192},{32,2... | collective-permute-start | bytes 393224 | tf_op jit(solution)/shard_map/ppermute | solution.py:37
  18.2 2.0 %collective-permute-start.6 = (bf16[128,512]{1,0:T(8,128)(2,1)S(1)}, bf16[128,512]{1,0:T(8,128)(2,1)S(1)}, u32[]{:S(2)}, u32[]{:S(2)}) collective-permute-start(bf16[128,512]{1,0:T(8,128)(2,1)S(1)} %collective-permute-done.5.refs_6_), channel_id=1, source_target_pairs={{224,0},{0,32},{32,64},{64,96},{96,128},{128,160},{160,192},{192,2... | collective-permute-start | bytes 393224 | tf_op jit(solution)/shard_map/ppermute | solution.py:37
  22.5 2.3 %collective-permute-done.3.refs_3_ = bf16[128,512]{1,0:T(8,128)(2,1)S(1)} collective-permute-done((bf16[128,512]{1,0:T(8,128)(2,1)S(1)}, bf16[128,512]{1,0:T(8,128)(2,1)S(1)}, u32[]{:S(2)}, u32[]{:S(2)}) %collective-permute-start.3) | collective-permute-done | bytes 131104 | tf_op jit(solution)/shard_map/ppermute | solution.py:37
  25.6 1.9 %collective-permute-done.8.got = bf16[8,64,512]{2,1,0:T(8,128)(2,1)S(1)} collective-permute-done((bf16[8,64,512]{2,1,0:T(8,128)(2,1)S(1)}, bf16[8,64,512]{2,1,0:T(8,128)(2,1)S(1)}, u32[]{:S(2)}, u32[]{:S(2)}) %collective-permute-start.8) | collective-permute-done | bytes 524320 | tf_op jit(solution)/shard_map/ppermute | solution.py:33
  27.7 16.4 %all_to_all.15.parts = bf16[8,64,512]{2,1,0:T(8,128)(2,1)S(1)} all-to-all(bf16[8,64,512]{2,1,0:T(8,128)(2,1)S(1)} %shard_map.84), channel_id=1, replica_groups=mesh['zh'=4,'zl'=2,'xl'=2,'xh'=2,'y'=4,'c'=2] {'xh','y'}, dimensions={0} | all-to-all | bytes 1048576 | tf_op jit(solution)/shard_map/all_to_all | solution.py:363
  44.8 3.7 %collective-permute-start.10 = (bf16[72,512]{1,0:T(8,128)(2,1)S(1)}, bf16[72,512]{1,0:T(8,128)(2,1)S(1)}, u32[]{:S(2)}, u32[]{:S(2)}) collective-permute-start(bf16[72,512]{1,0:T(8,128)(2,1)S(1)} %shard_map.85.refs_0_), channel_id=1, source_target_pairs={{64,0},{96,32},{128,64},{160,96},{192,128},{224,160},{0,192},{32,2... | collective-permute-start | bytes 221192 | tf_op jit(solution)/shard_map/ppermute | solution.py:37
  48.8 2.9 %collective-permute-start.9 = (bf16[72,512]{1,0:T(8,128)(2,1)S(1)}, bf16[72,512]{1,0:T(8,128)(2,1)S(1)}, u32[]{:S(2)}, u32[]{:S(2)}) collective-permute-start(bf16[72,512]{1,0:T(8,128)(2,1)S(1)} %shard_map.85.refs_0_), channel_id=1, source_target_pairs={{32,0},{64,32},{96,64},{128,96},{160,128},{192,160},{224,192},{0,2... | collective-permute-start | bytes 221192 | tf_op jit(solution)/shard_map/ppermute | solution.py:37
  51.8 4.5 %collective-permute-start.12 = (bf16[72,512]{1,0:T(8,128)(2,1)S(1)}, bf16[72,512]{1,0:T(8,128)(2,1)S(1)}, u32[]{:S(2)}, u32[]{:S(2)}) collective-permute-start(bf16[72,512]{1,0:T(8,128)(2,1)S(1)} %collective-permute-done.10.refs_2_), channel_id=1, source_target_pairs={{64,0},{96,32},{128,64},{160,96},{192,128},{224,160},{0,192},{32,2... | collective-permute-start | bytes 221192 | tf_op jit(solution)/shard_map/ppermute | solution.py:37
  58.7 2.0 %collective-permute-done.11.refs_3_ = bf16[72,512]{1,0:T(8,128)(2,1)S(1)} collective-permute-done((bf16[72,512]{1,0:T(8,128)(2,1)S(1)}, bf16[72,512]{1,0:T(8,128)(2,1)S(1)}, u32[]{:S(2)}, u32[]{:S(2)}) %collective-permute-start.11) | collective-permute-done | bytes 73760 | tf_op jit(solution)/shard_map/ppermute | solution.py:37
  61.9 28.7 %all_to_all.16 = bf16[16,16,4096]{2,1,0:T(8,128)(2,1)S(1)} all-to-all(bf16[16,16,4096]{2,1,0:T(8,128)(2,1)S(1)} %bitcast.10), channel_id=1, replica_groups=mesh['zh'=4,'zl'=2,'xl'=2,'xh'=2,'y'=4,'c'=2] {'y','xl','xh'}, dimensions={0} | all-to-all | bytes 4194304 | tf_op jit(solution)/shard_map/all_to_all | solution.py:368
  90.7 3.5 %shard_map.87.mine = bf16[256,4096]{1,0:T(8,128)(2,1)S(1)} custom-call(bf16[256,4096]{1,0:T(8,128)(2,1)S(1)} %bitcast.9, bf16[1,4096,384]{2,1,0:T(8,128)(2,1)S(1)} %copy-done, bf16[1,4096,384]{2,1,0:T(8,128)(2,1)S(1)} %copy-done.1, bf16[1,384,4096]{2,1,0:T(8,128)(2,1)S(1)} %copy-done.2), custom_call_target="tpu_custom_call" | custom-call | flops 2415919104 | bytes 13631488 | tf_op jit(solution)/shard_map/pallas_call | solution.py:278
  94.8 1.9 %shard_map.89 = bf16[128,4096]{1,0:T(8,128)(2,1)S(1)} custom-call(bf16[256,4096]{1,0:T(8,128)(2,1)S(1)} %collective-permute-done.16.rows, bf16[1,4096,384]{2,1,0:T(8,128)(2,1)S(1)} %copy-done, bf16[1,4096,384]{2,1,0:T(8,128)(2,1)S(1)} %copy-done.1, bf16[1,384,4096]{2,1,0:T(8,128)(2,1)S(1)} %copy-done.2), custom_call_target="tpu_custom_call" | custom-call | flops 1207959552 | bytes 11534336 | tf_op jit(solution)/shard_map/pallas_call | solution.py:278
  97.0 1.9 %shard_map.88 = bf16[128,4096]{1,0:T(8,128)(2,1)S(1)} custom-call(bf16[256,4096]{1,0:T(8,128)(2,1)S(1)} %collective-permute-done.16.rows, bf16[1,4096,384]{2,1,0:T(8,128)(2,1)S(1)} %copy-done, bf16[1,4096,384]{2,1,0:T(8,128)(2,1)S(1)} %copy-done.1, bf16[1,384,4096]{2,1,0:T(8,128)(2,1)S(1)} %copy-done.2), custom_call_target="tpu_custom_call" | custom-call | flops 1207959552 | bytes 11534336 | tf_op jit(solution)/shard_map/pallas_call | solution.py:278
  99.8 1.9 %collective-permute-done.17.part = bf16[128,4096]{1,0:T(8,128)(2,1)S(1)} collective-permute-done((bf16[128,4096]{1,0:T(8,128)(2,1)S(1)}, bf16[128,4096]{1,0:T(8,128)(2,1)S(1)}, u32[]{:S(2)}, u32[]{:S(2)}) %collective-permute-start.17) | collective-permute-done | bytes 1048608 | tf_op jit(solution)/shard_map/ppermute | solution.py:33
  102.0 33.3 %all_to_all.17 = bf16[32,8,4096]{2,1,0:T(8,128)(2,1)S(1)} all-to-all(bf16[32,8,4096]{2,1,0:T(8,128)(2,1)S(1)} %bitcast.6), channel_id=1, replica_groups=mesh['zh'=4,'zl'=2,'xl'=2,'xh'=2,'y'=4,'c'=2] {'y','xl','xh','zl'}, dimensions={0} | all-to-all | bytes 4194304 | tf_op jit(solution)/shard_map/all_to_all | solution.py:379
  136.1 3.0 %collective-permute-start.19 = (bf16[8,4096]{1,0:T(8,128)(2,1)S(1)}, bf16[8,4096]{1,0:T(8,128)(2,1)S(1)}, u32[]{:S(2)}, u32[]{:S(2)}) collective-permute-start(bf16[8,4096]{1,0:T(8,128)(2,1)S(1)} %get-tuple-element.30), channel_id=1, source_target_pairs={{128,0},{192,64},{0,128},{64,192},{129,1},{193,65},{1,129},{65,193... | collective-permute-start | bytes 196616 | tf_op jit(solution)/shard_map/ppermute | solution.py:37
  139.1 2.8 %collective-permute-start.20 = (bf16[8,4096]{1,0:T(8,128)(2,1)S(1)}, bf16[8,4096]{1,0:T(8,128)(2,1)S(1)}, u32[]{:S(2)}, u32[]{:S(2)}) collective-permute-start(bf16[8,4096]{1,0:T(8,128)(2,1)S(1)} %get-tuple-element.31), channel_id=1, source_target_pairs={{192,0},{0,64},{64,128},{128,192},{193,1},{1,65},{65,129},{129,193... | collective-permute-start | bytes 196616 | tf_op jit(solution)/shard_map/ppermute | solution.py:37
  141.9 1.3 collective-permute-start.21
  143.2 1.9 %collective-permute-done.19.refs_0_ = bf16[8,4096]{1,0:T(8,128)(2,1)S(1)} collective-permute-done((bf16[8,4096]{1,0:T(8,128)(2,1)S(1)}, bf16[8,4096]{1,0:T(8,128)(2,1)S(1)}, u32[]{:S(2)}, u32[]{:S(2)}) %collective-permute-start.19) | collective-permute-done | bytes 65568 | tf_op jit(solution)/shard_map/ppermute | solution.py:37
  145.1 1.4 collective-permute-done.20.refs_1_
  146.6 1.3 collective-permute-done.21.refs_2_
  (51 shorter events, 12.3 us)
Async XLA Ops:
  0.0 18.2 %collective-permute-start = (bf16[512,256]{1,0:T(8,128)(2,1)}, bf16[512,256]{1,0:T(8,128)(2,1)S(1)}, u32[]{:S(2)}, u32[]{:S(2)}) collective-permute-start(bf16[512,256]{1,0:T(8,128)(2,1)} %own.1), channel_id=1, source_target_pairs={{0,16},{16,0},{1,17},{17,1},{2,18},{18,2},{3,19},{19,3},{4,20},{20... | collective-permute-start | bytes 786440 | tf_op jit(solution)/shard_map/ppermute | solution.py:33
  0.8 12.7 %collective-permute-start.2 = (bf16[128,512]{1,0:T(8,128)(2,1)}, bf16[128,512]{1,0:T(8,128)(2,1)S(1)}, u32[]{:S(2)}, u32[]{:S(2)}) collective-permute-start(bf16[128,512]{1,0:T(8,128)(2,1)} %context.1), channel_id=1, source_target_pairs={{64,0},{96,32},{128,64},{160,96},{192,128},{224,160},{0,192},{32,2... | collective-permute-start | bytes 393224 | tf_op jit(solution)/shard_map/ppermute | solution.py:37
  7.1 11.0 %collective-permute-start.5 = (bf16[128,512]{1,0:T(8,128)(2,1)}, bf16[128,512]{1,0:T(8,128)(2,1)S(1)}, u32[]{:S(2)}, u32[]{:S(2)}) collective-permute-start(bf16[128,512]{1,0:T(8,128)(2,1)} %context.1), channel_id=1, source_target_pairs={{192,0},{224,32},{0,64},{32,96},{64,128},{96,160},{128,192},{160,2... | collective-permute-start | bytes 393224 | tf_op jit(solution)/shard_map/ppermute | solution.py:37
  7.1 15.0 %collective-permute-start.1 = (bf16[128,512]{1,0:T(8,128)(2,1)}, bf16[128,512]{1,0:T(8,128)(2,1)S(1)}, u32[]{:S(2)}, u32[]{:S(2)}) collective-permute-start(bf16[128,512]{1,0:T(8,128)(2,1)} %context.1), channel_id=1, source_target_pairs={{32,0},{64,32},{96,64},{128,96},{160,128},{192,160},{224,192},{0,2... | collective-permute-start | bytes 393224 | tf_op jit(solution)/shard_map/ppermute | solution.py:37
  10.8 11.3 %collective-permute-start.7 = (bf16[128,512]{1,0:T(8,128)(2,1)}, bf16[128,512]{1,0:T(8,128)(2,1)S(1)}, u32[]{:S(2)}, u32[]{:S(2)}) collective-permute-start(bf16[128,512]{1,0:T(8,128)(2,1)} %context.1), channel_id=1, source_target_pairs={{224,0},{0,32},{32,64},{64,96},{96,128},{128,160},{160,192},{192,2... | collective-permute-start | bytes 393224 | tf_op jit(solution)/shard_map/ppermute | solution.py:37
  13.5 9.0 %collective-permute-start.4 = (bf16[128,512]{1,0:T(8,128)(2,1)S(1)}, bf16[128,512]{1,0:T(8,128)(2,1)S(1)}, u32[]{:S(2)}, u32[]{:S(2)}) collective-permute-start(bf16[128,512]{1,0:T(8,128)(2,1)S(1)} %collective-permute-done.2.refs_2_), channel_id=1, source_target_pairs={{64,0},{96,32},{128,64},{160,96},{192,128},{224,160},{0,192},{32,2... | collective-permute-start | bytes 393224 | tf_op jit(solution)/shard_map/ppermute | solution.py:37
  18.2 6.6 %collective-permute-start.3 = (bf16[128,512]{1,0:T(8,128)(2,1)S(1)}, bf16[128,512]{1,0:T(8,128)(2,1)S(1)}, u32[]{:S(2)}, u32[]{:S(2)}) collective-permute-start(bf16[128,512]{1,0:T(8,128)(2,1)S(1)} %collective-permute-done.2.refs_2_), channel_id=1, source_target_pairs={{32,0},{64,32},{96,64},{128,96},{160,128},{192,160},{224,192},{0,2... | collective-permute-start | bytes 393224 | tf_op jit(solution)/shard_map/ppermute | solution.py:37
  18.2 6.6 %collective-permute-start.6 = (bf16[128,512]{1,0:T(8,128)(2,1)S(1)}, bf16[128,512]{1,0:T(8,128)(2,1)S(1)}, u32[]{:S(2)}, u32[]{:S(2)}) collective-permute-start(bf16[128,512]{1,0:T(8,128)(2,1)S(1)} %collective-permute-done.5.refs_6_), channel_id=1, source_target_pairs={{224,0},{0,32},{32,64},{64,96},{96,128},{128,160},{160,192},{192,2... | collective-permute-start | bytes 393224 | tf_op jit(solution)/shard_map/ppermute | solution.py:37
  24.8 65.9 %copy-start.2 = (bf16[1,384,4096]{2,1,0:T(8,128)(2,1)S(1)}, bf16[1,384,4096]{2,1,0:T(8,128)(2,1)}, u32[]{:S(2)}) copy-start(bf16[1,384,4096]{2,1,0:T(8,128)(2,1)} %w_down.5) | copy-start | bytes 9437188
  25.5 2.0 %collective-permute-start.8 = (bf16[8,64,512]{2,1,0:T(8,128)(2,1)S(1)}, bf16[8,64,512]{2,1,0:T(8,128)(2,1)S(1)}, u32[]{:S(2)}, u32[]{:S(2)}) collective-permute-start(bf16[8,64,512]{2,1,0:T(8,128)(2,1)S(1)} %get-tuple-element.22), channel_id=1, source_target_pairs={{0,1},{1,0},{2,3},{3,2},{4,5},{5,4},{6,7},{7,6},{8,9},{9,8},{10,11... | collective-permute-start | bytes 1572872 | tf_op jit(solution)/shard_map/ppermute | solution.py:33
  27.6 63.0 %copy-start.1 = (bf16[1,4096,384]{2,1,0:T(8,128)(2,1)S(1)}, bf16[1,4096,384]{2,1,0:T(8,128)(2,1)}, u32[]{:S(2)}) copy-start(bf16[1,4096,384]{2,1,0:T(8,128)(2,1)} %w_up.5) | copy-start | bytes 9437188
  44.2 7.6 %collective-permute-start.13 = (bf16[72,512]{1,0:T(8,128)(2,1)S(1)}, bf16[72,512]{1,0:T(8,128)(2,1)S(1)}, u32[]{:S(2)}, u32[]{:S(2)}) collective-permute-start(bf16[72,512]{1,0:T(8,128)(2,1)S(1)} %shard_map.85.refs_0_), channel_id=1, source_target_pairs={{192,0},{224,32},{0,64},{32,96},{64,128},{96,160},{128,192},{160,2... | collective-permute-start | bytes 221192 | tf_op jit(solution)/shard_map/ppermute | solution.py:37
  44.8 7.1 %collective-permute-start.10 = (bf16[72,512]{1,0:T(8,128)(2,1)S(1)}, bf16[72,512]{1,0:T(8,128)(2,1)S(1)}, u32[]{:S(2)}, u32[]{:S(2)}) collective-permute-start(bf16[72,512]{1,0:T(8,128)(2,1)S(1)} %shard_map.85.refs_0_), channel_id=1, source_target_pairs={{64,0},{96,32},{128,64},{160,96},{192,128},{224,160},{0,192},{32,2... | collective-permute-start | bytes 221192 | tf_op jit(solution)/shard_map/ppermute | solution.py:37
  48.4 7.9 %collective-permute-start.15 = (bf16[72,512]{1,0:T(8,128)(2,1)S(1)}, bf16[72,512]{1,0:T(8,128)(2,1)S(1)}, u32[]{:S(2)}, u32[]{:S(2)}) collective-permute-start(bf16[72,512]{1,0:T(8,128)(2,1)S(1)} %shard_map.85.refs_0_), channel_id=1, source_target_pairs={{224,0},{0,32},{32,64},{64,96},{96,128},{128,160},{160,192},{192,2... | collective-permute-start | bytes 221192 | tf_op jit(solution)/shard_map/ppermute | solution.py:37
  48.8 7.6 %collective-permute-start.9 = (bf16[72,512]{1,0:T(8,128)(2,1)S(1)}, bf16[72,512]{1,0:T(8,128)(2,1)S(1)}, u32[]{:S(2)}, u32[]{:S(2)}) collective-permute-start(bf16[72,512]{1,0:T(8,128)(2,1)S(1)} %shard_map.85.refs_0_), channel_id=1, source_target_pairs={{32,0},{64,32},{96,64},{128,96},{160,128},{192,160},{224,192},{0,2... | collective-permute-start | bytes 221192 | tf_op jit(solution)/shard_map/ppermute | solution.py:37
  51.8 5.6 %collective-permute-start.14 = (bf16[72,512]{1,0:T(8,128)(2,1)S(1)}, bf16[72,512]{1,0:T(8,128)(2,1)S(1)}, u32[]{:S(2)}, u32[]{:S(2)}) collective-permute-start(bf16[72,512]{1,0:T(8,128)(2,1)S(1)} %collective-permute-done.13.refs_6_), channel_id=1, source_target_pairs={{224,0},{0,32},{32,64},{64,96},{96,128},{128,160},{160,192},{192,2... | collective-permute-start | bytes 221192 | tf_op jit(solution)/shard_map/ppermute | solution.py:37
  51.8 6.8 %collective-permute-start.12 = (bf16[72,512]{1,0:T(8,128)(2,1)S(1)}, bf16[72,512]{1,0:T(8,128)(2,1)S(1)}, u32[]{:S(2)}, u32[]{:S(2)}) collective-permute-start(bf16[72,512]{1,0:T(8,128)(2,1)S(1)} %collective-permute-done.10.refs_2_), channel_id=1, source_target_pairs={{64,0},{96,32},{128,64},{160,96},{192,128},{224,160},{0,192},{32,2... | collective-permute-start | bytes 221192 | tf_op jit(solution)/shard_map/ppermute | solution.py:37
  56.3 4.4 %collective-permute-start.11 = (bf16[72,512]{1,0:T(8,128)(2,1)S(1)}, bf16[72,512]{1,0:T(8,128)(2,1)S(1)}, u32[]{:S(2)}, u32[]{:S(2)}) collective-permute-start(bf16[72,512]{1,0:T(8,128)(2,1)S(1)} %collective-permute-done.10.refs_2_), channel_id=1, source_target_pairs={{32,0},{64,32},{96,64},{128,96},{160,128},{192,160},{224,192},{0,2... | collective-permute-start | bytes 221192 | tf_op jit(solution)/shard_map/ppermute | solution.py:37
  90.7 4.2 %collective-permute-start.16 = (bf16[256,4096]{1,0:T(8,128)(2,1)S(1)}, bf16[256,4096]{1,0:T(8,128)(2,1)S(1)}, u32[]{:S(2)}, u32[]{:S(2)}) collective-permute-start(bf16[256,4096]{1,0:T(8,128)(2,1)S(1)} %bitcast.8), channel_id=1, source_target_pairs={{0,1},{1,0},{2,3},{3,2},{4,5},{5,4},{6,7},{7,6},{8,9},{9,8},{10,11... | collective-permute-start | bytes 6291464 | tf_op jit(solution)/shard_map/ppermute | solution.py:33
  96.8 2.7 %collective-permute-start.18 = (bf16[128,4096]{1,0:T(8,128)(2,1)S(1)}, bf16[128,4096]{1,0:T(8,128)(2,1)S(1)}, u32[]{:S(2)}, u32[]{:S(2)}) collective-permute-start(bf16[128,4096]{1,0:T(8,128)(2,1)S(1)} %shard_map.89), channel_id=1, source_target_pairs={{0,1},{1,0},{2,3},{3,2},{4,5},{5,4},{6,7},{7,6},{8,9},{9,8},{10,11... | collective-permute-start | bytes 3145736 | tf_op jit(solution)/shard_map/ppermute | solution.py:33
  98.9 2.8 %collective-permute-start.17 = (bf16[128,4096]{1,0:T(8,128)(2,1)S(1)}, bf16[128,4096]{1,0:T(8,128)(2,1)S(1)}, u32[]{:S(2)}, u32[]{:S(2)}) collective-permute-start(bf16[128,4096]{1,0:T(8,128)(2,1)S(1)} %shard_map.88), channel_id=1, source_target_pairs={{0,1},{1,0},{2,3},{3,2},{4,5},{5,4},{6,7},{7,6},{8,9},{9,8},{10,11... | collective-permute-start | bytes 3145736 | tf_op jit(solution)/shard_map/ppermute | solution.py:33
  136.1 9.1 %collective-permute-start.19 = (bf16[8,4096]{1,0:T(8,128)(2,1)S(1)}, bf16[8,4096]{1,0:T(8,128)(2,1)S(1)}, u32[]{:S(2)}, u32[]{:S(2)}) collective-permute-start(bf16[8,4096]{1,0:T(8,128)(2,1)S(1)} %get-tuple-element.30), channel_id=1, source_target_pairs={{128,0},{192,64},{0,128},{64,192},{129,1},{193,65},{1,129},{65,193... | collective-permute-start | bytes 196616 | tf_op jit(solution)/shard_map/ppermute | solution.py:37
  139.1 7.5 %collective-permute-start.20 = (bf16[8,4096]{1,0:T(8,128)(2,1)S(1)}, bf16[8,4096]{1,0:T(8,128)(2,1)S(1)}, u32[]{:S(2)}, u32[]{:S(2)}) collective-permute-start(bf16[8,4096]{1,0:T(8,128)(2,1)S(1)} %get-tuple-element.31), channel_id=1, source_target_pairs={{192,0},{0,64},{64,128},{128,192},{193,1},{1,65},{65,129},{129,193... | collective-permute-start | bytes 196616 | tf_op jit(solution)/shard_map/ppermute | solution.py:37
  141.9 6.0 %collective-permute-start.21 = (bf16[8,4096]{1,0:T(8,128)(2,1)S(1)}, bf16[8,4096]{1,0:T(8,128)(2,1)S(1)}, u32[]{:S(2)}, u32[]{:S(2)}) collective-permute-start(bf16[8,4096]{1,0:T(8,128)(2,1)S(1)} %get-tuple-element.32), channel_id=1, source_target_pairs={{64,0},{128,64},{192,128},{0,192},{65,1},{129,65},{193,129},{1,193... | collective-permute-start | bytes 196616 | tf_op jit(solution)/shard_map/ppermute | solution.py:37
  (6 other events, 104.3 us)
